TPU v7x, 32 devices: a whole 2x2x4 slice. The times are simulated.
32 devices in a mesh: blk: 8 (over y, x, core), head: 4 (over z).
Axes of the slice: x: 2, y: 2, z: 4, core: 2. Of those that a mesh axis runs over, the one named last changes fastest.
Arguments:
- queries: bfloat16 [4096, 3072], P(('blk', 'head')), may hold values from -100 to 100
- keys: bfloat16 [4096, 3072], P(('blk', 'head')), may hold values from -100 to 100
- values: bfloat16 [4096, 3072], P(('blk', 'head')), may hold values from -6 to 6
- query_gain: float32 [3072], replicated, may hold values from 1 to 4
- key_gain: float32 [3072], replicated, may hold values from 0.1 to 1.9
Outputs:
- attended: bfloat16 [4096, 3072], P(('blk', 'head'))
All inputs are finite; a program needn't handle non-finite values.
Results may differ from a plain program's by a relative error of at most 0.0075.
The roundings to bfloat16 on the way count: a program that leaves them out, or rounds other values in their place, can miss the bound.
Values may be sent and summed in bfloat16 or wider, within the bound.
No kernel may reach another device: no remote copies, remote signals or barrier semaphores. Data moves between devices by JAX's collectives and lax.ppermute only.
A program may use at most 128 MiB of HBM per device.

v0:
```python
import math

import jax
import jax.numpy as jnp
from jax import lax
from jax.sharding import PartitionSpec as P

HEAD_DIM = 128


def normalize(block, gain):
    wide = block.astype(jnp.float32)
    mean_sq = jnp.mean(wide * wide, axis=-1, keepdims=True)
    return (wide * lax.rsqrt(mean_sq + 1e-06) * gain).astype(jnp.bfloat16)


def absorb(carry, pieces, q_heads, factor):
    run_max, run_sum, accum = carry
    key_block, value_block = pieces
    scores = (
        jnp.einsum("qhd,khd->hqk", q_heads, key_block, preferred_element_type=jnp.float32) * factor
    )
    new_max = jnp.maximum(run_max, jnp.max(scores, axis=-1))
    shrink = jnp.exp(run_max - new_max)
    weights = jnp.exp(scores - new_max[:, :, None])
    new_sum = run_sum * shrink + jnp.sum(weights, axis=-1)
    mixed = jnp.einsum(
        "hqk,khd->hqd",
        weights.astype(jnp.bfloat16),
        value_block,
        preferred_element_type=jnp.float32,
    )
    return (new_max, new_sum, accum * shrink[:, :, None] + mixed)


def shards(queries, keys, values, query_gain, key_gain):
    group = lax.axis_size("head")
    width = queries.shape[1] // group
    heads_here = width // HEAD_DIM
    factor = 1.0 / math.sqrt(HEAD_DIM)
    first_part = normalize(queries, query_gain)
    second_part = normalize(keys, key_gain)
    q_local, k_local, v_local = (
        lax.all_to_all(first_part, "head", split_axis=1, concat_axis=0, tiled=True),
        lax.all_to_all(second_part, "head", split_axis=1, concat_axis=0, tiled=True),
        lax.all_to_all(values, "head", split_axis=1, concat_axis=0, tiled=True),
    )
    rows = q_local.shape[0]
    q_heads = q_local.reshape(rows, heads_here, HEAD_DIM)
    k_heads = k_local.reshape(rows, heads_here, HEAD_DIM)
    v_heads = v_local.reshape(rows, heads_here, HEAD_DIM)
    start_state = (
        jnp.full((heads_here, rows), -jnp.inf, jnp.float32),
        jnp.zeros((heads_here, rows), jnp.float32),
        jnp.zeros((heads_here, rows, HEAD_DIM), jnp.float32),
    )
    key_piece = lax.all_gather(k_heads, "blk", axis=0, tiled=True)
    value_piece = lax.all_gather(v_heads, "blk", axis=0, tiled=True)
    length = key_piece.shape[0]
    block_rows = math.gcd(length, 1024)
    count = length // block_rows
    key_blocks = key_piece.reshape(count, block_rows, heads_here, HEAD_DIM)
    value_blocks = value_piece.reshape(count, block_rows, heads_here, HEAD_DIM)

    def step_fn(state, blocks):
        return (absorb(state, blocks, q_heads, factor), None)

    final_state, unused = lax.scan(step_fn, start_state, (key_blocks, value_blocks))
    run_max, run_sum, accum = final_state
    result = accum / run_sum[:, :, None]
    result = jnp.transpose(result, (1, 0, 2)).reshape(rows, width).astype(jnp.bfloat16)
    return lax.all_to_all(result, "head", split_axis=0, concat_axis=1, tiled=True)


def solution(mesh):
    placed = (
        P(("blk", "head"), None),
        P(("blk", "head"), None),
        P(("blk", "head"), None),
        P(),
        P(),
    )
    return jax.shard_map(
        shards, mesh=mesh, in_specs=placed, out_specs=P(("blk", "head"), None), check_vma=False
    )
```

profile of v0, /device:TPU:0, one launch (start us, length us, event | category | flops | bytes accessed | tf_op | source)
XLA Modules:
  0.0 259.3 jit_solution(10543328005862081896)
XLA Ops:
  6.5 1.4 fusion.21
  7.9 1.4 fusion.23
  9.7 26.2 %all_to_all.64 = bf16[128,4,768]{0,2,1:T(8,128)(2,1)S(1)} all-to-all(bf16[128,4,768]{0,2,1:T(8,128)(2,1)S(1)} %bitcast.63), channel_id=1, replica_groups=mesh['blk'=8,'head'=4] {'head'}, dimensions={1} | all-to-all | bytes 1572864 | tf_op jit(solution)/shard_map/all_to_all | solution.py:45
  35.9 0.6 copy.31
  36.6 1.2 reshape.54
  38.2 22.2 %all_to_all.65 = bf16[128,4,768]{0,2,1:T(8,128)(2,1)S(1)} all-to-all(bf16[128,4,768]{0,2,1:T(8,128)(2,1)S(1)} %bitcast.67), channel_id=1, replica_groups=mesh['blk'=8,'head'=4] {'head'}, dimensions={1} | all-to-all | bytes 1572864 | tf_op jit(solution)/shard_map/all_to_all | solution.py:46
  60.4 0.6 copy.36
  61.0 1.2 reshape.57
  63.0 1.2 copy.33
  64.2 3.7 %all-to-all-start.1 = ((bf16[128,4,768]{0,2,1:T(8,128)(2,1)}), bf16[128,4,768]{0,2,1:T(8,128)(2,1)S(1)}, u32[]{:S(2)}, u32[]{:S(2)}) async-start(bf16[128,4,768]{0,2,1:T(8,128)(2,1)} %bitcast.3), calls=%async_computation.1 | async-start | bytes 1572864 | tf_op jit(solution)/shard_map/all_to_all | solution.py:44
  67.9 18.7 %all-to-all-done.1 = bf16[128,4,768]{0,2,1:T(8,128)(2,1)S(1)} async-done(((bf16[128,4,768]{0,2,1:T(8,128)(2,1)}), bf16[128,4,768]{0,2,1:T(8,128)(2,1)S(1)}, u32[]{:S(2)}, u32[]{:S(2)}) %all-to-all-start.1) | async-done | bytes 786464 | tf_op jit(solution)/shard_map/all_to_all | solution.py:44
  86.6 0.6 copy.34
  87.2 1.2 reshape.56
  88.5 1.5 copy.39
  90.0 8.7 %copy.32 = bf16[4096,6,128]{2,0,1:T(8,128)(2,1)} copy(bf16[4096,6,128]{0,2,1:T(8,128)(2,1)} %all-gather.3.cloned.1.call-done) | data formatting | bytes 12582912 | tf_op jit(solution)/shard_map/all_gather | solution.py:57
  98.7 33.6 %all-gather.5.cloned.1.call-done = bf16[4096,6,128]{0,2,1:T(8,128)(2,1)} async-done(((bf16[512,6,128]{0,2,1:T(8,128)(2,1)}), bf16[4096,6,128]{0,2,1:T(8,128)(2,1)}) %all-gather.5.cloned.1.call-update) | async-done | bytes 6291472 | tf_op jit(solution)/shard_map/all_gather | solution.py:58
  132.3 8.7 %copy.37 = bf16[4096,6,128]{2,0,1:T(8,128)(2,1)} copy(bf16[4096,6,128]{0,2,1:T(8,128)(2,1)} %all-gather.5.cloned.1.call-done) | data formatting | bytes 12582912 | tf_op jit(solution)/shard_map/all_gather | solution.py:58
  140.9 84.4 %while.15 = (s32[]{:T(128)}, f32[6,512]{1,0:T(8,128)S(1)}, f32[6,512]{1,0:T(8,128)S(1)}, f32[6,512,128]{2,1,0:T(8,128)S(1)}, bf16[4,1024,6,128]{3,1,0,2:T(8,128)...) while((s32[]{:T(128)}, f32[6,512]{1,0:T(8,128)S(1)}, ...), condition=%wide.region_5.6_spmd.clone, body=%wide.region_2.5_spmd.clone.sunk | while | flops 1636973568 | bytes 45024360 | solution.py:68
  140.9 7.8 %bitcast_reduce_fusion.2 = (f32[6,512]{1,0:T(8,128)S(1)}, f32[6,1024,512]{2,1,0:T(8,128)}) fusion(bf16[512,6,128]{2,0,1:T(8,128)(2,1)S(1)} %get-tuple-element.182, bf16[4,1024,6,128]{3,1,0,2:T(8,128)(2,1)} %get-tuple-element.181, s32[]{:T(128)} %get-tuple-element.168), kind=kOutput, calls=%fused_computation.1.clone.1 | convolution fusion | flops 811594752 | bytes 14955008 | tf_op jit(solution)/shard_map/while/body/eval_jaxpr/qhd,khd->hqk/dot_general | solution.py:21
  148.7 6.6 %fusion.38 = f32[6,512]{1,0:T(8,128)S(1)} fusion(f32[6,1024,512]{2,1,0:T(8,128)} %get-tuple-element.156, f32[6,512]{1,0:T(8,128)S(1)} %select_maximum_fusion.2), kind=kLoop, calls=%fused_computation.4.clone.1 | loop fusion | flops 9434112 | bytes 12607488 | tf_op jit(solution)/shard_map/while/body/eval_jaxpr/reduce_sum | solution.py:26
  155.3 6.6 %fusion.40 = f32[6,512,128]{2,1,0:T(8,128)S(1)} fusion(f32[6,512,128]{2,1,0:T(8,128)S(1)} %get-tuple-element.171, bf16[4,1024,6,128]{3,1,0,2:T(8,128)(2,1)} %get-tuple-element.183, s32[]{:T(128)} %get-tuple-element.168, f32[6,1024,512]{2,1,0:T(8,128)} %get-tuple-element.156, f32[6,512]{1,0:T(8,128)S(1)} %select_maximum_fusion.2, ...), kind=kOutput, calls=%fused_computation.12.clone.1 | convolution fusion | flops 815923200 | bytes 17326592 | tf_op jit(solution)/shard_map/while/body/eval_jaxpr/hqk,khd->hqd/dot_general | solution.py:27
  162.0 7.8 %bitcast_reduce_fusion.2 = (f32[6,512]{1,0:T(8,128)S(1)}, f32[6,1024,512]{2,1,0:T(8,128)}) fusion(bf16[512,6,128]{2,0,1:T(8,128)(2,1)S(1)} %get-tuple-element.182, bf16[4,1024,6,128]{3,1,0,2:T(8,128)(2,1)} %get-tuple-element.181, s32[]{:T(128)} %get-tuple-element.168), kind=kOutput, calls=%fused_computation.1.clone.1 | convolution fusion | flops 811594752 | bytes 14955008 | tf_op jit(solution)/shard_map/while/body/eval_jaxpr/qhd,khd->hqk/dot_general | solution.py:21
  169.8 6.6 %fusion.38 = f32[6,512]{1,0:T(8,128)S(1)} fusion(f32[6,1024,512]{2,1,0:T(8,128)} %get-tuple-element.156, f32[6,512]{1,0:T(8,128)S(1)} %select_maximum_fusion.2), kind=kLoop, calls=%fused_computation.4.clone.1 | loop fusion | flops 9434112 | bytes 12607488 | tf_op jit(solution)/shard_map/while/body/eval_jaxpr/reduce_sum | solution.py:26
  176.4 6.6 %fusion.40 = f32[6,512,128]{2,1,0:T(8,128)S(1)} fusion(f32[6,512,128]{2,1,0:T(8,128)S(1)} %get-tuple-element.171, bf16[4,1024,6,128]{3,1,0,2:T(8,128)(2,1)} %get-tuple-element.183, s32[]{:T(128)} %get-tuple-element.168, f32[6,1024,512]{2,1,0:T(8,128)} %get-tuple-element.156, f32[6,512]{1,0:T(8,128)S(1)} %select_maximum_fusion.2, ...), kind=kOutput, calls=%fused_computation.12.clone.1 | convolution fusion | flops 815923200 | bytes 17326592 | tf_op jit(solution)/shard_map/while/body/eval_jaxpr/hqk,khd->hqd/dot_general | solution.py:27
  183.1 7.8 %bitcast_reduce_fusion.2 = (f32[6,512]{1,0:T(8,128)S(1)}, f32[6,1024,512]{2,1,0:T(8,128)}) fusion(bf16[512,6,128]{2,0,1:T(8,128)(2,1)S(1)} %get-tuple-element.182, bf16[4,1024,6,128]{3,1,0,2:T(8,128)(2,1)} %get-tuple-element.181, s32[]{:T(128)} %get-tuple-element.168), kind=kOutput, calls=%fused_computation.1.clone.1 | convolution fusion | flops 811594752 | bytes 14955008 | tf_op jit(solution)/shard_map/while/body/eval_jaxpr/qhd,khd->hqk/dot_general | solution.py:21
  190.9 6.6 %fusion.38 = f32[6,512]{1,0:T(8,128)S(1)} fusion(f32[6,1024,512]{2,1,0:T(8,128)} %get-tuple-element.156, f32[6,512]{1,0:T(8,128)S(1)} %select_maximum_fusion.2), kind=kLoop, calls=%fused_computation.4.clone.1 | loop fusion | flops 9434112 | bytes 12607488 | tf_op jit(solution)/shard_map/while/body/eval_jaxpr/reduce_sum | solution.py:26
  197.5 6.6 %fusion.40 = f32[6,512,128]{2,1,0:T(8,128)S(1)} fusion(f32[6,512,128]{2,1,0:T(8,128)S(1)} %get-tuple-element.171, bf16[4,1024,6,128]{3,1,0,2:T(8,128)(2,1)} %get-tuple-element.183, s32[]{:T(128)} %get-tuple-element.168, f32[6,1024,512]{2,1,0:T(8,128)} %get-tuple-element.156, f32[6,512]{1,0:T(8,128)S(1)} %select_maximum_fusion.2, ...), kind=kOutput, calls=%fused_computation.12.clone.1 | convolution fusion | flops 815923200 | bytes 17326592 | tf_op jit(solution)/shard_map/while/body/eval_jaxpr/hqk,khd->hqd/dot_general | solution.py:27
  204.2 7.8 %bitcast_reduce_fusion.2 = (f32[6,512]{1,0:T(8,128)S(1)}, f32[6,1024,512]{2,1,0:T(8,128)}) fusion(bf16[512,6,128]{2,0,1:T(8,128)(2,1)S(1)} %get-tuple-element.182, bf16[4,1024,6,128]{3,1,0,2:T(8,128)(2,1)} %get-tuple-element.181, s32[]{:T(128)} %get-tuple-element.168), kind=kOutput, calls=%fused_computation.1.clone.1 | convolution fusion | flops 811594752 | bytes 14955008 | tf_op jit(solution)/shard_map/while/body/eval_jaxpr/qhd,khd->hqk/dot_general | solution.py:21
  212.0 6.6 %fusion.38 = f32[6,512]{1,0:T(8,128)S(1)} fusion(f32[6,1024,512]{2,1,0:T(8,128)} %get-tuple-element.156, f32[6,512]{1,0:T(8,128)S(1)} %select_maximum_fusion.2), kind=kLoop, calls=%fused_computation.4.clone.1 | loop fusion | flops 9434112 | bytes 12607488 | tf_op jit(solution)/shard_map/while/body/eval_jaxpr/reduce_sum | solution.py:26
  218.6 6.6 %fusion.40 = f32[6,512,128]{2,1,0:T(8,128)S(1)} fusion(f32[6,512,128]{2,1,0:T(8,128)S(1)} %get-tuple-element.171, bf16[4,1024,6,128]{3,1,0,2:T(8,128)(2,1)} %get-tuple-element.183, s32[]{:T(128)} %get-tuple-element.168, f32[6,1024,512]{2,1,0:T(8,128)} %get-tuple-element.156, f32[6,512]{1,0:T(8,128)S(1)} %select_maximum_fusion.2, ...), kind=kOutput, calls=%fused_computation.12.clone.1 | convolution fusion | flops 815923200 | bytes 17326592 | tf_op jit(solution)/shard_map/while/body/eval_jaxpr/hqk,khd->hqd/dot_general | solution.py:27
  226.4 24.9 %all_to_all.66 = bf16[4,128,768]{1,2,0:T(8,128)(2,1)S(1)} all-to-all(bf16[4,128,768]{1,2,0:T(8,128)(2,1)S(1)} %copy.42), channel_id=1, replica_groups=mesh['blk'=8,'head'=4] {'head'}, dimensions={0} | all-to-all | bytes 1572864 | tf_op jit(solution)/shard_map/all_to_all | solution.py:72
  251.3 1.2 copy.43
  (36 shorter events, 2.8 us)
Async XLA Ops:
  6.5 83.5 %all-gather.3.cloned.1.call-start = ((), (), s32[]{:S(2)}) async-start(), calls=%async_computation.4 | async-start | bytes 7077888 | tf_op jit(solution)/shard_map/all_gather | solution.py:57
  36.5 1.3 copy-start.1
  37.8 94.5 %all-gather.5.cloned.1.call-start = ((), (), s32[]{:S(2)}) async-start(), calls=%async_computation.5 | async-start | bytes 7077888 | tf_op jit(solution)/shard_map/all_gather | solution.py:58
  61.0 1.5 copy-start
  61.0 1.8 copy-start.2
  64.2 22.4 %all-to-all-start.1 = ((bf16[128,4,768]{0,2,1:T(8,128)(2,1)}), bf16[128,4,768]{0,2,1:T(8,128)(2,1)S(1)}, u32[]{:S(2)}, u32[]{:S(2)}) async-start(bf16[128,4,768]{0,2,1:T(8,128)(2,1)} %bitcast.3), calls=%async_computation.1 | async-start | bytes 1572864 | tf_op jit(solution)/shard_map/all_to_all | solution.py:44
Sparse Core Ops, SparseCore 0:
  37.9 45.7 all-gather.2
  85.6 46.6 all-gather.4
where the time goes:
time: 260 us; the launch traced here: 259 us
  blocking collectives  73.3 us (28%)
  matrix products  57.6 us (22%)
  waiting for transfers between devices  52.3 us (20%)
  other arithmetic  30.4 us (12%)
  local copies, waits for them, and re-layouts  28.2 us (11%)
  between operations  13.6 us (5%)
  starting transfers between devices  3.72 us (1%)
    all_gather x1, waiting for transfers between devices, shards(): value_piece = lax.all_gather(v_heads, 'blk', axis=0, tiled=True)  33.6 us
    dot_general x4, matrix products, absorb(): jnp.einsum('qhd,khd->hqk', q_heads, key_block, preferred_element_type=jnp...  31.1 us
    dot_general x4, matrix products, absorb(): jnp.einsum('hqk,khd->hqd', weights.astype(jnp.bfloat16), value_block, pre...  26.6 us
    reduce_sum x4, other arithmetic, absorb(): new_sum = run_sum * shrink + jnp.sum(weights, axis=-1)  26.5 us
    all_to_all x1, blocking collectives, shards(): lax.all_to_all(second_part, 'head', split_axis=1, concat_axis=0, tiled=True)  26.2 us
    all_to_all x1, blocking collectives, shards(): lax.all_to_all(result, 'head', split_axis=0, concat_axis=1, tiled=True)  24.9 us
    all_to_all x1, blocking collectives, shards(): lax.all_to_all(values, 'head', split_axis=1, concat_axis=0, tiled=True)  22.2 us
    all_to_all x1, waiting for transfers between devices, shards(): lax.all_to_all(first_part, 'head', split_axis=1, concat_axis=0, tiled=True)  18.7 us
  transfers between devices with their start and end apart: 3, of which 2 were waited for; matrix products, arithmetic and copies ran while one was open for 6% of the time, Pallas kernels for 0%

commit v1 on v0

v1 whole, which is shorter than its diff:
```python
import functools
import math

import jax
import jax.numpy as jnp
from jax import lax
from jax.experimental import pallas as pl
from jax.experimental.pallas import tpu as pltpu
from jax.sharding import PartitionSpec as P

HEAD_DIM = 128
AXES = ("blk", "head")
BF16 = jnp.bfloat16
F32 = jnp.float32
VMEM = pl.BlockSpec(memory_space=pltpu.VMEM)
PARAMS = pltpu.CompilerParams(vmem_limit_bytes=40 * 2**20)
EXPONENT = math.log2(math.e) / math.sqrt(HEAD_DIM)


def sds(*shape):
    return jax.ShapeDtypeStruct(shape, BF16)


def call(body, outs, *args, flops=0, exps=0):
    size = sum(math.prod(a.shape) * a.dtype.itemsize for a in (*args, *outs))
    return pl.pallas_call(
        body,
        out_shape=outs,
        in_specs=[VMEM] * len(args),
        out_specs=[VMEM] * len(outs),
        compiler_params=PARAMS,
        cost_estimate=pl.CostEstimate(flops=flops, bytes_accessed=size, transcendentals=exps),
    )(*args)


def attend_rows(q, keys, values):
    top = total = accum = None
    for k_ref, v_ref in zip(keys, values):
        scores = lax.dot_general(
            q, k_ref[...], (((1,), (1,)), ((), ())), preferred_element_type=F32
        )
        new_top = jnp.max(scores, axis=1, keepdims=True)
        if top is not None:
            new_top = jnp.maximum(top, new_top)
        weights = jnp.exp2((scores - new_top) * EXPONENT)
        part = jnp.sum(weights, axis=1, keepdims=True)
        mixed = jnp.dot(weights.astype(BF16), v_ref[...], preferred_element_type=F32)
        if top is None:
            total, accum = part, mixed
        else:
            shrink = jnp.exp2((top - new_top) * EXPONENT)
            total, accum = total * shrink + part, accum * shrink + mixed
        top = new_top
    return accum / total


def attend_body(slots, blocks, *refs):
    queries, refs = refs[:slots], refs[slots:]
    keys, values, outs = refs[:blocks], refs[blocks : 2 * blocks], refs[2 * blocks :]
    rows = queries[0].shape[0]
    for first in range(0, slots, 2):
        pair = queries[first : first + 2]
        q = jnp.concatenate([ref[...] for ref in pair], axis=0)
        result = attend_rows(q, keys, values).astype(BF16)
        for place in range(len(pair)):
            outs[first + place][...] = result[place * rows : (place + 1) * rows]


def attend(queries, keys, values):
    outs = [sds(*q.shape) for q in queries]
    pairs = sum(q.shape[0] for q in queries) * sum(k.shape[0] for k in keys)
    return call(
        functools.partial(attend_body, len(queries), len(keys)),
        outs,
        *queries,
        *keys,
        *values,
        flops=4 * pairs * HEAD_DIM,
        exps=pairs,
    )


def core_index():
    return lax.rem(lax.axis_index("blk"), 2)


def halves_body(x_ref, other_ref):
    half = x_ref.shape[1] // 2
    other = pl.multiple_of((1 - core_index()) * half, half)
    other_ref[...] = x_ref[:, pl.ds(other, half)]


def normalize_body(x_ref, gain_ref, own_ref, other_ref):
    half = x_ref.shape[1] // 2
    wide = x_ref[...].astype(F32)
    scale = lax.rsqrt(jnp.mean(wide * wide, axis=1, keepdims=True) + 1e-06)
    core = core_index()
    for ref, side in ((own_ref, core), (other_ref, 1 - core)):
        at = pl.ds(pl.multiple_of(side * half, half), half)
        ref[...] = (x_ref[:, at].astype(F32) * scale * gain_ref[:, at]).astype(BF16)


def column(piece, turn):
    z = lax.rem(lax.axis_index("head") + turn, 4)
    return pl.multiple_of(piece * 4 * HEAD_DIM + z * HEAD_DIM, HEAD_DIM)


def pack_body(groups, count, half, *refs):
    ins, outs = refs[:count], refs[count:]
    place = 0
    for pairs in groups:
        for turn in range(4):
            out = outs[place]
            place += 1
            rows = 0
            for tensor, piece in pairs:
                at = column(piece, turn)
                for ref in ins[2 * tensor : 2 * tensor + 2]:
                    tokens = ref.shape[0]
                    start = at
                    if ref.shape[1] != half:
                        start = pl.multiple_of(core_index() * half + at, HEAD_DIM)
                    out[rows : rows + tokens, :] = ref[:, pl.ds(start, HEAD_DIM)]
                    rows += tokens


def pack(groups, tensors):
    flat = [a for pair in tensors for a in pair]
    tokens = flat[0].shape[0]
    outs = [sds(2 * tokens * len(pairs), HEAD_DIM) for pairs in groups for _ in range(4)]
    half = min(a.shape[1] for a in flat)
    made = call(functools.partial(pack_body, groups, len(flat), half), outs, *flat)
    return [made[4 * g : 4 * g + 4] for g in range(len(groups))]


def join_body(parts, *refs):
    ins, outs = refs[:4], refs[4:]
    rows = ins[0].shape[0] // parts
    for part, out in enumerate(outs):
        for turn in range(4):
            out[turn * rows : (turn + 1) * rows, :] = ins[turn][part * rows : (part + 1) * rows, :]


def join(buffers, parts):
    rows = 4 * buffers[0].shape[0] // parts
    return call(functools.partial(join_body, parts), [sds(rows, HEAD_DIM)] * parts, *buffers)


def split_body(*refs):
    ins, out = refs[:-1], refs[-1]
    rows = ins[0].shape[0] // 2
    for turn, ref in enumerate(ins):
        out[turn * rows : (turn + 1) * rows, :] = ref[rows:, :]


def place_body(pieces, *refs):
    out = refs[-1]
    tokens, half = out.shape[0], out.shape[1] // 2
    core = core_index()
    for piece in range(pieces):
        for turn in range(4):
            at = column(piece, turn)
            here = pl.multiple_of(core * half + at, HEAD_DIM)
            there = pl.multiple_of((1 - core) * half + at, HEAD_DIM)
            out[:, pl.ds(here, HEAD_DIM)] = refs[5 * piece + turn][:tokens, :]
            out[:, pl.ds(there, HEAD_DIM)] = refs[5 * piece + 4][
                turn * tokens : (turn + 1) * tokens, :
            ]


def permute(array, move):
    pairs = []
    for y in range(2):
        for x in range(2):
            for core in range(2):
                for z in range(4):
                    to = move(y, x, core, z)
                    pairs.append(
                        ((y * 4 + x * 2 + core) * 4 + z, (to[0] * 4 + to[1] * 2 + to[2]) * 4 + to[3])
                    )
    return lax.ppermute(array, AXES, pairs)


def other_core(array):
    return permute(array, lambda y, x, core, z: (y, x, 1 - core, z))


def other_x(array):
    return permute(array, lambda y, x, core, z: (y, 1 - x, core, z))


def other_y(array):
    return permute(array, lambda y, x, core, z: (1 - y, x, core, z))


def along_z(array, turn):
    return permute(array, lambda y, x, core, z: (y, x, core, (z + turn) % 4))


def rotate(buffers):
    return [buffers[0]] + [along_z(buffers[turn], turn) for turn in (1, 2, 3)]


def rotate_back(buffers):
    return [buffers[0]] + [along_z(buffers[turn], 4 - turn) for turn in (1, 2, 3)]


def gather(keys, values):
    keys_x, values_x = other_x(keys), other_x(values)
    keys_y, values_y = other_y(keys), other_y(values)
    keys_far, values_far = other_x(keys_y), other_y(values_x)
    return (keys, keys_x, keys_y, keys_far), (values, values_x, values_y, values_far)


def shards_fast(queries, keys, values, query_gain, key_gain):
    tokens, width = queries.shape
    half = width // 2
    query_gain, key_gain = query_gain.reshape(1, width), key_gain.reshape(1, width)
    (v_other,) = call(halves_body, [sds(tokens, half)], values)
    v_got = other_core(v_other)
    k_own, k_other = call(normalize_body, [sds(tokens, half)] * 2, keys, key_gain)
    k_got = other_core(k_other)
    q_own, q_other = call(normalize_body, [sds(tokens, half)] * 2, queries, query_gain)
    q_got = other_core(q_other)
    v_pair, k_pair, q_pair = (values, v_got), (k_own, k_got), (q_own, q_got)

    (v0,) = pack([[(0, 0)]], [v_pair])
    v0 = rotate(v0)
    k0, kv1, kv2 = pack([[(0, 0)], [(0, 1), (1, 1)], [(0, 2), (1, 2)]], [k_pair, v_pair])
    k0 = rotate(k0)
    kv1 = rotate(kv1)
    q0, q1, q2 = pack([[(0, 0)], [(0, 1)], [(0, 2)]], [q_pair])
    q0 = rotate(q0)
    kv2 = rotate(kv2)
    q1, q2 = rotate(q1), rotate(q2)

    results = []
    for q_slots, blocks in ((q0, (k0, v0)), (q1, kv1), (q2, kv2)):
        if len(blocks) == 2:
            (key_block,), (value_block,) = join(blocks[0], 1), join(blocks[1], 1)
        else:
            key_block, value_block = join(blocks, 2)
        all_keys, all_values = gather(key_block, value_block)
        back = rotate_back(attend(q_slots, all_keys, all_values))
        (across,) = call(split_body, [sds(4 * tokens, HEAD_DIM)], *back)
        results += [*back, other_core(across)]
    (attended,) = call(functools.partial(place_body, 3), [sds(tokens, width)], *results)
    return attended


def whole_head_body(q_ref, k_ref, v_ref, out_ref, top, total, accum):
    step = pl.program_id(2)

    @pl.when(step == 0)
    def _():
        top[...] = jnp.full_like(top, -jnp.inf)
        total[...] = jnp.zeros_like(total)
        accum[...] = jnp.zeros_like(accum)

    scores = lax.dot_general(
        q_ref[...], k_ref[...], (((1,), (1,)), ((), ())), preferred_element_type=F32
    )
    new_top = jnp.maximum(top[...], jnp.max(scores, axis=1, keepdims=True))
    weights = jnp.exp2((scores - new_top) * EXPONENT)
    shrink = jnp.exp2((top[...] - new_top) * EXPONENT)
    total[...] = total[...] * shrink + jnp.sum(weights, axis=1, keepdims=True)
    accum[...] = accum[...] * shrink + jnp.dot(
        weights.astype(BF16), v_ref[...], preferred_element_type=F32
    )
    top[...] = new_top

    @pl.when(step == pl.num_programs(2) - 1)
    def _():
        out_ref[...] = (accum[...] / total[...]).astype(BF16)


def normalize(block, gain):
    wide = block.astype(F32)
    mean_sq = jnp.mean(wide * wide, axis=-1, keepdims=True)
    return (wide * lax.rsqrt(mean_sq + 1e-06) * gain).astype(BF16)


def shards_any(queries, keys, values, query_gain, key_gain):
    def regroup(x):
        return lax.all_to_all(x, "head", split_axis=1, concat_axis=0, tiled=True)

    q = regroup(normalize(queries, query_gain))
    k = lax.all_gather(regroup(normalize(keys, key_gain)), "blk", axis=0, tiled=True)
    v = lax.all_gather(regroup(values), "blk", axis=0, tiled=True)
    rows, width = q.shape
    length = k.shape[0]
    q_rows, k_rows = math.gcd(rows, 512), math.gcd(length, 1024)
    result = pl.pallas_call(
        whole_head_body,
        grid=(width // HEAD_DIM, rows // q_rows, length // k_rows),
        out_shape=sds(rows, width),
        in_specs=[
            pl.BlockSpec((q_rows, HEAD_DIM), lambda h, i, j: (i, h)),
            pl.BlockSpec((k_rows, HEAD_DIM), lambda h, i, j: (j, h)),
            pl.BlockSpec((k_rows, HEAD_DIM), lambda h, i, j: (j, h)),
        ],
        out_specs=pl.BlockSpec((q_rows, HEAD_DIM), lambda h, i, j: (i, h)),
        scratch_shapes=[
            pltpu.VMEM((q_rows, 1), F32),
            pltpu.VMEM((q_rows, 1), F32),
            pltpu.VMEM((q_rows, HEAD_DIM), F32),
        ],
        compiler_params=PARAMS,
    )(q, k, v)
    return lax.all_to_all(result, "head", split_axis=0, concat_axis=1, tiled=True)


def solution(mesh):
    fast = mesh.shape["blk"] == 8 and mesh.shape["head"] == 4
    rows = P(AXES, None)
    return jax.shard_map(
        shards_fast if fast else shards_any,
        mesh=mesh,
        in_specs=(rows, rows, rows, P(), P()),
        out_specs=rows,
        check_vma=False,
    )
```

time: 260 us -> 135 us (0.52)
  starting transfers between devices: 3.72 us -> 80.6 us
  blocking collectives: 73.3 us -> 0 us
  matrix products: 57.6 us -> 0 us
  other arithmetic: 30.4 us -> 0 us
  local copies, waits for them, and re-layouts: 28.2 us -> 2.98 us
  waiting for transfers between devices: 52.3 us -> 31.2 us
  Pallas kernels: 0 us -> 19.7 us
  between operations: 13.6 us -> 0.24 us
    ppermute x0 -> x54, starting transfers between devices: none -> 80.6 us  [permute(): return lax.ppermute(array, AXES, pairs)]
    all_to_all x3 -> x0, blocking collectives: 73.3 us -> none  [the longest x1 26.2 us: shards(): lax.all_to_all(second_part, 'head', split_axis=1, concat_axis=0, tiled=True)]
    dot_general x8 -> x0, matrix products: 57.6 us -> none  [the longest x4 31.1 us: absorb(): jnp.einsum('qhd,khd->hqk', q_heads, key_block, preferred_element_type=jnp...]
    all_gather x2 -> x0, waiting for transfers between devices: 33.6 us -> none  [the longest x1 33.6 us: shards(): value_piece = lax.all_gather(v_heads, 'blk', axis=0, tiled=True)]
    ppermute x0 -> x54, waiting for transfers between devices: none -> 31.2 us  [permute(): return lax.ppermute(array, AXES, pairs)]
    reduce_sum x6 -> x0, other arithmetic: 28.1 us -> none  [the longest x4 26.5 us: absorb(): new_sum = run_sum * shrink + jnp.sum(weights, axis=-1)]
    pallas_call x0 -> x17, Pallas kernels: none -> 19.7 us  [call(): pl.pallas_call(body, out_shape=outs, in_specs=[VMEM] * len(args), out_spe...]
    all_to_all x1 -> x0, waiting for transfers between devices: 18.7 us -> none  [shards(): lax.all_to_all(first_part, 'head', split_axis=1, concat_axis=0, tiled=True)]
  transfers between devices with their start and end apart: 3 -> 54, of which waited for: 2 -> 17; matrix products, arithmetic and copies ran while one was open for 6% -> 0% of each run, Pallas kernels for 0% -> 13%
where the time goes in v1:
time: 135 us
  starting transfers between devices  80.6 us (60%)
  waiting for transfers between devices  31.2 us (23%)
  Pallas kernels  19.7 us (15%)
  local copies, waits for them, and re-layouts  2.98 us (2%)
    ppermute x54, starting transfers between devices, permute(): return lax.ppermute(array, AXES, pairs)  80.6 us
    ppermute x54, waiting for transfers between devices, permute(): return lax.ppermute(array, AXES, pairs)  31.2 us
    pallas_call x17, Pallas kernels, call(): pl.pallas_call(body, out_shape=outs, in_specs=[VMEM] * len(args), out_spe...  19.7 us
    unnamed x10, local copies, waits for them, and re-layouts  2.98 us
  transfers between devices with their start and end apart: 54, of which 17 were waited for; matrix products, arithmetic and copies ran while one was open for 0% of the time, Pallas kernels for 13%

profile of v1, /device:TPU:0, one launch (start us, length us, event | category | flops | bytes accessed | tf_op | source)
XLA Modules:
  0.0 134.8 jit_solution(8809637553332056399)
XLA Ops:
  5.3 2.8 %collective-permute-start.1 = (bf16[256,128]{1,0:T(8,128)(2,1)S(1)}, bf16[256,128]{1,0:T(8,128)(2,1)S(1)}, u32[]{:S(2)}, u32[]{:S(2)}) collective-permute-start(bf16[256,128]{1,0:T(8,128)(2,1)S(1)} %get-tuple-element.56), channel_id=1, source_target_pairs={{0,1},{1,2},{2,3},{3,0},{4,5},{5,6},{6,7},{7,4},{8,9},{9,10},{10,1... | collective-permute-start | bytes 196616 | tf_op jit(solution)/shard_map/ppermute | solution.py:181
  8.1 2.6 %collective-permute-start.2 = (bf16[256,128]{1,0:T(8,128)(2,1)S(1)}, bf16[256,128]{1,0:T(8,128)(2,1)S(1)}, u32[]{:S(2)}, u32[]{:S(2)}) collective-permute-start(bf16[256,128]{1,0:T(8,128)(2,1)S(1)} %get-tuple-element.57), channel_id=1, source_target_pairs={{0,2},{1,3},{2,0},{3,1},{4,6},{5,7},{6,4},{7,5},{8,10},{9,11},{10,... | collective-permute-start | bytes 196616 | tf_op jit(solution)/shard_map/ppermute | solution.py:181
  13.3 2.8 %collective-permute-start.8 = (bf16[256,128]{1,0:T(8,128)(2,1)S(1)}, bf16[256,128]{1,0:T(8,128)(2,1)S(1)}, u32[]{:S(2)}, u32[]{:S(2)}) collective-permute-start(bf16[256,128]{1,0:T(8,128)(2,1)S(1)} %get-tuple-element.64), channel_id=1, source_target_pairs={{0,3},{1,0},{2,1},{3,2},{4,7},{5,4},{6,5},{7,6},{8,11},{9,8},{10,9... | collective-permute-start | bytes 196616 | tf_op jit(solution)/shard_map/ppermute | solution.py:181
  16.9 2.7 %collective-permute-start.13 = (bf16[256,128]{1,0:T(8,128)(2,1)S(1)}, bf16[256,128]{1,0:T(8,128)(2,1)S(1)}, u32[]{:S(2)}, u32[]{:S(2)}) collective-permute-start(bf16[256,128]{1,0:T(8,128)(2,1)S(1)} %get-tuple-element.67), channel_id=1, source_target_pairs={{0,2},{1,3},{2,0},{3,1},{4,6},{5,7},{6,4},{7,5},{8,10},{9,11},{10,... | collective-permute-start | bytes 196616 | tf_op jit(solution)/shard_map/ppermute | solution.py:181
  19.6 3.2 %collective-permute-start.14 = (bf16[256,128]{1,0:T(8,128)(2,1)S(1)}, bf16[256,128]{1,0:T(8,128)(2,1)S(1)}, u32[]{:S(2)}, u32[]{:S(2)}) collective-permute-start(bf16[256,128]{1,0:T(8,128)(2,1)S(1)} %get-tuple-element.68), channel_id=1, source_target_pairs={{0,3},{1,0},{2,1},{3,2},{4,7},{5,4},{6,5},{7,6},{8,11},{9,8},{10,9... | collective-permute-start | bytes 196616 | tf_op jit(solution)/shard_map/ppermute | solution.py:181
  23.4 3.9 %collective-permute-start.23 = (bf16[256,128]{1,0:T(8,128)(2,1)S(1)}, bf16[256,128]{1,0:T(8,128)(2,1)S(1)}, u32[]{:S(2)}, u32[]{:S(2)}) collective-permute-start(bf16[256,128]{1,0:T(8,128)(2,1)S(1)} %get-tuple-element.75), channel_id=1, source_target_pairs={{0,2},{1,3},{2,0},{3,1},{4,6},{5,7},{6,4},{7,5},{8,10},{9,11},{10,... | collective-permute-start | bytes 196616 | tf_op jit(solution)/shard_map/ppermute | solution.py:181
  29.0 2.1 %collective-permute-start.24 = (bf16[256,128]{1,0:T(8,128)(2,1)S(1)}, bf16[256,128]{1,0:T(8,128)(2,1)S(1)}, u32[]{:S(2)}, u32[]{:S(2)}) collective-permute-start(bf16[256,128]{1,0:T(8,128)(2,1)S(1)} %get-tuple-element.76), channel_id=1, source_target_pairs={{0,3},{1,0},{2,1},{3,2},{4,7},{5,4},{6,5},{7,6},{8,11},{9,8},{10,9... | collective-permute-start | bytes 196616 | tf_op jit(solution)/shard_map/ppermute | solution.py:181
  31.1 4.6 %collective-permute-start.38 = (bf16[256,128]{1,0:T(8,128)(2,1)S(1)}, bf16[256,128]{1,0:T(8,128)(2,1)S(1)}, u32[]{:S(2)}, u32[]{:S(2)}) collective-permute-start(bf16[256,128]{1,0:T(8,128)(2,1)S(1)} %get-tuple-element.88), channel_id=1, source_target_pairs={{0,1},{1,2},{2,3},{3,0},{4,5},{5,6},{6,7},{7,4},{8,9},{9,10},{10,1... | collective-permute-start | bytes 196616 | tf_op jit(solution)/shard_map/ppermute | solution.py:181
  35.7 3.9 %collective-permute-done.23.refs_2_ = bf16[256,128]{1,0:T(8,128)(2,1)S(1)} collective-permute-done((bf16[256,128]{1,0:T(8,128)(2,1)S(1)}, bf16[256,128]{1,0:T(8,128)(2,1)S(1)}, u32[]{:S(2)}, u32[]{:S(2)}) %collective-permute-start.23) | collective-permute-done | bytes 65568 | tf_op jit(solution)/shard_map/ppermute | solution.py:181
  40.4 6.7 %collective-permute-start.41 = (bf16[512,128]{1,0:T(8,128)(2,1)S(1)}, bf16[512,128]{1,0:T(8,128)(2,1)S(1)}, u32[]{:S(2)}, u32[]{:S(2)}) collective-permute-start(bf16[512,128]{1,0:T(8,128)(2,1)S(1)} %get-tuple-element.92), channel_id=1, source_target_pairs={{0,1},{1,2},{2,3},{3,0},{4,5},{5,6},{6,7},{7,4},{8,9},{9,10},{10,1... | collective-permute-start | bytes 393224 | tf_op jit(solution)/shard_map/ppermute | solution.py:181
  50.9 2.5 %collective-permute-start.42 = (bf16[512,128]{1,0:T(8,128)(2,1)S(1)}, bf16[512,128]{1,0:T(8,128)(2,1)S(1)}, u32[]{:S(2)}, u32[]{:S(2)}) collective-permute-start(bf16[512,128]{1,0:T(8,128)(2,1)S(1)} %get-tuple-element.93), channel_id=1, source_target_pairs={{0,2},{1,3},{2,0},{3,1},{4,6},{5,7},{6,4},{7,5},{8,10},{9,11},{10,... | collective-permute-start | bytes 393224 | tf_op jit(solution)/shard_map/ppermute | solution.py:181
  53.3 3.4 %collective-permute-start.43 = (bf16[512,128]{1,0:T(8,128)(2,1)S(1)}, bf16[512,128]{1,0:T(8,128)(2,1)S(1)}, u32[]{:S(2)}, u32[]{:S(2)}) collective-permute-start(bf16[512,128]{1,0:T(8,128)(2,1)S(1)} %get-tuple-element.94), channel_id=1, source_target_pairs={{0,3},{1,0},{2,1},{3,2},{4,7},{5,4},{6,5},{7,6},{8,11},{9,8},{10,9... | collective-permute-start | bytes 393224 | tf_op jit(solution)/shard_map/ppermute | solution.py:181
  56.7 3.9 %collective-permute-done.42.refs_2_ = bf16[512,128]{1,0:T(8,128)(2,1)S(1)} collective-permute-done((bf16[512,128]{1,0:T(8,128)(2,1)S(1)}, bf16[512,128]{1,0:T(8,128)(2,1)S(1)}, u32[]{:S(2)}, u32[]{:S(2)}) %collective-permute-start.42) | collective-permute-done | bytes 131104 | tf_op jit(solution)/shard_map/ppermute | solution.py:181
  60.6 1.7 %collective-permute-start.16 = (bf16[1024,128]{1,0:T(8,128)(2,1)S(1)}, bf16[1024,128]{1,0:T(8,128)(2,1)S(1)}, u32[]{:S(2)}, u32[]{:S(2)}) collective-permute-start(bf16[1024,128]{1,0:T(8,128)(2,1)S(1)} %shard_map.62.refs_8_), channel_id=1, source_target_pairs={{0,16},{1,17},{2,18},{3,19},{4,20},{5,21},{6,22},{7,23},{8,24},{9,... | collective-permute-start | bytes 786440 | tf_op jit(solution)/shard_map/ppermute | solution.py:181
  64.8 1.7 %collective-permute-start.32 = (bf16[1024,128]{1,0:T(8,128)(2,1)S(1)}, bf16[1024,128]{1,0:T(8,128)(2,1)S(1)}, u32[]{:S(2)}, u32[]{:S(2)}) collective-permute-start(bf16[1024,128]{1,0:T(8,128)(2,1)S(1)} %get-tuple-element.82.refs_8_), channel_id=1, source_target_pairs={{0,16},{1,17},{2,18},{3,19},{4,20},{5,21},{6,22},{7,23},{8,24},{9,... | collective-permute-start | bytes 786440 | tf_op jit(solution)/shard_map/ppermute | solution.py:181
  66.5 3.3 %collective-permute-done.16.refs_10_ = bf16[1024,128]{1,0:T(8,128)(2,1)S(1)} collective-permute-done((bf16[1024,128]{1,0:T(8,128)(2,1)S(1)}, bf16[1024,128]{1,0:T(8,128)(2,1)S(1)}, u32[]{:S(2)}, u32[]{:S(2)}) %collective-permute-start.16) | collective-permute-done | bytes 262176 | tf_op jit(solution)/shard_map/ppermute | solution.py:181
  69.8 1.7 %collective-permute-start.45 = (bf16[1024,128]{1,0:T(8,128)(2,1)S(1)}, bf16[1024,128]{1,0:T(8,128)(2,1)S(1)}, u32[]{:S(2)}, u32[]{:S(2)}) collective-permute-start(bf16[1024,128]{1,0:T(8,128)(2,1)S(1)} %get-tuple-element.95.refs_4_), channel_id=1, source_target_pairs={{0,16},{1,17},{2,18},{3,19},{4,20},{5,21},{6,22},{7,23},{8,24},{9,... | collective-permute-start | bytes 786440 | tf_op jit(solution)/shard_map/ppermute | solution.py:181
  73.2 2.3 %collective-permute-done.29.refs_6_ = bf16[1024,128]{1,0:T(8,128)(2,1)S(1)} collective-permute-done((bf16[1024,128]{1,0:T(8,128)(2,1)S(1)}, bf16[1024,128]{1,0:T(8,128)(2,1)S(1)}, u32[]{:S(2)}, u32[]{:S(2)}) %collective-permute-start.29) | collective-permute-done | bytes 262176 | tf_op jit(solution)/shard_map/ppermute | solution.py:181
  78.7 2.4 %collective-permute-done.32.refs_10_ = bf16[1024,128]{1,0:T(8,128)(2,1)S(1)} collective-permute-done((bf16[1024,128]{1,0:T(8,128)(2,1)S(1)}, bf16[1024,128]{1,0:T(8,128)(2,1)S(1)}, u32[]{:S(2)}, u32[]{:S(2)}) %collective-permute-start.32) | collective-permute-done | bytes 262176 | tf_op jit(solution)/shard_map/ppermute | solution.py:181
  82.6 4.1 %collective-permute-done.45.refs_6_ = bf16[1024,128]{1,0:T(8,128)(2,1)S(1)} collective-permute-done((bf16[1024,128]{1,0:T(8,128)(2,1)S(1)}, bf16[1024,128]{1,0:T(8,128)(2,1)S(1)}, u32[]{:S(2)}, u32[]{:S(2)}) %collective-permute-start.45) | collective-permute-done | bytes 262176 | tf_op jit(solution)/shard_map/ppermute | solution.py:181
  86.7 1.7 %collective-permute-start.33 = (bf16[1024,128]{1,0:T(8,128)(2,1)S(1)}, bf16[1024,128]{1,0:T(8,128)(2,1)S(1)}, u32[]{:S(2)}, u32[]{:S(2)}) collective-permute-start(bf16[1024,128]{1,0:T(8,128)(2,1)S(1)} %collective-permute-done.31.refs_9_), channel_id=1, source_target_pairs={{0,16},{1,17},{2,18},{3,19},{4,20},{5,21},{6,22},{7,23},{8,24},{9,... | collective-permute-start | bytes 786440 | tf_op jit(solution)/shard_map/ppermute | solution.py:181
  90.2 2.1 %collective-permute-done.17.refs_11_ = bf16[1024,128]{1,0:T(8,128)(2,1)S(1)} collective-permute-done((bf16[1024,128]{1,0:T(8,128)(2,1)S(1)}, bf16[1024,128]{1,0:T(8,128)(2,1)S(1)}, u32[]{:S(2)}, u32[]{:S(2)}) %collective-permute-start.17) | collective-permute-done | bytes 262176 | tf_op jit(solution)/shard_map/ppermute | solution.py:181
  95.5 5.7 %shard_map.63 = (bf16[256,128]{1,0:T(8,128)(2,1)S(1)}, bf16[256,128]{1,0:T(8,128)(2,1)S(1)}, bf16[256,128]{1,0:T(8,128)(2,1)S(1)}, bf16[256,128]{1,0:T(8,128)(2,1)S(1)}) custom-call(bf16[256,128]{1,0:T(8,128)(2,1)S(1)} %get-tuple-element.55.refs_0_, bf16[256,128]{1,0:T(8,128)(2,1)S(1)} %collective-permute-done.1.refs_1_, ...), custom_call_target="tpu_custom_call" | custom-call | flops 2147483648 | bytes 2621440 | tf_op jit(solution)/shard_map/pallas_call | solution.py:26
  101.2 3.8 %collective-permute-start.40 = (bf16[256,128]{1,0:T(8,128)(2,1)S(1)}, bf16[256,128]{1,0:T(8,128)(2,1)S(1)}, u32[]{:S(2)}, u32[]{:S(2)}) collective-permute-start(bf16[256,128]{1,0:T(8,128)(2,1)S(1)} %get-tuple-element.90), channel_id=1, source_target_pairs={{0,3},{1,0},{2,1},{3,2},{4,7},{5,4},{6,5},{7,6},{8,11},{9,8},{10,9... | collective-permute-start | bytes 196616 | tf_op jit(solution)/shard_map/ppermute | solution.py:181
  105.0 5.7 %shard_map.66 = (bf16[256,128]{1,0:T(8,128)(2,1)S(1)}, bf16[256,128]{1,0:T(8,128)(2,1)S(1)}, bf16[256,128]{1,0:T(8,128)(2,1)S(1)}, bf16[256,128]{1,0:T(8,128)(2,1)S(1)}) custom-call(bf16[256,128]{1,0:T(8,128)(2,1)S(1)} %get-tuple-element.73.refs_0_, bf16[256,128]{1,0:T(8,128)(2,1)S(1)} %collective-permute-done.22.refs_1_, ...), custom_call_target="tpu_custom_call" | custom-call | flops 2147483648 | bytes 2621440 | tf_op jit(solution)/shard_map/pallas_call | solution.py:26
  111.1 1.8 %collective-permute-start.20 = (bf16[256,128]{1,0:T(8,128)(2,1)S(1)}, bf16[256,128]{1,0:T(8,128)(2,1)S(1)}, u32[]{:S(2)}, u32[]{:S(2)}) collective-permute-start(bf16[256,128]{1,0:T(8,128)(2,1)S(1)} %get-tuple-element.72), channel_id=1, source_target_pairs={{0,1},{1,2},{2,3},{3,0},{4,5},{5,6},{6,7},{7,4},{8,9},{9,10},{10,1... | collective-permute-start | bytes 196616 | tf_op jit(solution)/shard_map/ppermute | solution.py:181
  112.9 2.6 %collective-permute-start.34 = (bf16[256,128]{1,0:T(8,128)(2,1)S(1)}, bf16[256,128]{1,0:T(8,128)(2,1)S(1)}, u32[]{:S(2)}, u32[]{:S(2)}) collective-permute-start(bf16[256,128]{1,0:T(8,128)(2,1)S(1)} %get-tuple-element.84), channel_id=1, source_target_pairs={{0,3},{1,0},{2,1},{3,2},{4,7},{5,4},{6,5},{7,6},{8,11},{9,8},{10,9... | collective-permute-start | bytes 196616 | tf_op jit(solution)/shard_map/ppermute | solution.py:181
  116.1 5.7 %shard_map.69 = (bf16[256,128]{1,0:T(8,128)(2,1)S(1)}, bf16[256,128]{1,0:T(8,128)(2,1)S(1)}, bf16[256,128]{1,0:T(8,128)(2,1)S(1)}, bf16[256,128]{1,0:T(8,128)(2,1)S(1)}) custom-call(bf16[256,128]{1,0:T(8,128)(2,1)S(1)} %get-tuple-element.87.refs_0_, bf16[256,128]{1,0:T(8,128)(2,1)S(1)} %collective-permute-done.38.refs_1_, ...), custom_call_target="tpu_custom_call" | custom-call | flops 2147483648 | bytes 2621440 | tf_op jit(solution)/shard_map/pallas_call | solution.py:26
  121.8 1.7 %collective-permute-start.36 = (bf16[256,128]{1,0:T(8,128)(2,1)S(1)}, bf16[256,128]{1,0:T(8,128)(2,1)S(1)}, u32[]{:S(2)}, u32[]{:S(2)}) collective-permute-start(bf16[256,128]{1,0:T(8,128)(2,1)S(1)} %get-tuple-element.86), channel_id=1, source_target_pairs={{0,1},{1,2},{2,3},{3,0},{4,5},{5,6},{6,7},{7,4},{8,9},{9,10},{10,1... | collective-permute-start | bytes 196616 | tf_op jit(solution)/shard_map/ppermute | solution.py:181
  123.5 2.1 %collective-permute-start.50 = (bf16[256,128]{1,0:T(8,128)(2,1)S(1)}, bf16[256,128]{1,0:T(8,128)(2,1)S(1)}, u32[]{:S(2)}, u32[]{:S(2)}) collective-permute-start(bf16[256,128]{1,0:T(8,128)(2,1)S(1)} %get-tuple-element.98), channel_id=1, source_target_pairs={{0,3},{1,0},{2,1},{3,2},{4,7},{5,4},{6,5},{7,6},{8,11},{9,8},{10,9... | collective-permute-start | bytes 196616 | tf_op jit(solution)/shard_map/ppermute | solution.py:181
  126.4 1.6 %collective-permute-done.36.refs_3_.refs_8_ = bf16[256,128]{1,0:T(8,128)(2,1)S(1)} collective-permute-done((bf16[256,128]{1,0:T(8,128)(2,1)S(1)}, bf16[256,128]{1,0:T(8,128)(2,1)S(1)}, u32[]{:S(2)}, u32[]{:S(2)}) %collective-permute-start.36) | collective-permute-done | bytes 65568 | tf_op jit(solution)/shard_map/ppermute | solution.py:181
  128.5 2.4 %collective-permute-done.51.refs_2_.refs_12_ = bf16[256,128]{1,0:T(8,128)(2,1)S(1)} collective-permute-done((bf16[256,128]{1,0:T(8,128)(2,1)S(1)}, bf16[256,128]{1,0:T(8,128)(2,1)S(1)}, u32[]{:S(2)}, u32[]{:S(2)}) %collective-permute-start.51) | collective-permute-done | bytes 65568 | tf_op jit(solution)/shard_map/ppermute | solution.py:181
  (103 shorter events, 35.4 us)
Async XLA Ops:
  13.0 10.4 %collective-permute-start.7 = (bf16[256,128]{1,0:T(8,128)(2,1)S(1)}, bf16[256,128]{1,0:T(8,128)(2,1)S(1)}, u32[]{:S(2)}, u32[]{:S(2)}) collective-permute-start(bf16[256,128]{1,0:T(8,128)(2,1)S(1)} %get-tuple-element.63), channel_id=1, source_target_pairs={{0,2},{1,3},{2,0},{3,1},{4,6},{5,7},{6,4},{7,5},{8,10},{9,11},{10,... | collective-permute-start | bytes 196616 | tf_op jit(solution)/shard_map/ppermute | solution.py:181
  13.3 10.0 %collective-permute-start.8 = (bf16[256,128]{1,0:T(8,128)(2,1)S(1)}, bf16[256,128]{1,0:T(8,128)(2,1)S(1)}, u32[]{:S(2)}, u32[]{:S(2)}) collective-permute-start(bf16[256,128]{1,0:T(8,128)(2,1)S(1)} %get-tuple-element.64), channel_id=1, source_target_pairs={{0,3},{1,0},{2,1},{3,2},{4,7},{5,4},{6,5},{7,6},{8,11},{9,8},{10,9... | collective-permute-start | bytes 196616 | tf_op jit(solution)/shard_map/ppermute | solution.py:181
  16.2 11.0 %collective-permute-start.12 = (bf16[256,128]{1,0:T(8,128)(2,1)S(1)}, bf16[256,128]{1,0:T(8,128)(2,1)S(1)}, u32[]{:S(2)}, u32[]{:S(2)}) collective-permute-start(bf16[256,128]{1,0:T(8,128)(2,1)S(1)} %get-tuple-element.66), channel_id=1, source_target_pairs={{0,1},{1,2},{2,3},{3,0},{4,5},{5,6},{6,7},{7,4},{8,9},{9,10},{10,1... | collective-permute-start | bytes 196616 | tf_op jit(solution)/shard_map/ppermute | solution.py:181
  16.9 10.9 %collective-permute-start.13 = (bf16[256,128]{1,0:T(8,128)(2,1)S(1)}, bf16[256,128]{1,0:T(8,128)(2,1)S(1)}, u32[]{:S(2)}, u32[]{:S(2)}) collective-permute-start(bf16[256,128]{1,0:T(8,128)(2,1)S(1)} %get-tuple-element.67), channel_id=1, source_target_pairs={{0,2},{1,3},{2,0},{3,1},{4,6},{5,7},{6,4},{7,5},{8,10},{9,11},{10,... | collective-permute-start | bytes 196616 | tf_op jit(solution)/shard_map/ppermute | solution.py:181
  23.4 16.2 %collective-permute-start.23 = (bf16[256,128]{1,0:T(8,128)(2,1)S(1)}, bf16[256,128]{1,0:T(8,128)(2,1)S(1)}, u32[]{:S(2)}, u32[]{:S(2)}) collective-permute-start(bf16[256,128]{1,0:T(8,128)(2,1)S(1)} %get-tuple-element.75), channel_id=1, source_target_pairs={{0,2},{1,3},{2,0},{3,1},{4,6},{5,7},{6,4},{7,5},{8,10},{9,11},{10,... | collective-permute-start | bytes 196616 | tf_op jit(solution)/shard_map/ppermute | solution.py:181
  27.3 21.4 %collective-permute-start.25 = (bf16[512,128]{1,0:T(8,128)(2,1)S(1)}, bf16[512,128]{1,0:T(8,128)(2,1)S(1)}, u32[]{:S(2)}, u32[]{:S(2)}) collective-permute-start(bf16[512,128]{1,0:T(8,128)(2,1)S(1)} %get-tuple-element.78), channel_id=1, source_target_pairs={{0,1},{1,2},{2,3},{3,0},{4,5},{5,6},{6,7},{7,4},{8,9},{9,10},{10,1... | collective-permute-start | bytes 393224 | tf_op jit(solution)/shard_map/ppermute | solution.py:181
  27.8 22.5 %collective-permute-start.26 = (bf16[512,128]{1,0:T(8,128)(2,1)S(1)}, bf16[512,128]{1,0:T(8,128)(2,1)S(1)}, u32[]{:S(2)}, u32[]{:S(2)}) collective-permute-start(bf16[512,128]{1,0:T(8,128)(2,1)S(1)} %get-tuple-element.79), channel_id=1, source_target_pairs={{0,2},{1,3},{2,0},{3,1},{4,6},{5,7},{6,4},{7,5},{8,10},{9,11},{10,... | collective-permute-start | bytes 393224 | tf_op jit(solution)/shard_map/ppermute | solution.py:181
  29.0 11.4 %collective-permute-start.24 = (bf16[256,128]{1,0:T(8,128)(2,1)S(1)}, bf16[256,128]{1,0:T(8,128)(2,1)S(1)}, u32[]{:S(2)}, u32[]{:S(2)}) collective-permute-start(bf16[256,128]{1,0:T(8,128)(2,1)S(1)} %get-tuple-element.76), channel_id=1, source_target_pairs={{0,3},{1,0},{2,1},{3,2},{4,7},{5,4},{6,5},{7,6},{8,11},{9,8},{10,9... | collective-permute-start | bytes 196616 | tf_op jit(solution)/shard_map/ppermute | solution.py:181
  40.4 10.5 %collective-permute-start.27 = (bf16[512,128]{1,0:T(8,128)(2,1)S(1)}, bf16[512,128]{1,0:T(8,128)(2,1)S(1)}, u32[]{:S(2)}, u32[]{:S(2)}) collective-permute-start(bf16[512,128]{1,0:T(8,128)(2,1)S(1)} %get-tuple-element.80), channel_id=1, source_target_pairs={{0,3},{1,0},{2,1},{3,2},{4,7},{5,4},{6,5},{7,6},{8,11},{9,8},{10,9... | collective-permute-start | bytes 393224 | tf_op jit(solution)/shard_map/ppermute | solution.py:181
  40.4 13.0 %collective-permute-start.41 = (bf16[512,128]{1,0:T(8,128)(2,1)S(1)}, bf16[512,128]{1,0:T(8,128)(2,1)S(1)}, u32[]{:S(2)}, u32[]{:S(2)}) collective-permute-start(bf16[512,128]{1,0:T(8,128)(2,1)S(1)} %get-tuple-element.92), channel_id=1, source_target_pairs={{0,1},{1,2},{2,3},{3,0},{4,5},{5,6},{6,7},{7,4},{8,9},{9,10},{10,1... | collective-permute-start | bytes 393224 | tf_op jit(solution)/shard_map/ppermute | solution.py:181
  47.1 16.8 %collective-permute-start.9 = (bf16[1024,128]{1,0:T(8,128)(2,1)S(1)}, bf16[1024,128]{1,0:T(8,128)(2,1)S(1)}, u32[]{:S(2)}, u32[]{:S(2)}) collective-permute-start(bf16[1024,128]{1,0:T(8,128)(2,1)S(1)} %shard_map.60.refs_4_), channel_id=1, source_target_pairs={{0,8},{1,9},{2,10},{3,11},{4,12},{5,13},{6,14},{7,15},{8,0},{9,1},... | collective-permute-start | bytes 786440 | tf_op jit(solution)/shard_map/ppermute | solution.py:181
  48.7 15.5 %collective-permute-start.10 = (bf16[1024,128]{1,0:T(8,128)(2,1)S(1)}, bf16[1024,128]{1,0:T(8,128)(2,1)S(1)}, u32[]{:S(2)}, u32[]{:S(2)}) collective-permute-start(bf16[1024,128]{1,0:T(8,128)(2,1)S(1)} %shard_map.60.refs_4_), channel_id=1, source_target_pairs={{0,16},{1,17},{2,18},{3,19},{4,20},{5,21},{6,22},{7,23},{8,24},{9,... | collective-permute-start | bytes 786440 | tf_op jit(solution)/shard_map/ppermute | solution.py:181
  50.2 14.5 %collective-permute-start.15 = (bf16[1024,128]{1,0:T(8,128)(2,1)S(1)}, bf16[1024,128]{1,0:T(8,128)(2,1)S(1)}, u32[]{:S(2)}, u32[]{:S(2)}) collective-permute-start(bf16[1024,128]{1,0:T(8,128)(2,1)S(1)} %shard_map.62.refs_8_), channel_id=1, source_target_pairs={{0,8},{1,9},{2,10},{3,11},{4,12},{5,13},{6,14},{7,15},{8,0},{9,1},... | collective-permute-start | bytes 786440 | tf_op jit(solution)/shard_map/ppermute | solution.py:181
  50.9 9.7 %collective-permute-start.42 = (bf16[512,128]{1,0:T(8,128)(2,1)S(1)}, bf16[512,128]{1,0:T(8,128)(2,1)S(1)}, u32[]{:S(2)}, u32[]{:S(2)}) collective-permute-start(bf16[512,128]{1,0:T(8,128)(2,1)S(1)} %get-tuple-element.93), channel_id=1, source_target_pairs={{0,2},{1,3},{2,0},{3,1},{4,6},{5,7},{6,4},{7,5},{8,10},{9,11},{10,... | collective-permute-start | bytes 393224 | tf_op jit(solution)/shard_map/ppermute | solution.py:181
  63.9 11.5 %collective-permute-start.29 = (bf16[1024,128]{1,0:T(8,128)(2,1)S(1)}, bf16[1024,128]{1,0:T(8,128)(2,1)S(1)}, u32[]{:S(2)}, u32[]{:S(2)}) collective-permute-start(bf16[1024,128]{1,0:T(8,128)(2,1)S(1)} %get-tuple-element.81.refs_4_), channel_id=1, source_target_pairs={{0,16},{1,17},{2,18},{3,19},{4,20},{5,21},{6,22},{7,23},{8,24},{9,... | collective-permute-start | bytes 786440 | tf_op jit(solution)/shard_map/ppermute | solution.py:181
  64.2 13.1 %collective-permute-start.31 = (bf16[1024,128]{1,0:T(8,128)(2,1)S(1)}, bf16[1024,128]{1,0:T(8,128)(2,1)S(1)}, u32[]{:S(2)}, u32[]{:S(2)}) collective-permute-start(bf16[1024,128]{1,0:T(8,128)(2,1)S(1)} %get-tuple-element.82.refs_8_), channel_id=1, source_target_pairs={{0,8},{1,9},{2,10},{3,11},{4,12},{5,13},{6,14},{7,15},{8,0},{9,1},... | collective-permute-start | bytes 786440 | tf_op jit(solution)/shard_map/ppermute | solution.py:181
  64.8 16.3 %collective-permute-start.32 = (bf16[1024,128]{1,0:T(8,128)(2,1)S(1)}, bf16[1024,128]{1,0:T(8,128)(2,1)S(1)}, u32[]{:S(2)}, u32[]{:S(2)}) collective-permute-start(bf16[1024,128]{1,0:T(8,128)(2,1)S(1)} %get-tuple-element.82.refs_8_), channel_id=1, source_target_pairs={{0,16},{1,17},{2,18},{3,19},{4,20},{5,21},{6,22},{7,23},{8,24},{9,... | collective-permute-start | bytes 786440 | tf_op jit(solution)/shard_map/ppermute | solution.py:181
  69.8 16.9 %collective-permute-start.45 = (bf16[1024,128]{1,0:T(8,128)(2,1)S(1)}, bf16[1024,128]{1,0:T(8,128)(2,1)S(1)}, u32[]{:S(2)}, u32[]{:S(2)}) collective-permute-start(bf16[1024,128]{1,0:T(8,128)(2,1)S(1)} %get-tuple-element.95.refs_4_), channel_id=1, source_target_pairs={{0,16},{1,17},{2,18},{3,19},{4,20},{5,21},{6,22},{7,23},{8,24},{9,... | collective-permute-start | bytes 786440 | tf_op jit(solution)/shard_map/ppermute | solution.py:181
  71.7 16.7 %collective-permute-start.47 = (bf16[1024,128]{1,0:T(8,128)(2,1)S(1)}, bf16[1024,128]{1,0:T(8,128)(2,1)S(1)}, u32[]{:S(2)}, u32[]{:S(2)}) collective-permute-start(bf16[1024,128]{1,0:T(8,128)(2,1)S(1)} %get-tuple-element.96.refs_8_), channel_id=1, source_target_pairs={{0,8},{1,9},{2,10},{3,11},{4,12},{5,13},{6,14},{7,15},{8,0},{9,1},... | collective-permute-start | bytes 786440 | tf_op jit(solution)/shard_map/ppermute | solution.py:181
  75.4 14.5 %collective-permute-start.11 = (bf16[1024,128]{1,0:T(8,128)(2,1)S(1)}, bf16[1024,128]{1,0:T(8,128)(2,1)S(1)}, u32[]{:S(2)}, u32[]{:S(2)}) collective-permute-start(bf16[1024,128]{1,0:T(8,128)(2,1)S(1)} %collective-permute-done.10.refs_6_), channel_id=1, source_target_pairs={{0,8},{1,9},{2,10},{3,11},{4,12},{5,13},{6,14},{7,15},{8,0},{9,1},... | collective-permute-start | bytes 786440 | tf_op jit(solution)/shard_map/ppermute | solution.py:181
  77.3 15.0 %collective-permute-start.17 = (bf16[1024,128]{1,0:T(8,128)(2,1)S(1)}, bf16[1024,128]{1,0:T(8,128)(2,1)S(1)}, u32[]{:S(2)}, u32[]{:S(2)}) collective-permute-start(bf16[1024,128]{1,0:T(8,128)(2,1)S(1)} %collective-permute-done.15.refs_9_), channel_id=1, source_target_pairs={{0,16},{1,17},{2,18},{3,19},{4,20},{5,21},{6,22},{7,23},{8,24},{9,... | collective-permute-start | bytes 786440 | tf_op jit(solution)/shard_map/ppermute | solution.py:181
  81.1 13.0 %collective-permute-start.30 = (bf16[1024,128]{1,0:T(8,128)(2,1)S(1)}, bf16[1024,128]{1,0:T(8,128)(2,1)S(1)}, u32[]{:S(2)}, u32[]{:S(2)}) collective-permute-start(bf16[1024,128]{1,0:T(8,128)(2,1)S(1)} %collective-permute-done.29.refs_6_), channel_id=1, source_target_pairs={{0,8},{1,9},{2,10},{3,11},{4,12},{5,13},{6,14},{7,15},{8,0},{9,1},... | collective-permute-start | bytes 786440 | tf_op jit(solution)/shard_map/ppermute | solution.py:181
  86.7 14.6 %collective-permute-start.33 = (bf16[1024,128]{1,0:T(8,128)(2,1)S(1)}, bf16[1024,128]{1,0:T(8,128)(2,1)S(1)}, u32[]{:S(2)}, u32[]{:S(2)}) collective-permute-start(bf16[1024,128]{1,0:T(8,128)(2,1)S(1)} %collective-permute-done.31.refs_9_), channel_id=1, source_target_pairs={{0,16},{1,17},{2,18},{3,19},{4,20},{5,21},{6,22},{7,23},{8,24},{9,... | collective-permute-start | bytes 786440 | tf_op jit(solution)/shard_map/ppermute | solution.py:181
  88.4 22.7 %collective-permute-start.44 = (bf16[1024,128]{1,0:T(8,128)(2,1)S(1)}, bf16[1024,128]{1,0:T(8,128)(2,1)S(1)}, u32[]{:S(2)}, u32[]{:S(2)}) collective-permute-start(bf16[1024,128]{1,0:T(8,128)(2,1)S(1)} %get-tuple-element.95.refs_4_), channel_id=1, source_target_pairs={{0,8},{1,9},{2,10},{3,11},{4,12},{5,13},{6,14},{7,15},{8,0},{9,1},... | collective-permute-start | bytes 786440 | tf_op jit(solution)/shard_map/ppermute | solution.py:181
  89.9 21.2 %collective-permute-start.48 = (bf16[1024,128]{1,0:T(8,128)(2,1)S(1)}, bf16[1024,128]{1,0:T(8,128)(2,1)S(1)}, u32[]{:S(2)}, u32[]{:S(2)}) collective-permute-start(bf16[1024,128]{1,0:T(8,128)(2,1)S(1)} %get-tuple-element.96.refs_8_), channel_id=1, source_target_pairs={{0,16},{1,17},{2,18},{3,19},{4,20},{5,21},{6,22},{7,23},{8,24},{9,... | collective-permute-start | bytes 786440 | tf_op jit(solution)/shard_map/ppermute | solution.py:181
  92.3 20.6 %collective-permute-start.46 = (bf16[1024,128]{1,0:T(8,128)(2,1)S(1)}, bf16[1024,128]{1,0:T(8,128)(2,1)S(1)}, u32[]{:S(2)}, u32[]{:S(2)}) collective-permute-start(bf16[1024,128]{1,0:T(8,128)(2,1)S(1)} %collective-permute-done.45.refs_6_), channel_id=1, source_target_pairs={{0,8},{1,9},{2,10},{3,11},{4,12},{5,13},{6,14},{7,15},{8,0},{9,1},... | collective-permute-start | bytes 786440 | tf_op jit(solution)/shard_map/ppermute | solution.py:181
  94.1 21.4 %collective-permute-start.49 = (bf16[1024,128]{1,0:T(8,128)(2,1)S(1)}, bf16[1024,128]{1,0:T(8,128)(2,1)S(1)}, u32[]{:S(2)}, u32[]{:S(2)}) collective-permute-start(bf16[1024,128]{1,0:T(8,128)(2,1)S(1)} %collective-permute-done.47.refs_9_), channel_id=1, source_target_pairs={{0,16},{1,17},{2,18},{3,19},{4,20},{5,21},{6,22},{7,23},{8,24},{9,... | collective-permute-start | bytes 786440 | tf_op jit(solution)/shard_map/ppermute | solution.py:181
  110.7 11.1 %collective-permute-start.18 = (bf16[256,128]{1,0:T(8,128)(2,1)S(1)}, bf16[256,128]{1,0:T(8,128)(2,1)S(1)}, u32[]{:S(2)}, u32[]{:S(2)}) collective-permute-start(bf16[256,128]{1,0:T(8,128)(2,1)S(1)} %get-tuple-element.70), channel_id=1, source_target_pairs={{0,3},{1,0},{2,1},{3,2},{4,7},{5,4},{6,5},{7,6},{8,11},{9,8},{10,9... | collective-permute-start | bytes 196616 | tf_op jit(solution)/shard_map/ppermute | solution.py:181
  111.1 12.4 %collective-permute-start.19 = (bf16[256,128]{1,0:T(8,128)(2,1)S(1)}, bf16[256,128]{1,0:T(8,128)(2,1)S(1)}, u32[]{:S(2)}, u32[]{:S(2)}) collective-permute-start(bf16[256,128]{1,0:T(8,128)(2,1)S(1)} %get-tuple-element.71), channel_id=1, source_target_pairs={{0,2},{1,3},{2,0},{3,1},{4,6},{5,7},{6,4},{7,5},{8,10},{9,11},{10,... | collective-permute-start | bytes 196616 | tf_op jit(solution)/shard_map/ppermute | solution.py:181
  111.1 14.5 %collective-permute-start.20 = (bf16[256,128]{1,0:T(8,128)(2,1)S(1)}, bf16[256,128]{1,0:T(8,128)(2,1)S(1)}, u32[]{:S(2)}, u32[]{:S(2)}) collective-permute-start(bf16[256,128]{1,0:T(8,128)(2,1)S(1)} %get-tuple-element.72), channel_id=1, source_target_pairs={{0,1},{1,2},{2,3},{3,0},{4,5},{5,6},{6,7},{7,4},{8,9},{9,10},{10,1... | collective-permute-start | bytes 196616 | tf_op jit(solution)/shard_map/ppermute | solution.py:181
  112.9 13.3 %collective-permute-start.34 = (bf16[256,128]{1,0:T(8,128)(2,1)S(1)}, bf16[256,128]{1,0:T(8,128)(2,1)S(1)}, u32[]{:S(2)}, u32[]{:S(2)}) collective-permute-start(bf16[256,128]{1,0:T(8,128)(2,1)S(1)} %get-tuple-element.84), channel_id=1, source_target_pairs={{0,3},{1,0},{2,1},{3,2},{4,7},{5,4},{6,5},{7,6},{8,11},{9,8},{10,9... | collective-permute-start | bytes 196616 | tf_op jit(solution)/shard_map/ppermute | solution.py:181
  115.5 10.9 %collective-permute-start.35 = (bf16[256,128]{1,0:T(8,128)(2,1)S(1)}, bf16[256,128]{1,0:T(8,128)(2,1)S(1)}, u32[]{:S(2)}, u32[]{:S(2)}) collective-permute-start(bf16[256,128]{1,0:T(8,128)(2,1)S(1)} %get-tuple-element.85), channel_id=1, source_target_pairs={{0,2},{1,3},{2,0},{3,1},{4,6},{5,7},{6,4},{7,5},{8,10},{9,11},{10,... | collective-permute-start | bytes 196616 | tf_op jit(solution)/shard_map/ppermute | solution.py:181
  (27 other events, 159.3 us)

commit v2 on v1

v2 whole, which is shorter than its diff:
```python
import functools
import math

import jax
import jax.numpy as jnp
from jax import lax
from jax.experimental import pallas as pl
from jax.experimental.pallas import tpu as pltpu
from jax.sharding import PartitionSpec as P

HEAD_DIM = 128
AXES = ("blk", "head")
BF16 = jnp.bfloat16
F32 = jnp.float32
VMEM = pl.BlockSpec(memory_space=pltpu.VMEM)
PARAMS = pltpu.CompilerParams(vmem_limit_bytes=40 * 2**20)
EXPONENT = math.log2(math.e) / math.sqrt(HEAD_DIM)


def sds(*shape):
    return jax.ShapeDtypeStruct(shape, BF16)


class Line:
    def __init__(self):
        self.last = ()

    def call(self, body, outs, *args, flops=0, exps=0):
        skip = len(self.last)

        def without_last(*refs):
            body(*refs[skip:])

        size = sum(math.prod(a.shape) * a.dtype.itemsize for a in (*args, *outs))
        made = pl.pallas_call(
            without_last,
            out_shape=outs,
            in_specs=[pl.BlockSpec(memory_space=pl.ANY)] * skip + [VMEM] * len(args),
            out_specs=[VMEM] * len(outs),
            compiler_params=PARAMS,
            cost_estimate=pl.CostEstimate(flops=flops, bytes_accessed=size, transcendentals=exps),
        )(*self.last, *args)
        self.last = made[:1]
        return made


def read(refs, pieces):
    parts = [refs[source][first : first + rows, :] for source, first, rows in pieces]
    return parts[0] if len(parts) == 1 else jnp.concatenate(parts, axis=0)


def absorb(state, q, k, v):
    scores = lax.dot_general(q, k, (((1,), (1,)), ((), ())), preferred_element_type=F32)
    new_top = jnp.max(scores, axis=1, keepdims=True)
    if state is not None:
        top, total, accum = state
        new_top = jnp.maximum(top, new_top)
    weights = jnp.exp2((scores - new_top) * EXPONENT)
    part = jnp.sum(weights, axis=1, keepdims=True)
    mixed = jnp.dot(weights.astype(BF16), v, preferred_element_type=F32)
    if state is not None:
        shrink = jnp.exp2((top - new_top) * EXPONENT)
        part, mixed = total * shrink + part, accum * shrink + mixed
    return new_top, part, mixed


STEP = 512


def attend_body(queries, blocks, count, *refs):
    refs, outs = refs[:count], refs[count:]
    rows = outs[0].shape[0]
    per = STEP // rows
    for first in range(0, len(outs), per):
        q = read(refs, queries[first : first + per])
        state = None
        for keys, values in blocks:
            state = absorb(state, q, read(refs, keys), read(refs, values))
        _, total, accum = state
        result = (accum / total).astype(BF16)
        for place in range(per):
            outs[first + place][...] = result[place * rows : (place + 1) * rows]


class Arrays:
    def __init__(self):
        self.arrays = []

    def piece(self, array, first, rows):
        for place, known in enumerate(self.arrays):
            if known is array:
                return place, first, rows
        self.arrays.append(array)
        return len(self.arrays) - 1, first, rows

    def pieces(self, parts):
        return [self.piece(*part) for part in parts]


def attend(line, queries, blocks):
    known = Arrays()
    queries = known.pieces(queries)
    blocks = [(known.pieces(keys), known.pieces(values)) for keys, values in blocks]
    pairs = sum(q[2] for q in queries) * sum(k[2] for keys, _ in blocks for k in keys)
    return line.call(
        functools.partial(attend_body, queries, blocks, len(known.arrays)),
        [sds(q[2], HEAD_DIM) for q in queries],
        *known.arrays,
        flops=4 * pairs * HEAD_DIM,
        exps=pairs,
    )


def core_index():
    return lax.rem(lax.axis_index("blk"), 2)


def halves_body(x_ref, other_ref):
    half = x_ref.shape[1] // 2
    other = pl.multiple_of((1 - core_index()) * half, half)
    other_ref[...] = x_ref[:, pl.ds(other, half)]


def normalize_body(x_ref, gain_ref, own_ref, other_ref):
    half = x_ref.shape[1] // 2
    wide = x_ref[...].astype(F32)
    scale = lax.rsqrt(jnp.mean(wide * wide, axis=1, keepdims=True) + 1e-06)
    core = core_index()
    for ref, side in ((own_ref, core), (other_ref, 1 - core)):
        at = pl.ds(pl.multiple_of(side * half, half), half)
        ref[...] = (x_ref[:, at].astype(F32) * scale * gain_ref[:, at]).astype(BF16)


def column(piece, hop):
    z = lax.axis_index("head")
    bit, pair = lax.rem(z, 2), lax.div(z, 2)
    bit = 1 - bit if hop & 1 else bit
    pair = 1 - pair if hop & 2 else pair
    return pl.multiple_of((piece * 4 + pair * 2 + bit) * HEAD_DIM, HEAD_DIM)


def pack_body(heads, half, *refs):
    ins, outs = refs[: -len(heads)], refs[-len(heads) :]
    for out, group in zip(outs, heads):
        at = 0
        for tensor, piece, hop in group:
            start = column(piece, hop)
            for ref in ins[2 * tensor : 2 * tensor + 2]:
                tokens = ref.shape[0]
                here = start
                if ref.shape[1] != half:
                    here = pl.multiple_of(core_index() * half + start, HEAD_DIM)
                out[at : at + tokens, :] = ref[:, pl.ds(here, HEAD_DIM)]
                at += tokens


def pack(line, heads, tensors):
    flat = [a for pair in tensors for a in pair]
    tokens = flat[0].shape[0]
    half = min(a.shape[1] for a in flat)
    outs = [sds(2 * tokens * len(group), HEAD_DIM) for group in heads]
    return line.call(functools.partial(pack_body, heads, half), outs, *flat)


def join_body(layout, count, *refs):
    for out, pieces in zip(refs[count:], layout):
        at = 0
        for source, first, rows in pieces:
            out[at : at + rows, :] = refs[source][first : first + rows, :]
            at += rows


def join(line, layout):
    known = Arrays()
    layout = [known.pieces(parts) for parts in layout]
    outs = [sds(sum(rows for _, _, rows in parts), HEAD_DIM) for parts in layout]
    return line.call(functools.partial(join_body, layout, len(known.arrays)), outs, *known.arrays)


def place_body(pieces, *refs):
    out = refs[-1]
    tokens, half = out.shape[0], out.shape[1] // 2
    core = core_index()
    for piece in range(pieces):
        own, across = refs[2 * piece : 2 * piece + 2]
        for hop in range(4):
            at = column(piece, hop)
            here = pl.multiple_of(core * half + at, HEAD_DIM)
            there = pl.multiple_of((1 - core) * half + at, HEAD_DIM)
            rows = slice(hop * tokens, (hop + 1) * tokens)
            out[:, pl.ds(here, HEAD_DIM)] = own[rows, :]
            out[:, pl.ds(there, HEAD_DIM)] = across[rows, :]


def permute(array, move):
    pairs = []
    for y in range(2):
        for x in range(2):
            for core in range(2):
                for z in range(4):
                    to = move(y, x, core, z)
                    pairs.append(
                        ((y * 4 + x * 2 + core) * 4 + z, (to[0] * 4 + to[1] * 2 + to[2]) * 4 + to[3])
                    )
    return lax.ppermute(array, AXES, pairs)


def other_core(array):
    return permute(array, lambda y, x, core, z: (y, x, 1 - core, z))


def other_x(array):
    return permute(array, lambda y, x, core, z: (y, 1 - x, core, z))


def other_y(array):
    return permute(array, lambda y, x, core, z: (1 - y, x, core, z))


def hop_z(array, hop):
    return permute(array, lambda y, x, core, z: (y, x, core, z ^ hop))


def hops(buffers):
    return [hop_z(buffer, hop) for hop, buffer in enumerate(buffers, 1)]


def shards_fast(queries, keys, values, query_gain, key_gain):
    tokens, width = queries.shape
    half, part = width // 2, 2 * tokens
    rest = 3 * part
    query_gain, key_gain = query_gain.reshape(1, width), key_gain.reshape(1, width)
    line = Line()

    def swap_halves(x, gain):
        own, other = line.call(normalize_body, [sds(tokens, half)] * 2, x, gain)
        return own, other_core(other)

    def hand_back(outs):
        back = [outs[0], *hops(outs[1:])]
        layout = [[(a, 0, tokens) for a in back], [(a, tokens, tokens) for a in back]]
        own, across = join(line, layout)
        return own, other_core(across)

    (v_other,) = line.call(halves_body, [sds(tokens, half)], values)
    v_pair = (values, other_core(v_other))
    k_pair = swap_halves(keys, key_gain)
    q_pair = swap_halves(queries, query_gain)
    tensors = (k_pair, v_pair, q_pair)
    k, v, q = range(3)

    out = pack(
        line,
        [[(t, c, 0) for c in range(3) for t in (k, v)]]
        + [[(k, 0, hop), (v, 0, hop)] for hop in (1, 2, 3)],
        tensors[:2],
    )
    own = out[0]
    came = hops(out[1:])
    own_x, own_y = other_x(own), other_y(own)

    def key_rows(array, chunk):
        return array, 2 * chunk * part, part

    def value_rows(array, chunk):
        return array, (2 * chunk + 1) * part, part

    sends, received = [], []
    results = []
    q_slots = []
    for step in range(5):
        if step == 0:
            along_x = [key_rows(own_y, c) for c in range(3)]
            along_y = [value_rows(own_x, c) for c in range(3)]
        elif step < 4:
            got_x, got_y = received[-1]
            along_x = [(got_y, rest, rest)]
            along_y = [(got_x, 2 * rest, rest)]
        if step < 3:
            block = [(a, 0, part) for a in came] + [(a, part, part) for a in came]
            along_x, along_y = along_x + block, along_y + block
        if step < 4:
            x_out, y_out = join(line, [along_x, along_y])
            sends.append(x_out)
            received.append((other_x(x_out), other_y(y_out)))
        if step == 2:
            q_slots.append([(own_q, 0, part)] + [(a, 2 * part, part) for a in came])
        if step == 3:
            for c in (0, 1):
                q_slots.append([(own_q, (c + 1) * part, part)] + [(a, c * part, part) for a in came])
        if step == 0:
            (*out,) = pack(line, [[(k, 1, hop), (v, 1, hop)] for hop in (1, 2, 3)], tensors[:2])
            came = hops(out)
        if step == 1:
            own_q, *out = pack(
                line,
                [[(q, c, 0) for c in range(3)]]
                + [[(k, 2, hop), (v, 2, hop), (q, 0, hop)] for hop in (1, 2, 3)],
                tensors,
            )
            came = hops(out)
        if step == 2:
            out = pack(line, [[(0, 1, hop), (0, 2, hop)] for hop in (1, 2, 3)], (q_pair,))
            came = hops(out)
        if step >= 2:
            chunk = step - 2
            got_x, got_y = received[chunk]
            far_x, far_y = received[chunk + 1]
            blocks = []
            for mine, more in ((own, sends[chunk]), (own_x, got_x), (own_y, got_y)):
                blocks.append(
                    (
                        [key_rows(mine, chunk), (more, rest, rest)],
                        [value_rows(mine, chunk), (more, 2 * rest, rest)],
                    )
                )
            first_x, first_y = received[0]
            blocks.append(
                (
                    [(first_x, chunk * part, part), (far_x, 0, rest)],
                    [(first_y, chunk * part, part), (far_y, 0, rest)],
                )
            )
            results += hand_back(attend(line, q_slots[chunk], blocks))
    (attended,) = line.call(functools.partial(place_body, 3), [sds(tokens, width)], *results)
    return attended


def whole_head_body(q_ref, k_ref, v_ref, out_ref, top, total, accum):
    step = pl.program_id(2)

    @pl.when(step == 0)
    def _():
        top[...] = jnp.full_like(top, -jnp.inf)
        total[...] = jnp.zeros_like(total)
        accum[...] = jnp.zeros_like(accum)

    scores = lax.dot_general(
        q_ref[...], k_ref[...], (((1,), (1,)), ((), ())), preferred_element_type=F32
    )
    new_top = jnp.maximum(top[...], jnp.max(scores, axis=1, keepdims=True))
    weights = jnp.exp2((scores - new_top) * EXPONENT)
    shrink = jnp.exp2((top[...] - new_top) * EXPONENT)
    total[...] = total[...] * shrink + jnp.sum(weights, axis=1, keepdims=True)
    accum[...] = accum[...] * shrink + jnp.dot(
        weights.astype(BF16), v_ref[...], preferred_element_type=F32
    )
    top[...] = new_top

    @pl.when(step == pl.num_programs(2) - 1)
    def _():
        out_ref[...] = (accum[...] / total[...]).astype(BF16)


def normalize(block, gain):
    wide = block.astype(F32)
    mean_sq = jnp.mean(wide * wide, axis=-1, keepdims=True)
    return (wide * lax.rsqrt(mean_sq + 1e-06) * gain).astype(BF16)


def shards_any(queries, keys, values, query_gain, key_gain):
    def regroup(x):
        return lax.all_to_all(x, "head", split_axis=1, concat_axis=0, tiled=True)

    q = regroup(normalize(queries, query_gain))
    k = lax.all_gather(regroup(normalize(keys, key_gain)), "blk", axis=0, tiled=True)
    v = lax.all_gather(regroup(values), "blk", axis=0, tiled=True)
    rows, width = q.shape
    length = k.shape[0]
    q_rows, k_rows = math.gcd(rows, 512), math.gcd(length, 1024)
    result = pl.pallas_call(
        whole_head_body,
        grid=(width // HEAD_DIM, rows // q_rows, length // k_rows),
        out_shape=sds(rows, width),
        in_specs=[
            pl.BlockSpec((q_rows, HEAD_DIM), lambda h, i, j: (i, h)),
            pl.BlockSpec((k_rows, HEAD_DIM), lambda h, i, j: (j, h)),
            pl.BlockSpec((k_rows, HEAD_DIM), lambda h, i, j: (j, h)),
        ],
        out_specs=pl.BlockSpec((q_rows, HEAD_DIM), lambda h, i, j: (i, h)),
        scratch_shapes=[
            pltpu.VMEM((q_rows, 1), F32),
            pltpu.VMEM((q_rows, 1), F32),
            pltpu.VMEM((q_rows, HEAD_DIM), F32),
        ],
        compiler_params=PARAMS,
    )(q, k, v)
    return lax.all_to_all(result, "head", split_axis=0, concat_axis=1, tiled=True)


def solution(mesh):
    fast = mesh.shape["blk"] == 8 and mesh.shape["head"] == 4
    rows = P(AXES, None)
    return jax.shard_map(
        shards_fast if fast else shards_any,
        mesh=mesh,
        in_specs=(rows, rows, rows, P(), P()),
        out_specs=rows,
        check_vma=False,
    )
```

time: 135 us -> 119 us (0.88)
  starting transfers between devices: 80.6 us -> 46.3 us
  waiting for transfers between devices: 31.2 us -> 50.9 us
    ppermute x54 -> x37, starting transfers between devices: 80.6 us -> 46.3 us  [permute(): return lax.ppermute(array, AXES, pairs)]
    ppermute x54 -> x37, waiting for transfers between devices: 31.2 us -> 50.9 us  [permute(): return lax.ppermute(array, AXES, pairs)]
    unnamed x10 -> x12, local copies, waits for them, and re-layouts: 2.98 us -> 1.72 us
    pallas_call x17 -> x18, Pallas kernels: 19.7 us -> 20.1 us  [call(): pl.pallas_call(without_last, out_shape=outs, in_specs=[pl.BlockSpec(memor...]
  transfers between devices with their start and end apart: 54 -> 37, of which waited for: 17 -> 16; matrix products, arithmetic and copies ran while one was open for 0% -> 0% of each run, Pallas kernels for 13% -> 11%
where the time goes in v2:
time: 119 us
  waiting for transfers between devices  50.9 us (43%)
  starting transfers between devices  46.3 us (39%)
  Pallas kernels  20.1 us (17%)
  local copies, waits for them, and re-layouts  1.72 us (1%)
    ppermute x37, waiting for transfers between devices, permute(): return lax.ppermute(array, AXES, pairs)  50.9 us
    ppermute x37, starting transfers between devices, permute(): return lax.ppermute(array, AXES, pairs)  46.3 us
    pallas_call x18, Pallas kernels, call(): pl.pallas_call(without_last, out_shape=outs, in_specs=[pl.BlockSpec(memor...  20.1 us
  transfers between devices with their start and end apart: 37, of which 16 were waited for; matrix products, arithmetic and copies ran while one was open for 0% of the time, Pallas kernels for 11%

profile of v2, /device:TPU:0, one launch (start us, length us, event | category | flops | bytes accessed | tf_op | source)
XLA Modules:
  0.0 119.3 jit_solution(7292282997631680702)
XLA Ops:
  4.8 2.9 %collective-permute-start.6 = (bf16[1536,128]{1,0:T(8,128)(2,1)S(1)}, bf16[1536,128]{1,0:T(8,128)(2,1)S(1)}, u32[]{:S(2)}, u32[]{:S(2)}) collective-permute-start(bf16[1536,128]{1,0:T(8,128)(2,1)S(1)} %get-tuple-element.52.refs_0_.refs_5_), channel_id=1, source_target_pairs={{0,8},{1,9},{2,10},{3,11},{4,12},{5,13},{6,14},{7,15},{8,0},{9,1},... | collective-permute-start | bytes 1179656 | tf_op jit(solution)/shard_map/ppermute | solution.py:205
  7.7 1.5 %collective-permute-start.2 = (bf16[1536,128]{1,0:T(8,128)(2,1)S(1)}, bf16[1536,128]{1,0:T(8,128)(2,1)S(1)}, u32[]{:S(2)}, u32[]{:S(2)}) collective-permute-start(bf16[1536,128]{1,0:T(8,128)(2,1)S(1)} %get-tuple-element.52.refs_0_.refs_5_), channel_id=1, source_target_pairs={{0,16},{1,17},{2,18},{3,19},{4,20},{5,21},{6,22},{7,23},{8,24},{9,... | collective-permute-start | bytes 1179656 | tf_op jit(solution)/shard_map/ppermute | solution.py:205
  9.2 1.6 %collective-permute-start.3 = (bf16[512,128]{1,0:T(8,128)(2,1)S(1)}, bf16[512,128]{1,0:T(8,128)(2,1)S(1)}, u32[]{:S(2)}, u32[]{:S(2)}) collective-permute-start(bf16[512,128]{1,0:T(8,128)(2,1)S(1)} %get-tuple-element.53), channel_id=1, source_target_pairs={{0,1},{1,0},{2,3},{3,2},{4,5},{5,4},{6,7},{7,6},{8,9},{9,8},{10,11... | collective-permute-start | bytes 393224 | tf_op jit(solution)/shard_map/ppermute | solution.py:205
  10.8 2.6 %collective-permute-start.4 = (bf16[512,128]{1,0:T(8,128)(2,1)S(1)}, bf16[512,128]{1,0:T(8,128)(2,1)S(1)}, u32[]{:S(2)}, u32[]{:S(2)}) collective-permute-start(bf16[512,128]{1,0:T(8,128)(2,1)S(1)} %get-tuple-element.54), channel_id=1, source_target_pairs={{0,2},{1,3},{2,0},{3,1},{4,6},{5,7},{6,4},{7,5},{8,10},{9,11},{10,... | collective-permute-start | bytes 393224 | tf_op jit(solution)/shard_map/ppermute | solution.py:205
  13.6 2.1 %collective-permute-done.3.refs_2_ = bf16[512,128]{1,0:T(8,128)(2,1)S(1)} collective-permute-done((bf16[512,128]{1,0:T(8,128)(2,1)S(1)}, bf16[512,128]{1,0:T(8,128)(2,1)S(1)}, u32[]{:S(2)}, u32[]{:S(2)}) %collective-permute-start.3) | collective-permute-done | bytes 131104 | tf_op jit(solution)/shard_map/ppermute | solution.py:205
  15.7 7.8 %collective-permute-done.4.refs_3_ = bf16[512,128]{1,0:T(8,128)(2,1)S(1)} collective-permute-done((bf16[512,128]{1,0:T(8,128)(2,1)S(1)}, bf16[512,128]{1,0:T(8,128)(2,1)S(1)}, u32[]{:S(2)}, u32[]{:S(2)}) %collective-permute-start.4) | collective-permute-done | bytes 131104 | tf_op jit(solution)/shard_map/ppermute | solution.py:205
  24.8 3.0 %collective-permute-start.9 = (bf16[512,128]{1,0:T(8,128)(2,1)S(1)}, bf16[512,128]{1,0:T(8,128)(2,1)S(1)}, u32[]{:S(2)}, u32[]{:S(2)}) collective-permute-start(bf16[512,128]{1,0:T(8,128)(2,1)S(1)} %get-tuple-element.59), channel_id=1, source_target_pairs={{0,2},{1,3},{2,0},{3,1},{4,6},{5,7},{6,4},{7,5},{8,10},{9,11},{10,... | collective-permute-start | bytes 393224 | tf_op jit(solution)/shard_map/ppermute | solution.py:205
  27.8 1.4 %collective-permute-start.10 = (bf16[512,128]{1,0:T(8,128)(2,1)S(1)}, bf16[512,128]{1,0:T(8,128)(2,1)S(1)}, u32[]{:S(2)}, u32[]{:S(2)}) collective-permute-start(bf16[512,128]{1,0:T(8,128)(2,1)S(1)} %get-tuple-element.60), channel_id=1, source_target_pairs={{0,3},{1,2},{2,1},{3,0},{4,7},{5,6},{6,5},{7,4},{8,11},{9,10},{10,... | collective-permute-start | bytes 393224 | tf_op jit(solution)/shard_map/ppermute | solution.py:205
  29.2 7.3 %collective-permute-done.9.refs_3_ = bf16[512,128]{1,0:T(8,128)(2,1)S(1)} collective-permute-done((bf16[512,128]{1,0:T(8,128)(2,1)S(1)}, bf16[512,128]{1,0:T(8,128)(2,1)S(1)}, u32[]{:S(2)}, u32[]{:S(2)}) %collective-permute-start.9) | collective-permute-done | bytes 131104 | tf_op jit(solution)/shard_map/ppermute | solution.py:205
  36.8 1.6 %collective-permute-start.13 = (bf16[2304,128]{1,0:T(8,128)(2,1)S(1)}, bf16[2304,128]{1,0:T(8,128)(2,1)S(1)}, u32[]{:S(2)}, u32[]{:S(2)}) collective-permute-start(bf16[2304,128]{1,0:T(8,128)(2,1)S(1)} %get-tuple-element.64), channel_id=1, source_target_pairs={{0,16},{1,17},{2,18},{3,19},{4,20},{5,21},{6,22},{7,23},{8,24},{9,... | collective-permute-start | bytes 1769480 | tf_op jit(solution)/shard_map/ppermute | solution.py:205
  38.3 1.5 %collective-permute-start.17 = (bf16[2304,128]{1,0:T(8,128)(2,1)S(1)}, bf16[2304,128]{1,0:T(8,128)(2,1)S(1)}, u32[]{:S(2)}, u32[]{:S(2)}) collective-permute-start(bf16[2304,128]{1,0:T(8,128)(2,1)S(1)} %get-tuple-element.61.refs_0_.refs_6_), channel_id=1, source_target_pairs={{0,8},{1,9},{2,10},{3,11},{4,12},{5,13},{6,14},{7,15},{8,0},{9,1},... | collective-permute-start | bytes 1769480 | tf_op jit(solution)/shard_map/ppermute | solution.py:205
  40.0 2.1 %collective-permute-start.14 = (bf16[768,128]{1,0:T(8,128)(2,1)S(1)}, bf16[768,128]{1,0:T(8,128)(2,1)S(1)}, u32[]{:S(2)}, u32[]{:S(2)}) collective-permute-start(bf16[768,128]{1,0:T(8,128)(2,1)S(1)} %get-tuple-element.65), channel_id=1, source_target_pairs={{0,1},{1,0},{2,3},{3,2},{4,5},{5,4},{6,7},{7,6},{8,9},{9,8},{10,11... | collective-permute-start | bytes 589832 | tf_op jit(solution)/shard_map/ppermute | solution.py:205
  43.4 1.4 %collective-permute-start.16 = (bf16[768,128]{1,0:T(8,128)(2,1)S(1)}, bf16[768,128]{1,0:T(8,128)(2,1)S(1)}, u32[]{:S(2)}, u32[]{:S(2)}) collective-permute-start(bf16[768,128]{1,0:T(8,128)(2,1)S(1)} %get-tuple-element.67), channel_id=1, source_target_pairs={{0,3},{1,2},{2,1},{3,0},{4,7},{5,6},{6,5},{7,4},{8,11},{9,10},{10,... | collective-permute-start | bytes 589832 | tf_op jit(solution)/shard_map/ppermute | solution.py:205
  44.7 6.9 %collective-permute-done.14.refs_2_ = bf16[768,128]{1,0:T(8,128)(2,1)S(1)} collective-permute-done((bf16[768,128]{1,0:T(8,128)(2,1)S(1)}, bf16[768,128]{1,0:T(8,128)(2,1)S(1)}, u32[]{:S(2)}, u32[]{:S(2)}) %collective-permute-start.14) | collective-permute-done | bytes 196640 | tf_op jit(solution)/shard_map/ppermute | solution.py:205
  51.6 5.8 %collective-permute-done.15.refs_3_ = bf16[768,128]{1,0:T(8,128)(2,1)S(1)} collective-permute-done((bf16[768,128]{1,0:T(8,128)(2,1)S(1)}, bf16[768,128]{1,0:T(8,128)(2,1)S(1)}, u32[]{:S(2)}, u32[]{:S(2)}) %collective-permute-start.15) | collective-permute-done | bytes 196640 | tf_op jit(solution)/shard_map/ppermute | solution.py:205
  58.1 1.4 %collective-permute-start.22 = (bf16[2304,128]{1,0:T(8,128)(2,1)S(1)}, bf16[2304,128]{1,0:T(8,128)(2,1)S(1)}, u32[]{:S(2)}, u32[]{:S(2)}) collective-permute-start(bf16[2304,128]{1,0:T(8,128)(2,1)S(1)} %get-tuple-element.68.refs_0_.refs_6_), channel_id=1, source_target_pairs={{0,8},{1,9},{2,10},{3,11},{4,12},{5,13},{6,14},{7,15},{8,0},{9,1},... | collective-permute-start | bytes 1769480 | tf_op jit(solution)/shard_map/ppermute | solution.py:205
  59.6 5.7 %shard_map.65 = (bf16[256,128]{1,0:T(8,128)(2,1)S(1)}, bf16[256,128]{1,0:T(8,128)(2,1)S(1)}, bf16[256,128]{1,0:T(8,128)(2,1)S(1)}, bf16[256,128]{1,0:T(8,128)(2,1)S(1)}) custom-call(bf16[512,128]{1,0:T(8,128)(2,1)S(1)} %get-tuple-element.69.refs_0_, bf16[768,128]{1,0:T(8,128)(2,1)S(1)} %get-tuple-element.63.refs_0_.refs_1_, ...), custom_call_target="tpu_custom_call" | custom-call | flops 2147483648 | bytes 5177344 | tf_op jit(solution)/shard_map/pallas_call | solution.py:35
  65.3 3.4 %collective-permute-start.18 = (bf16[256,128]{1,0:T(8,128)(2,1)S(1)}, bf16[256,128]{1,0:T(8,128)(2,1)S(1)}, u32[]{:S(2)}, u32[]{:S(2)}) collective-permute-start(bf16[256,128]{1,0:T(8,128)(2,1)S(1)} %get-tuple-element.71), channel_id=1, source_target_pairs={{0,1},{1,0},{2,3},{3,2},{4,5},{5,4},{6,7},{7,6},{8,9},{9,8},{10,11... | collective-permute-start | bytes 196616 | tf_op jit(solution)/shard_map/ppermute | solution.py:205
  69.1 2.0 %collective-permute-start.20 = (bf16[256,128]{1,0:T(8,128)(2,1)S(1)}, bf16[256,128]{1,0:T(8,128)(2,1)S(1)}, u32[]{:S(2)}, u32[]{:S(2)}) collective-permute-start(bf16[256,128]{1,0:T(8,128)(2,1)S(1)} %get-tuple-element.73), channel_id=1, source_target_pairs={{0,3},{1,2},{2,1},{3,0},{4,7},{5,6},{6,5},{7,4},{8,11},{9,10},{10,... | collective-permute-start | bytes 196616 | tf_op jit(solution)/shard_map/ppermute | solution.py:205
  73.3 6.4 %collective-permute-done.19.refs_3_ = bf16[256,128]{1,0:T(8,128)(2,1)S(1)} collective-permute-done((bf16[256,128]{1,0:T(8,128)(2,1)S(1)}, bf16[256,128]{1,0:T(8,128)(2,1)S(1)}, u32[]{:S(2)}, u32[]{:S(2)}) %collective-permute-start.19) | collective-permute-done | bytes 65568 | tf_op jit(solution)/shard_map/ppermute | solution.py:205
  79.7 1.9 %collective-permute-start.25 = (bf16[512,128]{1,0:T(8,128)(2,1)S(1)}, bf16[512,128]{1,0:T(8,128)(2,1)S(1)}, u32[]{:S(2)}, u32[]{:S(2)}) collective-permute-start(bf16[512,128]{1,0:T(8,128)(2,1)S(1)} %get-tuple-element.78), channel_id=1, source_target_pairs={{0,3},{1,2},{2,1},{3,0},{4,7},{5,6},{6,5},{7,4},{8,11},{9,10},{10,... | collective-permute-start | bytes 393224 | tf_op jit(solution)/shard_map/ppermute | solution.py:205
  82.0 1.5 %collective-permute-start.30 = (bf16[768,128]{1,0:T(8,128)(2,1)S(1)}, bf16[768,128]{1,0:T(8,128)(2,1)S(1)}, u32[]{:S(2)}, u32[]{:S(2)}) collective-permute-start(bf16[768,128]{1,0:T(8,128)(2,1)S(1)} %get-tuple-element.84), channel_id=1, source_target_pairs={{0,16},{1,17},{2,18},{3,19},{4,20},{5,21},{6,22},{7,23},{8,24},{9,... | collective-permute-start | bytes 589832 | tf_op jit(solution)/shard_map/ppermute | solution.py:205
  84.5 2.1 %collective-permute-done.25.refs_4_ = bf16[512,128]{1,0:T(8,128)(2,1)S(1)} collective-permute-done((bf16[512,128]{1,0:T(8,128)(2,1)S(1)}, bf16[512,128]{1,0:T(8,128)(2,1)S(1)}, u32[]{:S(2)}, u32[]{:S(2)}) %collective-permute-start.25) | collective-permute-done | bytes 131104 | tf_op jit(solution)/shard_map/ppermute | solution.py:205
  87.9 5.9 %shard_map.68 = (bf16[256,128]{1,0:T(8,128)(2,1)S(1)}, bf16[256,128]{1,0:T(8,128)(2,1)S(1)}, bf16[256,128]{1,0:T(8,128)(2,1)S(1)}, bf16[256,128]{1,0:T(8,128)(2,1)S(1)}) custom-call(bf16[768,128]{1,0:T(8,128)(2,1)S(1)} %get-tuple-element.76.refs_0_, bf16[768,128]{1,0:T(8,128)(2,1)S(1)} %get-tuple-element.63.refs_0_.refs_1_, ...), custom_call_target="tpu_custom_call" | custom-call | flops 2147483648 | bytes 6160384 | tf_op jit(solution)/shard_map/pallas_call | solution.py:35
  93.9 2.4 %collective-permute-start.27 = (bf16[256,128]{1,0:T(8,128)(2,1)S(1)}, bf16[256,128]{1,0:T(8,128)(2,1)S(1)}, u32[]{:S(2)}, u32[]{:S(2)}) collective-permute-start(bf16[256,128]{1,0:T(8,128)(2,1)S(1)} %get-tuple-element.81), channel_id=1, source_target_pairs={{0,2},{1,3},{2,0},{3,1},{4,6},{5,7},{6,4},{7,5},{8,10},{9,11},{10,... | collective-permute-start | bytes 196616 | tf_op jit(solution)/shard_map/ppermute | solution.py:205
  96.3 2.0 %collective-permute-start.28 = (bf16[256,128]{1,0:T(8,128)(2,1)S(1)}, bf16[256,128]{1,0:T(8,128)(2,1)S(1)}, u32[]{:S(2)}, u32[]{:S(2)}) collective-permute-start(bf16[256,128]{1,0:T(8,128)(2,1)S(1)} %get-tuple-element.82), channel_id=1, source_target_pairs={{0,3},{1,2},{2,1},{3,0},{4,7},{5,6},{6,5},{7,4},{8,11},{9,10},{10,... | collective-permute-start | bytes 196616 | tf_op jit(solution)/shard_map/ppermute | solution.py:205
  99.1 3.2 %collective-permute-done.28.refs_4_ = bf16[256,128]{1,0:T(8,128)(2,1)S(1)} collective-permute-done((bf16[256,128]{1,0:T(8,128)(2,1)S(1)}, bf16[256,128]{1,0:T(8,128)(2,1)S(1)}, u32[]{:S(2)}, u32[]{:S(2)}) %collective-permute-start.28) | collective-permute-done | bytes 65568 | tf_op jit(solution)/shard_map/ppermute | solution.py:205
  102.4 5.7 %shard_map.70 = (bf16[256,128]{1,0:T(8,128)(2,1)S(1)}, bf16[256,128]{1,0:T(8,128)(2,1)S(1)}, bf16[256,128]{1,0:T(8,128)(2,1)S(1)}, bf16[256,128]{1,0:T(8,128)(2,1)S(1)}) custom-call(bf16[512,128]{1,0:T(8,128)(2,1)S(1)} %get-tuple-element.83.refs_0_.refs_3_, bf16[768,128]{1,0:T(8,128)(2,1)S(1)} %get-tuple-element.63.refs_0_.refs_1_, ...), custom_call_target="tpu_custom_call" | custom-call | flops 2147483648 | bytes 5373952 | tf_op jit(solution)/shard_map/pallas_call | solution.py:35
  108.2 2.5 %collective-permute-start.32 = (bf16[256,128]{1,0:T(8,128)(2,1)S(1)}, bf16[256,128]{1,0:T(8,128)(2,1)S(1)}, u32[]{:S(2)}, u32[]{:S(2)}) collective-permute-start(bf16[256,128]{1,0:T(8,128)(2,1)S(1)} %get-tuple-element.87), channel_id=1, source_target_pairs={{0,2},{1,3},{2,0},{3,1},{4,6},{5,7},{6,4},{7,5},{8,10},{9,11},{10,... | collective-permute-start | bytes 196616 | tf_op jit(solution)/shard_map/ppermute | solution.py:205
  110.7 1.8 %collective-permute-start.33 = (bf16[256,128]{1,0:T(8,128)(2,1)S(1)}, bf16[256,128]{1,0:T(8,128)(2,1)S(1)}, u32[]{:S(2)}, u32[]{:S(2)}) collective-permute-start(bf16[256,128]{1,0:T(8,128)(2,1)S(1)} %get-tuple-element.88), channel_id=1, source_target_pairs={{0,3},{1,2},{2,1},{3,0},{4,7},{5,6},{6,5},{7,4},{8,11},{9,10},{10,... | collective-permute-start | bytes 196616 | tf_op jit(solution)/shard_map/ppermute | solution.py:205
  113.4 3.4 %collective-permute-done.33.refs_4_ = bf16[256,128]{1,0:T(8,128)(2,1)S(1)} collective-permute-done((bf16[256,128]{1,0:T(8,128)(2,1)S(1)}, bf16[256,128]{1,0:T(8,128)(2,1)S(1)}, u32[]{:S(2)}, u32[]{:S(2)}) %collective-permute-start.33) | collective-permute-done | bytes 65568 | tf_op jit(solution)/shard_map/ppermute | solution.py:205
  116.9 1.3 %collective-permute-done.36.refs_6_ = bf16[512,128]{1,0:T(8,128)(2,1)S(1)} collective-permute-done((bf16[512,128]{1,0:T(8,128)(2,1)S(1)}, bf16[512,128]{1,0:T(8,128)(2,1)S(1)}, u32[]{:S(2)}, u32[]{:S(2)}) %collective-permute-start.36) | collective-permute-done | bytes 131104 | tf_op jit(solution)/shard_map/ppermute | solution.py:205
  (72 shorter events, 17.2 us)
Async XLA Ops:
  4.8 18.7 %collective-permute-start.6 = (bf16[1536,128]{1,0:T(8,128)(2,1)S(1)}, bf16[1536,128]{1,0:T(8,128)(2,1)S(1)}, u32[]{:S(2)}, u32[]{:S(2)}) collective-permute-start(bf16[1536,128]{1,0:T(8,128)(2,1)S(1)} %get-tuple-element.52.refs_0_.refs_5_), channel_id=1, source_target_pairs={{0,8},{1,9},{2,10},{3,11},{4,12},{5,13},{6,14},{7,15},{8,0},{9,1},... | collective-permute-start | bytes 1179656 | tf_op jit(solution)/shard_map/ppermute | solution.py:205
  7.7 15.8 %collective-permute-start.2 = (bf16[1536,128]{1,0:T(8,128)(2,1)S(1)}, bf16[1536,128]{1,0:T(8,128)(2,1)S(1)}, u32[]{:S(2)}, u32[]{:S(2)}) collective-permute-start(bf16[1536,128]{1,0:T(8,128)(2,1)S(1)} %get-tuple-element.52.refs_0_.refs_5_), channel_id=1, source_target_pairs={{0,16},{1,17},{2,18},{3,19},{4,20},{5,21},{6,22},{7,23},{8,24},{9,... | collective-permute-start | bytes 1179656 | tf_op jit(solution)/shard_map/ppermute | solution.py:205
  9.2 6.5 %collective-permute-start.3 = (bf16[512,128]{1,0:T(8,128)(2,1)S(1)}, bf16[512,128]{1,0:T(8,128)(2,1)S(1)}, u32[]{:S(2)}, u32[]{:S(2)}) collective-permute-start(bf16[512,128]{1,0:T(8,128)(2,1)S(1)} %get-tuple-element.53), channel_id=1, source_target_pairs={{0,1},{1,0},{2,3},{3,2},{4,5},{5,4},{6,7},{7,6},{8,9},{9,8},{10,11... | collective-permute-start | bytes 393224 | tf_op jit(solution)/shard_map/ppermute | solution.py:205
  10.8 12.7 %collective-permute-start.4 = (bf16[512,128]{1,0:T(8,128)(2,1)S(1)}, bf16[512,128]{1,0:T(8,128)(2,1)S(1)}, u32[]{:S(2)}, u32[]{:S(2)}) collective-permute-start(bf16[512,128]{1,0:T(8,128)(2,1)S(1)} %get-tuple-element.54), channel_id=1, source_target_pairs={{0,2},{1,3},{2,0},{3,1},{4,6},{5,7},{6,4},{7,5},{8,10},{9,11},{10,... | collective-permute-start | bytes 393224 | tf_op jit(solution)/shard_map/ppermute | solution.py:205
  13.4 10.1 %collective-permute-start.5 = (bf16[512,128]{1,0:T(8,128)(2,1)S(1)}, bf16[512,128]{1,0:T(8,128)(2,1)S(1)}, u32[]{:S(2)}, u32[]{:S(2)}) collective-permute-start(bf16[512,128]{1,0:T(8,128)(2,1)S(1)} %get-tuple-element.55), channel_id=1, source_target_pairs={{0,3},{1,2},{2,1},{3,0},{4,7},{5,6},{6,5},{7,4},{8,11},{9,10},{10,... | collective-permute-start | bytes 393224 | tf_op jit(solution)/shard_map/ppermute | solution.py:205
  23.6 13.1 %collective-permute-start.7 = (bf16[2304,128]{1,0:T(8,128)(2,1)S(1)}, bf16[2304,128]{1,0:T(8,128)(2,1)S(1)}, u32[]{:S(2)}, u32[]{:S(2)}) collective-permute-start(bf16[2304,128]{1,0:T(8,128)(2,1)S(1)} %get-tuple-element.58), channel_id=1, source_target_pairs={{0,16},{1,17},{2,18},{3,19},{4,20},{5,21},{6,22},{7,23},{8,24},{9,... | collective-permute-start | bytes 1769480 | tf_op jit(solution)/shard_map/ppermute | solution.py:205
  24.2 12.5 %collective-permute-start.11 = (bf16[2304,128]{1,0:T(8,128)(2,1)S(1)}, bf16[2304,128]{1,0:T(8,128)(2,1)S(1)}, u32[]{:S(2)}, u32[]{:S(2)}) collective-permute-start(bf16[2304,128]{1,0:T(8,128)(2,1)S(1)} %get-tuple-element.56.refs_0_.refs_6_), channel_id=1, source_target_pairs={{0,8},{1,9},{2,10},{3,11},{4,12},{5,13},{6,14},{7,15},{8,0},{9,1},... | collective-permute-start | bytes 1769480 | tf_op jit(solution)/shard_map/ppermute | solution.py:205
  24.8 11.7 %collective-permute-start.9 = (bf16[512,128]{1,0:T(8,128)(2,1)S(1)}, bf16[512,128]{1,0:T(8,128)(2,1)S(1)}, u32[]{:S(2)}, u32[]{:S(2)}) collective-permute-start(bf16[512,128]{1,0:T(8,128)(2,1)S(1)} %get-tuple-element.59), channel_id=1, source_target_pairs={{0,2},{1,3},{2,0},{3,1},{4,6},{5,7},{6,4},{7,5},{8,10},{9,11},{10,... | collective-permute-start | bytes 393224 | tf_op jit(solution)/shard_map/ppermute | solution.py:205
  27.8 8.6 %collective-permute-start.10 = (bf16[512,128]{1,0:T(8,128)(2,1)S(1)}, bf16[512,128]{1,0:T(8,128)(2,1)S(1)}, u32[]{:S(2)}, u32[]{:S(2)}) collective-permute-start(bf16[512,128]{1,0:T(8,128)(2,1)S(1)} %get-tuple-element.60), channel_id=1, source_target_pairs={{0,3},{1,2},{2,1},{3,0},{4,7},{5,6},{6,5},{7,4},{8,11},{9,10},{10,... | collective-permute-start | bytes 393224 | tf_op jit(solution)/shard_map/ppermute | solution.py:205
  29.2 7.5 %collective-permute-start.8 = (bf16[512,128]{1,0:T(8,128)(2,1)S(1)}, bf16[512,128]{1,0:T(8,128)(2,1)S(1)}, u32[]{:S(2)}, u32[]{:S(2)}) collective-permute-start(bf16[512,128]{1,0:T(8,128)(2,1)S(1)} %get-tuple-element.57.refs_0_), channel_id=1, source_target_pairs={{0,1},{1,0},{2,3},{3,2},{4,5},{5,4},{6,7},{7,6},{8,9},{9,8},{10,11... | collective-permute-start | bytes 393224 | tf_op jit(solution)/shard_map/ppermute | solution.py:205
  36.8 20.6 %collective-permute-start.13 = (bf16[2304,128]{1,0:T(8,128)(2,1)S(1)}, bf16[2304,128]{1,0:T(8,128)(2,1)S(1)}, u32[]{:S(2)}, u32[]{:S(2)}) collective-permute-start(bf16[2304,128]{1,0:T(8,128)(2,1)S(1)} %get-tuple-element.64), channel_id=1, source_target_pairs={{0,16},{1,17},{2,18},{3,19},{4,20},{5,21},{6,22},{7,23},{8,24},{9,... | collective-permute-start | bytes 1769480 | tf_op jit(solution)/shard_map/ppermute | solution.py:205
  38.3 19.0 %collective-permute-start.17 = (bf16[2304,128]{1,0:T(8,128)(2,1)S(1)}, bf16[2304,128]{1,0:T(8,128)(2,1)S(1)}, u32[]{:S(2)}, u32[]{:S(2)}) collective-permute-start(bf16[2304,128]{1,0:T(8,128)(2,1)S(1)} %get-tuple-element.61.refs_0_.refs_6_), channel_id=1, source_target_pairs={{0,8},{1,9},{2,10},{3,11},{4,12},{5,13},{6,14},{7,15},{8,0},{9,1},... | collective-permute-start | bytes 1769480 | tf_op jit(solution)/shard_map/ppermute | solution.py:205
  40.0 11.6 %collective-permute-start.14 = (bf16[768,128]{1,0:T(8,128)(2,1)S(1)}, bf16[768,128]{1,0:T(8,128)(2,1)S(1)}, u32[]{:S(2)}, u32[]{:S(2)}) collective-permute-start(bf16[768,128]{1,0:T(8,128)(2,1)S(1)} %get-tuple-element.65), channel_id=1, source_target_pairs={{0,1},{1,0},{2,3},{3,2},{4,5},{5,4},{6,7},{7,6},{8,9},{9,8},{10,11... | collective-permute-start | bytes 589832 | tf_op jit(solution)/shard_map/ppermute | solution.py:205
  42.1 15.3 %collective-permute-start.15 = (bf16[768,128]{1,0:T(8,128)(2,1)S(1)}, bf16[768,128]{1,0:T(8,128)(2,1)S(1)}, u32[]{:S(2)}, u32[]{:S(2)}) collective-permute-start(bf16[768,128]{1,0:T(8,128)(2,1)S(1)} %get-tuple-element.66), channel_id=1, source_target_pairs={{0,2},{1,3},{2,0},{3,1},{4,6},{5,7},{6,4},{7,5},{8,10},{9,11},{10,... | collective-permute-start | bytes 589832 | tf_op jit(solution)/shard_map/ppermute | solution.py:205
  43.4 14.0 %collective-permute-start.16 = (bf16[768,128]{1,0:T(8,128)(2,1)S(1)}, bf16[768,128]{1,0:T(8,128)(2,1)S(1)}, u32[]{:S(2)}, u32[]{:S(2)}) collective-permute-start(bf16[768,128]{1,0:T(8,128)(2,1)S(1)} %get-tuple-element.67), channel_id=1, source_target_pairs={{0,3},{1,2},{2,1},{3,0},{4,7},{5,6},{6,5},{7,4},{8,11},{9,10},{10,... | collective-permute-start | bytes 589832 | tf_op jit(solution)/shard_map/ppermute | solution.py:205
  57.5 24.5 %collective-permute-start.21 = (bf16[2304,128]{1,0:T(8,128)(2,1)S(1)}, bf16[2304,128]{1,0:T(8,128)(2,1)S(1)}, u32[]{:S(2)}, u32[]{:S(2)}) collective-permute-start(bf16[2304,128]{1,0:T(8,128)(2,1)S(1)} %get-tuple-element.75), channel_id=1, source_target_pairs={{0,16},{1,17},{2,18},{3,19},{4,20},{5,21},{6,22},{7,23},{8,24},{9,... | collective-permute-start | bytes 1769480 | tf_op jit(solution)/shard_map/ppermute | solution.py:205
  58.1 23.9 %collective-permute-start.22 = (bf16[2304,128]{1,0:T(8,128)(2,1)S(1)}, bf16[2304,128]{1,0:T(8,128)(2,1)S(1)}, u32[]{:S(2)}, u32[]{:S(2)}) collective-permute-start(bf16[2304,128]{1,0:T(8,128)(2,1)S(1)} %get-tuple-element.68.refs_0_.refs_6_), channel_id=1, source_target_pairs={{0,8},{1,9},{2,10},{3,11},{4,12},{5,13},{6,14},{7,15},{8,0},{9,1},... | collective-permute-start | bytes 1769480 | tf_op jit(solution)/shard_map/ppermute | solution.py:205
  65.3 7.0 %collective-permute-start.18 = (bf16[256,128]{1,0:T(8,128)(2,1)S(1)}, bf16[256,128]{1,0:T(8,128)(2,1)S(1)}, u32[]{:S(2)}, u32[]{:S(2)}) collective-permute-start(bf16[256,128]{1,0:T(8,128)(2,1)S(1)} %get-tuple-element.71), channel_id=1, source_target_pairs={{0,1},{1,0},{2,3},{3,2},{4,5},{5,4},{6,7},{7,6},{8,9},{9,8},{10,11... | collective-permute-start | bytes 196616 | tf_op jit(solution)/shard_map/ppermute | solution.py:205
  68.6 11.0 %collective-permute-start.19 = (bf16[256,128]{1,0:T(8,128)(2,1)S(1)}, bf16[256,128]{1,0:T(8,128)(2,1)S(1)}, u32[]{:S(2)}, u32[]{:S(2)}) collective-permute-start(bf16[256,128]{1,0:T(8,128)(2,1)S(1)} %get-tuple-element.72), channel_id=1, source_target_pairs={{0,2},{1,3},{2,0},{3,1},{4,6},{5,7},{6,4},{7,5},{8,10},{9,11},{10,... | collective-permute-start | bytes 196616 | tf_op jit(solution)/shard_map/ppermute | solution.py:205
  69.1 12.5 %collective-permute-start.20 = (bf16[256,128]{1,0:T(8,128)(2,1)S(1)}, bf16[256,128]{1,0:T(8,128)(2,1)S(1)}, u32[]{:S(2)}, u32[]{:S(2)}) collective-permute-start(bf16[256,128]{1,0:T(8,128)(2,1)S(1)} %get-tuple-element.73), channel_id=1, source_target_pairs={{0,3},{1,2},{2,1},{3,0},{4,7},{5,6},{6,5},{7,4},{8,11},{9,10},{10,... | collective-permute-start | bytes 196616 | tf_op jit(solution)/shard_map/ppermute | solution.py:205
  72.3 12.3 %collective-permute-start.24 = (bf16[512,128]{1,0:T(8,128)(2,1)S(1)}, bf16[512,128]{1,0:T(8,128)(2,1)S(1)}, u32[]{:S(2)}, u32[]{:S(2)}) collective-permute-start(bf16[512,128]{1,0:T(8,128)(2,1)S(1)} %get-tuple-element.77), channel_id=1, source_target_pairs={{0,2},{1,3},{2,0},{3,1},{4,6},{5,7},{6,4},{7,5},{8,10},{9,11},{10,... | collective-permute-start | bytes 393224 | tf_op jit(solution)/shard_map/ppermute | solution.py:205
  79.7 7.0 %collective-permute-start.25 = (bf16[512,128]{1,0:T(8,128)(2,1)S(1)}, bf16[512,128]{1,0:T(8,128)(2,1)S(1)}, u32[]{:S(2)}, u32[]{:S(2)}) collective-permute-start(bf16[512,128]{1,0:T(8,128)(2,1)S(1)} %get-tuple-element.78), channel_id=1, source_target_pairs={{0,3},{1,2},{2,1},{3,0},{4,7},{5,6},{6,5},{7,4},{8,11},{9,10},{10,... | collective-permute-start | bytes 393224 | tf_op jit(solution)/shard_map/ppermute | solution.py:205
  81.6 6.3 %collective-permute-start.23 = (bf16[512,128]{1,0:T(8,128)(2,1)S(1)}, bf16[512,128]{1,0:T(8,128)(2,1)S(1)}, u32[]{:S(2)}, u32[]{:S(2)}) collective-permute-start(bf16[512,128]{1,0:T(8,128)(2,1)S(1)} %get-tuple-element.69.refs_0_), channel_id=1, source_target_pairs={{0,1},{1,0},{2,3},{3,2},{4,5},{5,4},{6,7},{7,6},{8,9},{9,8},{10,11... | collective-permute-start | bytes 393224 | tf_op jit(solution)/shard_map/ppermute | solution.py:205
  82.0 20.4 %collective-permute-start.30 = (bf16[768,128]{1,0:T(8,128)(2,1)S(1)}, bf16[768,128]{1,0:T(8,128)(2,1)S(1)}, u32[]{:S(2)}, u32[]{:S(2)}) collective-permute-start(bf16[768,128]{1,0:T(8,128)(2,1)S(1)} %get-tuple-element.84), channel_id=1, source_target_pairs={{0,16},{1,17},{2,18},{3,19},{4,20},{5,21},{6,22},{7,23},{8,24},{9,... | collective-permute-start | bytes 589832 | tf_op jit(solution)/shard_map/ppermute | solution.py:205
  83.5 18.9 %collective-permute-start.29 = (bf16[768,128]{1,0:T(8,128)(2,1)S(1)}, bf16[768,128]{1,0:T(8,128)(2,1)S(1)}, u32[]{:S(2)}, u32[]{:S(2)}) collective-permute-start(bf16[768,128]{1,0:T(8,128)(2,1)S(1)} %get-tuple-element.76.refs_0_), channel_id=1, source_target_pairs={{0,8},{1,9},{2,10},{3,11},{4,12},{5,13},{6,14},{7,15},{8,0},{9,1},... | collective-permute-start | bytes 589832 | tf_op jit(solution)/shard_map/ppermute | solution.py:205
  93.8 4.5 %collective-permute-start.26 = (bf16[256,128]{1,0:T(8,128)(2,1)S(1)}, bf16[256,128]{1,0:T(8,128)(2,1)S(1)}, u32[]{:S(2)}, u32[]{:S(2)}) collective-permute-start(bf16[256,128]{1,0:T(8,128)(2,1)S(1)} %get-tuple-element.80), channel_id=1, source_target_pairs={{0,1},{1,0},{2,3},{3,2},{4,5},{5,4},{6,7},{7,6},{8,9},{9,8},{10,11... | collective-permute-start | bytes 196616 | tf_op jit(solution)/shard_map/ppermute | solution.py:205
  93.9 5.2 %collective-permute-start.27 = (bf16[256,128]{1,0:T(8,128)(2,1)S(1)}, bf16[256,128]{1,0:T(8,128)(2,1)S(1)}, u32[]{:S(2)}, u32[]{:S(2)}) collective-permute-start(bf16[256,128]{1,0:T(8,128)(2,1)S(1)} %get-tuple-element.81), channel_id=1, source_target_pairs={{0,2},{1,3},{2,0},{3,1},{4,6},{5,7},{6,4},{7,5},{8,10},{9,11},{10,... | collective-permute-start | bytes 196616 | tf_op jit(solution)/shard_map/ppermute | solution.py:205
  96.3 6.1 %collective-permute-start.28 = (bf16[256,128]{1,0:T(8,128)(2,1)S(1)}, bf16[256,128]{1,0:T(8,128)(2,1)S(1)}, u32[]{:S(2)}, u32[]{:S(2)}) collective-permute-start(bf16[256,128]{1,0:T(8,128)(2,1)S(1)} %get-tuple-element.82), channel_id=1, source_target_pairs={{0,3},{1,2},{2,1},{3,0},{4,7},{5,6},{6,5},{7,4},{8,11},{9,10},{10,... | collective-permute-start | bytes 196616 | tf_op jit(solution)/shard_map/ppermute | solution.py:205
  108.1 5.0 %collective-permute-start.31 = (bf16[256,128]{1,0:T(8,128)(2,1)S(1)}, bf16[256,128]{1,0:T(8,128)(2,1)S(1)}, u32[]{:S(2)}, u32[]{:S(2)}) collective-permute-start(bf16[256,128]{1,0:T(8,128)(2,1)S(1)} %get-tuple-element.86), channel_id=1, source_target_pairs={{0,1},{1,0},{2,3},{3,2},{4,5},{5,4},{6,7},{7,6},{8,9},{9,8},{10,11... | collective-permute-start | bytes 196616 | tf_op jit(solution)/shard_map/ppermute | solution.py:205
  108.2 5.2 %collective-permute-start.32 = (bf16[256,128]{1,0:T(8,128)(2,1)S(1)}, bf16[256,128]{1,0:T(8,128)(2,1)S(1)}, u32[]{:S(2)}, u32[]{:S(2)}) collective-permute-start(bf16[256,128]{1,0:T(8,128)(2,1)S(1)} %get-tuple-element.87), channel_id=1, source_target_pairs={{0,2},{1,3},{2,0},{3,1},{4,6},{5,7},{6,4},{7,5},{8,10},{9,11},{10,... | collective-permute-start | bytes 196616 | tf_op jit(solution)/shard_map/ppermute | solution.py:205
  110.7 6.1 %collective-permute-start.33 = (bf16[256,128]{1,0:T(8,128)(2,1)S(1)}, bf16[256,128]{1,0:T(8,128)(2,1)S(1)}, u32[]{:S(2)}, u32[]{:S(2)}) collective-permute-start(bf16[256,128]{1,0:T(8,128)(2,1)S(1)} %get-tuple-element.88), channel_id=1, source_target_pairs={{0,3},{1,2},{2,1},{3,0},{4,7},{5,6},{6,5},{7,4},{8,11},{9,10},{10,... | collective-permute-start | bytes 196616 | tf_op jit(solution)/shard_map/ppermute | solution.py:205
  112.6 4.3 %collective-permute-start.35 = (bf16[512,128]{1,0:T(8,128)(2,1)S(1)}, bf16[512,128]{1,0:T(8,128)(2,1)S(1)}, u32[]{:S(2)}, u32[]{:S(2)}) collective-permute-start(bf16[512,128]{1,0:T(8,128)(2,1)S(1)} %get-tuple-element.91), channel_id=1, source_target_pairs={{0,4},{1,5},{2,6},{3,7},{4,0},{5,1},{6,2},{7,3},{8,12},{9,13},{10,... | collective-permute-start | bytes 393224 | tf_op jit(solution)/shard_map/ppermute | solution.py:205
  (11 other events, 22.1 us)

commit v3 on v2

--- a/solution.py
+++ b/solution.py
@@ -25,8 +25,9 @@
     def __init__(self):
         self.last = ()
 
-    def call(self, body, outs, *args, flops=0, exps=0):
-        skip = len(self.last)
+    def call(self, body, outs, *args, after=(), flops=0, exps=0):
+        behind = (*self.last, *after)
+        skip = len(behind)
 
         def without_last(*refs):
             body(*refs[skip:])
@@ -39,7 +40,7 @@
             out_specs=[VMEM] * len(outs),
             compiler_params=PARAMS,
             cost_estimate=pl.CostEstimate(flops=flops, bytes_accessed=size, transcendentals=exps),
-        )(*self.last, *args)
+        )(*behind, *args)
         self.last = made[:1]
         return made
 
@@ -64,22 +65,22 @@
     return new_top, part, mixed
 
 
-STEP = 512
-
-
 def attend_body(queries, blocks, count, *refs):
     refs, outs = refs[:count], refs[count:]
-    rows = outs[0].shape[0]
-    per = STEP // rows
-    for first in range(0, len(outs), per):
-        q = read(refs, queries[first : first + per])
+    for pair in range(0, len(queries), 2):
+        q = read(refs, queries[pair : pair + 2])
         state = None
         for keys, values in blocks:
             state = absorb(state, q, read(refs, keys), read(refs, values))
         _, total, accum = state
         result = (accum / total).astype(BF16)
-        for place in range(per):
-            outs[first + place][...] = result[place * rows : (place + 1) * rows]
+        first = pair // 2 * q.shape[0]
+        at = 0
+        for out in outs:
+            low, high = max(at, first), min(at + out.shape[0], first + q.shape[0])
+            if low < high:
+                out[low - at : high - at, :] = result[low - first : high - first, :]
+            at += out.shape[0]
 
 
 class Arrays:
@@ -97,18 +98,22 @@
         return [self.piece(*part) for part in parts]
 
 
-def attend(line, queries, blocks):
+def attend(line, queries, blocks, outs):
     known = Arrays()
     queries = known.pieces(queries)
     blocks = [(known.pieces(keys), known.pieces(values)) for keys, values in blocks]
-    pairs = sum(q[2] for q in queries) * sum(k[2] for keys, _ in blocks for k in keys)
+    pairs = sum(outs) * sum(k[2] for keys, _ in blocks for k in keys)
     return line.call(
         functools.partial(attend_body, queries, blocks, len(known.arrays)),
-        [sds(q[2], HEAD_DIM) for q in queries],
+        [sds(rows, HEAD_DIM) for rows in outs],
         *known.arrays,
         flops=4 * pairs * HEAD_DIM,
         exps=pairs,
     )
+
+
+KEPT, SECOND, FIRST, OPPOSITE = range(4)
+HOPS = (KEPT, SECOND, FIRST, OPPOSITE)
 
 
 def core_index():
@@ -132,11 +137,13 @@
 
 
 def column(piece, hop):
-    z = lax.axis_index("head")
-    bit, pair = lax.rem(z, 2), lax.div(z, 2)
-    bit = 1 - bit if hop & 1 else bit
-    pair = 1 - pair if hop & 2 else pair
-    return pl.multiple_of((piece * 4 + pair * 2 + bit) * HEAD_DIM, HEAD_DIM)
+    z, core = lax.axis_index("head"), core_index()
+    low, high = lax.rem(z, 2), lax.div(z, 2)
+    if hop in (FIRST, OPPOSITE):
+        low, high = lax.rem(low + core, 2), lax.rem(high + 1 - core, 2)
+    if hop in (SECOND, OPPOSITE):
+        low, high = lax.rem(low + 1 - core, 2), lax.rem(high + core, 2)
+    return pl.multiple_of((piece * 4 + high * 2 + low) * HEAD_DIM, HEAD_DIM)
 
 
 def pack_body(heads, half, *refs):
@@ -154,12 +161,12 @@
                 at += tokens
 
 
-def pack(line, heads, tensors):
+def pack(line, heads, tensors, after=()):
     flat = [a for pair in tensors for a in pair]
     tokens = flat[0].shape[0]
     half = min(a.shape[1] for a in flat)
     outs = [sds(2 * tokens * len(group), HEAD_DIM) for group in heads]
-    return line.call(functools.partial(pack_body, heads, half), outs, *flat)
+    return line.call(functools.partial(pack_body, heads, half), outs, *flat, after=after)
 
 
 def join_body(layout, count, *refs):
@@ -170,11 +177,13 @@
             at += rows
 
 
-def join(line, layout):
+def join(line, layout, after=()):
     known = Arrays()
     layout = [known.pieces(parts) for parts in layout]
     outs = [sds(sum(rows for _, _, rows in parts), HEAD_DIM) for parts in layout]
-    return line.call(functools.partial(join_body, layout, len(known.arrays)), outs, *known.arrays)
+    return line.call(
+        functools.partial(join_body, layout, len(known.arrays)), outs, *known.arrays, after=after
+    )
 
 
 def place_body(pieces, *refs):
@@ -183,7 +192,7 @@
     core = core_index()
     for piece in range(pieces):
         own, across = refs[2 * piece : 2 * piece + 2]
-        for hop in range(4):
+        for hop in HOPS:
             at = column(piece, hop)
             here = pl.multiple_of(core * half + at, HEAD_DIM)
             there = pl.multiple_of((1 - core) * half + at, HEAD_DIM)
@@ -209,20 +218,19 @@
     return permute(array, lambda y, x, core, z: (y, x, 1 - core, z))
 
 
-def other_x(array):
-    return permute(array, lambda y, x, core, z: (y, 1 - x, core, z))
-
-
-def other_y(array):
-    return permute(array, lambda y, x, core, z: (1 - y, x, core, z))
-
-
 def hop_z(array, hop):
-    return permute(array, lambda y, x, core, z: (y, x, core, z ^ hop))
-
-
-def hops(buffers):
-    return [hop_z(buffer, hop) for hop, buffer in enumerate(buffers, 1)]
+    def move(y, x, core, z):
+        first, second = (2, 1) if core == 0 else (1, 2)
+        return y, x, core, z ^ {FIRST: first, SECOND: second, OPPOSITE: 3}[hop]
+
+    return permute(array, move)
+
+
+def hop_xy(array, hop):
+    def move(y, x, core, z):
+        return (y, 1 - x, core, z) if (hop == FIRST) == (core == 0) else (1 - y, x, core, z)
+
+    return permute(array, move)
 
 
 def shards_fast(queries, keys, values, query_gain, key_gain):
@@ -236,12 +244,6 @@
         own, other = line.call(normalize_body, [sds(tokens, half)] * 2, x, gain)
         return own, other_core(other)
 
-    def hand_back(outs):
-        back = [outs[0], *hops(outs[1:])]
-        layout = [[(a, 0, tokens) for a in back], [(a, tokens, tokens) for a in back]]
-        own, across = join(line, layout)
-        return own, other_core(across)
-
     (v_other,) = line.call(halves_body, [sds(tokens, half)], values)
     v_pair = (values, other_core(v_other))
     k_pair = swap_halves(keys, key_gain)
@@ -249,79 +251,82 @@
     tensors = (k_pair, v_pair, q_pair)
     k, v, q = range(3)
 
-    out = pack(
-        line,
-        [[(t, c, 0) for c in range(3) for t in (k, v)]]
-        + [[(k, 0, hop), (v, 0, hop)] for hop in (1, 2, 3)],
-        tensors[:2],
-    )
-    own = out[0]
-    came = hops(out[1:])
-    own_x, own_y = other_x(own), other_y(own)
-
-    def key_rows(array, chunk):
-        return array, 2 * chunk * part, part
-
-    def value_rows(array, chunk):
-        return array, (2 * chunk + 1) * part, part
-
-    sends, received = [], []
-    results = []
-    q_slots = []
-    for step in range(5):
-        if step == 0:
-            along_x = [key_rows(own_y, c) for c in range(3)]
-            along_y = [value_rows(own_x, c) for c in range(3)]
-        elif step < 4:
-            got_x, got_y = received[-1]
-            along_x = [(got_y, rest, rest)]
-            along_y = [(got_x, 2 * rest, rest)]
-        if step < 3:
-            block = [(a, 0, part) for a in came] + [(a, part, part) for a in came]
-            along_x, along_y = along_x + block, along_y + block
-        if step < 4:
-            x_out, y_out = join(line, [along_x, along_y])
-            sends.append(x_out)
-            received.append((other_x(x_out), other_y(y_out)))
-        if step == 2:
-            q_slots.append([(own_q, 0, part)] + [(a, 2 * part, part) for a in came])
-        if step == 3:
-            for c in (0, 1):
-                q_slots.append([(own_q, (c + 1) * part, part)] + [(a, c * part, part) for a in came])
-        if step == 0:
-            (*out,) = pack(line, [[(k, 1, hop), (v, 1, hop)] for hop in (1, 2, 3)], tensors[:2])
-            came = hops(out)
-        if step == 1:
-            own_q, *out = pack(
-                line,
-                [[(q, c, 0) for c in range(3)]]
-                + [[(k, 2, hop), (v, 2, hop), (q, 0, hop)] for hop in (1, 2, 3)],
-                tensors,
-            )
-            came = hops(out)
-        if step == 2:
-            out = pack(line, [[(0, 1, hop), (0, 2, hop)] for hop in (1, 2, 3)], (q_pair,))
-            came = hops(out)
-        if step >= 2:
-            chunk = step - 2
-            got_x, got_y = received[chunk]
-            far_x, far_y = received[chunk + 1]
-            blocks = []
-            for mine, more in ((own, sends[chunk]), (own_x, got_x), (own_y, got_y)):
-                blocks.append(
-                    (
-                        [key_rows(mine, chunk), (more, rest, rest)],
-                        [value_rows(mine, chunk), (more, 2 * rest, rest)],
-                    )
-                )
-            first_x, first_y = received[0]
-            blocks.append(
-                (
-                    [(first_x, chunk * part, part), (far_x, 0, rest)],
-                    [(first_y, chunk * part, part), (far_y, 0, rest)],
-                )
-            )
-            results += hand_back(attend(line, q_slots[chunk], blocks))
+    def swap(heads, after=()):
+        used = sorted({t for t, _ in heads})
+        groups = [[(used.index(t), c, hop) for t, c in heads] for hop in HOPS[1:]]
+        outs = pack(line, groups, [tensors[t] for t in used], after)
+        return [hop_z(out, hop) for hop, out in zip(HOPS[1:], outs)]
+
+    def slots(swapped, first, rows):
+        return [(array, first, rows) for array in swapped]
+
+    def send_xy(far, swapped):
+        block = slots(swapped, 0, part) + slots(swapped, part, part)
+        whole = [(far, 0, far.shape[0])]
+        out, both = join(line, [block, whole + block])
+        got = hop_xy(both, FIRST)
+        return out, got, hop_xy(out, SECOND)
+
+    def blocks_of(chunk, sent, far):
+        block, got, got_second = sent
+        four = (
+            (own, 0, block, 0),
+            (own_first, 0, got, got.shape[0] - 2 * rest),
+            (own_second, 0, got_second, 0),
+            (sent0[1], 0, far, 0),
+        )
+        blocks = []
+        for kept, kept_at, array, at in four:
+            kept_at += 2 * chunk * part
+            keys = [(kept, kept_at, part), (array, at, rest)]
+            blocks.append((keys, [(a, first + rows, rows) for a, first, rows in keys]))
+        return [
+            (low[0] + high[0], low[1] + high[1]) for low, high in zip(blocks[::2], blocks[1::2])
+        ]
+
+    def queries_of(chunk, swapped, first):
+        return dict(zip(HOPS, [(own_q, chunk * part, part)] + slots(swapped, first, part)))
+
+    def core_swap(back):
+        kept, second, first, opposite = back
+        other = kept, first, second, opposite
+        layout = [[(a, 0, tokens) for a in back], [(a, tokens, tokens) for a in other]]
+        own, across = join(line, layout)
+        return own, other_core(across)
+
+    def attend_back(slots, blocks, hops):
+        outs = attend(line, [slots[hop] for hop in hops], blocks, [part] * len(hops))
+        return {hop: out if hop == KEPT else hop_z(out, hop) for hop, out in zip(hops, outs)}
+
+    def by_hop(back):
+        return [back[hop] for hop in HOPS]
+
+    group0, group1 = [(k, 0), (v, 0)], [(k, 1), (v, 1)]
+    group2, group3 = [(k, 2), (v, 2), (q, 0)], [(q, 1), (q, 2)]
+
+    swap0 = swap(group0)
+    (own,) = pack(line, [[(t, c, KEPT) for c in range(3) for t in (k, v)]], tensors[:2])
+    own_first, own_second = hop_xy(own, FIRST), hop_xy(own, SECOND)
+    swap1 = swap(group1, after=(*swap0, own_first, own_second))
+    sent0 = send_xy(own_second, swap0)
+    swap2 = swap(group2, after=(*swap1, *sent0))
+    sent1 = send_xy(sent0[2], swap1)
+    swap3 = swap(group3, after=(*swap2, *sent1))
+    sent2 = send_xy(sent1[2], swap2)
+    (own_q,) = pack(line, [[(0, c, KEPT) for c in range(3)]], (q_pair,))
+    back0 = attend_back(
+        queries_of(0, swap2, 2 * part), blocks_of(0, sent0, sent1[1]), (OPPOSITE, FIRST, KEPT, SECOND)
+    )
+    (last,) = join(line, [[(sent2[2], 0, 2 * rest)]], after=swap3)
+    far = hop_xy(last, FIRST)
+    back1 = attend_back(
+        queries_of(1, swap3, 0), blocks_of(1, sent1, sent2[1]), (OPPOSITE, FIRST, KEPT, SECOND)
+    )
+    results = core_swap(by_hop(back0))
+    slots2, blocks2 = queries_of(2, swap3, part), blocks_of(2, sent2, far)
+    back2 = attend_back(slots2, blocks2, (OPPOSITE, FIRST, KEPT, SECOND))
+    results += core_swap(by_hop(back1))
+    results += core_swap(by_hop(back2))
     (attended,) = line.call(functools.partial(place_body, 3), [sds(tokens, width)], *results)
     return attended
 

time: 119 us -> 108 us (0.908)
  waiting for transfers between devices: 50.9 us -> 38.4 us
  starting transfers between devices: 46.3 us -> 47.7 us
    ppermute x37 -> x36, waiting for transfers between devices: 50.9 us -> 38.4 us  [permute(): return lax.ppermute(array, AXES, pairs)]
    ppermute x37 -> x36, starting transfers between devices: 46.3 us -> 47.7 us  [permute(): return lax.ppermute(array, AXES, pairs)]
    pallas_call x18 -> x20, Pallas kernels: 20.1 us -> 19.1 us  [call(): pl.pallas_call(without_last, out_shape=outs, in_specs=[pl.BlockSpec(memor...]
  transfers between devices with their start and end apart: 37 -> 36, of which waited for: 16 -> 14; matrix products, arithmetic and copies ran while one was open for 0% -> 0% of each run, Pallas kernels for 11% -> 16%
where the time goes in v3:
time: 108 us
  starting transfers between devices  47.7 us (44%)
  waiting for transfers between devices  38.4 us (36%)
  Pallas kernels  19.1 us (18%)
  local copies, waits for them, and re-layouts  2.24 us (2%)
    ppermute x36, starting transfers between devices, permute(): return lax.ppermute(array, AXES, pairs)  47.7 us
    ppermute x36, waiting for transfers between devices, permute(): return lax.ppermute(array, AXES, pairs)  38.4 us
    pallas_call x20, Pallas kernels, call(): pl.pallas_call(without_last, out_shape=outs, in_specs=[pl.BlockSpec(memor...  19.1 us
    unnamed x12, local copies, waits for them, and re-layouts  2.24 us
  transfers between devices with their start and end apart: 36, of which 14 were waited for; matrix products, arithmetic and copies ran while one was open for 0% of the time, Pallas kernels for 16%

profile of v3, /device:TPU:0, one launch (start us, length us, event | category | flops | bytes accessed | tf_op | source)
XLA Modules:
  0.0 107.6 jit_solution(184072034790230488)
XLA Ops:
  0.0 1.1 %copy-done = bf16[128,3072]{1,0:T(8,128)(2,1)S(1)} copy-done((bf16[128,3072]{1,0:T(8,128)(2,1)S(1)}, bf16[128,3072]{1,0:T(8,128)(2,1)}, u32[]{:S(2)}) %copy-start) | copy-done | bytes 786456
  5.4 3.0 %collective-permute-start.6 = (bf16[1536,128]{1,0:T(8,128)(2,1)S(1)}, bf16[1536,128]{1,0:T(8,128)(2,1)S(1)}, u32[]{:S(2)}, u32[]{:S(2)}) collective-permute-start(bf16[1536,128]{1,0:T(8,128)(2,1)S(1)} %shard_map.59.refs_0_.refs_5_), channel_id=1, source_target_pairs={{0,16},{1,17},{2,18},{3,19},{4,12},{5,13},{6,14},{7,15},{8,24},{9,... | collective-permute-start | bytes 1179656 | tf_op jit(solution)/shard_map/ppermute | solution.py:214
  8.3 1.5 %collective-permute-start.5 = (bf16[1536,128]{1,0:T(8,128)(2,1)S(1)}, bf16[1536,128]{1,0:T(8,128)(2,1)S(1)}, u32[]{:S(2)}, u32[]{:S(2)}) collective-permute-start(bf16[1536,128]{1,0:T(8,128)(2,1)S(1)} %shard_map.59.refs_0_.refs_5_), channel_id=1, source_target_pairs={{0,8},{1,9},{2,10},{3,11},{4,20},{5,21},{6,22},{7,23},{8,0},{9,1},... | collective-permute-start | bytes 1179656 | tf_op jit(solution)/shard_map/ppermute | solution.py:214
  9.8 1.6 %collective-permute-start.2 = (bf16[512,128]{1,0:T(8,128)(2,1)S(1)}, bf16[512,128]{1,0:T(8,128)(2,1)S(1)}, u32[]{:S(2)}, u32[]{:S(2)}) collective-permute-start(bf16[512,128]{1,0:T(8,128)(2,1)S(1)} %get-tuple-element.48.refs_0_), channel_id=1, source_target_pairs={{0,1},{1,0},{2,3},{3,2},{4,6},{5,7},{6,4},{7,5},{8,9},{9,8},{10,11... | collective-permute-start | bytes 393224 | tf_op jit(solution)/shard_map/ppermute | solution.py:214
  11.4 2.6 %collective-permute-start.3 = (bf16[512,128]{1,0:T(8,128)(2,1)S(1)}, bf16[512,128]{1,0:T(8,128)(2,1)S(1)}, u32[]{:S(2)}, u32[]{:S(2)}) collective-permute-start(bf16[512,128]{1,0:T(8,128)(2,1)S(1)} %get-tuple-element.49), channel_id=1, source_target_pairs={{0,2},{1,3},{2,0},{3,1},{4,5},{5,4},{6,7},{7,6},{8,10},{9,11},{10,... | collective-permute-start | bytes 393224 | tf_op jit(solution)/shard_map/ppermute | solution.py:214
  14.2 3.5 %collective-permute-done.2.refs_1_ = bf16[512,128]{1,0:T(8,128)(2,1)S(1)} collective-permute-done((bf16[512,128]{1,0:T(8,128)(2,1)S(1)}, bf16[512,128]{1,0:T(8,128)(2,1)S(1)}, u32[]{:S(2)}, u32[]{:S(2)}) %collective-permute-start.2) | collective-permute-done | bytes 131104 | tf_op jit(solution)/shard_map/ppermute | solution.py:214
  17.7 5.0 %collective-permute-done.3.refs_2_ = bf16[512,128]{1,0:T(8,128)(2,1)S(1)} collective-permute-done((bf16[512,128]{1,0:T(8,128)(2,1)S(1)}, bf16[512,128]{1,0:T(8,128)(2,1)S(1)}, u32[]{:S(2)}, u32[]{:S(2)}) %collective-permute-start.3) | collective-permute-done | bytes 131104 | tf_op jit(solution)/shard_map/ppermute | solution.py:214
  24.0 2.1 %collective-permute-start.7 = (bf16[512,128]{1,0:T(8,128)(2,1)S(1)}, bf16[512,128]{1,0:T(8,128)(2,1)S(1)}, u32[]{:S(2)}, u32[]{:S(2)}) collective-permute-start(bf16[512,128]{1,0:T(8,128)(2,1)S(1)} %get-tuple-element.51.refs_0_), channel_id=1, source_target_pairs={{0,1},{1,0},{2,3},{3,2},{4,6},{5,7},{6,4},{7,5},{8,9},{9,8},{10,11... | collective-permute-start | bytes 393224 | tf_op jit(solution)/shard_map/ppermute | solution.py:214
  26.1 1.9 %collective-permute-start.8 = (bf16[512,128]{1,0:T(8,128)(2,1)S(1)}, bf16[512,128]{1,0:T(8,128)(2,1)S(1)}, u32[]{:S(2)}, u32[]{:S(2)}) collective-permute-start(bf16[512,128]{1,0:T(8,128)(2,1)S(1)} %get-tuple-element.53), channel_id=1, source_target_pairs={{0,2},{1,3},{2,0},{3,1},{4,5},{5,4},{6,7},{7,6},{8,10},{9,11},{10,... | collective-permute-start | bytes 393224 | tf_op jit(solution)/shard_map/ppermute | solution.py:214
  28.1 1.5 %collective-permute-start.9 = (bf16[512,128]{1,0:T(8,128)(2,1)S(1)}, bf16[512,128]{1,0:T(8,128)(2,1)S(1)}, u32[]{:S(2)}, u32[]{:S(2)}) collective-permute-start(bf16[512,128]{1,0:T(8,128)(2,1)S(1)} %get-tuple-element.54), channel_id=1, source_target_pairs={{0,3},{1,2},{2,1},{3,0},{4,7},{5,6},{6,5},{7,4},{8,11},{9,10},{10,... | collective-permute-start | bytes 393224 | tf_op jit(solution)/shard_map/ppermute | solution.py:214
  29.5 9.3 %collective-permute-done.8.refs_2_ = bf16[512,128]{1,0:T(8,128)(2,1)S(1)} collective-permute-done((bf16[512,128]{1,0:T(8,128)(2,1)S(1)}, bf16[512,128]{1,0:T(8,128)(2,1)S(1)}, u32[]{:S(2)}, u32[]{:S(2)}) %collective-permute-start.8) | collective-permute-done | bytes 131104 | tf_op jit(solution)/shard_map/ppermute | solution.py:214
  41.0 2.3 %collective-permute-start.13 = (bf16[768,128]{1,0:T(8,128)(2,1)S(1)}, bf16[768,128]{1,0:T(8,128)(2,1)S(1)}, u32[]{:S(2)}, u32[]{:S(2)}) collective-permute-start(bf16[768,128]{1,0:T(8,128)(2,1)S(1)} %get-tuple-element.57.refs_0_), channel_id=1, source_target_pairs={{0,1},{1,0},{2,3},{3,2},{4,6},{5,7},{6,4},{7,5},{8,9},{9,8},{10,11... | collective-permute-start | bytes 589832 | tf_op jit(solution)/shard_map/ppermute | solution.py:214
  43.3 1.2 %collective-permute-start.14 = (bf16[768,128]{1,0:T(8,128)(2,1)S(1)}, bf16[768,128]{1,0:T(8,128)(2,1)S(1)}, u32[]{:S(2)}, u32[]{:S(2)}) collective-permute-start(bf16[768,128]{1,0:T(8,128)(2,1)S(1)} %get-tuple-element.59), channel_id=1, source_target_pairs={{0,2},{1,3},{2,0},{3,1},{4,5},{5,4},{6,7},{7,6},{8,10},{9,11},{10,... | collective-permute-start | bytes 589832 | tf_op jit(solution)/shard_map/ppermute | solution.py:214
  44.5 1.5 %collective-permute-start.15 = (bf16[768,128]{1,0:T(8,128)(2,1)S(1)}, bf16[768,128]{1,0:T(8,128)(2,1)S(1)}, u32[]{:S(2)}, u32[]{:S(2)}) collective-permute-start(bf16[768,128]{1,0:T(8,128)(2,1)S(1)} %get-tuple-element.60), channel_id=1, source_target_pairs={{0,3},{1,2},{2,1},{3,0},{4,7},{5,6},{6,5},{7,4},{8,11},{9,10},{10,... | collective-permute-start | bytes 589832 | tf_op jit(solution)/shard_map/ppermute | solution.py:214
  46.0 5.4 %collective-permute-done.13.refs_1_.refs_4_ = bf16[768,128]{1,0:T(8,128)(2,1)S(1)} collective-permute-done((bf16[768,128]{1,0:T(8,128)(2,1)S(1)}, bf16[768,128]{1,0:T(8,128)(2,1)S(1)}, u32[]{:S(2)}, u32[]{:S(2)}) %collective-permute-start.13) | collective-permute-done | bytes 196640 | tf_op jit(solution)/shard_map/ppermute | solution.py:214
  51.3 1.5 %collective-permute-done.14.refs_2_ = bf16[768,128]{1,0:T(8,128)(2,1)S(1)} collective-permute-done((bf16[768,128]{1,0:T(8,128)(2,1)S(1)}, bf16[768,128]{1,0:T(8,128)(2,1)S(1)}, u32[]{:S(2)}, u32[]{:S(2)}) %collective-permute-start.14) | collective-permute-done | bytes 196640 | tf_op jit(solution)/shard_map/ppermute | solution.py:214
  52.9 5.2 %collective-permute-done.15.refs_3_.refs_1_ = bf16[768,128]{1,0:T(8,128)(2,1)S(1)} collective-permute-done((bf16[768,128]{1,0:T(8,128)(2,1)S(1)}, bf16[768,128]{1,0:T(8,128)(2,1)S(1)}, u32[]{:S(2)}, u32[]{:S(2)}) %collective-permute-start.15) | collective-permute-done | bytes 196640 | tf_op jit(solution)/shard_map/ppermute | solution.py:214
  58.3 1.7 %collective-permute-start.22 = (bf16[3072,128]{1,0:T(8,128)(2,1)S(1)}, bf16[3072,128]{1,0:T(8,128)(2,1)S(1)}, u32[]{:S(2)}, u32[]{:S(2)}) collective-permute-start(bf16[3072,128]{1,0:T(8,128)(2,1)S(1)} %get-tuple-element.67), channel_id=1, source_target_pairs={{0,8},{1,9},{2,10},{3,11},{4,20},{5,21},{6,22},{7,23},{8,0},{9,1},... | collective-permute-start | bytes 2359304 | tf_op jit(solution)/shard_map/ppermute | solution.py:214
  60.0 1.5 %collective-permute-start.21 = (bf16[1536,128]{1,0:T(8,128)(2,1)S(1)}, bf16[1536,128]{1,0:T(8,128)(2,1)S(1)}, u32[]{:S(2)}, u32[]{:S(2)}) collective-permute-start(bf16[1536,128]{1,0:T(8,128)(2,1)S(1)} %get-tuple-element.63.refs_0_.refs_6_), channel_id=1, source_target_pairs={{0,16},{1,17},{2,18},{3,19},{4,12},{5,13},{6,14},{7,15},{8,24},{9,... | collective-permute-start | bytes 1179656 | tf_op jit(solution)/shard_map/ppermute | solution.py:214
  61.5 2.5 %collective-permute-start.18 = (bf16[512,128]{1,0:T(8,128)(2,1)S(1)}, bf16[512,128]{1,0:T(8,128)(2,1)S(1)}, u32[]{:S(2)}, u32[]{:S(2)}) collective-permute-start(bf16[512,128]{1,0:T(8,128)(2,1)S(1)} %get-tuple-element.62.refs_0_), channel_id=1, source_target_pairs={{0,1},{1,0},{2,3},{3,2},{4,6},{5,7},{6,4},{7,5},{8,9},{9,8},{10,11... | collective-permute-start | bytes 393224 | tf_op jit(solution)/shard_map/ppermute | solution.py:214
  64.0 1.5 %collective-permute-start.19 = (bf16[512,128]{1,0:T(8,128)(2,1)S(1)}, bf16[512,128]{1,0:T(8,128)(2,1)S(1)}, u32[]{:S(2)}, u32[]{:S(2)}) collective-permute-start(bf16[512,128]{1,0:T(8,128)(2,1)S(1)} %get-tuple-element.65), channel_id=1, source_target_pairs={{0,2},{1,3},{2,0},{3,1},{4,5},{5,4},{6,7},{7,6},{8,10},{9,11},{10,... | collective-permute-start | bytes 393224 | tf_op jit(solution)/shard_map/ppermute | solution.py:214
  65.6 1.5 %collective-permute-start.20 = (bf16[512,128]{1,0:T(8,128)(2,1)S(1)}, bf16[512,128]{1,0:T(8,128)(2,1)S(1)}, u32[]{:S(2)}, u32[]{:S(2)}) collective-permute-start(bf16[512,128]{1,0:T(8,128)(2,1)S(1)} %get-tuple-element.66), channel_id=1, source_target_pairs={{0,3},{1,2},{2,1},{3,0},{4,7},{5,6},{6,5},{7,4},{8,11},{9,10},{10,... | collective-permute-start | bytes 393224 | tf_op jit(solution)/shard_map/ppermute | solution.py:214
  67.1 5.3 %shard_map.67 = (bf16[256,128]{1,0:T(8,128)(2,1)S(1)}, bf16[256,128]{1,0:T(8,128)(2,1)S(1)}, bf16[256,128]{1,0:T(8,128)(2,1)S(1)}, bf16[256,128]{1,0:T(8,128)(2,1)S(1)}) custom-call(bf16[768,128]{1,0:T(8,128)(2,1)S(1)} %shard_map.66.refs_0_.refs_3_, bf16[768,128]{1,0:T(8,128)(2,1)S(1)} %collective-permute-done.15.refs_3_.refs_1_, ...), custom_call_target="tpu_custom_call" | custom-call | flops 2147483648 | bytes 4587520 | tf_op jit(solution)/shard_map/pallas_call | solution.py:36
  73.7 4.8 %collective-permute-start.25 = (bf16[256,128]{1,0:T(8,128)(2,1)S(1)}, bf16[256,128]{1,0:T(8,128)(2,1)S(1)}, u32[]{:S(2)}, u32[]{:S(2)}) collective-permute-start(bf16[256,128]{1,0:T(8,128)(2,1)S(1)} %get-tuple-element.64.refs_0_), channel_id=1, source_target_pairs={{0,3},{1,2},{2,1},{3,0},{4,7},{5,6},{6,5},{7,4},{8,11},{9,10},{10,... | collective-permute-start | bytes 196616 | tf_op jit(solution)/shard_map/ppermute | solution.py:214
  78.5 1.3 %collective-permute-start.23 = (bf16[256,128]{1,0:T(8,128)(2,1)S(1)}, bf16[256,128]{1,0:T(8,128)(2,1)S(1)}, u32[]{:S(2)}, u32[]{:S(2)}) collective-permute-start(bf16[256,128]{1,0:T(8,128)(2,1)S(1)} %get-tuple-element.70), channel_id=1, source_target_pairs={{0,1},{1,0},{2,3},{3,2},{4,6},{5,7},{6,4},{7,5},{8,9},{9,8},{10,11... | collective-permute-start | bytes 196616 | tf_op jit(solution)/shard_map/ppermute | solution.py:214
  79.8 5.5 %shard_map.69 = (bf16[256,128]{1,0:T(8,128)(2,1)S(1)}, bf16[256,128]{1,0:T(8,128)(2,1)S(1)}, bf16[256,128]{1,0:T(8,128)(2,1)S(1)}, bf16[256,128]{1,0:T(8,128)(2,1)S(1)}) custom-call(bf16[1536,128]{1,0:T(8,128)(2,1)S(1)} %shard_map.68.refs_0_, bf16[512,128]{1,0:T(8,128)(2,1)S(1)} %collective-permute-done.20.refs_3_.refs_1_, ...), custom_call_target="tpu_custom_call" | custom-call | flops 2147483648 | bytes 5177344 | tf_op jit(solution)/shard_map/pallas_call | solution.py:36
  85.3 1.6 %collective-permute-start.27 = (bf16[256,128]{1,0:T(8,128)(2,1)S(1)}, bf16[256,128]{1,0:T(8,128)(2,1)S(1)}, u32[]{:S(2)}, u32[]{:S(2)}) collective-permute-start(bf16[256,128]{1,0:T(8,128)(2,1)S(1)} %get-tuple-element.75), channel_id=1, source_target_pairs={{0,1},{1,0},{2,3},{3,2},{4,6},{5,7},{6,4},{7,5},{8,9},{9,8},{10,11... | collective-permute-start | bytes 196616 | tf_op jit(solution)/shard_map/ppermute | solution.py:214
  86.9 2.1 %collective-permute-start.28 = (bf16[256,128]{1,0:T(8,128)(2,1)S(1)}, bf16[256,128]{1,0:T(8,128)(2,1)S(1)}, u32[]{:S(2)}, u32[]{:S(2)}) collective-permute-start(bf16[256,128]{1,0:T(8,128)(2,1)S(1)} %get-tuple-element.76), channel_id=1, source_target_pairs={{0,2},{1,3},{2,0},{3,1},{4,5},{5,4},{6,7},{7,6},{8,10},{9,11},{10,... | collective-permute-start | bytes 196616 | tf_op jit(solution)/shard_map/ppermute | solution.py:214
  89.9 5.3 %shard_map.71 = (bf16[256,128]{1,0:T(8,128)(2,1)S(1)}, bf16[256,128]{1,0:T(8,128)(2,1)S(1)}, bf16[256,128]{1,0:T(8,128)(2,1)S(1)}, bf16[256,128]{1,0:T(8,128)(2,1)S(1)}) custom-call(bf16[512,128]{1,0:T(8,128)(2,1)S(1)} %get-tuple-element.72.refs_0_.refs_1_, bf16[512,128]{1,0:T(8,128)(2,1)S(1)} %collective-permute-done.20.refs_3_.refs_1_, ...), custom_call_target="tpu_custom_call" | custom-call | flops 2147483648 | bytes 4784128 | tf_op jit(solution)/shard_map/pallas_call | solution.py:36
  95.8 3.0 %collective-permute-start.31 = (bf16[256,128]{1,0:T(8,128)(2,1)S(1)}, bf16[256,128]{1,0:T(8,128)(2,1)S(1)}, u32[]{:S(2)}, u32[]{:S(2)}) collective-permute-start(bf16[256,128]{1,0:T(8,128)(2,1)S(1)} %get-tuple-element.80), channel_id=1, source_target_pairs={{0,2},{1,3},{2,0},{3,1},{4,5},{5,4},{6,7},{7,6},{8,10},{9,11},{10,... | collective-permute-start | bytes 196616 | tf_op jit(solution)/shard_map/ppermute | solution.py:214
  99.7 1.4 %collective-permute-done.31.refs_3_ = bf16[256,128]{1,0:T(8,128)(2,1)S(1)} collective-permute-done((bf16[256,128]{1,0:T(8,128)(2,1)S(1)}, bf16[256,128]{1,0:T(8,128)(2,1)S(1)}, u32[]{:S(2)}, u32[]{:S(2)}) %collective-permute-start.31) | collective-permute-done | bytes 65568 | tf_op jit(solution)/shard_map/ppermute | solution.py:214
  101.1 3.8 %collective-permute-done.32.refs_4_ = bf16[256,128]{1,0:T(8,128)(2,1)S(1)} collective-permute-done((bf16[256,128]{1,0:T(8,128)(2,1)S(1)}, bf16[256,128]{1,0:T(8,128)(2,1)S(1)}, u32[]{:S(2)}, u32[]{:S(2)}) %collective-permute-start.32) | collective-permute-done | bytes 65568 | tf_op jit(solution)/shard_map/ppermute | solution.py:214
  (72 shorter events, 14.4 us)
Async XLA Ops:
  5.4 17.4 %collective-permute-start.6 = (bf16[1536,128]{1,0:T(8,128)(2,1)S(1)}, bf16[1536,128]{1,0:T(8,128)(2,1)S(1)}, u32[]{:S(2)}, u32[]{:S(2)}) collective-permute-start(bf16[1536,128]{1,0:T(8,128)(2,1)S(1)} %shard_map.59.refs_0_.refs_5_), channel_id=1, source_target_pairs={{0,16},{1,17},{2,18},{3,19},{4,12},{5,13},{6,14},{7,15},{8,24},{9,... | collective-permute-start | bytes 1179656 | tf_op jit(solution)/shard_map/ppermute | solution.py:214
  8.3 14.4 %collective-permute-start.5 = (bf16[1536,128]{1,0:T(8,128)(2,1)S(1)}, bf16[1536,128]{1,0:T(8,128)(2,1)S(1)}, u32[]{:S(2)}, u32[]{:S(2)}) collective-permute-start(bf16[1536,128]{1,0:T(8,128)(2,1)S(1)} %shard_map.59.refs_0_.refs_5_), channel_id=1, source_target_pairs={{0,8},{1,9},{2,10},{3,11},{4,20},{5,21},{6,22},{7,23},{8,0},{9,1},... | collective-permute-start | bytes 1179656 | tf_op jit(solution)/shard_map/ppermute | solution.py:214
  9.8 7.9 %collective-permute-start.2 = (bf16[512,128]{1,0:T(8,128)(2,1)S(1)}, bf16[512,128]{1,0:T(8,128)(2,1)S(1)}, u32[]{:S(2)}, u32[]{:S(2)}) collective-permute-start(bf16[512,128]{1,0:T(8,128)(2,1)S(1)} %get-tuple-element.48.refs_0_), channel_id=1, source_target_pairs={{0,1},{1,0},{2,3},{3,2},{4,6},{5,7},{6,4},{7,5},{8,9},{9,8},{10,11... | collective-permute-start | bytes 393224 | tf_op jit(solution)/shard_map/ppermute | solution.py:214
  11.4 11.3 %collective-permute-start.3 = (bf16[512,128]{1,0:T(8,128)(2,1)S(1)}, bf16[512,128]{1,0:T(8,128)(2,1)S(1)}, u32[]{:S(2)}, u32[]{:S(2)}) collective-permute-start(bf16[512,128]{1,0:T(8,128)(2,1)S(1)} %get-tuple-element.49), channel_id=1, source_target_pairs={{0,2},{1,3},{2,0},{3,1},{4,5},{5,4},{6,7},{7,6},{8,10},{9,11},{10,... | collective-permute-start | bytes 393224 | tf_op jit(solution)/shard_map/ppermute | solution.py:214
  14.0 8.7 %collective-permute-start.4 = (bf16[512,128]{1,0:T(8,128)(2,1)S(1)}, bf16[512,128]{1,0:T(8,128)(2,1)S(1)}, u32[]{:S(2)}, u32[]{:S(2)}) collective-permute-start(bf16[512,128]{1,0:T(8,128)(2,1)S(1)} %get-tuple-element.50), channel_id=1, source_target_pairs={{0,3},{1,2},{2,1},{3,0},{4,7},{5,6},{6,5},{7,4},{8,11},{9,10},{10,... | collective-permute-start | bytes 393224 | tf_op jit(solution)/shard_map/ppermute | solution.py:214
  23.0 16.3 %collective-permute-start.10 = (bf16[3072,128]{1,0:T(8,128)(2,1)S(1)}, bf16[3072,128]{1,0:T(8,128)(2,1)S(1)}, u32[]{:S(2)}, u32[]{:S(2)}) collective-permute-start(bf16[3072,128]{1,0:T(8,128)(2,1)S(1)} %get-tuple-element.55), channel_id=1, source_target_pairs={{0,8},{1,9},{2,10},{3,11},{4,20},{5,21},{6,22},{7,23},{8,0},{9,1},... | collective-permute-start | bytes 2359304 | tf_op jit(solution)/shard_map/ppermute | solution.py:214
  23.6 4.5 %collective-permute-start.12 = (bf16[128,1536]{1,0:T(8,128)(2,1)S(1)}, bf16[128,1536]{1,0:T(8,128)(2,1)S(1)}, u32[]{:S(2)}, u32[]{:S(2)}) collective-permute-start(bf16[128,1536]{1,0:T(8,128)(2,1)S(1)} %get-tuple-element.56), channel_id=1, source_target_pairs={{0,4},{1,5},{2,6},{3,7},{4,0},{5,1},{6,2},{7,3},{8,12},{9,13},{10,... | collective-permute-start | bytes 1179656 | tf_op jit(solution)/shard_map/ppermute | solution.py:214
  23.6 15.2 %collective-permute-start.11 = (bf16[1536,128]{1,0:T(8,128)(2,1)S(1)}, bf16[1536,128]{1,0:T(8,128)(2,1)S(1)}, u32[]{:S(2)}, u32[]{:S(2)}) collective-permute-start(bf16[1536,128]{1,0:T(8,128)(2,1)S(1)} %get-tuple-element.52.refs_0_.refs_4_.refs_6_), channel_id=1, source_target_pairs={{0,16},{1,17},{2,18},{3,19},{4,12},{5,13},{6,14},{7,15},{8,24},{9,... | collective-permute-start | bytes 1179656 | tf_op jit(solution)/shard_map/ppermute | solution.py:214
  24.0 5.5 %collective-permute-start.7 = (bf16[512,128]{1,0:T(8,128)(2,1)S(1)}, bf16[512,128]{1,0:T(8,128)(2,1)S(1)}, u32[]{:S(2)}, u32[]{:S(2)}) collective-permute-start(bf16[512,128]{1,0:T(8,128)(2,1)S(1)} %get-tuple-element.51.refs_0_), channel_id=1, source_target_pairs={{0,1},{1,0},{2,3},{3,2},{4,6},{5,7},{6,4},{7,5},{8,9},{9,8},{10,11... | collective-permute-start | bytes 393224 | tf_op jit(solution)/shard_map/ppermute | solution.py:214
  26.1 12.7 %collective-permute-start.8 = (bf16[512,128]{1,0:T(8,128)(2,1)S(1)}, bf16[512,128]{1,0:T(8,128)(2,1)S(1)}, u32[]{:S(2)}, u32[]{:S(2)}) collective-permute-start(bf16[512,128]{1,0:T(8,128)(2,1)S(1)} %get-tuple-element.53), channel_id=1, source_target_pairs={{0,2},{1,3},{2,0},{3,1},{4,5},{5,4},{6,7},{7,6},{8,10},{9,11},{10,... | collective-permute-start | bytes 393224 | tf_op jit(solution)/shard_map/ppermute | solution.py:214
  28.1 10.8 %collective-permute-start.9 = (bf16[512,128]{1,0:T(8,128)(2,1)S(1)}, bf16[512,128]{1,0:T(8,128)(2,1)S(1)}, u32[]{:S(2)}, u32[]{:S(2)}) collective-permute-start(bf16[512,128]{1,0:T(8,128)(2,1)S(1)} %get-tuple-element.54), channel_id=1, source_target_pairs={{0,3},{1,2},{2,1},{3,0},{4,7},{5,6},{6,5},{7,4},{8,11},{9,10},{10,... | collective-permute-start | bytes 393224 | tf_op jit(solution)/shard_map/ppermute | solution.py:214
  39.4 18.7 %collective-permute-start.16 = (bf16[3072,128]{1,0:T(8,128)(2,1)S(1)}, bf16[3072,128]{1,0:T(8,128)(2,1)S(1)}, u32[]{:S(2)}, u32[]{:S(2)}) collective-permute-start(bf16[3072,128]{1,0:T(8,128)(2,1)S(1)} %get-tuple-element.61), channel_id=1, source_target_pairs={{0,8},{1,9},{2,10},{3,11},{4,20},{5,21},{6,22},{7,23},{8,0},{9,1},... | collective-permute-start | bytes 2359304 | tf_op jit(solution)/shard_map/ppermute | solution.py:214
  40.1 18.1 %collective-permute-start.17 = (bf16[1536,128]{1,0:T(8,128)(2,1)S(1)}, bf16[1536,128]{1,0:T(8,128)(2,1)S(1)}, u32[]{:S(2)}, u32[]{:S(2)}) collective-permute-start(bf16[1536,128]{1,0:T(8,128)(2,1)S(1)} %get-tuple-element.58.refs_0_.refs_4_.refs_6_), channel_id=1, source_target_pairs={{0,16},{1,17},{2,18},{3,19},{4,12},{5,13},{6,14},{7,15},{8,24},{9,... | collective-permute-start | bytes 1179656 | tf_op jit(solution)/shard_map/ppermute | solution.py:214
  41.0 10.3 %collective-permute-start.13 = (bf16[768,128]{1,0:T(8,128)(2,1)S(1)}, bf16[768,128]{1,0:T(8,128)(2,1)S(1)}, u32[]{:S(2)}, u32[]{:S(2)}) collective-permute-start(bf16[768,128]{1,0:T(8,128)(2,1)S(1)} %get-tuple-element.57.refs_0_), channel_id=1, source_target_pairs={{0,1},{1,0},{2,3},{3,2},{4,6},{5,7},{6,4},{7,5},{8,9},{9,8},{10,11... | collective-permute-start | bytes 589832 | tf_op jit(solution)/shard_map/ppermute | solution.py:214
  43.3 9.6 %collective-permute-start.14 = (bf16[768,128]{1,0:T(8,128)(2,1)S(1)}, bf16[768,128]{1,0:T(8,128)(2,1)S(1)}, u32[]{:S(2)}, u32[]{:S(2)}) collective-permute-start(bf16[768,128]{1,0:T(8,128)(2,1)S(1)} %get-tuple-element.59), channel_id=1, source_target_pairs={{0,2},{1,3},{2,0},{3,1},{4,5},{5,4},{6,7},{7,6},{8,10},{9,11},{10,... | collective-permute-start | bytes 589832 | tf_op jit(solution)/shard_map/ppermute | solution.py:214
  44.5 13.6 %collective-permute-start.15 = (bf16[768,128]{1,0:T(8,128)(2,1)S(1)}, bf16[768,128]{1,0:T(8,128)(2,1)S(1)}, u32[]{:S(2)}, u32[]{:S(2)}) collective-permute-start(bf16[768,128]{1,0:T(8,128)(2,1)S(1)} %get-tuple-element.60), channel_id=1, source_target_pairs={{0,3},{1,2},{2,1},{3,0},{4,7},{5,6},{6,5},{7,4},{8,11},{9,10},{10,... | collective-permute-start | bytes 589832 | tf_op jit(solution)/shard_map/ppermute | solution.py:214
  58.3 21.5 %collective-permute-start.22 = (bf16[3072,128]{1,0:T(8,128)(2,1)S(1)}, bf16[3072,128]{1,0:T(8,128)(2,1)S(1)}, u32[]{:S(2)}, u32[]{:S(2)}) collective-permute-start(bf16[3072,128]{1,0:T(8,128)(2,1)S(1)} %get-tuple-element.67), channel_id=1, source_target_pairs={{0,8},{1,9},{2,10},{3,11},{4,20},{5,21},{6,22},{7,23},{8,0},{9,1},... | collective-permute-start | bytes 2359304 | tf_op jit(solution)/shard_map/ppermute | solution.py:214
  60.0 12.9 %collective-permute-start.21 = (bf16[1536,128]{1,0:T(8,128)(2,1)S(1)}, bf16[1536,128]{1,0:T(8,128)(2,1)S(1)}, u32[]{:S(2)}, u32[]{:S(2)}) collective-permute-start(bf16[1536,128]{1,0:T(8,128)(2,1)S(1)} %get-tuple-element.63.refs_0_.refs_6_), channel_id=1, source_target_pairs={{0,16},{1,17},{2,18},{3,19},{4,12},{5,13},{6,14},{7,15},{8,24},{9,... | collective-permute-start | bytes 1179656 | tf_op jit(solution)/shard_map/ppermute | solution.py:214
  61.5 10.9 %collective-permute-start.18 = (bf16[512,128]{1,0:T(8,128)(2,1)S(1)}, bf16[512,128]{1,0:T(8,128)(2,1)S(1)}, u32[]{:S(2)}, u32[]{:S(2)}) collective-permute-start(bf16[512,128]{1,0:T(8,128)(2,1)S(1)} %get-tuple-element.62.refs_0_), channel_id=1, source_target_pairs={{0,1},{1,0},{2,3},{3,2},{4,6},{5,7},{6,4},{7,5},{8,9},{9,8},{10,11... | collective-permute-start | bytes 393224 | tf_op jit(solution)/shard_map/ppermute | solution.py:214
  64.0 8.4 %collective-permute-start.19 = (bf16[512,128]{1,0:T(8,128)(2,1)S(1)}, bf16[512,128]{1,0:T(8,128)(2,1)S(1)}, u32[]{:S(2)}, u32[]{:S(2)}) collective-permute-start(bf16[512,128]{1,0:T(8,128)(2,1)S(1)} %get-tuple-element.65), channel_id=1, source_target_pairs={{0,2},{1,3},{2,0},{3,1},{4,5},{5,4},{6,7},{7,6},{8,10},{9,11},{10,... | collective-permute-start | bytes 393224 | tf_op jit(solution)/shard_map/ppermute | solution.py:214
  65.6 7.3 %collective-permute-start.20 = (bf16[512,128]{1,0:T(8,128)(2,1)S(1)}, bf16[512,128]{1,0:T(8,128)(2,1)S(1)}, u32[]{:S(2)}, u32[]{:S(2)}) collective-permute-start(bf16[512,128]{1,0:T(8,128)(2,1)S(1)} %get-tuple-element.66), channel_id=1, source_target_pairs={{0,3},{1,2},{2,1},{3,0},{4,7},{5,6},{6,5},{7,4},{8,11},{9,10},{10,... | collective-permute-start | bytes 393224 | tf_op jit(solution)/shard_map/ppermute | solution.py:214
  72.9 16.9 %collective-permute-start.26 = (bf16[1536,128]{1,0:T(8,128)(2,1)S(1)}, bf16[1536,128]{1,0:T(8,128)(2,1)S(1)}, u32[]{:S(2)}, u32[]{:S(2)}) collective-permute-start(bf16[1536,128]{1,0:T(8,128)(2,1)S(1)} %shard_map.68.refs_0_), channel_id=1, source_target_pairs={{0,8},{1,9},{2,10},{3,11},{4,20},{5,21},{6,22},{7,23},{8,0},{9,1},... | collective-permute-start | bytes 1179656 | tf_op jit(solution)/shard_map/ppermute | solution.py:214
  73.7 16.2 %collective-permute-start.25 = (bf16[256,128]{1,0:T(8,128)(2,1)S(1)}, bf16[256,128]{1,0:T(8,128)(2,1)S(1)}, u32[]{:S(2)}, u32[]{:S(2)}) collective-permute-start(bf16[256,128]{1,0:T(8,128)(2,1)S(1)} %get-tuple-element.64.refs_0_), channel_id=1, source_target_pairs={{0,3},{1,2},{2,1},{3,0},{4,7},{5,6},{6,5},{7,4},{8,11},{9,10},{10,... | collective-permute-start | bytes 196616 | tf_op jit(solution)/shard_map/ppermute | solution.py:214
  78.5 8.4 %collective-permute-start.23 = (bf16[256,128]{1,0:T(8,128)(2,1)S(1)}, bf16[256,128]{1,0:T(8,128)(2,1)S(1)}, u32[]{:S(2)}, u32[]{:S(2)}) collective-permute-start(bf16[256,128]{1,0:T(8,128)(2,1)S(1)} %get-tuple-element.70), channel_id=1, source_target_pairs={{0,1},{1,0},{2,3},{3,2},{4,6},{5,7},{6,4},{7,5},{8,9},{9,8},{10,11... | collective-permute-start | bytes 196616 | tf_op jit(solution)/shard_map/ppermute | solution.py:214
  79.8 9.3 %collective-permute-start.24 = (bf16[256,128]{1,0:T(8,128)(2,1)S(1)}, bf16[256,128]{1,0:T(8,128)(2,1)S(1)}, u32[]{:S(2)}, u32[]{:S(2)}) collective-permute-start(bf16[256,128]{1,0:T(8,128)(2,1)S(1)} %get-tuple-element.71), channel_id=1, source_target_pairs={{0,2},{1,3},{2,0},{3,1},{4,5},{5,4},{6,7},{7,6},{8,10},{9,11},{10,... | collective-permute-start | bytes 196616 | tf_op jit(solution)/shard_map/ppermute | solution.py:214
  85.3 13.6 %collective-permute-start.27 = (bf16[256,128]{1,0:T(8,128)(2,1)S(1)}, bf16[256,128]{1,0:T(8,128)(2,1)S(1)}, u32[]{:S(2)}, u32[]{:S(2)}) collective-permute-start(bf16[256,128]{1,0:T(8,128)(2,1)S(1)} %get-tuple-element.75), channel_id=1, source_target_pairs={{0,1},{1,0},{2,3},{3,2},{4,6},{5,7},{6,4},{7,5},{8,9},{9,8},{10,11... | collective-permute-start | bytes 196616 | tf_op jit(solution)/shard_map/ppermute | solution.py:214
  86.9 12.7 %collective-permute-start.28 = (bf16[256,128]{1,0:T(8,128)(2,1)S(1)}, bf16[256,128]{1,0:T(8,128)(2,1)S(1)}, u32[]{:S(2)}, u32[]{:S(2)}) collective-permute-start(bf16[256,128]{1,0:T(8,128)(2,1)S(1)} %get-tuple-element.76), channel_id=1, source_target_pairs={{0,2},{1,3},{2,0},{3,1},{4,5},{5,4},{6,7},{7,6},{8,10},{9,11},{10,... | collective-permute-start | bytes 196616 | tf_op jit(solution)/shard_map/ppermute | solution.py:214
  89.0 10.6 %collective-permute-start.29 = (bf16[256,128]{1,0:T(8,128)(2,1)S(1)}, bf16[256,128]{1,0:T(8,128)(2,1)S(1)}, u32[]{:S(2)}, u32[]{:S(2)}) collective-permute-start(bf16[256,128]{1,0:T(8,128)(2,1)S(1)} %get-tuple-element.68.refs_0_), channel_id=1, source_target_pairs={{0,3},{1,2},{2,1},{3,0},{4,7},{5,6},{6,5},{7,4},{8,11},{9,10},{10,... | collective-permute-start | bytes 196616 | tf_op jit(solution)/shard_map/ppermute | solution.py:214
  95.2 4.5 %collective-permute-start.30 = (bf16[256,128]{1,0:T(8,128)(2,1)S(1)}, bf16[256,128]{1,0:T(8,128)(2,1)S(1)}, u32[]{:S(2)}, u32[]{:S(2)}) collective-permute-start(bf16[256,128]{1,0:T(8,128)(2,1)S(1)} %get-tuple-element.79), channel_id=1, source_target_pairs={{0,1},{1,0},{2,3},{3,2},{4,6},{5,7},{6,4},{7,5},{8,9},{9,8},{10,11... | collective-permute-start | bytes 196616 | tf_op jit(solution)/shard_map/ppermute | solution.py:214
  95.8 5.3 %collective-permute-start.31 = (bf16[256,128]{1,0:T(8,128)(2,1)S(1)}, bf16[256,128]{1,0:T(8,128)(2,1)S(1)}, u32[]{:S(2)}, u32[]{:S(2)}) collective-permute-start(bf16[256,128]{1,0:T(8,128)(2,1)S(1)} %get-tuple-element.80), channel_id=1, source_target_pairs={{0,2},{1,3},{2,0},{3,1},{4,5},{5,4},{6,7},{7,6},{8,10},{9,11},{10,... | collective-permute-start | bytes 196616 | tf_op jit(solution)/shard_map/ppermute | solution.py:214
  98.9 6.1 %collective-permute-start.32 = (bf16[256,128]{1,0:T(8,128)(2,1)S(1)}, bf16[256,128]{1,0:T(8,128)(2,1)S(1)}, u32[]{:S(2)}, u32[]{:S(2)}) collective-permute-start(bf16[256,128]{1,0:T(8,128)(2,1)S(1)} %get-tuple-element.73.refs_0_), channel_id=1, source_target_pairs={{0,3},{1,2},{2,1},{3,0},{4,7},{5,6},{6,5},{7,4},{8,11},{9,10},{10,... | collective-permute-start | bytes 196616 | tf_op jit(solution)/shard_map/ppermute | solution.py:214
  99.7 5.9 %collective-permute-start.33 = (bf16[512,128]{1,0:T(8,128)(2,1)S(1)}, bf16[512,128]{1,0:T(8,128)(2,1)S(1)}, u32[]{:S(2)}, u32[]{:S(2)}) collective-permute-start(bf16[512,128]{1,0:T(8,128)(2,1)S(1)} %get-tuple-element.82), channel_id=1, source_target_pairs={{0,4},{1,5},{2,6},{3,7},{4,0},{5,1},{6,2},{7,3},{8,12},{9,13},{10,... | collective-permute-start | bytes 393224 | tf_op jit(solution)/shard_map/ppermute | solution.py:214
  (10 other events, 15.9 us)

commit v4 on v3

--- a/solution.py
+++ b/solution.py
@@ -17,6 +17,10 @@
 EXPONENT = math.log2(math.e) / math.sqrt(HEAD_DIM)
 
 
+def nothing_body(out):
+    out[...] = jnp.zeros_like(out)
+
+
 def sds(*shape):
     return jax.ShapeDtypeStruct(shape, BF16)
 
@@ -36,13 +40,17 @@
         made = pl.pallas_call(
             without_last,
             out_shape=outs,
-            in_specs=[pl.BlockSpec(memory_space=pl.ANY)] * skip + [VMEM] * len(args),
+            in_specs=[pl.BlockSpec(memory_space=pl.ANY)] * skip
+            + [VMEM] * len(args),
             out_specs=[VMEM] * len(outs),
             compiler_params=PARAMS,
             cost_estimate=pl.CostEstimate(flops=flops, bytes_accessed=size, transcendentals=exps),
         )(*behind, *args)
         self.last = made[:1]
         return made
+
+    def mark(self):
+        self.call(nothing_body, [sds(16, HEAD_DIM)], flops=2 * 10**10)
 
 
 def read(refs, pieces):
@@ -186,19 +194,16 @@
     )
 
 
-def place_body(pieces, *refs):
-    out = refs[-1]
+def place_body(own, across, out):
     tokens, half = out.shape[0], out.shape[1] // 2
     core = core_index()
-    for piece in range(pieces):
-        own, across = refs[2 * piece : 2 * piece + 2]
-        for hop in HOPS:
-            at = column(piece, hop)
-            here = pl.multiple_of(core * half + at, HEAD_DIM)
-            there = pl.multiple_of((1 - core) * half + at, HEAD_DIM)
-            rows = slice(hop * tokens, (hop + 1) * tokens)
-            out[:, pl.ds(here, HEAD_DIM)] = own[rows, :]
-            out[:, pl.ds(there, HEAD_DIM)] = across[rows, :]
+    for at in range(0, own.shape[0], tokens):
+        place = column(at // tokens // 4, at // tokens % 4)
+        here = pl.multiple_of(core * half + place, HEAD_DIM)
+        there = pl.multiple_of((1 - core) * half + place, HEAD_DIM)
+        rows = slice(at, at + tokens)
+        out[:, pl.ds(here, HEAD_DIM)] = own[rows, :]
+        out[:, pl.ds(there, HEAD_DIM)] = across[rows, :]
 
 
 def permute(array, move):
@@ -244,9 +249,9 @@
         own, other = line.call(normalize_body, [sds(tokens, half)] * 2, x, gain)
         return own, other_core(other)
 
+    k_pair = swap_halves(keys, key_gain)
     (v_other,) = line.call(halves_body, [sds(tokens, half)], values)
     v_pair = (values, other_core(v_other))
-    k_pair = swap_halves(keys, key_gain)
     q_pair = swap_halves(queries, query_gain)
     tensors = (k_pair, v_pair, q_pair)
     k, v, q = range(3)
@@ -260,25 +265,20 @@
     def slots(swapped, first, rows):
         return [(array, first, rows) for array in swapped]
 
-    def send_xy(far, swapped):
-        block = slots(swapped, 0, part) + slots(swapped, part, part)
-        whole = [(far, 0, far.shape[0])]
-        out, both = join(line, [block, whole + block])
-        got = hop_xy(both, FIRST)
-        return out, got, hop_xy(out, SECOND)
-
-    def blocks_of(chunk, sent, far):
-        block, got, got_second = sent
-        four = (
-            (own, 0, block, 0),
-            (own_first, 0, got, got.shape[0] - 2 * rest),
-            (own_second, 0, got_second, 0),
-            (sent0[1], 0, far, 0),
-        )
+    def start_gather(swapped):
+        (block,) = join(line, [slots(swapped, 0, part) + slots(swapped, part, part)])
+        return block, hop_xy(block, FIRST)
+
+    def end_gather(block, got, after=()):
+        rows = block.shape[0]
+        (both,) = join(line, [[(block, 0, rows), (got, 0, rows)]], after)
+        more = hop_xy(both, SECOND)
+        return [(block, 0), (got, 0), (more, 0), (more, rows)]
+
+    def blocks_of(chunk, gathered):
         blocks = []
-        for kept, kept_at, array, at in four:
-            kept_at += 2 * chunk * part
-            keys = [(kept, kept_at, part), (array, at, rest)]
+        for (kept, kept_at), (array, at) in zip(own_gathered, gathered):
+            keys = [(kept, kept_at + 2 * chunk * part, part), (array, at, rest)]
             blocks.append((keys, [(a, first + rows, rows) for a, first, rows in keys]))
         return [
             (low[0] + high[0], low[1] + high[1]) for low, high in zip(blocks[::2], blocks[1::2])
@@ -287,47 +287,46 @@
     def queries_of(chunk, swapped, first):
         return dict(zip(HOPS, [(own_q, chunk * part, part)] + slots(swapped, first, part)))
 
-    def core_swap(back):
-        kept, second, first, opposite = back
-        other = kept, first, second, opposite
-        layout = [[(a, 0, tokens) for a in back], [(a, tokens, tokens) for a in other]]
-        own, across = join(line, layout)
+    def core_swap(groups):
+        own, other = [], []
+        for back, chunks in groups:
+            kept, second, first, opposite = back
+            for c in range(chunks):
+                own += [(a, 2 * c * tokens, tokens) for a in back]
+                other += [(a, (2 * c + 1) * tokens, tokens) for a in (kept, first, second, opposite)]
+        own, across = join(line, [own, other])
         return own, other_core(across)
 
-    def attend_back(slots, blocks, hops):
-        outs = attend(line, [slots[hop] for hop in hops], blocks, [part] * len(hops))
-        return {hop: out if hop == KEPT else hop_z(out, hop) for hop, out in zip(hops, outs)}
-
-    def by_hop(back):
-        return [back[hop] for hop in HOPS]
+    def send_back(outs):
+        return [outs[KEPT]] + [hop_z(outs[hop], hop) for hop in HOPS[1:]]
 
     group0, group1 = [(k, 0), (v, 0)], [(k, 1), (v, 1)]
     group2, group3 = [(k, 2), (v, 2), (q, 0)], [(q, 1), (q, 2)]
+    outs = [part] * 4
 
     swap0 = swap(group0)
     (own,) = pack(line, [[(t, c, KEPT) for c in range(3) for t in (k, v)]], tensors[:2])
-    own_first, own_second = hop_xy(own, FIRST), hop_xy(own, SECOND)
-    swap1 = swap(group1, after=(*swap0, own_first, own_second))
-    sent0 = send_xy(own_second, swap0)
-    swap2 = swap(group2, after=(*swap1, *sent0))
-    sent1 = send_xy(sent0[2], swap1)
-    swap3 = swap(group3, after=(*swap2, *sent1))
-    sent2 = send_xy(sent1[2], swap2)
+    own_got = hop_xy(own, FIRST)
+    line.mark()
+    swap1 = swap(group1, after=(*swap0, own_got))
+    own_gathered = end_gather(own, own_got)
+    gather0 = start_gather(swap0)
+    line.mark()
+    swap2 = swap(group2, after=(*swap1, own_gathered[2][0], gather0[1]))
+    gathered0 = end_gather(*gather0)
+    gather1 = start_gather(swap1)
+    line.mark()
+    swap3 = swap(group3, after=(*swap2, gathered0[2][0], gather1[1]))
+    gathered1 = end_gather(*gather1)
+    gather2 = start_gather(swap2)
     (own_q,) = pack(line, [[(0, c, KEPT) for c in range(3)]], (q_pair,))
-    back0 = attend_back(
-        queries_of(0, swap2, 2 * part), blocks_of(0, sent0, sent1[1]), (OPPOSITE, FIRST, KEPT, SECOND)
-    )
-    (last,) = join(line, [[(sent2[2], 0, 2 * rest)]], after=swap3)
-    far = hop_xy(last, FIRST)
-    back1 = attend_back(
-        queries_of(1, swap3, 0), blocks_of(1, sent1, sent2[1]), (OPPOSITE, FIRST, KEPT, SECOND)
-    )
-    results = core_swap(by_hop(back0))
-    slots2, blocks2 = queries_of(2, swap3, part), blocks_of(2, sent2, far)
-    back2 = attend_back(slots2, blocks2, (OPPOSITE, FIRST, KEPT, SECOND))
-    results += core_swap(by_hop(back1))
-    results += core_swap(by_hop(back2))
-    (attended,) = line.call(functools.partial(place_body, 3), [sds(tokens, width)], *results)
+    out0 = attend(line, list(queries_of(0, swap2, 2 * part).values()), blocks_of(0, gathered0), outs)
+    gathered2 = end_gather(*gather2, after=swap3)
+    out1 = attend(line, list(queries_of(1, swap3, 0).values()), blocks_of(1, gathered1), outs)
+    back01 = send_back(join(line, [[(x, 0, part), (y, 0, part)] for x, y in zip(out0, out1)]))
+    out2 = attend(line, list(queries_of(2, swap3, part).values()), blocks_of(2, gathered2), outs)
+    results = core_swap([(back01, 2), (send_back(out2), 1)])
+    (attended,) = line.call(place_body, [sds(tokens, width)], *results)
     return attended
 
 

time: 108 us -> 100 us (0.926)
  starting transfers between devices: 47.7 us -> 40.2 us
    ppermute x36 -> x30, starting transfers between devices: 47.7 us -> 40.2 us  [permute(): return lax.ppermute(array, AXES, pairs)]
    ppermute x36 -> x30, waiting for transfers between devices: 38.4 us -> 37.8 us  [permute(): return lax.ppermute(array, AXES, pairs)]
    pallas_call x20 -> x25, Pallas kernels: 19.1 us -> 19.4 us  [call(): pl.pallas_call(without_last, out_shape=outs, in_specs=[pl.BlockSpec(memor...]
    unnamed x12 -> x10, local copies, waits for them, and re-layouts: 2.24 us -> 2.39 us
  transfers between devices with their start and end apart: 36 -> 30, of which waited for: 14 -> 12; matrix products, arithmetic and copies ran while one was open for 0% -> 0% of each run, Pallas kernels for 16% -> 17%
where the time goes in v4:
time: 100 us
  starting transfers between devices  40.2 us (40%)
  waiting for transfers between devices  37.8 us (38%)
  Pallas kernels  19.4 us (19%)
  local copies, waits for them, and re-layouts  2.39 us (2%)
    ppermute x30, starting transfers between devices, permute(): return lax.ppermute(array, AXES, pairs)  40.2 us
    ppermute x30, waiting for transfers between devices, permute(): return lax.ppermute(array, AXES, pairs)  37.8 us
    pallas_call x25, Pallas kernels, call(): pl.pallas_call(without_last, out_shape=outs, in_specs=[pl.BlockSpec(memor...  19.4 us
    unnamed x10, local copies, waits for them, and re-layouts  2.39 us
  transfers between devices with their start and end apart: 30, of which 12 were waited for; matrix products, arithmetic and copies ran while one was open for 0% of the time, Pallas kernels for 17%

profile of v4, /device:TPU:0, one launch (start us, length us, event | category | flops | bytes accessed | tf_op | source)
XLA Modules:
  0.0 100.0 jit_solution(496619985015996636)
XLA Ops:
  0.0 1.2 %copy-done.1 = bf16[128,3072]{1,0:T(8,128)(2,1)S(1)} copy-done((bf16[128,3072]{1,0:T(8,128)(2,1)S(1)}, bf16[128,3072]{1,0:T(8,128)(2,1)}, u32[]{:S(2)}) %copy-start.1) | copy-done | bytes 786456
  5.0 3.0 %collective-permute-start.2 = (bf16[512,128]{1,0:T(8,128)(2,1)S(1)}, bf16[512,128]{1,0:T(8,128)(2,1)S(1)}, u32[]{:S(2)}, u32[]{:S(2)}) collective-permute-start(bf16[512,128]{1,0:T(8,128)(2,1)S(1)} %get-tuple-element.42.refs_0_), channel_id=1, source_target_pairs={{0,1},{1,0},{2,3},{3,2},{4,6},{5,7},{6,4},{7,5},{8,9},{9,8},{10,11... | collective-permute-start | bytes 393224 | tf_op jit(solution)/shard_map/ppermute | solution.py:219
  8.1 1.6 %collective-permute-start.5 = (bf16[1536,128]{1,0:T(8,128)(2,1)S(1)}, bf16[1536,128]{1,0:T(8,128)(2,1)S(1)}, u32[]{:S(2)}, u32[]{:S(2)}) collective-permute-start(bf16[1536,128]{1,0:T(8,128)(2,1)S(1)} %shard_map.59.refs_0_.refs_1_.refs_5_), channel_id=1, source_target_pairs={{0,8},{1,9},{2,10},{3,11},{4,20},{5,21},{6,22},{7,23},{8,0},{9,1},... | collective-permute-start | bytes 1179656 | tf_op jit(solution)/shard_map/ppermute | solution.py:219
  9.7 2.6 %collective-permute-start.3 = (bf16[512,128]{1,0:T(8,128)(2,1)S(1)}, bf16[512,128]{1,0:T(8,128)(2,1)S(1)}, u32[]{:S(2)}, u32[]{:S(2)}) collective-permute-start(bf16[512,128]{1,0:T(8,128)(2,1)S(1)} %get-tuple-element.43), channel_id=1, source_target_pairs={{0,2},{1,3},{2,0},{3,1},{4,5},{5,4},{6,7},{7,6},{8,10},{9,11},{10,... | collective-permute-start | bytes 393224 | tf_op jit(solution)/shard_map/ppermute | solution.py:219
  12.5 8.6 %collective-permute-done.3.refs_2_ = bf16[512,128]{1,0:T(8,128)(2,1)S(1)} collective-permute-done((bf16[512,128]{1,0:T(8,128)(2,1)S(1)}, bf16[512,128]{1,0:T(8,128)(2,1)S(1)}, u32[]{:S(2)}, u32[]{:S(2)}) %collective-permute-start.3) | collective-permute-done | bytes 131104 | tf_op jit(solution)/shard_map/ppermute | solution.py:219
  21.2 2.0 %collective-permute-start.6 = (bf16[512,128]{1,0:T(8,128)(2,1)S(1)}, bf16[512,128]{1,0:T(8,128)(2,1)S(1)}, u32[]{:S(2)}, u32[]{:S(2)}) collective-permute-start(bf16[512,128]{1,0:T(8,128)(2,1)S(1)} %get-tuple-element.45.refs_0_), channel_id=1, source_target_pairs={{0,1},{1,0},{2,3},{3,2},{4,6},{5,7},{6,4},{7,5},{8,9},{9,8},{10,11... | collective-permute-start | bytes 393224 | tf_op jit(solution)/shard_map/ppermute | solution.py:219
  23.3 1.5 %collective-permute-start.9 = (bf16[3072,128]{1,0:T(8,128)(2,1)S(1)}, bf16[3072,128]{1,0:T(8,128)(2,1)S(1)}, u32[]{:S(2)}, u32[]{:S(2)}) collective-permute-start(bf16[3072,128]{1,0:T(8,128)(2,1)S(1)} %shard_map.62.refs_0_), channel_id=1, source_target_pairs={{0,16},{1,17},{2,18},{3,19},{4,12},{5,13},{6,14},{7,15},{8,24},{9,... | collective-permute-start | bytes 2359304 | tf_op jit(solution)/shard_map/ppermute | solution.py:219
  25.4 1.9 %collective-permute-start.7 = (bf16[512,128]{1,0:T(8,128)(2,1)S(1)}, bf16[512,128]{1,0:T(8,128)(2,1)S(1)}, u32[]{:S(2)}, u32[]{:S(2)}) collective-permute-start(bf16[512,128]{1,0:T(8,128)(2,1)S(1)} %get-tuple-element.46), channel_id=1, source_target_pairs={{0,2},{1,3},{2,0},{3,1},{4,5},{5,4},{6,7},{7,6},{8,10},{9,11},{10,... | collective-permute-start | bytes 393224 | tf_op jit(solution)/shard_map/ppermute | solution.py:219
  27.4 1.4 %collective-permute-start.8 = (bf16[512,128]{1,0:T(8,128)(2,1)S(1)}, bf16[512,128]{1,0:T(8,128)(2,1)S(1)}, u32[]{:S(2)}, u32[]{:S(2)}) collective-permute-start(bf16[512,128]{1,0:T(8,128)(2,1)S(1)} %get-tuple-element.47), channel_id=1, source_target_pairs={{0,3},{1,2},{2,1},{3,0},{4,7},{5,6},{6,5},{7,4},{8,11},{9,10},{10,... | collective-permute-start | bytes 393224 | tf_op jit(solution)/shard_map/ppermute | solution.py:219
  28.8 7.6 %collective-permute-done.7.refs_2_ = bf16[512,128]{1,0:T(8,128)(2,1)S(1)} collective-permute-done((bf16[512,128]{1,0:T(8,128)(2,1)S(1)}, bf16[512,128]{1,0:T(8,128)(2,1)S(1)}, u32[]{:S(2)}, u32[]{:S(2)}) %collective-permute-start.7) | collective-permute-done | bytes 131104 | tf_op jit(solution)/shard_map/ppermute | solution.py:219
  36.9 2.7 %collective-permute-done.9.refs_4_.refs_9_ = bf16[3072,128]{1,0:T(8,128)(2,1)S(1)} collective-permute-done((bf16[3072,128]{1,0:T(8,128)(2,1)S(1)}, bf16[3072,128]{1,0:T(8,128)(2,1)S(1)}, u32[]{:S(2)}, u32[]{:S(2)}) %collective-permute-start.9) | collective-permute-done | bytes 786464 | tf_op jit(solution)/shard_map/ppermute | solution.py:219
  39.8 1.5 %collective-permute-start.15 = (bf16[3072,128]{1,0:T(8,128)(2,1)S(1)}, bf16[3072,128]{1,0:T(8,128)(2,1)S(1)}, u32[]{:S(2)}, u32[]{:S(2)}) collective-permute-start(bf16[3072,128]{1,0:T(8,128)(2,1)S(1)} %shard_map.66.refs_0_), channel_id=1, source_target_pairs={{0,16},{1,17},{2,18},{3,19},{4,12},{5,13},{6,14},{7,15},{8,24},{9,... | collective-permute-start | bytes 2359304 | tf_op jit(solution)/shard_map/ppermute | solution.py:219
  42.8 3.4 %collective-permute-start.14 = (bf16[768,128]{1,0:T(8,128)(2,1)S(1)}, bf16[768,128]{1,0:T(8,128)(2,1)S(1)}, u32[]{:S(2)}, u32[]{:S(2)}) collective-permute-start(bf16[768,128]{1,0:T(8,128)(2,1)S(1)} %get-tuple-element.51), channel_id=1, source_target_pairs={{0,3},{1,2},{2,1},{3,0},{4,7},{5,6},{6,5},{7,4},{8,11},{9,10},{10,... | collective-permute-start | bytes 589832 | tf_op jit(solution)/shard_map/ppermute | solution.py:219
  46.2 5.1 %collective-permute-done.12.refs_1_.refs_2_ = bf16[768,128]{1,0:T(8,128)(2,1)S(1)} collective-permute-done((bf16[768,128]{1,0:T(8,128)(2,1)S(1)}, bf16[768,128]{1,0:T(8,128)(2,1)S(1)}, u32[]{:S(2)}, u32[]{:S(2)}) %collective-permute-start.12) | collective-permute-done | bytes 196640 | tf_op jit(solution)/shard_map/ppermute | solution.py:219
  51.2 4.3 %collective-permute-done.13.refs_2_.refs_3_ = bf16[768,128]{1,0:T(8,128)(2,1)S(1)} collective-permute-done((bf16[768,128]{1,0:T(8,128)(2,1)S(1)}, bf16[768,128]{1,0:T(8,128)(2,1)S(1)}, u32[]{:S(2)}, u32[]{:S(2)}) %collective-permute-start.13) | collective-permute-done | bytes 196640 | tf_op jit(solution)/shard_map/ppermute | solution.py:219
  55.8 1.6 %collective-permute-start.20 = (bf16[1536,128]{1,0:T(8,128)(2,1)S(1)}, bf16[1536,128]{1,0:T(8,128)(2,1)S(1)}, u32[]{:S(2)}, u32[]{:S(2)}) collective-permute-start(bf16[1536,128]{1,0:T(8,128)(2,1)S(1)} %shard_map.71.refs_0_.refs_4_.refs_6_), channel_id=1, source_target_pairs={{0,8},{1,9},{2,10},{3,11},{4,20},{5,21},{6,22},{7,23},{8,0},{9,1},... | collective-permute-start | bytes 1179656 | tf_op jit(solution)/shard_map/ppermute | solution.py:219
  57.4 1.2 %collective-permute-start.21 = (bf16[3072,128]{1,0:T(8,128)(2,1)S(1)}, bf16[3072,128]{1,0:T(8,128)(2,1)S(1)}, u32[]{:S(2)}, u32[]{:S(2)}) collective-permute-start(bf16[3072,128]{1,0:T(8,128)(2,1)S(1)} %shard_map.70.refs_0_), channel_id=1, source_target_pairs={{0,16},{1,17},{2,18},{3,19},{4,12},{5,13},{6,14},{7,15},{8,24},{9,... | collective-permute-start | bytes 2359304 | tf_op jit(solution)/shard_map/ppermute | solution.py:219
  58.6 2.6 %collective-permute-start.17 = (bf16[512,128]{1,0:T(8,128)(2,1)S(1)}, bf16[512,128]{1,0:T(8,128)(2,1)S(1)}, u32[]{:S(2)}, u32[]{:S(2)}) collective-permute-start(bf16[512,128]{1,0:T(8,128)(2,1)S(1)} %get-tuple-element.52.refs_0_), channel_id=1, source_target_pairs={{0,1},{1,0},{2,3},{3,2},{4,6},{5,7},{6,4},{7,5},{8,9},{9,8},{10,11... | collective-permute-start | bytes 393224 | tf_op jit(solution)/shard_map/ppermute | solution.py:219
  61.7 1.9 %collective-permute-start.19 = (bf16[512,128]{1,0:T(8,128)(2,1)S(1)}, bf16[512,128]{1,0:T(8,128)(2,1)S(1)}, u32[]{:S(2)}, u32[]{:S(2)}) collective-permute-start(bf16[512,128]{1,0:T(8,128)(2,1)S(1)} %get-tuple-element.55), channel_id=1, source_target_pairs={{0,3},{1,2},{2,1},{3,0},{4,7},{5,6},{6,5},{7,4},{8,11},{9,10},{10,... | collective-permute-start | bytes 393224 | tf_op jit(solution)/shard_map/ppermute | solution.py:219
  63.6 5.4 %shard_map.73 = (bf16[256,128]{1,0:T(8,128)(2,1)S(1)}, bf16[256,128]{1,0:T(8,128)(2,1)S(1)}, bf16[256,128]{1,0:T(8,128)(2,1)S(1)}, bf16[256,128]{1,0:T(8,128)(2,1)S(1)}) custom-call(bf16[768,128]{1,0:T(8,128)(2,1)S(1)} %shard_map.72.refs_0_.refs_1_, bf16[768,128]{1,0:T(8,128)(2,1)S(1)} %shard_map.72.refs_0_.refs_1_, ...), custom_call_target="tpu_custom_call" | custom-call | flops 2147483648 | bytes 4194304 | tf_op jit(solution)/shard_map/pallas_call | solution.py:40
  70.8 5.5 %shard_map.75 = (bf16[256,128]{1,0:T(8,128)(2,1)S(1)}, bf16[256,128]{1,0:T(8,128)(2,1)S(1)}, bf16[256,128]{1,0:T(8,128)(2,1)S(1)}, bf16[256,128]{1,0:T(8,128)(2,1)S(1)}) custom-call(bf16[3072,128]{1,0:T(8,128)(2,1)S(1)} %shard_map.74.refs_0_, bf16[768,128]{1,0:T(8,128)(2,1)S(1)} %shard_map.72.refs_0_.refs_1_, ...), custom_call_target="tpu_custom_call" | custom-call | flops 2147483648 | bytes 3997696 | tf_op jit(solution)/shard_map/pallas_call | solution.py:40
  76.4 2.0 %collective-permute-start.23 = (bf16[512,128]{1,0:T(8,128)(2,1)S(1)}, bf16[512,128]{1,0:T(8,128)(2,1)S(1)}, u32[]{:S(2)}, u32[]{:S(2)}) collective-permute-start(bf16[512,128]{1,0:T(8,128)(2,1)S(1)} %get-tuple-element.65), channel_id=1, source_target_pairs={{0,1},{1,0},{2,3},{3,2},{4,6},{5,7},{6,4},{7,5},{8,9},{9,8},{10,11... | collective-permute-start | bytes 393224 | tf_op jit(solution)/shard_map/ppermute | solution.py:219
  78.4 1.2 %collective-permute-start.24 = (bf16[512,128]{1,0:T(8,128)(2,1)S(1)}, bf16[512,128]{1,0:T(8,128)(2,1)S(1)}, u32[]{:S(2)}, u32[]{:S(2)}) collective-permute-start(bf16[512,128]{1,0:T(8,128)(2,1)S(1)} %get-tuple-element.66), channel_id=1, source_target_pairs={{0,2},{1,3},{2,0},{3,1},{4,5},{5,4},{6,7},{7,6},{8,10},{9,11},{10,... | collective-permute-start | bytes 393224 | tf_op jit(solution)/shard_map/ppermute | solution.py:219
  79.7 1.4 %collective-permute-start.25 = (bf16[512,128]{1,0:T(8,128)(2,1)S(1)}, bf16[512,128]{1,0:T(8,128)(2,1)S(1)}, u32[]{:S(2)}, u32[]{:S(2)}) collective-permute-start(bf16[512,128]{1,0:T(8,128)(2,1)S(1)} %get-tuple-element.67), channel_id=1, source_target_pairs={{0,3},{1,2},{2,1},{3,0},{4,7},{5,6},{6,5},{7,4},{8,11},{9,10},{10,... | collective-permute-start | bytes 393224 | tf_op jit(solution)/shard_map/ppermute | solution.py:219
  81.1 1.2 %collective-permute-done.22.refs_10_ = bf16[3072,128]{1,0:T(8,128)(2,1)S(1)} collective-permute-done((bf16[3072,128]{1,0:T(8,128)(2,1)S(1)}, bf16[3072,128]{1,0:T(8,128)(2,1)S(1)}, u32[]{:S(2)}, u32[]{:S(2)}) %collective-permute-start.22) | collective-permute-done | bytes 786464 | tf_op jit(solution)/shard_map/ppermute | solution.py:219
  82.2 5.4 %shard_map.77 = (bf16[256,128]{1,0:T(8,128)(2,1)S(1)}, bf16[256,128]{1,0:T(8,128)(2,1)S(1)}, bf16[256,128]{1,0:T(8,128)(2,1)S(1)}, bf16[256,128]{1,0:T(8,128)(2,1)S(1)}) custom-call(bf16[512,128]{1,0:T(8,128)(2,1)S(1)} %get-tuple-element.63.refs_0_.refs_1_, bf16[768,128]{1,0:T(8,128)(2,1)S(1)} %shard_map.72.refs_0_.refs_1_, ...), custom_call_target="tpu_custom_call" | custom-call | flops 2147483648 | bytes 3997696 | tf_op jit(solution)/shard_map/pallas_call | solution.py:40
  87.7 2.0 %collective-permute-start.26 = (bf16[256,128]{1,0:T(8,128)(2,1)S(1)}, bf16[256,128]{1,0:T(8,128)(2,1)S(1)}, u32[]{:S(2)}, u32[]{:S(2)}) collective-permute-start(bf16[256,128]{1,0:T(8,128)(2,1)S(1)} %get-tuple-element.68), channel_id=1, source_target_pairs={{0,1},{1,0},{2,3},{3,2},{4,6},{5,7},{6,4},{7,5},{8,9},{9,8},{10,11... | collective-permute-start | bytes 196616 | tf_op jit(solution)/shard_map/ppermute | solution.py:219
  89.7 1.2 %collective-permute-start.27 = (bf16[256,128]{1,0:T(8,128)(2,1)S(1)}, bf16[256,128]{1,0:T(8,128)(2,1)S(1)}, u32[]{:S(2)}, u32[]{:S(2)}) collective-permute-start(bf16[256,128]{1,0:T(8,128)(2,1)S(1)} %get-tuple-element.69), channel_id=1, source_target_pairs={{0,2},{1,3},{2,0},{3,1},{4,5},{5,4},{6,7},{7,6},{8,10},{9,11},{10,... | collective-permute-start | bytes 196616 | tf_op jit(solution)/shard_map/ppermute | solution.py:219
  90.9 1.4 %collective-permute-start.28 = (bf16[256,128]{1,0:T(8,128)(2,1)S(1)}, bf16[256,128]{1,0:T(8,128)(2,1)S(1)}, u32[]{:S(2)}, u32[]{:S(2)}) collective-permute-start(bf16[256,128]{1,0:T(8,128)(2,1)S(1)} %get-tuple-element.70), channel_id=1, source_target_pairs={{0,3},{1,2},{2,1},{3,0},{4,7},{5,6},{6,5},{7,4},{8,11},{9,10},{10,... | collective-permute-start | bytes 196616 | tf_op jit(solution)/shard_map/ppermute | solution.py:219
  92.3 3.3 %collective-permute-done.27.refs_7_ = bf16[256,128]{1,0:T(8,128)(2,1)S(1)} collective-permute-done((bf16[256,128]{1,0:T(8,128)(2,1)S(1)}, bf16[256,128]{1,0:T(8,128)(2,1)S(1)}, u32[]{:S(2)}, u32[]{:S(2)}) %collective-permute-start.27) | collective-permute-done | bytes 65568 | tf_op jit(solution)/shard_map/ppermute | solution.py:219
  95.6 1.5 %collective-permute-done.28.refs_8_ = bf16[256,128]{1,0:T(8,128)(2,1)S(1)} collective-permute-done((bf16[256,128]{1,0:T(8,128)(2,1)S(1)}, bf16[256,128]{1,0:T(8,128)(2,1)S(1)}, u32[]{:S(2)}, u32[]{:S(2)}) %collective-permute-start.28) | collective-permute-done | bytes 65568 | tf_op jit(solution)/shard_map/ppermute | solution.py:219
  97.2 1.7 %collective-permute-done.29.refs_2_ = bf16[1536,128]{1,0:T(8,128)(2,1)S(1)} collective-permute-done((bf16[1536,128]{1,0:T(8,128)(2,1)S(1)}, bf16[1536,128]{1,0:T(8,128)(2,1)S(1)}, u32[]{:S(2)}, u32[]{:S(2)}) %collective-permute-start.29) | collective-permute-done | bytes 393248 | tf_op jit(solution)/shard_map/ppermute | solution.py:219
  (63 shorter events, 10.9 us)
Async XLA Ops:
  0.0 2.4 %copy-start = (bf16[128,3072]{1,0:T(8,128)(2,1)S(1)}, bf16[128,3072]{1,0:T(8,128)(2,1)}, u32[]{:S(2)}) copy-start(bf16[128,3072]{1,0:T(8,128)(2,1)} %refs_8_.1) | copy-start | bytes 2359300
  0.0 1.2 %copy-start.1 = (bf16[128,3072]{1,0:T(8,128)(2,1)S(1)}, bf16[128,3072]{1,0:T(8,128)(2,1)}, u32[]{:S(2)}) copy-start(bf16[128,3072]{1,0:T(8,128)(2,1)} %refs_0_.1) | copy-start | bytes 2359300
  2.5 2.1 %collective-permute-start.1 = (bf16[128,1536]{1,0:T(8,128)(2,1)S(1)}, bf16[128,1536]{1,0:T(8,128)(2,1)S(1)}, u32[]{:S(2)}, u32[]{:S(2)}) collective-permute-start(bf16[128,1536]{1,0:T(8,128)(2,1)S(1)} %shard_map.56.refs_0_), channel_id=1, source_target_pairs={{0,4},{1,5},{2,6},{3,7},{4,0},{5,1},{6,2},{7,3},{8,12},{9,13},{10,... | collective-permute-start | bytes 1179656 | tf_op jit(solution)/shard_map/ppermute | solution.py:219
  3.0 1.9 %collective-permute-start = (bf16[128,1536]{1,0:T(8,128)(2,1)S(1)}, bf16[128,1536]{1,0:T(8,128)(2,1)S(1)}, u32[]{:S(2)}, u32[]{:S(2)}) collective-permute-start(bf16[128,1536]{1,0:T(8,128)(2,1)S(1)} %get-tuple-element.41), channel_id=1, source_target_pairs={{0,4},{1,5},{2,6},{3,7},{4,0},{5,1},{6,2},{7,3},{8,12},{9,13},{10,... | collective-permute-start | bytes 1179656 | tf_op jit(solution)/shard_map/ppermute | solution.py:219
  4.1 23.3 %collective-permute-start.11 = (bf16[128,1536]{1,0:T(8,128)(2,1)S(1)}, bf16[128,1536]{1,0:T(8,128)(2,1)S(1)}, u32[]{:S(2)}, u32[]{:S(2)}) collective-permute-start(bf16[128,1536]{1,0:T(8,128)(2,1)S(1)} %get-tuple-element.48), channel_id=1, source_target_pairs={{0,4},{1,5},{2,6},{3,7},{4,0},{5,1},{6,2},{7,3},{8,12},{9,13},{10,... | collective-permute-start | bytes 1179656 | tf_op jit(solution)/shard_map/ppermute | solution.py:219
  5.0 7.5 %collective-permute-start.2 = (bf16[512,128]{1,0:T(8,128)(2,1)S(1)}, bf16[512,128]{1,0:T(8,128)(2,1)S(1)}, u32[]{:S(2)}, u32[]{:S(2)}) collective-permute-start(bf16[512,128]{1,0:T(8,128)(2,1)S(1)} %get-tuple-element.42.refs_0_), channel_id=1, source_target_pairs={{0,1},{1,0},{2,3},{3,2},{4,6},{5,7},{6,4},{7,5},{8,9},{9,8},{10,11... | collective-permute-start | bytes 393224 | tf_op jit(solution)/shard_map/ppermute | solution.py:219
  8.1 13.0 %collective-permute-start.5 = (bf16[1536,128]{1,0:T(8,128)(2,1)S(1)}, bf16[1536,128]{1,0:T(8,128)(2,1)S(1)}, u32[]{:S(2)}, u32[]{:S(2)}) collective-permute-start(bf16[1536,128]{1,0:T(8,128)(2,1)S(1)} %shard_map.59.refs_0_.refs_1_.refs_5_), channel_id=1, source_target_pairs={{0,8},{1,9},{2,10},{3,11},{4,20},{5,21},{6,22},{7,23},{8,0},{9,1},... | collective-permute-start | bytes 1179656 | tf_op jit(solution)/shard_map/ppermute | solution.py:219
  9.7 11.4 %collective-permute-start.3 = (bf16[512,128]{1,0:T(8,128)(2,1)S(1)}, bf16[512,128]{1,0:T(8,128)(2,1)S(1)}, u32[]{:S(2)}, u32[]{:S(2)}) collective-permute-start(bf16[512,128]{1,0:T(8,128)(2,1)S(1)} %get-tuple-element.43), channel_id=1, source_target_pairs={{0,2},{1,3},{2,0},{3,1},{4,5},{5,4},{6,7},{7,6},{8,10},{9,11},{10,... | collective-permute-start | bytes 393224 | tf_op jit(solution)/shard_map/ppermute | solution.py:219
  12.2 8.8 %collective-permute-start.4 = (bf16[512,128]{1,0:T(8,128)(2,1)S(1)}, bf16[512,128]{1,0:T(8,128)(2,1)S(1)}, u32[]{:S(2)}, u32[]{:S(2)}) collective-permute-start(bf16[512,128]{1,0:T(8,128)(2,1)S(1)} %get-tuple-element.44), channel_id=1, source_target_pairs={{0,3},{1,2},{2,1},{3,0},{4,7},{5,6},{6,5},{7,4},{8,11},{9,10},{10,... | collective-permute-start | bytes 393224 | tf_op jit(solution)/shard_map/ppermute | solution.py:219
  21.2 7.6 %collective-permute-start.6 = (bf16[512,128]{1,0:T(8,128)(2,1)S(1)}, bf16[512,128]{1,0:T(8,128)(2,1)S(1)}, u32[]{:S(2)}, u32[]{:S(2)}) collective-permute-start(bf16[512,128]{1,0:T(8,128)(2,1)S(1)} %get-tuple-element.45.refs_0_), channel_id=1, source_target_pairs={{0,1},{1,0},{2,3},{3,2},{4,6},{5,7},{6,4},{7,5},{8,9},{9,8},{10,11... | collective-permute-start | bytes 393224 | tf_op jit(solution)/shard_map/ppermute | solution.py:219
  23.3 16.3 %collective-permute-start.9 = (bf16[3072,128]{1,0:T(8,128)(2,1)S(1)}, bf16[3072,128]{1,0:T(8,128)(2,1)S(1)}, u32[]{:S(2)}, u32[]{:S(2)}) collective-permute-start(bf16[3072,128]{1,0:T(8,128)(2,1)S(1)} %shard_map.62.refs_0_), channel_id=1, source_target_pairs={{0,16},{1,17},{2,18},{3,19},{4,12},{5,13},{6,14},{7,15},{8,24},{9,... | collective-permute-start | bytes 2359304 | tf_op jit(solution)/shard_map/ppermute | solution.py:219
  24.8 12.1 %collective-permute-start.10 = (bf16[1536,128]{1,0:T(8,128)(2,1)S(1)}, bf16[1536,128]{1,0:T(8,128)(2,1)S(1)}, u32[]{:S(2)}, u32[]{:S(2)}) collective-permute-start(bf16[1536,128]{1,0:T(8,128)(2,1)S(1)} %shard_map.63.refs_0_.refs_1_.refs_6_), channel_id=1, source_target_pairs={{0,8},{1,9},{2,10},{3,11},{4,20},{5,21},{6,22},{7,23},{8,0},{9,1},... | collective-permute-start | bytes 1179656 | tf_op jit(solution)/shard_map/ppermute | solution.py:219
  25.4 10.9 %collective-permute-start.7 = (bf16[512,128]{1,0:T(8,128)(2,1)S(1)}, bf16[512,128]{1,0:T(8,128)(2,1)S(1)}, u32[]{:S(2)}, u32[]{:S(2)}) collective-permute-start(bf16[512,128]{1,0:T(8,128)(2,1)S(1)} %get-tuple-element.46), channel_id=1, source_target_pairs={{0,2},{1,3},{2,0},{3,1},{4,5},{5,4},{6,7},{7,6},{8,10},{9,11},{10,... | collective-permute-start | bytes 393224 | tf_op jit(solution)/shard_map/ppermute | solution.py:219
  27.4 9.0 %collective-permute-start.8 = (bf16[512,128]{1,0:T(8,128)(2,1)S(1)}, bf16[512,128]{1,0:T(8,128)(2,1)S(1)}, u32[]{:S(2)}, u32[]{:S(2)}) collective-permute-start(bf16[512,128]{1,0:T(8,128)(2,1)S(1)} %get-tuple-element.47), channel_id=1, source_target_pairs={{0,3},{1,2},{2,1},{3,0},{4,7},{5,6},{6,5},{7,4},{8,11},{9,10},{10,... | collective-permute-start | bytes 393224 | tf_op jit(solution)/shard_map/ppermute | solution.py:219
  39.6 11.6 %collective-permute-start.12 = (bf16[768,128]{1,0:T(8,128)(2,1)S(1)}, bf16[768,128]{1,0:T(8,128)(2,1)S(1)}, u32[]{:S(2)}, u32[]{:S(2)}) collective-permute-start(bf16[768,128]{1,0:T(8,128)(2,1)S(1)} %get-tuple-element.49.refs_0_), channel_id=1, source_target_pairs={{0,1},{1,0},{2,3},{3,2},{4,6},{5,7},{6,4},{7,5},{8,9},{9,8},{10,11... | collective-permute-start | bytes 589832 | tf_op jit(solution)/shard_map/ppermute | solution.py:219
  39.8 15.8 %collective-permute-start.15 = (bf16[3072,128]{1,0:T(8,128)(2,1)S(1)}, bf16[3072,128]{1,0:T(8,128)(2,1)S(1)}, u32[]{:S(2)}, u32[]{:S(2)}) collective-permute-start(bf16[3072,128]{1,0:T(8,128)(2,1)S(1)} %shard_map.66.refs_0_), channel_id=1, source_target_pairs={{0,16},{1,17},{2,18},{3,19},{4,12},{5,13},{6,14},{7,15},{8,24},{9,... | collective-permute-start | bytes 2359304 | tf_op jit(solution)/shard_map/ppermute | solution.py:219
  41.3 14.3 %collective-permute-start.16 = (bf16[1536,128]{1,0:T(8,128)(2,1)S(1)}, bf16[1536,128]{1,0:T(8,128)(2,1)S(1)}, u32[]{:S(2)}, u32[]{:S(2)}) collective-permute-start(bf16[1536,128]{1,0:T(8,128)(2,1)S(1)} %shard_map.67.refs_0_.refs_1_.refs_6_), channel_id=1, source_target_pairs={{0,8},{1,9},{2,10},{3,11},{4,20},{5,21},{6,22},{7,23},{8,0},{9,1},... | collective-permute-start | bytes 1179656 | tf_op jit(solution)/shard_map/ppermute | solution.py:219
  41.8 13.8 %collective-permute-start.13 = (bf16[768,128]{1,0:T(8,128)(2,1)S(1)}, bf16[768,128]{1,0:T(8,128)(2,1)S(1)}, u32[]{:S(2)}, u32[]{:S(2)}) collective-permute-start(bf16[768,128]{1,0:T(8,128)(2,1)S(1)} %get-tuple-element.50), channel_id=1, source_target_pairs={{0,2},{1,3},{2,0},{3,1},{4,5},{5,4},{6,7},{7,6},{8,10},{9,11},{10,... | collective-permute-start | bytes 589832 | tf_op jit(solution)/shard_map/ppermute | solution.py:219
  42.8 12.8 %collective-permute-start.14 = (bf16[768,128]{1,0:T(8,128)(2,1)S(1)}, bf16[768,128]{1,0:T(8,128)(2,1)S(1)}, u32[]{:S(2)}, u32[]{:S(2)}) collective-permute-start(bf16[768,128]{1,0:T(8,128)(2,1)S(1)} %get-tuple-element.51), channel_id=1, source_target_pairs={{0,3},{1,2},{2,1},{3,0},{4,7},{5,6},{6,5},{7,4},{8,11},{9,10},{10,... | collective-permute-start | bytes 589832 | tf_op jit(solution)/shard_map/ppermute | solution.py:219
  55.8 14.4 %collective-permute-start.20 = (bf16[1536,128]{1,0:T(8,128)(2,1)S(1)}, bf16[1536,128]{1,0:T(8,128)(2,1)S(1)}, u32[]{:S(2)}, u32[]{:S(2)}) collective-permute-start(bf16[1536,128]{1,0:T(8,128)(2,1)S(1)} %shard_map.71.refs_0_.refs_4_.refs_6_), channel_id=1, source_target_pairs={{0,8},{1,9},{2,10},{3,11},{4,20},{5,21},{6,22},{7,23},{8,0},{9,1},... | collective-permute-start | bytes 1179656 | tf_op jit(solution)/shard_map/ppermute | solution.py:219
  57.4 13.5 %collective-permute-start.21 = (bf16[3072,128]{1,0:T(8,128)(2,1)S(1)}, bf16[3072,128]{1,0:T(8,128)(2,1)S(1)}, u32[]{:S(2)}, u32[]{:S(2)}) collective-permute-start(bf16[3072,128]{1,0:T(8,128)(2,1)S(1)} %shard_map.70.refs_0_), channel_id=1, source_target_pairs={{0,16},{1,17},{2,18},{3,19},{4,12},{5,13},{6,14},{7,15},{8,24},{9,... | collective-permute-start | bytes 2359304 | tf_op jit(solution)/shard_map/ppermute | solution.py:219
  58.6 10.5 %collective-permute-start.17 = (bf16[512,128]{1,0:T(8,128)(2,1)S(1)}, bf16[512,128]{1,0:T(8,128)(2,1)S(1)}, u32[]{:S(2)}, u32[]{:S(2)}) collective-permute-start(bf16[512,128]{1,0:T(8,128)(2,1)S(1)} %get-tuple-element.52.refs_0_), channel_id=1, source_target_pairs={{0,1},{1,0},{2,3},{3,2},{4,6},{5,7},{6,4},{7,5},{8,9},{9,8},{10,11... | collective-permute-start | bytes 393224 | tf_op jit(solution)/shard_map/ppermute | solution.py:219
  61.2 8.9 %collective-permute-start.18 = (bf16[512,128]{1,0:T(8,128)(2,1)S(1)}, bf16[512,128]{1,0:T(8,128)(2,1)S(1)}, u32[]{:S(2)}, u32[]{:S(2)}) collective-permute-start(bf16[512,128]{1,0:T(8,128)(2,1)S(1)} %get-tuple-element.54), channel_id=1, source_target_pairs={{0,2},{1,3},{2,0},{3,1},{4,5},{5,4},{6,7},{7,6},{8,10},{9,11},{10,... | collective-permute-start | bytes 393224 | tf_op jit(solution)/shard_map/ppermute | solution.py:219
  61.7 8.4 %collective-permute-start.19 = (bf16[512,128]{1,0:T(8,128)(2,1)S(1)}, bf16[512,128]{1,0:T(8,128)(2,1)S(1)}, u32[]{:S(2)}, u32[]{:S(2)}) collective-permute-start(bf16[512,128]{1,0:T(8,128)(2,1)S(1)} %get-tuple-element.55), channel_id=1, source_target_pairs={{0,3},{1,2},{2,1},{3,0},{4,7},{5,6},{6,5},{7,4},{8,11},{9,10},{10,... | collective-permute-start | bytes 393224 | tf_op jit(solution)/shard_map/ppermute | solution.py:219
  70.2 12.1 %collective-permute-start.22 = (bf16[3072,128]{1,0:T(8,128)(2,1)S(1)}, bf16[3072,128]{1,0:T(8,128)(2,1)S(1)}, u32[]{:S(2)}, u32[]{:S(2)}) collective-permute-start(bf16[3072,128]{1,0:T(8,128)(2,1)S(1)} %shard_map.74.refs_0_), channel_id=1, source_target_pairs={{0,16},{1,17},{2,18},{3,19},{4,12},{5,13},{6,14},{7,15},{8,24},{9,... | collective-permute-start | bytes 2359304 | tf_op jit(solution)/shard_map/ppermute | solution.py:219
  76.4 14.5 %collective-permute-start.23 = (bf16[512,128]{1,0:T(8,128)(2,1)S(1)}, bf16[512,128]{1,0:T(8,128)(2,1)S(1)}, u32[]{:S(2)}, u32[]{:S(2)}) collective-permute-start(bf16[512,128]{1,0:T(8,128)(2,1)S(1)} %get-tuple-element.65), channel_id=1, source_target_pairs={{0,1},{1,0},{2,3},{3,2},{4,6},{5,7},{6,4},{7,5},{8,9},{9,8},{10,11... | collective-permute-start | bytes 393224 | tf_op jit(solution)/shard_map/ppermute | solution.py:219
  78.4 13.9 %collective-permute-start.24 = (bf16[512,128]{1,0:T(8,128)(2,1)S(1)}, bf16[512,128]{1,0:T(8,128)(2,1)S(1)}, u32[]{:S(2)}, u32[]{:S(2)}) collective-permute-start(bf16[512,128]{1,0:T(8,128)(2,1)S(1)} %get-tuple-element.66), channel_id=1, source_target_pairs={{0,2},{1,3},{2,0},{3,1},{4,5},{5,4},{6,7},{7,6},{8,10},{9,11},{10,... | collective-permute-start | bytes 393224 | tf_op jit(solution)/shard_map/ppermute | solution.py:219
  79.7 12.6 %collective-permute-start.25 = (bf16[512,128]{1,0:T(8,128)(2,1)S(1)}, bf16[512,128]{1,0:T(8,128)(2,1)S(1)}, u32[]{:S(2)}, u32[]{:S(2)}) collective-permute-start(bf16[512,128]{1,0:T(8,128)(2,1)S(1)} %get-tuple-element.67), channel_id=1, source_target_pairs={{0,3},{1,2},{2,1},{3,0},{4,7},{5,6},{6,5},{7,4},{8,11},{9,10},{10,... | collective-permute-start | bytes 393224 | tf_op jit(solution)/shard_map/ppermute | solution.py:219
  87.7 4.6 %collective-permute-start.26 = (bf16[256,128]{1,0:T(8,128)(2,1)S(1)}, bf16[256,128]{1,0:T(8,128)(2,1)S(1)}, u32[]{:S(2)}, u32[]{:S(2)}) collective-permute-start(bf16[256,128]{1,0:T(8,128)(2,1)S(1)} %get-tuple-element.68), channel_id=1, source_target_pairs={{0,1},{1,0},{2,3},{3,2},{4,6},{5,7},{6,4},{7,5},{8,9},{9,8},{10,11... | collective-permute-start | bytes 196616 | tf_op jit(solution)/shard_map/ppermute | solution.py:219
  89.7 5.9 %collective-permute-start.27 = (bf16[256,128]{1,0:T(8,128)(2,1)S(1)}, bf16[256,128]{1,0:T(8,128)(2,1)S(1)}, u32[]{:S(2)}, u32[]{:S(2)}) collective-permute-start(bf16[256,128]{1,0:T(8,128)(2,1)S(1)} %get-tuple-element.69), channel_id=1, source_target_pairs={{0,2},{1,3},{2,0},{3,1},{4,5},{5,4},{6,7},{7,6},{8,10},{9,11},{10,... | collective-permute-start | bytes 196616 | tf_op jit(solution)/shard_map/ppermute | solution.py:219
  90.9 6.2 %collective-permute-start.28 = (bf16[256,128]{1,0:T(8,128)(2,1)S(1)}, bf16[256,128]{1,0:T(8,128)(2,1)S(1)}, u32[]{:S(2)}, u32[]{:S(2)}) collective-permute-start(bf16[256,128]{1,0:T(8,128)(2,1)S(1)} %get-tuple-element.70), channel_id=1, source_target_pairs={{0,3},{1,2},{2,1},{3,0},{4,7},{5,6},{6,5},{7,4},{8,11},{9,10},{10,... | collective-permute-start | bytes 196616 | tf_op jit(solution)/shard_map/ppermute | solution.py:219
  97.2 1.8 %collective-permute-start.29 = (bf16[1536,128]{1,0:T(8,128)(2,1)S(1)}, bf16[1536,128]{1,0:T(8,128)(2,1)S(1)}, u32[]{:S(2)}, u32[]{:S(2)}) collective-permute-start(bf16[1536,128]{1,0:T(8,128)(2,1)S(1)} %get-tuple-element.72), channel_id=1, source_target_pairs={{0,4},{1,5},{2,6},{3,7},{4,0},{5,1},{6,2},{7,3},{8,12},{9,13},{10,... | collective-permute-start | bytes 1179656 | tf_op jit(solution)/shard_map/ppermute | solution.py:219
  (3 other events, 3.0 us)

commit v5 on v4

--- a/solution.py
+++ b/solution.py
@@ -194,16 +194,20 @@
     )
 
 
-def place_body(own, across, out):
+def place_body(*refs):
+    out = refs[-1]
     tokens, half = out.shape[0], out.shape[1] // 2
     core = core_index()
-    for at in range(0, own.shape[0], tokens):
-        place = column(at // tokens // 4, at // tokens % 4)
-        here = pl.multiple_of(core * half + place, HEAD_DIM)
-        there = pl.multiple_of((1 - core) * half + place, HEAD_DIM)
-        rows = slice(at, at + tokens)
-        out[:, pl.ds(here, HEAD_DIM)] = own[rows, :]
-        out[:, pl.ds(there, HEAD_DIM)] = across[rows, :]
+    place = 0
+    for own, across in zip(refs[:-1:2], refs[1:-1:2]):
+        for at in range(0, own.shape[0], tokens):
+            start = column(place // 4, place % 4)
+            here = pl.multiple_of(core * half + start, HEAD_DIM)
+            there = pl.multiple_of((1 - core) * half + start, HEAD_DIM)
+            rows = slice(at, at + tokens)
+            out[:, pl.ds(here, HEAD_DIM)] = own[rows, :]
+            out[:, pl.ds(there, HEAD_DIM)] = across[rows, :]
+            place += 1
 
 
 def permute(array, move):
@@ -265,15 +269,16 @@
     def slots(swapped, first, rows):
         return [(array, first, rows) for array in swapped]
 
-    def start_gather(swapped):
-        (block,) = join(line, [slots(swapped, 0, part) + slots(swapped, part, part)])
+    def start_gather(swapped, *ahead):
+        layout = slots(swapped, 0, part) + slots(swapped, part, part)
+        (block,) = join(line, [[(a, 0, a.shape[0]) for a in ahead] + layout])
         return block, hop_xy(block, FIRST)
 
-    def end_gather(block, got, after=()):
-        rows = block.shape[0]
-        (both,) = join(line, [[(block, 0, rows), (got, 0, rows)]], after)
+    def end_gather(block, got, skip=0, after=()):
+        rows = block.shape[0] - skip
+        (both,) = join(line, [[(block, skip, rows), (got, skip, rows)]], after)
         more = hop_xy(both, SECOND)
-        return [(block, 0), (got, 0), (more, 0), (more, rows)]
+        return [(block, skip), (got, skip), (more, 0), (more, rows)]
 
     def blocks_of(chunk, gathered):
         blocks = []
@@ -287,13 +292,12 @@
     def queries_of(chunk, swapped, first):
         return dict(zip(HOPS, [(own_q, chunk * part, part)] + slots(swapped, first, part)))
 
-    def core_swap(groups):
+    def core_swap(back, chunks):
+        kept, second, first, opposite = back
         own, other = [], []
-        for back, chunks in groups:
-            kept, second, first, opposite = back
-            for c in range(chunks):
-                own += [(a, 2 * c * tokens, tokens) for a in back]
-                other += [(a, (2 * c + 1) * tokens, tokens) for a in (kept, first, second, opposite)]
+        for c in range(chunks):
+            own += [(a, 2 * c * tokens, tokens) for a in back]
+            other += [(a, (2 * c + 1) * tokens, tokens) for a in (kept, first, second, opposite)]
         own, across = join(line, [own, other])
         return own, other_core(across)
 
@@ -306,14 +310,15 @@
 
     swap0 = swap(group0)
     (own,) = pack(line, [[(t, c, KEPT) for c in range(3) for t in (k, v)]], tensors[:2])
-    own_got = hop_xy(own, FIRST)
+    own_first, own_second = hop_xy(own, FIRST), hop_xy(own, SECOND)
     line.mark()
-    swap1 = swap(group1, after=(*swap0, own_got))
-    own_gathered = end_gather(own, own_got)
-    gather0 = start_gather(swap0)
+    swap1 = swap(group1, after=(*swap0, own_first, own_second))
+    gather0 = start_gather(swap0, own_second)
     line.mark()
-    swap2 = swap(group2, after=(*swap1, own_gathered[2][0], gather0[1]))
-    gathered0 = end_gather(*gather0)
+    swap2 = swap(group2, after=(*swap1, gather0[1]))
+    skip = own.shape[0]
+    own_gathered = [(own, 0), (own_first, 0), (own_second, 0), (gather0[1], 0)]
+    gathered0 = end_gather(*gather0, skip)
     gather1 = start_gather(swap1)
     line.mark()
     swap3 = swap(group3, after=(*swap2, gathered0[2][0], gather1[1]))
@@ -325,7 +330,10 @@
     out1 = attend(line, list(queries_of(1, swap3, 0).values()), blocks_of(1, gathered1), outs)
     back01 = send_back(join(line, [[(x, 0, part), (y, 0, part)] for x, y in zip(out0, out1)]))
     out2 = attend(line, list(queries_of(2, swap3, part).values()), blocks_of(2, gathered2), outs)
-    results = core_swap([(back01, 2), (send_back(out2), 1)])
+    back2 = send_back(out2)
+    results = core_swap(back01, 2)
+    line.mark()
+    results += core_swap(back2, 1)
     (attended,) = line.call(place_body, [sds(tokens, width)], *results)
     return attended
 

time: 100 us -> 97.1 us (0.971)
  waiting for transfers between devices: 37.8 us -> 36.2 us
  starting transfers between devices: 40.2 us -> 38.7 us
    ppermute x30 -> x31, waiting for transfers between devices: 37.8 us -> 36.2 us  [permute(): return lax.ppermute(array, AXES, pairs)]
    ppermute x30 -> x31, starting transfers between devices: 40.2 us -> 38.7 us  [permute(): return lax.ppermute(array, AXES, pairs)]
    pallas_call x25 -> x26, Pallas kernels: 19.4 us -> 19.4 us  [call(): pl.pallas_call(without_last, out_shape=outs, in_specs=[pl.BlockSpec(memor...]
  transfers between devices with their start and end apart: 30 -> 31, of which waited for: 12 -> 13; matrix products, arithmetic and copies ran while one was open for 0% -> 0% of each run, Pallas kernels for 17% -> 18%
where the time goes in v5:
time: 97.1 us; the launch traced here: 96.9 us
  starting transfers between devices  38.7 us (40%)
  waiting for transfers between devices  36.2 us (37%)
  Pallas kernels  19.4 us (20%)
  local copies, waits for them, and re-layouts  2.39 us (2%)
    ppermute x31, starting transfers between devices, permute(): return lax.ppermute(array, AXES, pairs)  38.7 us
    ppermute x31, waiting for transfers between devices, permute(): return lax.ppermute(array, AXES, pairs)  36.2 us
    pallas_call x26, Pallas kernels, call(): pl.pallas_call(without_last, out_shape=outs, in_specs=[pl.BlockSpec(memor...  19.4 us
    unnamed x10, local copies, waits for them, and re-layouts  2.39 us
  transfers between devices with their start and end apart: 31, of which 13 were waited for; matrix products, arithmetic and copies ran while one was open for 0% of the time, Pallas kernels for 18%

profile of v5, /device:TPU:0, one launch (start us, length us, event | category | flops | bytes accessed | tf_op | source)
XLA Modules:
  0.0 96.9 jit_solution(7396588416408430903)
XLA Ops:
  0.0 1.2 %copy-done.1 = bf16[128,3072]{1,0:T(8,128)(2,1)S(1)} copy-done((bf16[128,3072]{1,0:T(8,128)(2,1)S(1)}, bf16[128,3072]{1,0:T(8,128)(2,1)}, u32[]{:S(2)}) %copy-start.1) | copy-done | bytes 786456
  5.1 3.0 %collective-permute-start.6 = (bf16[1536,128]{1,0:T(8,128)(2,1)S(1)}, bf16[1536,128]{1,0:T(8,128)(2,1)S(1)}, u32[]{:S(2)}, u32[]{:S(2)}) collective-permute-start(bf16[1536,128]{1,0:T(8,128)(2,1)S(1)} %shard_map.59.refs_0_.refs_5_), channel_id=1, source_target_pairs={{0,16},{1,17},{2,18},{3,19},{4,12},{5,13},{6,14},{7,15},{8,24},{9,... | collective-permute-start | bytes 1179656 | tf_op jit(solution)/shard_map/ppermute | solution.py:223
  8.1 1.5 %collective-permute-start.5 = (bf16[1536,128]{1,0:T(8,128)(2,1)S(1)}, bf16[1536,128]{1,0:T(8,128)(2,1)S(1)}, u32[]{:S(2)}, u32[]{:S(2)}) collective-permute-start(bf16[1536,128]{1,0:T(8,128)(2,1)S(1)} %shard_map.59.refs_0_.refs_5_), channel_id=1, source_target_pairs={{0,8},{1,9},{2,10},{3,11},{4,20},{5,21},{6,22},{7,23},{8,0},{9,1},... | collective-permute-start | bytes 1179656 | tf_op jit(solution)/shard_map/ppermute | solution.py:223
  9.5 1.6 %collective-permute-start.2 = (bf16[512,128]{1,0:T(8,128)(2,1)S(1)}, bf16[512,128]{1,0:T(8,128)(2,1)S(1)}, u32[]{:S(2)}, u32[]{:S(2)}) collective-permute-start(bf16[512,128]{1,0:T(8,128)(2,1)S(1)} %get-tuple-element.44.refs_0_), channel_id=1, source_target_pairs={{0,1},{1,0},{2,3},{3,2},{4,6},{5,7},{6,4},{7,5},{8,9},{9,8},{10,11... | collective-permute-start | bytes 393224 | tf_op jit(solution)/shard_map/ppermute | solution.py:223
  11.1 2.6 %collective-permute-start.3 = (bf16[512,128]{1,0:T(8,128)(2,1)S(1)}, bf16[512,128]{1,0:T(8,128)(2,1)S(1)}, u32[]{:S(2)}, u32[]{:S(2)}) collective-permute-start(bf16[512,128]{1,0:T(8,128)(2,1)S(1)} %get-tuple-element.45), channel_id=1, source_target_pairs={{0,2},{1,3},{2,0},{3,1},{4,5},{5,4},{6,7},{7,6},{8,10},{9,11},{10,... | collective-permute-start | bytes 393224 | tf_op jit(solution)/shard_map/ppermute | solution.py:223
  13.9 3.5 %collective-permute-done.2.refs_1_.refs_2_ = bf16[512,128]{1,0:T(8,128)(2,1)S(1)} collective-permute-done((bf16[512,128]{1,0:T(8,128)(2,1)S(1)}, bf16[512,128]{1,0:T(8,128)(2,1)S(1)}, u32[]{:S(2)}, u32[]{:S(2)}) %collective-permute-start.2) | collective-permute-done | bytes 131104 | tf_op jit(solution)/shard_map/ppermute | solution.py:223
  17.4 5.0 %collective-permute-done.3.refs_2_.refs_3_ = bf16[512,128]{1,0:T(8,128)(2,1)S(1)} collective-permute-done((bf16[512,128]{1,0:T(8,128)(2,1)S(1)}, bf16[512,128]{1,0:T(8,128)(2,1)S(1)}, u32[]{:S(2)}, u32[]{:S(2)}) %collective-permute-start.3) | collective-permute-done | bytes 131104 | tf_op jit(solution)/shard_map/ppermute | solution.py:223
  22.6 2.1 %collective-permute-start.7 = (bf16[512,128]{1,0:T(8,128)(2,1)S(1)}, bf16[512,128]{1,0:T(8,128)(2,1)S(1)}, u32[]{:S(2)}, u32[]{:S(2)}) collective-permute-start(bf16[512,128]{1,0:T(8,128)(2,1)S(1)} %get-tuple-element.47.refs_0_), channel_id=1, source_target_pairs={{0,1},{1,0},{2,3},{3,2},{4,6},{5,7},{6,4},{7,5},{8,9},{9,8},{10,11... | collective-permute-start | bytes 393224 | tf_op jit(solution)/shard_map/ppermute | solution.py:223
  25.4 1.9 %collective-permute-start.8 = (bf16[512,128]{1,0:T(8,128)(2,1)S(1)}, bf16[512,128]{1,0:T(8,128)(2,1)S(1)}, u32[]{:S(2)}, u32[]{:S(2)}) collective-permute-start(bf16[512,128]{1,0:T(8,128)(2,1)S(1)} %get-tuple-element.48), channel_id=1, source_target_pairs={{0,2},{1,3},{2,0},{3,1},{4,5},{5,4},{6,7},{7,6},{8,10},{9,11},{10,... | collective-permute-start | bytes 393224 | tf_op jit(solution)/shard_map/ppermute | solution.py:223
  27.3 1.4 %collective-permute-start.9 = (bf16[512,128]{1,0:T(8,128)(2,1)S(1)}, bf16[512,128]{1,0:T(8,128)(2,1)S(1)}, u32[]{:S(2)}, u32[]{:S(2)}) collective-permute-start(bf16[512,128]{1,0:T(8,128)(2,1)S(1)} %get-tuple-element.49), channel_id=1, source_target_pairs={{0,3},{1,2},{2,1},{3,0},{4,7},{5,6},{6,5},{7,4},{8,11},{9,10},{10,... | collective-permute-start | bytes 393224 | tf_op jit(solution)/shard_map/ppermute | solution.py:223
  28.8 7.9 %collective-permute-done.8.refs_2_ = bf16[512,128]{1,0:T(8,128)(2,1)S(1)} collective-permute-done((bf16[512,128]{1,0:T(8,128)(2,1)S(1)}, bf16[512,128]{1,0:T(8,128)(2,1)S(1)}, u32[]{:S(2)}, u32[]{:S(2)}) %collective-permute-start.8) | collective-permute-done | bytes 131104 | tf_op jit(solution)/shard_map/ppermute | solution.py:223
  36.9 1.9 %collective-permute-start.12 = (bf16[768,128]{1,0:T(8,128)(2,1)S(1)}, bf16[768,128]{1,0:T(8,128)(2,1)S(1)}, u32[]{:S(2)}, u32[]{:S(2)}) collective-permute-start(bf16[768,128]{1,0:T(8,128)(2,1)S(1)} %get-tuple-element.51.refs_0_), channel_id=1, source_target_pairs={{0,1},{1,0},{2,3},{3,2},{4,6},{5,7},{6,4},{7,5},{8,9},{9,8},{10,11... | collective-permute-start | bytes 589832 | tf_op jit(solution)/shard_map/ppermute | solution.py:223
  39.7 1.5 %collective-permute-start.16 = (bf16[1536,128]{1,0:T(8,128)(2,1)S(1)}, bf16[1536,128]{1,0:T(8,128)(2,1)S(1)}, u32[]{:S(2)}, u32[]{:S(2)}) collective-permute-start(bf16[1536,128]{1,0:T(8,128)(2,1)S(1)} %shard_map.66.refs_0_.refs_1_.refs_6_), channel_id=1, source_target_pairs={{0,8},{1,9},{2,10},{3,11},{4,20},{5,21},{6,22},{7,23},{8,0},{9,1},... | collective-permute-start | bytes 1179656 | tf_op jit(solution)/shard_map/ppermute | solution.py:223
  41.2 1.0 %collective-permute-start.13 = (bf16[768,128]{1,0:T(8,128)(2,1)S(1)}, bf16[768,128]{1,0:T(8,128)(2,1)S(1)}, u32[]{:S(2)}, u32[]{:S(2)}) collective-permute-start(bf16[768,128]{1,0:T(8,128)(2,1)S(1)} %get-tuple-element.52), channel_id=1, source_target_pairs={{0,2},{1,3},{2,0},{3,1},{4,5},{5,4},{6,7},{7,6},{8,10},{9,11},{10,... | collective-permute-start | bytes 589832 | tf_op jit(solution)/shard_map/ppermute | solution.py:223
  42.2 1.4 %collective-permute-start.14 = (bf16[768,128]{1,0:T(8,128)(2,1)S(1)}, bf16[768,128]{1,0:T(8,128)(2,1)S(1)}, u32[]{:S(2)}, u32[]{:S(2)}) collective-permute-start(bf16[768,128]{1,0:T(8,128)(2,1)S(1)} %get-tuple-element.53), channel_id=1, source_target_pairs={{0,3},{1,2},{2,1},{3,0},{4,7},{5,6},{6,5},{7,4},{8,11},{9,10},{10,... | collective-permute-start | bytes 589832 | tf_op jit(solution)/shard_map/ppermute | solution.py:223
  43.6 3.7 %collective-permute-done.12.refs_1_.refs_2_ = bf16[768,128]{1,0:T(8,128)(2,1)S(1)} collective-permute-done((bf16[768,128]{1,0:T(8,128)(2,1)S(1)}, bf16[768,128]{1,0:T(8,128)(2,1)S(1)}, u32[]{:S(2)}, u32[]{:S(2)}) %collective-permute-start.12) | collective-permute-done | bytes 196640 | tf_op jit(solution)/shard_map/ppermute | solution.py:223
  47.4 7.5 %collective-permute-done.13.refs_2_.refs_3_ = bf16[768,128]{1,0:T(8,128)(2,1)S(1)} collective-permute-done((bf16[768,128]{1,0:T(8,128)(2,1)S(1)}, bf16[768,128]{1,0:T(8,128)(2,1)S(1)}, u32[]{:S(2)}, u32[]{:S(2)}) %collective-permute-start.13) | collective-permute-done | bytes 196640 | tf_op jit(solution)/shard_map/ppermute | solution.py:223
  55.4 1.3 %collective-permute-start.21 = (bf16[3072,128]{1,0:T(8,128)(2,1)S(1)}, bf16[3072,128]{1,0:T(8,128)(2,1)S(1)}, u32[]{:S(2)}, u32[]{:S(2)}) collective-permute-start(bf16[3072,128]{1,0:T(8,128)(2,1)S(1)} %shard_map.69.refs_0_), channel_id=1, source_target_pairs={{0,16},{1,17},{2,18},{3,19},{4,12},{5,13},{6,14},{7,15},{8,24},{9,... | collective-permute-start | bytes 2359304 | tf_op jit(solution)/shard_map/ppermute | solution.py:223
  56.7 2.6 %collective-permute-start.17 = (bf16[512,128]{1,0:T(8,128)(2,1)S(1)}, bf16[512,128]{1,0:T(8,128)(2,1)S(1)}, u32[]{:S(2)}, u32[]{:S(2)}) collective-permute-start(bf16[512,128]{1,0:T(8,128)(2,1)S(1)} %get-tuple-element.54.refs_0_), channel_id=1, source_target_pairs={{0,1},{1,0},{2,3},{3,2},{4,6},{5,7},{6,4},{7,5},{8,9},{9,8},{10,11... | collective-permute-start | bytes 393224 | tf_op jit(solution)/shard_map/ppermute | solution.py:223
  59.7 1.9 %collective-permute-start.19 = (bf16[512,128]{1,0:T(8,128)(2,1)S(1)}, bf16[512,128]{1,0:T(8,128)(2,1)S(1)}, u32[]{:S(2)}, u32[]{:S(2)}) collective-permute-start(bf16[512,128]{1,0:T(8,128)(2,1)S(1)} %get-tuple-element.57), channel_id=1, source_target_pairs={{0,3},{1,2},{2,1},{3,0},{4,7},{5,6},{6,5},{7,4},{8,11},{9,10},{10,... | collective-permute-start | bytes 393224 | tf_op jit(solution)/shard_map/ppermute | solution.py:223
  61.7 5.4 %shard_map.72 = (bf16[256,128]{1,0:T(8,128)(2,1)S(1)}, bf16[256,128]{1,0:T(8,128)(2,1)S(1)}, bf16[256,128]{1,0:T(8,128)(2,1)S(1)}, bf16[256,128]{1,0:T(8,128)(2,1)S(1)}) custom-call(bf16[768,128]{1,0:T(8,128)(2,1)S(1)} %shard_map.71.refs_0_.refs_1_, bf16[768,128]{1,0:T(8,128)(2,1)S(1)} %shard_map.71.refs_0_.refs_1_, ...), custom_call_target="tpu_custom_call" | custom-call | flops 2147483648 | bytes 4587520 | tf_op jit(solution)/shard_map/pallas_call | solution.py:40
  67.2 0.8 collective-permute-done.18.refs_2_.refs_3_
  68.9 5.6 %shard_map.74 = (bf16[256,128]{1,0:T(8,128)(2,1)S(1)}, bf16[256,128]{1,0:T(8,128)(2,1)S(1)}, bf16[256,128]{1,0:T(8,128)(2,1)S(1)}, bf16[256,128]{1,0:T(8,128)(2,1)S(1)}) custom-call(bf16[3072,128]{1,0:T(8,128)(2,1)S(1)} %shard_map.73.refs_0_, bf16[768,128]{1,0:T(8,128)(2,1)S(1)} %shard_map.71.refs_0_.refs_1_, ...), custom_call_target="tpu_custom_call" | custom-call | flops 2147483648 | bytes 4390912 | tf_op jit(solution)/shard_map/pallas_call | solution.py:40
  74.5 2.1 %collective-permute-start.23 = (bf16[512,128]{1,0:T(8,128)(2,1)S(1)}, bf16[512,128]{1,0:T(8,128)(2,1)S(1)}, u32[]{:S(2)}, u32[]{:S(2)}) collective-permute-start(bf16[512,128]{1,0:T(8,128)(2,1)S(1)} %get-tuple-element.67), channel_id=1, source_target_pairs={{0,1},{1,0},{2,3},{3,2},{4,6},{5,7},{6,4},{7,5},{8,9},{9,8},{10,11... | collective-permute-start | bytes 393224 | tf_op jit(solution)/shard_map/ppermute | solution.py:223
  77.3 1.7 %collective-permute-start.25 = (bf16[512,128]{1,0:T(8,128)(2,1)S(1)}, bf16[512,128]{1,0:T(8,128)(2,1)S(1)}, u32[]{:S(2)}, u32[]{:S(2)}) collective-permute-start(bf16[512,128]{1,0:T(8,128)(2,1)S(1)} %get-tuple-element.69), channel_id=1, source_target_pairs={{0,3},{1,2},{2,1},{3,0},{4,7},{5,6},{6,5},{7,4},{8,11},{9,10},{10,... | collective-permute-start | bytes 393224 | tf_op jit(solution)/shard_map/ppermute | solution.py:223
  79.0 1.1 %collective-permute-done.22.refs_10_ = bf16[3072,128]{1,0:T(8,128)(2,1)S(1)} collective-permute-done((bf16[3072,128]{1,0:T(8,128)(2,1)S(1)}, bf16[3072,128]{1,0:T(8,128)(2,1)S(1)}, u32[]{:S(2)}, u32[]{:S(2)}) %collective-permute-start.22) | collective-permute-done | bytes 786464 | tf_op jit(solution)/shard_map/ppermute | solution.py:223
  80.1 5.4 %shard_map.76 = (bf16[256,128]{1,0:T(8,128)(2,1)S(1)}, bf16[256,128]{1,0:T(8,128)(2,1)S(1)}, bf16[256,128]{1,0:T(8,128)(2,1)S(1)}, bf16[256,128]{1,0:T(8,128)(2,1)S(1)}) custom-call(bf16[512,128]{1,0:T(8,128)(2,1)S(1)} %get-tuple-element.65.refs_0_.refs_1_, bf16[768,128]{1,0:T(8,128)(2,1)S(1)} %shard_map.71.refs_0_.refs_1_, ...), custom_call_target="tpu_custom_call" | custom-call | flops 2147483648 | bytes 4390912 | tf_op jit(solution)/shard_map/pallas_call | solution.py:40
  85.5 2.0 %collective-permute-start.26 = (bf16[256,128]{1,0:T(8,128)(2,1)S(1)}, bf16[256,128]{1,0:T(8,128)(2,1)S(1)}, u32[]{:S(2)}, u32[]{:S(2)}) collective-permute-start(bf16[256,128]{1,0:T(8,128)(2,1)S(1)} %get-tuple-element.71), channel_id=1, source_target_pairs={{0,1},{1,0},{2,3},{3,2},{4,6},{5,7},{6,4},{7,5},{8,9},{9,8},{10,11... | collective-permute-start | bytes 196616 | tf_op jit(solution)/shard_map/ppermute | solution.py:223
  88.1 1.9 %collective-permute-start.28 = (bf16[256,128]{1,0:T(8,128)(2,1)S(1)}, bf16[256,128]{1,0:T(8,128)(2,1)S(1)}, u32[]{:S(2)}, u32[]{:S(2)}) collective-permute-start(bf16[256,128]{1,0:T(8,128)(2,1)S(1)} %get-tuple-element.73), channel_id=1, source_target_pairs={{0,3},{1,2},{2,1},{3,0},{4,7},{5,6},{6,5},{7,4},{8,11},{9,10},{10,... | collective-permute-start | bytes 196616 | tf_op jit(solution)/shard_map/ppermute | solution.py:223
  90.3 4.1 %collective-permute-done.27.refs_3_ = bf16[256,128]{1,0:T(8,128)(2,1)S(1)} collective-permute-done((bf16[256,128]{1,0:T(8,128)(2,1)S(1)}, bf16[256,128]{1,0:T(8,128)(2,1)S(1)}, u32[]{:S(2)}, u32[]{:S(2)}) %collective-permute-start.27) | collective-permute-done | bytes 65568 | tf_op jit(solution)/shard_map/ppermute | solution.py:223
  94.5 1.3 %collective-permute-done.30.refs_4_ = bf16[512,128]{1,0:T(8,128)(2,1)S(1)} collective-permute-done((bf16[512,128]{1,0:T(8,128)(2,1)S(1)}, bf16[512,128]{1,0:T(8,128)(2,1)S(1)}, u32[]{:S(2)}, u32[]{:S(2)}) %collective-permute-start.30) | collective-permute-done | bytes 131104 | tf_op jit(solution)/shard_map/ppermute | solution.py:223
  95.8 1.1 %shard_map.80 = bf16[128,3072]{1,0:T(8,128)(2,1)} custom-call(bf16[512,128]{1,0:T(8,128)(2,1)S(1)} %get-tuple-element.74.refs_0_.refs_3_, bf16[1024,128]{1,0:T(8,128)(2,1)S(1)} %get-tuple-element.70.refs_0_.refs_1_, bf16[1024,128]{1,0:T(8,128)(2,1)S(1)} %collective-permute-done.29.refs_2_, bf16[512,128]{1,0:T(8,128)(2,1)S(1)} %get-tuple-element.74.refs_0_.refs_3_, ...), custom_call_target="tpu_custom_call" | custom-call | bytes 1572864 | tf_op jit(solution)/shard_map/pallas_call | solution.py:40
  (66 shorter events, 9.4 us)
Async XLA Ops:
  0.0 2.4 %copy-start = (bf16[128,3072]{1,0:T(8,128)(2,1)S(1)}, bf16[128,3072]{1,0:T(8,128)(2,1)}, u32[]{:S(2)}) copy-start(bf16[128,3072]{1,0:T(8,128)(2,1)} %refs_7_.1) | copy-start | bytes 2359300
  2.5 1.9 %collective-permute-start.1 = (bf16[128,1536]{1,0:T(8,128)(2,1)S(1)}, bf16[128,1536]{1,0:T(8,128)(2,1)S(1)}, u32[]{:S(2)}, u32[]{:S(2)}) collective-permute-start(bf16[128,1536]{1,0:T(8,128)(2,1)S(1)} %shard_map.56.refs_0_), channel_id=1, source_target_pairs={{0,4},{1,5},{2,6},{3,7},{4,0},{5,1},{6,2},{7,3},{8,12},{9,13},{10,... | collective-permute-start | bytes 1179656 | tf_op jit(solution)/shard_map/ppermute | solution.py:223
  3.0 1.9 %collective-permute-start = (bf16[128,1536]{1,0:T(8,128)(2,1)S(1)}, bf16[128,1536]{1,0:T(8,128)(2,1)S(1)}, u32[]{:S(2)}, u32[]{:S(2)}) collective-permute-start(bf16[128,1536]{1,0:T(8,128)(2,1)S(1)} %get-tuple-element.43), channel_id=1, source_target_pairs={{0,4},{1,5},{2,6},{3,7},{4,0},{5,1},{6,2},{7,3},{8,12},{9,13},{10,... | collective-permute-start | bytes 1179656 | tf_op jit(solution)/shard_map/ppermute | solution.py:223
  5.1 17.4 %collective-permute-start.6 = (bf16[1536,128]{1,0:T(8,128)(2,1)S(1)}, bf16[1536,128]{1,0:T(8,128)(2,1)S(1)}, u32[]{:S(2)}, u32[]{:S(2)}) collective-permute-start(bf16[1536,128]{1,0:T(8,128)(2,1)S(1)} %shard_map.59.refs_0_.refs_5_), channel_id=1, source_target_pairs={{0,16},{1,17},{2,18},{3,19},{4,12},{5,13},{6,14},{7,15},{8,24},{9,... | collective-permute-start | bytes 1179656 | tf_op jit(solution)/shard_map/ppermute | solution.py:223
  8.1 14.4 %collective-permute-start.5 = (bf16[1536,128]{1,0:T(8,128)(2,1)S(1)}, bf16[1536,128]{1,0:T(8,128)(2,1)S(1)}, u32[]{:S(2)}, u32[]{:S(2)}) collective-permute-start(bf16[1536,128]{1,0:T(8,128)(2,1)S(1)} %shard_map.59.refs_0_.refs_5_), channel_id=1, source_target_pairs={{0,8},{1,9},{2,10},{3,11},{4,20},{5,21},{6,22},{7,23},{8,0},{9,1},... | collective-permute-start | bytes 1179656 | tf_op jit(solution)/shard_map/ppermute | solution.py:223
  9.5 7.9 %collective-permute-start.2 = (bf16[512,128]{1,0:T(8,128)(2,1)S(1)}, bf16[512,128]{1,0:T(8,128)(2,1)S(1)}, u32[]{:S(2)}, u32[]{:S(2)}) collective-permute-start(bf16[512,128]{1,0:T(8,128)(2,1)S(1)} %get-tuple-element.44.refs_0_), channel_id=1, source_target_pairs={{0,1},{1,0},{2,3},{3,2},{4,6},{5,7},{6,4},{7,5},{8,9},{9,8},{10,11... | collective-permute-start | bytes 393224 | tf_op jit(solution)/shard_map/ppermute | solution.py:223
  11.1 11.3 %collective-permute-start.3 = (bf16[512,128]{1,0:T(8,128)(2,1)S(1)}, bf16[512,128]{1,0:T(8,128)(2,1)S(1)}, u32[]{:S(2)}, u32[]{:S(2)}) collective-permute-start(bf16[512,128]{1,0:T(8,128)(2,1)S(1)} %get-tuple-element.45), channel_id=1, source_target_pairs={{0,2},{1,3},{2,0},{3,1},{4,5},{5,4},{6,7},{7,6},{8,10},{9,11},{10,... | collective-permute-start | bytes 393224 | tf_op jit(solution)/shard_map/ppermute | solution.py:223
  13.7 8.7 %collective-permute-start.4 = (bf16[512,128]{1,0:T(8,128)(2,1)S(1)}, bf16[512,128]{1,0:T(8,128)(2,1)S(1)}, u32[]{:S(2)}, u32[]{:S(2)}) collective-permute-start(bf16[512,128]{1,0:T(8,128)(2,1)S(1)} %get-tuple-element.46), channel_id=1, source_target_pairs={{0,3},{1,2},{2,1},{3,0},{4,7},{5,6},{6,5},{7,4},{8,11},{9,10},{10,... | collective-permute-start | bytes 393224 | tf_op jit(solution)/shard_map/ppermute | solution.py:223
  17.4 11.3 %collective-permute-start.11 = (bf16[128,1536]{1,0:T(8,128)(2,1)S(1)}, bf16[128,1536]{1,0:T(8,128)(2,1)S(1)}, u32[]{:S(2)}, u32[]{:S(2)}) collective-permute-start(bf16[128,1536]{1,0:T(8,128)(2,1)S(1)} %get-tuple-element.50), channel_id=1, source_target_pairs={{0,4},{1,5},{2,6},{3,7},{4,0},{5,1},{6,2},{7,3},{8,12},{9,13},{10,... | collective-permute-start | bytes 1179656 | tf_op jit(solution)/shard_map/ppermute | solution.py:223
  22.6 6.2 %collective-permute-start.7 = (bf16[512,128]{1,0:T(8,128)(2,1)S(1)}, bf16[512,128]{1,0:T(8,128)(2,1)S(1)}, u32[]{:S(2)}, u32[]{:S(2)}) collective-permute-start(bf16[512,128]{1,0:T(8,128)(2,1)S(1)} %get-tuple-element.47.refs_0_), channel_id=1, source_target_pairs={{0,1},{1,0},{2,3},{3,2},{4,6},{5,7},{6,4},{7,5},{8,9},{9,8},{10,11... | collective-permute-start | bytes 393224 | tf_op jit(solution)/shard_map/ppermute | solution.py:223
  24.7 12.1 %collective-permute-start.10 = (bf16[3072,128]{1,0:T(8,128)(2,1)S(1)}, bf16[3072,128]{1,0:T(8,128)(2,1)S(1)}, u32[]{:S(2)}, u32[]{:S(2)}) collective-permute-start(bf16[3072,128]{1,0:T(8,128)(2,1)S(1)} %shard_map.62.refs_0_.refs_1_.refs_6_), channel_id=1, source_target_pairs={{0,8},{1,9},{2,10},{3,11},{4,20},{5,21},{6,22},{7,23},{8,0},{9,1},... | collective-permute-start | bytes 2359304 | tf_op jit(solution)/shard_map/ppermute | solution.py:223
  25.4 11.3 %collective-permute-start.8 = (bf16[512,128]{1,0:T(8,128)(2,1)S(1)}, bf16[512,128]{1,0:T(8,128)(2,1)S(1)}, u32[]{:S(2)}, u32[]{:S(2)}) collective-permute-start(bf16[512,128]{1,0:T(8,128)(2,1)S(1)} %get-tuple-element.48), channel_id=1, source_target_pairs={{0,2},{1,3},{2,0},{3,1},{4,5},{5,4},{6,7},{7,6},{8,10},{9,11},{10,... | collective-permute-start | bytes 393224 | tf_op jit(solution)/shard_map/ppermute | solution.py:223
  27.3 9.4 %collective-permute-start.9 = (bf16[512,128]{1,0:T(8,128)(2,1)S(1)}, bf16[512,128]{1,0:T(8,128)(2,1)S(1)}, u32[]{:S(2)}, u32[]{:S(2)}) collective-permute-start(bf16[512,128]{1,0:T(8,128)(2,1)S(1)} %get-tuple-element.49), channel_id=1, source_target_pairs={{0,3},{1,2},{2,1},{3,0},{4,7},{5,6},{6,5},{7,4},{8,11},{9,10},{10,... | collective-permute-start | bytes 393224 | tf_op jit(solution)/shard_map/ppermute | solution.py:223
  36.9 10.4 %collective-permute-start.12 = (bf16[768,128]{1,0:T(8,128)(2,1)S(1)}, bf16[768,128]{1,0:T(8,128)(2,1)S(1)}, u32[]{:S(2)}, u32[]{:S(2)}) collective-permute-start(bf16[768,128]{1,0:T(8,128)(2,1)S(1)} %get-tuple-element.51.refs_0_), channel_id=1, source_target_pairs={{0,1},{1,0},{2,3},{3,2},{4,6},{5,7},{6,4},{7,5},{8,9},{9,8},{10,11... | collective-permute-start | bytes 589832 | tf_op jit(solution)/shard_map/ppermute | solution.py:223
  38.9 15.9 %collective-permute-start.15 = (bf16[3072,128]{1,0:T(8,128)(2,1)S(1)}, bf16[3072,128]{1,0:T(8,128)(2,1)S(1)}, u32[]{:S(2)}, u32[]{:S(2)}) collective-permute-start(bf16[3072,128]{1,0:T(8,128)(2,1)S(1)} %shard_map.65.refs_0_), channel_id=1, source_target_pairs={{0,16},{1,17},{2,18},{3,19},{4,12},{5,13},{6,14},{7,15},{8,24},{9,... | collective-permute-start | bytes 2359304 | tf_op jit(solution)/shard_map/ppermute | solution.py:223
  39.7 15.2 %collective-permute-start.16 = (bf16[1536,128]{1,0:T(8,128)(2,1)S(1)}, bf16[1536,128]{1,0:T(8,128)(2,1)S(1)}, u32[]{:S(2)}, u32[]{:S(2)}) collective-permute-start(bf16[1536,128]{1,0:T(8,128)(2,1)S(1)} %shard_map.66.refs_0_.refs_1_.refs_6_), channel_id=1, source_target_pairs={{0,8},{1,9},{2,10},{3,11},{4,20},{5,21},{6,22},{7,23},{8,0},{9,1},... | collective-permute-start | bytes 1179656 | tf_op jit(solution)/shard_map/ppermute | solution.py:223
  41.2 13.7 %collective-permute-start.13 = (bf16[768,128]{1,0:T(8,128)(2,1)S(1)}, bf16[768,128]{1,0:T(8,128)(2,1)S(1)}, u32[]{:S(2)}, u32[]{:S(2)}) collective-permute-start(bf16[768,128]{1,0:T(8,128)(2,1)S(1)} %get-tuple-element.52), channel_id=1, source_target_pairs={{0,2},{1,3},{2,0},{3,1},{4,5},{5,4},{6,7},{7,6},{8,10},{9,11},{10,... | collective-permute-start | bytes 589832 | tf_op jit(solution)/shard_map/ppermute | solution.py:223
  42.2 12.6 %collective-permute-start.14 = (bf16[768,128]{1,0:T(8,128)(2,1)S(1)}, bf16[768,128]{1,0:T(8,128)(2,1)S(1)}, u32[]{:S(2)}, u32[]{:S(2)}) collective-permute-start(bf16[768,128]{1,0:T(8,128)(2,1)S(1)} %get-tuple-element.53), channel_id=1, source_target_pairs={{0,3},{1,2},{2,1},{3,0},{4,7},{5,6},{6,5},{7,4},{8,11},{9,10},{10,... | collective-permute-start | bytes 589832 | tf_op jit(solution)/shard_map/ppermute | solution.py:223
  55.1 12.9 %collective-permute-start.20 = (bf16[1536,128]{1,0:T(8,128)(2,1)S(1)}, bf16[1536,128]{1,0:T(8,128)(2,1)S(1)}, u32[]{:S(2)}, u32[]{:S(2)}) collective-permute-start(bf16[1536,128]{1,0:T(8,128)(2,1)S(1)} %shard_map.70.refs_0_.refs_4_.refs_6_), channel_id=1, source_target_pairs={{0,8},{1,9},{2,10},{3,11},{4,20},{5,21},{6,22},{7,23},{8,0},{9,1},... | collective-permute-start | bytes 1179656 | tf_op jit(solution)/shard_map/ppermute | solution.py:223
  55.4 13.5 %collective-permute-start.21 = (bf16[3072,128]{1,0:T(8,128)(2,1)S(1)}, bf16[3072,128]{1,0:T(8,128)(2,1)S(1)}, u32[]{:S(2)}, u32[]{:S(2)}) collective-permute-start(bf16[3072,128]{1,0:T(8,128)(2,1)S(1)} %shard_map.69.refs_0_), channel_id=1, source_target_pairs={{0,16},{1,17},{2,18},{3,19},{4,12},{5,13},{6,14},{7,15},{8,24},{9,... | collective-permute-start | bytes 2359304 | tf_op jit(solution)/shard_map/ppermute | solution.py:223
  56.7 10.5 %collective-permute-start.17 = (bf16[512,128]{1,0:T(8,128)(2,1)S(1)}, bf16[512,128]{1,0:T(8,128)(2,1)S(1)}, u32[]{:S(2)}, u32[]{:S(2)}) collective-permute-start(bf16[512,128]{1,0:T(8,128)(2,1)S(1)} %get-tuple-element.54.refs_0_), channel_id=1, source_target_pairs={{0,1},{1,0},{2,3},{3,2},{4,6},{5,7},{6,4},{7,5},{8,9},{9,8},{10,11... | collective-permute-start | bytes 393224 | tf_op jit(solution)/shard_map/ppermute | solution.py:223
  59.3 8.7 %collective-permute-start.18 = (bf16[512,128]{1,0:T(8,128)(2,1)S(1)}, bf16[512,128]{1,0:T(8,128)(2,1)S(1)}, u32[]{:S(2)}, u32[]{:S(2)}) collective-permute-start(bf16[512,128]{1,0:T(8,128)(2,1)S(1)} %get-tuple-element.56), channel_id=1, source_target_pairs={{0,2},{1,3},{2,0},{3,1},{4,5},{5,4},{6,7},{7,6},{8,10},{9,11},{10,... | collective-permute-start | bytes 393224 | tf_op jit(solution)/shard_map/ppermute | solution.py:223
  59.7 8.3 %collective-permute-start.19 = (bf16[512,128]{1,0:T(8,128)(2,1)S(1)}, bf16[512,128]{1,0:T(8,128)(2,1)S(1)}, u32[]{:S(2)}, u32[]{:S(2)}) collective-permute-start(bf16[512,128]{1,0:T(8,128)(2,1)S(1)} %get-tuple-element.57), channel_id=1, source_target_pairs={{0,3},{1,2},{2,1},{3,0},{4,7},{5,6},{6,5},{7,4},{8,11},{9,10},{10,... | collective-permute-start | bytes 393224 | tf_op jit(solution)/shard_map/ppermute | solution.py:223
  68.1 12.1 %collective-permute-start.22 = (bf16[3072,128]{1,0:T(8,128)(2,1)S(1)}, bf16[3072,128]{1,0:T(8,128)(2,1)S(1)}, u32[]{:S(2)}, u32[]{:S(2)}) collective-permute-start(bf16[3072,128]{1,0:T(8,128)(2,1)S(1)} %shard_map.73.refs_0_), channel_id=1, source_target_pairs={{0,16},{1,17},{2,18},{3,19},{4,12},{5,13},{6,14},{7,15},{8,24},{9,... | collective-permute-start | bytes 2359304 | tf_op jit(solution)/shard_map/ppermute | solution.py:223
  74.5 13.6 %collective-permute-start.23 = (bf16[512,128]{1,0:T(8,128)(2,1)S(1)}, bf16[512,128]{1,0:T(8,128)(2,1)S(1)}, u32[]{:S(2)}, u32[]{:S(2)}) collective-permute-start(bf16[512,128]{1,0:T(8,128)(2,1)S(1)} %get-tuple-element.67), channel_id=1, source_target_pairs={{0,1},{1,0},{2,3},{3,2},{4,6},{5,7},{6,4},{7,5},{8,9},{9,8},{10,11... | collective-permute-start | bytes 393224 | tf_op jit(solution)/shard_map/ppermute | solution.py:223
  76.6 13.4 %collective-permute-start.24 = (bf16[512,128]{1,0:T(8,128)(2,1)S(1)}, bf16[512,128]{1,0:T(8,128)(2,1)S(1)}, u32[]{:S(2)}, u32[]{:S(2)}) collective-permute-start(bf16[512,128]{1,0:T(8,128)(2,1)S(1)} %get-tuple-element.68), channel_id=1, source_target_pairs={{0,2},{1,3},{2,0},{3,1},{4,5},{5,4},{6,7},{7,6},{8,10},{9,11},{10,... | collective-permute-start | bytes 393224 | tf_op jit(solution)/shard_map/ppermute | solution.py:223
  77.3 12.7 %collective-permute-start.25 = (bf16[512,128]{1,0:T(8,128)(2,1)S(1)}, bf16[512,128]{1,0:T(8,128)(2,1)S(1)}, u32[]{:S(2)}, u32[]{:S(2)}) collective-permute-start(bf16[512,128]{1,0:T(8,128)(2,1)S(1)} %get-tuple-element.69), channel_id=1, source_target_pairs={{0,3},{1,2},{2,1},{3,0},{4,7},{5,6},{6,5},{7,4},{8,11},{9,10},{10,... | collective-permute-start | bytes 393224 | tf_op jit(solution)/shard_map/ppermute | solution.py:223
  85.5 4.8 %collective-permute-start.26 = (bf16[256,128]{1,0:T(8,128)(2,1)S(1)}, bf16[256,128]{1,0:T(8,128)(2,1)S(1)}, u32[]{:S(2)}, u32[]{:S(2)}) collective-permute-start(bf16[256,128]{1,0:T(8,128)(2,1)S(1)} %get-tuple-element.71), channel_id=1, source_target_pairs={{0,1},{1,0},{2,3},{3,2},{4,6},{5,7},{6,4},{7,5},{8,9},{9,8},{10,11... | collective-permute-start | bytes 196616 | tf_op jit(solution)/shard_map/ppermute | solution.py:223
  87.5 6.8 %collective-permute-start.27 = (bf16[256,128]{1,0:T(8,128)(2,1)S(1)}, bf16[256,128]{1,0:T(8,128)(2,1)S(1)}, u32[]{:S(2)}, u32[]{:S(2)}) collective-permute-start(bf16[256,128]{1,0:T(8,128)(2,1)S(1)} %get-tuple-element.72), channel_id=1, source_target_pairs={{0,2},{1,3},{2,0},{3,1},{4,5},{5,4},{6,7},{7,6},{8,10},{9,11},{10,... | collective-permute-start | bytes 196616 | tf_op jit(solution)/shard_map/ppermute | solution.py:223
  88.1 6.2 %collective-permute-start.28 = (bf16[256,128]{1,0:T(8,128)(2,1)S(1)}, bf16[256,128]{1,0:T(8,128)(2,1)S(1)}, u32[]{:S(2)}, u32[]{:S(2)}) collective-permute-start(bf16[256,128]{1,0:T(8,128)(2,1)S(1)} %get-tuple-element.73), channel_id=1, source_target_pairs={{0,3},{1,2},{2,1},{3,0},{4,7},{5,6},{6,5},{7,4},{8,11},{9,10},{10,... | collective-permute-start | bytes 196616 | tf_op jit(solution)/shard_map/ppermute | solution.py:223
  90.0 5.8 %collective-permute-start.29 = (bf16[1024,128]{1,0:T(8,128)(2,1)S(1)}, bf16[1024,128]{1,0:T(8,128)(2,1)S(1)}, u32[]{:S(2)}, u32[]{:S(2)}) collective-permute-start(bf16[1024,128]{1,0:T(8,128)(2,1)S(1)} %get-tuple-element.75), channel_id=1, source_target_pairs={{0,4},{1,5},{2,6},{3,7},{4,0},{5,1},{6,2},{7,3},{8,12},{9,13},{10,... | collective-permute-start | bytes 786440 | tf_op jit(solution)/shard_map/ppermute | solution.py:223
  94.4 1.4 %collective-permute-start.30 = (bf16[512,128]{1,0:T(8,128)(2,1)S(1)}, bf16[512,128]{1,0:T(8,128)(2,1)S(1)}, u32[]{:S(2)}, u32[]{:S(2)}) collective-permute-start(bf16[512,128]{1,0:T(8,128)(2,1)S(1)} %get-tuple-element.76), channel_id=1, source_target_pairs={{0,4},{1,5},{2,6},{3,7},{4,0},{5,1},{6,2},{7,3},{8,12},{9,13},{10,... | collective-permute-start | bytes 393224 | tf_op jit(solution)/shard_map/ppermute | solution.py:223
  (4 other events, 4.2 us)

commit v6 on v5

--- a/solution.py
+++ b/solution.py
@@ -49,6 +49,27 @@
         self.last = made[:1]
         return made
 
+    def place(self, body, outs, *args, onto=None):
+        behind = self.last if onto is None else (onto,)
+        tokens = outs[0].shape[0]
+
+        def without_last(*refs):
+            body(*refs[len(behind) :])
+
+        made = pl.pallas_call(
+            without_last,
+            out_shape=outs,
+            in_specs=[pl.BlockSpec(memory_space=pl.ANY)] * len(behind) + [VMEM] * len(args),
+            out_specs=[pl.BlockSpec(memory_space=pl.ANY)],
+            scratch_shapes=[
+                pltpu.SemaphoreType.DMA((sum(a.shape[0] for a in args) // tokens,))
+            ],
+            input_output_aliases={} if onto is None else {0: 0},
+            compiler_params=PARAMS,
+        )(*behind, *args)
+        self.last = made[:1]
+        return made
+
     def mark(self):
         self.call(nothing_body, [sds(16, HEAD_DIM)], flops=2 * 10**10)
 
@@ -58,34 +79,48 @@
     return parts[0] if len(parts) == 1 else jnp.concatenate(parts, axis=0)
 
 
-def absorb(state, q, k, v):
-    scores = lax.dot_general(q, k, (((1,), (1,)), ((), ())), preferred_element_type=F32)
+def scores_of(q, k):
+    return lax.dot_general(q, k, (((1,), (1,)), ((), ())), preferred_element_type=F32)
+
+
+def absorb(state, scores, v):
     new_top = jnp.max(scores, axis=1, keepdims=True)
     if state is not None:
-        top, total, accum = state
+        top, accum = state
         new_top = jnp.maximum(top, new_top)
     weights = jnp.exp2((scores - new_top) * EXPONENT)
-    part = jnp.sum(weights, axis=1, keepdims=True)
-    mixed = jnp.dot(weights.astype(BF16), v, preferred_element_type=F32)
+    both = jnp.concatenate([v, jnp.ones_like(v)], axis=1)
+    mixed = jnp.dot(weights.astype(BF16), both, preferred_element_type=F32)
     if state is not None:
-        shrink = jnp.exp2((top - new_top) * EXPONENT)
-        part, mixed = total * shrink + part, accum * shrink + mixed
-    return new_top, part, mixed
+        mixed = accum * jnp.exp2((top - new_top) * EXPONENT) + mixed
+    return new_top, mixed
 
 
 def attend_body(queries, blocks, count, *refs):
     refs, outs = refs[:count], refs[count:]
-    for pair in range(0, len(queries), 2):
-        q = read(refs, queries[pair : pair + 2])
-        state = None
-        for keys, values in blocks:
-            state = absorb(state, q, read(refs, keys), read(refs, values))
-        _, total, accum = state
-        result = (accum / total).astype(BF16)
-        first = pair // 2 * q.shape[0]
+    steps = [(pair, block) for pair in range(0, len(queries), 2) for block in blocks]
+
+    def scores_at(step):
+        pair, (keys, _) = steps[step]
+        return scores_of(read(refs, queries[pair : pair + 2]), read(refs, keys))
+
+    ahead = scores_at(0)
+    state = None
+    for step, (pair, (keys, values)) in enumerate(steps):
+        scores = ahead
+        if step + 1 < len(steps):
+            ahead = scores_at(step + 1)
+        if keys is blocks[0][0]:
+            state = None
+        state = absorb(state, scores, read(refs, values))
+        if keys is not blocks[-1][0]:
+            continue
+        accum = state[1]
+        result = (accum[:, :HEAD_DIM] / accum[:, HEAD_DIM:]).astype(BF16)
+        first = pair // 2 * result.shape[0]
         at = 0
         for out in outs:
-            low, high = max(at, first), min(at + out.shape[0], first + q.shape[0])
+            low, high = max(at, first), min(at + out.shape[0], first + result.shape[0])
             if low < high:
                 out[low - at : high - at, :] = result[low - first : high - first, :]
             at += out.shape[0]
@@ -194,20 +229,23 @@
     )
 
 
-def place_body(*refs):
-    out = refs[-1]
+def place_body(parts, *refs):
+    out, sems = refs[-2:]
     tokens, half = out.shape[0], out.shape[1] // 2
-    core = core_index()
-    place = 0
-    for own, across in zip(refs[:-1:2], refs[1:-1:2]):
-        for at in range(0, own.shape[0], tokens):
-            start = column(place // 4, place % 4)
-            here = pl.multiple_of(core * half + start, HEAD_DIM)
-            there = pl.multiple_of((1 - core) * half + start, HEAD_DIM)
-            rows = slice(at, at + tokens)
-            out[:, pl.ds(here, HEAD_DIM)] = own[rows, :]
-            out[:, pl.ds(there, HEAD_DIM)] = across[rows, :]
-            place += 1
+    copies = []
+    for ref, (chunk, across) in zip(refs, parts):
+        core = 1 - core_index() if across else core_index()
+        for place in range(ref.shape[0] // tokens):
+            start = core * half + column(chunk + place // 4, place % 4)
+            columns = pl.ds(pl.multiple_of(start, HEAD_DIM), HEAD_DIM)
+            rows = pl.ds(place * tokens, tokens)
+            copies.append(
+                pltpu.make_async_copy(ref.at[rows], out.at[:, columns], sems.at[len(copies)])
+            )
+    for copy in copies:
+        copy.start()
+    for copy in copies:
+        copy.wait()
 
 
 def permute(array, move):
@@ -331,10 +369,15 @@
     back01 = send_back(join(line, [[(x, 0, part), (y, 0, part)] for x, y in zip(out0, out1)]))
     out2 = attend(line, list(queries_of(2, swap3, part).values()), blocks_of(2, gathered2), outs)
     back2 = send_back(out2)
-    results = core_swap(back01, 2)
+    own01, across01 = core_swap(back01, 2)
     line.mark()
-    results += core_swap(back2, 1)
-    (attended,) = line.call(place_body, [sds(tokens, width)], *results)
+    own2, across2 = core_swap(back2, 1)
+    shape = [sds(tokens, width)]
+    early = [(0, False), (0, True), (2, False)]
+    (attended,) = line.place(functools.partial(place_body, early), shape, own01, across01, own2)
+    (attended,) = line.place(
+        functools.partial(place_body, [(2, True)]), shape, across2, onto=attended
+    )
     return attended
 
 

time: 97.1 us -> 96.5 us (level)
    pallas_call x26 -> x25, Pallas kernels: 19.4 us -> 17.1 us  [call(): pl.pallas_call(without_last, out_shape=outs, in_specs=[pl.BlockSpec(memor...]
    pallas_call x0 -> x2, Pallas kernels: none -> 1.69 us  [place(): pl.pallas_call(without_last, out_shape=outs, in_specs=[pl.BlockSpec(memor...]
where the time goes in v6:
time: 96.5 us; the launch traced here: 96.3 us
  starting transfers between devices  38.7 us (40%)
  waiting for transfers between devices  36 us (37%)
  Pallas kernels  18.8 us (19%)
  local copies, waits for them, and re-layouts  2.39 us (2%)
    ppermute x31, starting transfers between devices, permute(): return lax.ppermute(array, AXES, pairs)  38.7 us
    ppermute x31, waiting for transfers between devices, permute(): return lax.ppermute(array, AXES, pairs)  36 us
    pallas_call x25, Pallas kernels, call(): pl.pallas_call(without_last, out_shape=outs, in_specs=[pl.BlockSpec(memor...  17.1 us
    unnamed x10, local copies, waits for them, and re-layouts  2.39 us
  transfers between devices with their start and end apart: 31, of which 13 were waited for; matrix products, arithmetic and copies ran while one was open for 0% of the time, Pallas kernels for 18%

profile of v6, /device:TPU:0, one launch (start us, length us, event | category | flops | bytes accessed | tf_op | source)
XLA Modules:
  0.0 96.3 jit_solution(16053411147042034809)
XLA Ops:
  0.0 1.2 %copy-done.1 = bf16[128,3072]{1,0:T(8,128)(2,1)S(1)} copy-done((bf16[128,3072]{1,0:T(8,128)(2,1)S(1)}, bf16[128,3072]{1,0:T(8,128)(2,1)}, u32[]{:S(2)}) %copy-start.1) | copy-done | bytes 786456
  5.1 3.0 %collective-permute-start.6 = (bf16[1536,128]{1,0:T(8,128)(2,1)S(1)}, bf16[1536,128]{1,0:T(8,128)(2,1)S(1)}, u32[]{:S(2)}, u32[]{:S(2)}) collective-permute-start(bf16[1536,128]{1,0:T(8,128)(2,1)S(1)} %shard_map.59.refs_0_.refs_5_), channel_id=1, source_target_pairs={{0,16},{1,17},{2,18},{3,19},{4,12},{5,13},{6,14},{7,15},{8,24},{9,... | collective-permute-start | bytes 1179656 | tf_op jit(solution)/shard_map/ppermute | solution.py:261
  8.1 1.5 %collective-permute-start.5 = (bf16[1536,128]{1,0:T(8,128)(2,1)S(1)}, bf16[1536,128]{1,0:T(8,128)(2,1)S(1)}, u32[]{:S(2)}, u32[]{:S(2)}) collective-permute-start(bf16[1536,128]{1,0:T(8,128)(2,1)S(1)} %shard_map.59.refs_0_.refs_5_), channel_id=1, source_target_pairs={{0,8},{1,9},{2,10},{3,11},{4,20},{5,21},{6,22},{7,23},{8,0},{9,1},... | collective-permute-start | bytes 1179656 | tf_op jit(solution)/shard_map/ppermute | solution.py:261
  9.5 1.6 %collective-permute-start.2 = (bf16[512,128]{1,0:T(8,128)(2,1)S(1)}, bf16[512,128]{1,0:T(8,128)(2,1)S(1)}, u32[]{:S(2)}, u32[]{:S(2)}) collective-permute-start(bf16[512,128]{1,0:T(8,128)(2,1)S(1)} %get-tuple-element.44.refs_0_), channel_id=1, source_target_pairs={{0,1},{1,0},{2,3},{3,2},{4,6},{5,7},{6,4},{7,5},{8,9},{9,8},{10,11... | collective-permute-start | bytes 393224 | tf_op jit(solution)/shard_map/ppermute | solution.py:261
  11.1 2.6 %collective-permute-start.3 = (bf16[512,128]{1,0:T(8,128)(2,1)S(1)}, bf16[512,128]{1,0:T(8,128)(2,1)S(1)}, u32[]{:S(2)}, u32[]{:S(2)}) collective-permute-start(bf16[512,128]{1,0:T(8,128)(2,1)S(1)} %get-tuple-element.45), channel_id=1, source_target_pairs={{0,2},{1,3},{2,0},{3,1},{4,5},{5,4},{6,7},{7,6},{8,10},{9,11},{10,... | collective-permute-start | bytes 393224 | tf_op jit(solution)/shard_map/ppermute | solution.py:261
  13.9 3.5 %collective-permute-done.2.refs_1_.refs_2_ = bf16[512,128]{1,0:T(8,128)(2,1)S(1)} collective-permute-done((bf16[512,128]{1,0:T(8,128)(2,1)S(1)}, bf16[512,128]{1,0:T(8,128)(2,1)S(1)}, u32[]{:S(2)}, u32[]{:S(2)}) %collective-permute-start.2) | collective-permute-done | bytes 131104 | tf_op jit(solution)/shard_map/ppermute | solution.py:261
  17.4 5.0 %collective-permute-done.3.refs_2_.refs_3_ = bf16[512,128]{1,0:T(8,128)(2,1)S(1)} collective-permute-done((bf16[512,128]{1,0:T(8,128)(2,1)S(1)}, bf16[512,128]{1,0:T(8,128)(2,1)S(1)}, u32[]{:S(2)}, u32[]{:S(2)}) %collective-permute-start.3) | collective-permute-done | bytes 131104 | tf_op jit(solution)/shard_map/ppermute | solution.py:261
  22.6 2.1 %collective-permute-start.7 = (bf16[512,128]{1,0:T(8,128)(2,1)S(1)}, bf16[512,128]{1,0:T(8,128)(2,1)S(1)}, u32[]{:S(2)}, u32[]{:S(2)}) collective-permute-start(bf16[512,128]{1,0:T(8,128)(2,1)S(1)} %get-tuple-element.47.refs_0_), channel_id=1, source_target_pairs={{0,1},{1,0},{2,3},{3,2},{4,6},{5,7},{6,4},{7,5},{8,9},{9,8},{10,11... | collective-permute-start | bytes 393224 | tf_op jit(solution)/shard_map/ppermute | solution.py:261
  25.4 1.9 %collective-permute-start.8 = (bf16[512,128]{1,0:T(8,128)(2,1)S(1)}, bf16[512,128]{1,0:T(8,128)(2,1)S(1)}, u32[]{:S(2)}, u32[]{:S(2)}) collective-permute-start(bf16[512,128]{1,0:T(8,128)(2,1)S(1)} %get-tuple-element.48), channel_id=1, source_target_pairs={{0,2},{1,3},{2,0},{3,1},{4,5},{5,4},{6,7},{7,6},{8,10},{9,11},{10,... | collective-permute-start | bytes 393224 | tf_op jit(solution)/shard_map/ppermute | solution.py:261
  27.3 1.4 %collective-permute-start.9 = (bf16[512,128]{1,0:T(8,128)(2,1)S(1)}, bf16[512,128]{1,0:T(8,128)(2,1)S(1)}, u32[]{:S(2)}, u32[]{:S(2)}) collective-permute-start(bf16[512,128]{1,0:T(8,128)(2,1)S(1)} %get-tuple-element.49), channel_id=1, source_target_pairs={{0,3},{1,2},{2,1},{3,0},{4,7},{5,6},{6,5},{7,4},{8,11},{9,10},{10,... | collective-permute-start | bytes 393224 | tf_op jit(solution)/shard_map/ppermute | solution.py:261
  28.8 7.9 %collective-permute-done.8.refs_2_ = bf16[512,128]{1,0:T(8,128)(2,1)S(1)} collective-permute-done((bf16[512,128]{1,0:T(8,128)(2,1)S(1)}, bf16[512,128]{1,0:T(8,128)(2,1)S(1)}, u32[]{:S(2)}, u32[]{:S(2)}) %collective-permute-start.8) | collective-permute-done | bytes 131104 | tf_op jit(solution)/shard_map/ppermute | solution.py:261
  36.9 1.9 %collective-permute-start.12 = (bf16[768,128]{1,0:T(8,128)(2,1)S(1)}, bf16[768,128]{1,0:T(8,128)(2,1)S(1)}, u32[]{:S(2)}, u32[]{:S(2)}) collective-permute-start(bf16[768,128]{1,0:T(8,128)(2,1)S(1)} %get-tuple-element.51.refs_0_), channel_id=1, source_target_pairs={{0,1},{1,0},{2,3},{3,2},{4,6},{5,7},{6,4},{7,5},{8,9},{9,8},{10,11... | collective-permute-start | bytes 589832 | tf_op jit(solution)/shard_map/ppermute | solution.py:261
  39.7 1.5 %collective-permute-start.16 = (bf16[1536,128]{1,0:T(8,128)(2,1)S(1)}, bf16[1536,128]{1,0:T(8,128)(2,1)S(1)}, u32[]{:S(2)}, u32[]{:S(2)}) collective-permute-start(bf16[1536,128]{1,0:T(8,128)(2,1)S(1)} %shard_map.66.refs_0_.refs_1_.refs_6_), channel_id=1, source_target_pairs={{0,8},{1,9},{2,10},{3,11},{4,20},{5,21},{6,22},{7,23},{8,0},{9,1},... | collective-permute-start | bytes 1179656 | tf_op jit(solution)/shard_map/ppermute | solution.py:261
  41.2 1.0 %collective-permute-start.13 = (bf16[768,128]{1,0:T(8,128)(2,1)S(1)}, bf16[768,128]{1,0:T(8,128)(2,1)S(1)}, u32[]{:S(2)}, u32[]{:S(2)}) collective-permute-start(bf16[768,128]{1,0:T(8,128)(2,1)S(1)} %get-tuple-element.52), channel_id=1, source_target_pairs={{0,2},{1,3},{2,0},{3,1},{4,5},{5,4},{6,7},{7,6},{8,10},{9,11},{10,... | collective-permute-start | bytes 589832 | tf_op jit(solution)/shard_map/ppermute | solution.py:261
  42.2 1.4 %collective-permute-start.14 = (bf16[768,128]{1,0:T(8,128)(2,1)S(1)}, bf16[768,128]{1,0:T(8,128)(2,1)S(1)}, u32[]{:S(2)}, u32[]{:S(2)}) collective-permute-start(bf16[768,128]{1,0:T(8,128)(2,1)S(1)} %get-tuple-element.53), channel_id=1, source_target_pairs={{0,3},{1,2},{2,1},{3,0},{4,7},{5,6},{6,5},{7,4},{8,11},{9,10},{10,... | collective-permute-start | bytes 589832 | tf_op jit(solution)/shard_map/ppermute | solution.py:261
  43.6 3.7 %collective-permute-done.12.refs_1_.refs_2_ = bf16[768,128]{1,0:T(8,128)(2,1)S(1)} collective-permute-done((bf16[768,128]{1,0:T(8,128)(2,1)S(1)}, bf16[768,128]{1,0:T(8,128)(2,1)S(1)}, u32[]{:S(2)}, u32[]{:S(2)}) %collective-permute-start.12) | collective-permute-done | bytes 196640 | tf_op jit(solution)/shard_map/ppermute | solution.py:261
  47.4 7.5 %collective-permute-done.13.refs_2_.refs_3_ = bf16[768,128]{1,0:T(8,128)(2,1)S(1)} collective-permute-done((bf16[768,128]{1,0:T(8,128)(2,1)S(1)}, bf16[768,128]{1,0:T(8,128)(2,1)S(1)}, u32[]{:S(2)}, u32[]{:S(2)}) %collective-permute-start.13) | collective-permute-done | bytes 196640 | tf_op jit(solution)/shard_map/ppermute | solution.py:261
  55.4 1.3 %collective-permute-start.21 = (bf16[3072,128]{1,0:T(8,128)(2,1)S(1)}, bf16[3072,128]{1,0:T(8,128)(2,1)S(1)}, u32[]{:S(2)}, u32[]{:S(2)}) collective-permute-start(bf16[3072,128]{1,0:T(8,128)(2,1)S(1)} %shard_map.69.refs_0_), channel_id=1, source_target_pairs={{0,16},{1,17},{2,18},{3,19},{4,12},{5,13},{6,14},{7,15},{8,24},{9,... | collective-permute-start | bytes 2359304 | tf_op jit(solution)/shard_map/ppermute | solution.py:261
  56.7 2.6 %collective-permute-start.17 = (bf16[512,128]{1,0:T(8,128)(2,1)S(1)}, bf16[512,128]{1,0:T(8,128)(2,1)S(1)}, u32[]{:S(2)}, u32[]{:S(2)}) collective-permute-start(bf16[512,128]{1,0:T(8,128)(2,1)S(1)} %get-tuple-element.54.refs_0_), channel_id=1, source_target_pairs={{0,1},{1,0},{2,3},{3,2},{4,6},{5,7},{6,4},{7,5},{8,9},{9,8},{10,11... | collective-permute-start | bytes 393224 | tf_op jit(solution)/shard_map/ppermute | solution.py:261
  59.7 1.9 %collective-permute-start.19 = (bf16[512,128]{1,0:T(8,128)(2,1)S(1)}, bf16[512,128]{1,0:T(8,128)(2,1)S(1)}, u32[]{:S(2)}, u32[]{:S(2)}) collective-permute-start(bf16[512,128]{1,0:T(8,128)(2,1)S(1)} %get-tuple-element.57), channel_id=1, source_target_pairs={{0,3},{1,2},{2,1},{3,0},{4,7},{5,6},{6,5},{7,4},{8,11},{9,10},{10,... | collective-permute-start | bytes 393224 | tf_op jit(solution)/shard_map/ppermute | solution.py:261
  61.7 5.0 %shard_map.72 = (bf16[256,128]{1,0:T(8,128)(2,1)S(1)}, bf16[256,128]{1,0:T(8,128)(2,1)S(1)}, bf16[256,128]{1,0:T(8,128)(2,1)S(1)}, bf16[256,128]{1,0:T(8,128)(2,1)S(1)}) custom-call(bf16[768,128]{1,0:T(8,128)(2,1)S(1)} %shard_map.71.refs_0_.refs_1_, bf16[768,128]{1,0:T(8,128)(2,1)S(1)} %shard_map.71.refs_0_.refs_1_, ...), custom_call_target="tpu_custom_call" | custom-call | flops 2147483648 | bytes 4587520 | tf_op jit(solution)/shard_map/pallas_call | solution.py:40
  66.8 1.2 %collective-permute-done.18.refs_2_.refs_3_ = bf16[512,128]{1,0:T(8,128)(2,1)S(1)} collective-permute-done((bf16[512,128]{1,0:T(8,128)(2,1)S(1)}, bf16[512,128]{1,0:T(8,128)(2,1)S(1)}, u32[]{:S(2)}, u32[]{:S(2)}) %collective-permute-start.18) | collective-permute-done | bytes 131104 | tf_op jit(solution)/shard_map/ppermute | solution.py:261
  68.9 5.2 %shard_map.74 = (bf16[256,128]{1,0:T(8,128)(2,1)S(1)}, bf16[256,128]{1,0:T(8,128)(2,1)S(1)}, bf16[256,128]{1,0:T(8,128)(2,1)S(1)}, bf16[256,128]{1,0:T(8,128)(2,1)S(1)}) custom-call(bf16[3072,128]{1,0:T(8,128)(2,1)S(1)} %shard_map.73.refs_0_, bf16[768,128]{1,0:T(8,128)(2,1)S(1)} %shard_map.71.refs_0_.refs_1_, ...), custom_call_target="tpu_custom_call" | custom-call | flops 2147483648 | bytes 4390912 | tf_op jit(solution)/shard_map/pallas_call | solution.py:40
  74.1 2.1 %collective-permute-start.23 = (bf16[512,128]{1,0:T(8,128)(2,1)S(1)}, bf16[512,128]{1,0:T(8,128)(2,1)S(1)}, u32[]{:S(2)}, u32[]{:S(2)}) collective-permute-start(bf16[512,128]{1,0:T(8,128)(2,1)S(1)} %get-tuple-element.67), channel_id=1, source_target_pairs={{0,1},{1,0},{2,3},{3,2},{4,6},{5,7},{6,4},{7,5},{8,9},{9,8},{10,11... | collective-permute-start | bytes 393224 | tf_op jit(solution)/shard_map/ppermute | solution.py:261
  76.9 1.7 %collective-permute-start.25 = (bf16[512,128]{1,0:T(8,128)(2,1)S(1)}, bf16[512,128]{1,0:T(8,128)(2,1)S(1)}, u32[]{:S(2)}, u32[]{:S(2)}) collective-permute-start(bf16[512,128]{1,0:T(8,128)(2,1)S(1)} %get-tuple-element.69), channel_id=1, source_target_pairs={{0,3},{1,2},{2,1},{3,0},{4,7},{5,6},{6,5},{7,4},{8,11},{9,10},{10,... | collective-permute-start | bytes 393224 | tf_op jit(solution)/shard_map/ppermute | solution.py:261
  78.6 1.5 %collective-permute-done.22.refs_10_ = bf16[3072,128]{1,0:T(8,128)(2,1)S(1)} collective-permute-done((bf16[3072,128]{1,0:T(8,128)(2,1)S(1)}, bf16[3072,128]{1,0:T(8,128)(2,1)S(1)}, u32[]{:S(2)}, u32[]{:S(2)}) %collective-permute-start.22) | collective-permute-done | bytes 786464 | tf_op jit(solution)/shard_map/ppermute | solution.py:261
  80.1 5.0 %shard_map.76 = (bf16[256,128]{1,0:T(8,128)(2,1)S(1)}, bf16[256,128]{1,0:T(8,128)(2,1)S(1)}, bf16[256,128]{1,0:T(8,128)(2,1)S(1)}, bf16[256,128]{1,0:T(8,128)(2,1)S(1)}) custom-call(bf16[512,128]{1,0:T(8,128)(2,1)S(1)} %get-tuple-element.65.refs_0_.refs_1_, bf16[768,128]{1,0:T(8,128)(2,1)S(1)} %shard_map.71.refs_0_.refs_1_, ...), custom_call_target="tpu_custom_call" | custom-call | flops 2147483648 | bytes 4390912 | tf_op jit(solution)/shard_map/pallas_call | solution.py:40
  85.1 2.0 %collective-permute-start.26 = (bf16[256,128]{1,0:T(8,128)(2,1)S(1)}, bf16[256,128]{1,0:T(8,128)(2,1)S(1)}, u32[]{:S(2)}, u32[]{:S(2)}) collective-permute-start(bf16[256,128]{1,0:T(8,128)(2,1)S(1)} %get-tuple-element.71), channel_id=1, source_target_pairs={{0,1},{1,0},{2,3},{3,2},{4,6},{5,7},{6,4},{7,5},{8,9},{9,8},{10,11... | collective-permute-start | bytes 196616 | tf_op jit(solution)/shard_map/ppermute | solution.py:261
  87.7 1.9 %collective-permute-start.28 = (bf16[256,128]{1,0:T(8,128)(2,1)S(1)}, bf16[256,128]{1,0:T(8,128)(2,1)S(1)}, u32[]{:S(2)}, u32[]{:S(2)}) collective-permute-start(bf16[256,128]{1,0:T(8,128)(2,1)S(1)} %get-tuple-element.73), channel_id=1, source_target_pairs={{0,3},{1,2},{2,1},{3,0},{4,7},{5,6},{6,5},{7,4},{8,11},{9,10},{10,... | collective-permute-start | bytes 196616 | tf_op jit(solution)/shard_map/ppermute | solution.py:261
  89.7 0.9 collective-permute-done.26.refs_2_
  90.6 3.4 %collective-permute-done.27.refs_3_ = bf16[256,128]{1,0:T(8,128)(2,1)S(1)} collective-permute-done((bf16[256,128]{1,0:T(8,128)(2,1)S(1)}, bf16[256,128]{1,0:T(8,128)(2,1)S(1)}, u32[]{:S(2)}, u32[]{:S(2)}) %collective-permute-start.27) | collective-permute-done | bytes 65568 | tf_op jit(solution)/shard_map/ppermute | solution.py:261
  94.1 1.0 %shard_map.80.refs_0_ = bf16[128,3072]{1,0:T(8,128)(2,1)} custom-call(bf16[512,128]{1,0:T(8,128)(2,1)S(1)} %get-tuple-element.74.refs_0_.refs_3_, bf16[1024,128]{1,0:T(8,128)(2,1)S(1)} %get-tuple-element.70.refs_0_.refs_1_, bf16[1024,128]{1,0:T(8,128)(2,1)S(1)} %collective-permute-done.29.refs_2_, bf16[512,128]{1,0:T(8,128)(2,1)S(1)} %get-tuple-element.74.refs_0_.refs_3_), custom_call_target="tpu_custom_call" | custom-call | tf_op jit(solution)/shard_map/pallas_call | solution.py:59
  (67 shorter events, 10.2 us)
Async XLA Ops:
  0.0 2.4 %copy-start = (bf16[128,3072]{1,0:T(8,128)(2,1)S(1)}, bf16[128,3072]{1,0:T(8,128)(2,1)}, u32[]{:S(2)}) copy-start(bf16[128,3072]{1,0:T(8,128)(2,1)} %refs_7_.1) | copy-start | bytes 2359300
  2.5 1.9 %collective-permute-start.1 = (bf16[128,1536]{1,0:T(8,128)(2,1)S(1)}, bf16[128,1536]{1,0:T(8,128)(2,1)S(1)}, u32[]{:S(2)}, u32[]{:S(2)}) collective-permute-start(bf16[128,1536]{1,0:T(8,128)(2,1)S(1)} %shard_map.56.refs_0_), channel_id=1, source_target_pairs={{0,4},{1,5},{2,6},{3,7},{4,0},{5,1},{6,2},{7,3},{8,12},{9,13},{10,... | collective-permute-start | bytes 1179656 | tf_op jit(solution)/shard_map/ppermute | solution.py:261
  3.0 1.9 %collective-permute-start = (bf16[128,1536]{1,0:T(8,128)(2,1)S(1)}, bf16[128,1536]{1,0:T(8,128)(2,1)S(1)}, u32[]{:S(2)}, u32[]{:S(2)}) collective-permute-start(bf16[128,1536]{1,0:T(8,128)(2,1)S(1)} %get-tuple-element.43), channel_id=1, source_target_pairs={{0,4},{1,5},{2,6},{3,7},{4,0},{5,1},{6,2},{7,3},{8,12},{9,13},{10,... | collective-permute-start | bytes 1179656 | tf_op jit(solution)/shard_map/ppermute | solution.py:261
  5.1 17.4 %collective-permute-start.6 = (bf16[1536,128]{1,0:T(8,128)(2,1)S(1)}, bf16[1536,128]{1,0:T(8,128)(2,1)S(1)}, u32[]{:S(2)}, u32[]{:S(2)}) collective-permute-start(bf16[1536,128]{1,0:T(8,128)(2,1)S(1)} %shard_map.59.refs_0_.refs_5_), channel_id=1, source_target_pairs={{0,16},{1,17},{2,18},{3,19},{4,12},{5,13},{6,14},{7,15},{8,24},{9,... | collective-permute-start | bytes 1179656 | tf_op jit(solution)/shard_map/ppermute | solution.py:261
  8.1 14.4 %collective-permute-start.5 = (bf16[1536,128]{1,0:T(8,128)(2,1)S(1)}, bf16[1536,128]{1,0:T(8,128)(2,1)S(1)}, u32[]{:S(2)}, u32[]{:S(2)}) collective-permute-start(bf16[1536,128]{1,0:T(8,128)(2,1)S(1)} %shard_map.59.refs_0_.refs_5_), channel_id=1, source_target_pairs={{0,8},{1,9},{2,10},{3,11},{4,20},{5,21},{6,22},{7,23},{8,0},{9,1},... | collective-permute-start | bytes 1179656 | tf_op jit(solution)/shard_map/ppermute | solution.py:261
  9.5 7.9 %collective-permute-start.2 = (bf16[512,128]{1,0:T(8,128)(2,1)S(1)}, bf16[512,128]{1,0:T(8,128)(2,1)S(1)}, u32[]{:S(2)}, u32[]{:S(2)}) collective-permute-start(bf16[512,128]{1,0:T(8,128)(2,1)S(1)} %get-tuple-element.44.refs_0_), channel_id=1, source_target_pairs={{0,1},{1,0},{2,3},{3,2},{4,6},{5,7},{6,4},{7,5},{8,9},{9,8},{10,11... | collective-permute-start | bytes 393224 | tf_op jit(solution)/shard_map/ppermute | solution.py:261
  11.1 11.3 %collective-permute-start.3 = (bf16[512,128]{1,0:T(8,128)(2,1)S(1)}, bf16[512,128]{1,0:T(8,128)(2,1)S(1)}, u32[]{:S(2)}, u32[]{:S(2)}) collective-permute-start(bf16[512,128]{1,0:T(8,128)(2,1)S(1)} %get-tuple-element.45), channel_id=1, source_target_pairs={{0,2},{1,3},{2,0},{3,1},{4,5},{5,4},{6,7},{7,6},{8,10},{9,11},{10,... | collective-permute-start | bytes 393224 | tf_op jit(solution)/shard_map/ppermute | solution.py:261
  13.7 8.7 %collective-permute-start.4 = (bf16[512,128]{1,0:T(8,128)(2,1)S(1)}, bf16[512,128]{1,0:T(8,128)(2,1)S(1)}, u32[]{:S(2)}, u32[]{:S(2)}) collective-permute-start(bf16[512,128]{1,0:T(8,128)(2,1)S(1)} %get-tuple-element.46), channel_id=1, source_target_pairs={{0,3},{1,2},{2,1},{3,0},{4,7},{5,6},{6,5},{7,4},{8,11},{9,10},{10,... | collective-permute-start | bytes 393224 | tf_op jit(solution)/shard_map/ppermute | solution.py:261
  17.4 11.3 %collective-permute-start.11 = (bf16[128,1536]{1,0:T(8,128)(2,1)S(1)}, bf16[128,1536]{1,0:T(8,128)(2,1)S(1)}, u32[]{:S(2)}, u32[]{:S(2)}) collective-permute-start(bf16[128,1536]{1,0:T(8,128)(2,1)S(1)} %get-tuple-element.50), channel_id=1, source_target_pairs={{0,4},{1,5},{2,6},{3,7},{4,0},{5,1},{6,2},{7,3},{8,12},{9,13},{10,... | collective-permute-start | bytes 1179656 | tf_op jit(solution)/shard_map/ppermute | solution.py:261
  22.6 6.2 %collective-permute-start.7 = (bf16[512,128]{1,0:T(8,128)(2,1)S(1)}, bf16[512,128]{1,0:T(8,128)(2,1)S(1)}, u32[]{:S(2)}, u32[]{:S(2)}) collective-permute-start(bf16[512,128]{1,0:T(8,128)(2,1)S(1)} %get-tuple-element.47.refs_0_), channel_id=1, source_target_pairs={{0,1},{1,0},{2,3},{3,2},{4,6},{5,7},{6,4},{7,5},{8,9},{9,8},{10,11... | collective-permute-start | bytes 393224 | tf_op jit(solution)/shard_map/ppermute | solution.py:261
  24.7 12.1 %collective-permute-start.10 = (bf16[3072,128]{1,0:T(8,128)(2,1)S(1)}, bf16[3072,128]{1,0:T(8,128)(2,1)S(1)}, u32[]{:S(2)}, u32[]{:S(2)}) collective-permute-start(bf16[3072,128]{1,0:T(8,128)(2,1)S(1)} %shard_map.62.refs_0_.refs_1_.refs_6_), channel_id=1, source_target_pairs={{0,8},{1,9},{2,10},{3,11},{4,20},{5,21},{6,22},{7,23},{8,0},{9,1},... | collective-permute-start | bytes 2359304 | tf_op jit(solution)/shard_map/ppermute | solution.py:261
  25.4 11.3 %collective-permute-start.8 = (bf16[512,128]{1,0:T(8,128)(2,1)S(1)}, bf16[512,128]{1,0:T(8,128)(2,1)S(1)}, u32[]{:S(2)}, u32[]{:S(2)}) collective-permute-start(bf16[512,128]{1,0:T(8,128)(2,1)S(1)} %get-tuple-element.48), channel_id=1, source_target_pairs={{0,2},{1,3},{2,0},{3,1},{4,5},{5,4},{6,7},{7,6},{8,10},{9,11},{10,... | collective-permute-start | bytes 393224 | tf_op jit(solution)/shard_map/ppermute | solution.py:261
  27.3 9.4 %collective-permute-start.9 = (bf16[512,128]{1,0:T(8,128)(2,1)S(1)}, bf16[512,128]{1,0:T(8,128)(2,1)S(1)}, u32[]{:S(2)}, u32[]{:S(2)}) collective-permute-start(bf16[512,128]{1,0:T(8,128)(2,1)S(1)} %get-tuple-element.49), channel_id=1, source_target_pairs={{0,3},{1,2},{2,1},{3,0},{4,7},{5,6},{6,5},{7,4},{8,11},{9,10},{10,... | collective-permute-start | bytes 393224 | tf_op jit(solution)/shard_map/ppermute | solution.py:261
  36.9 10.4 %collective-permute-start.12 = (bf16[768,128]{1,0:T(8,128)(2,1)S(1)}, bf16[768,128]{1,0:T(8,128)(2,1)S(1)}, u32[]{:S(2)}, u32[]{:S(2)}) collective-permute-start(bf16[768,128]{1,0:T(8,128)(2,1)S(1)} %get-tuple-element.51.refs_0_), channel_id=1, source_target_pairs={{0,1},{1,0},{2,3},{3,2},{4,6},{5,7},{6,4},{7,5},{8,9},{9,8},{10,11... | collective-permute-start | bytes 589832 | tf_op jit(solution)/shard_map/ppermute | solution.py:261
  38.9 15.9 %collective-permute-start.15 = (bf16[3072,128]{1,0:T(8,128)(2,1)S(1)}, bf16[3072,128]{1,0:T(8,128)(2,1)S(1)}, u32[]{:S(2)}, u32[]{:S(2)}) collective-permute-start(bf16[3072,128]{1,0:T(8,128)(2,1)S(1)} %shard_map.65.refs_0_), channel_id=1, source_target_pairs={{0,16},{1,17},{2,18},{3,19},{4,12},{5,13},{6,14},{7,15},{8,24},{9,... | collective-permute-start | bytes 2359304 | tf_op jit(solution)/shard_map/ppermute | solution.py:261
  39.7 15.2 %collective-permute-start.16 = (bf16[1536,128]{1,0:T(8,128)(2,1)S(1)}, bf16[1536,128]{1,0:T(8,128)(2,1)S(1)}, u32[]{:S(2)}, u32[]{:S(2)}) collective-permute-start(bf16[1536,128]{1,0:T(8,128)(2,1)S(1)} %shard_map.66.refs_0_.refs_1_.refs_6_), channel_id=1, source_target_pairs={{0,8},{1,9},{2,10},{3,11},{4,20},{5,21},{6,22},{7,23},{8,0},{9,1},... | collective-permute-start | bytes 1179656 | tf_op jit(solution)/shard_map/ppermute | solution.py:261
  41.2 13.7 %collective-permute-start.13 = (bf16[768,128]{1,0:T(8,128)(2,1)S(1)}, bf16[768,128]{1,0:T(8,128)(2,1)S(1)}, u32[]{:S(2)}, u32[]{:S(2)}) collective-permute-start(bf16[768,128]{1,0:T(8,128)(2,1)S(1)} %get-tuple-element.52), channel_id=1, source_target_pairs={{0,2},{1,3},{2,0},{3,1},{4,5},{5,4},{6,7},{7,6},{8,10},{9,11},{10,... | collective-permute-start | bytes 589832 | tf_op jit(solution)/shard_map/ppermute | solution.py:261
  42.2 12.6 %collective-permute-start.14 = (bf16[768,128]{1,0:T(8,128)(2,1)S(1)}, bf16[768,128]{1,0:T(8,128)(2,1)S(1)}, u32[]{:S(2)}, u32[]{:S(2)}) collective-permute-start(bf16[768,128]{1,0:T(8,128)(2,1)S(1)} %get-tuple-element.53), channel_id=1, source_target_pairs={{0,3},{1,2},{2,1},{3,0},{4,7},{5,6},{6,5},{7,4},{8,11},{9,10},{10,... | collective-permute-start | bytes 589832 | tf_op jit(solution)/shard_map/ppermute | solution.py:261
  55.1 12.9 %collective-permute-start.20 = (bf16[1536,128]{1,0:T(8,128)(2,1)S(1)}, bf16[1536,128]{1,0:T(8,128)(2,1)S(1)}, u32[]{:S(2)}, u32[]{:S(2)}) collective-permute-start(bf16[1536,128]{1,0:T(8,128)(2,1)S(1)} %shard_map.70.refs_0_.refs_4_.refs_6_), channel_id=1, source_target_pairs={{0,8},{1,9},{2,10},{3,11},{4,20},{5,21},{6,22},{7,23},{8,0},{9,1},... | collective-permute-start | bytes 1179656 | tf_op jit(solution)/shard_map/ppermute | solution.py:261
  55.4 13.5 %collective-permute-start.21 = (bf16[3072,128]{1,0:T(8,128)(2,1)S(1)}, bf16[3072,128]{1,0:T(8,128)(2,1)S(1)}, u32[]{:S(2)}, u32[]{:S(2)}) collective-permute-start(bf16[3072,128]{1,0:T(8,128)(2,1)S(1)} %shard_map.69.refs_0_), channel_id=1, source_target_pairs={{0,16},{1,17},{2,18},{3,19},{4,12},{5,13},{6,14},{7,15},{8,24},{9,... | collective-permute-start | bytes 2359304 | tf_op jit(solution)/shard_map/ppermute | solution.py:261
  56.7 10.1 %collective-permute-start.17 = (bf16[512,128]{1,0:T(8,128)(2,1)S(1)}, bf16[512,128]{1,0:T(8,128)(2,1)S(1)}, u32[]{:S(2)}, u32[]{:S(2)}) collective-permute-start(bf16[512,128]{1,0:T(8,128)(2,1)S(1)} %get-tuple-element.54.refs_0_), channel_id=1, source_target_pairs={{0,1},{1,0},{2,3},{3,2},{4,6},{5,7},{6,4},{7,5},{8,9},{9,8},{10,11... | collective-permute-start | bytes 393224 | tf_op jit(solution)/shard_map/ppermute | solution.py:261
  59.3 8.7 %collective-permute-start.18 = (bf16[512,128]{1,0:T(8,128)(2,1)S(1)}, bf16[512,128]{1,0:T(8,128)(2,1)S(1)}, u32[]{:S(2)}, u32[]{:S(2)}) collective-permute-start(bf16[512,128]{1,0:T(8,128)(2,1)S(1)} %get-tuple-element.56), channel_id=1, source_target_pairs={{0,2},{1,3},{2,0},{3,1},{4,5},{5,4},{6,7},{7,6},{8,10},{9,11},{10,... | collective-permute-start | bytes 393224 | tf_op jit(solution)/shard_map/ppermute | solution.py:261
  59.7 8.3 %collective-permute-start.19 = (bf16[512,128]{1,0:T(8,128)(2,1)S(1)}, bf16[512,128]{1,0:T(8,128)(2,1)S(1)}, u32[]{:S(2)}, u32[]{:S(2)}) collective-permute-start(bf16[512,128]{1,0:T(8,128)(2,1)S(1)} %get-tuple-element.57), channel_id=1, source_target_pairs={{0,3},{1,2},{2,1},{3,0},{4,7},{5,6},{6,5},{7,4},{8,11},{9,10},{10,... | collective-permute-start | bytes 393224 | tf_op jit(solution)/shard_map/ppermute | solution.py:261
  68.1 12.1 %collective-permute-start.22 = (bf16[3072,128]{1,0:T(8,128)(2,1)S(1)}, bf16[3072,128]{1,0:T(8,128)(2,1)S(1)}, u32[]{:S(2)}, u32[]{:S(2)}) collective-permute-start(bf16[3072,128]{1,0:T(8,128)(2,1)S(1)} %shard_map.73.refs_0_), channel_id=1, source_target_pairs={{0,16},{1,17},{2,18},{3,19},{4,12},{5,13},{6,14},{7,15},{8,24},{9,... | collective-permute-start | bytes 2359304 | tf_op jit(solution)/shard_map/ppermute | solution.py:261
  74.1 13.6 %collective-permute-start.23 = (bf16[512,128]{1,0:T(8,128)(2,1)S(1)}, bf16[512,128]{1,0:T(8,128)(2,1)S(1)}, u32[]{:S(2)}, u32[]{:S(2)}) collective-permute-start(bf16[512,128]{1,0:T(8,128)(2,1)S(1)} %get-tuple-element.67), channel_id=1, source_target_pairs={{0,1},{1,0},{2,3},{3,2},{4,6},{5,7},{6,4},{7,5},{8,9},{9,8},{10,11... | collective-permute-start | bytes 393224 | tf_op jit(solution)/shard_map/ppermute | solution.py:261
  76.2 13.4 %collective-permute-start.24 = (bf16[512,128]{1,0:T(8,128)(2,1)S(1)}, bf16[512,128]{1,0:T(8,128)(2,1)S(1)}, u32[]{:S(2)}, u32[]{:S(2)}) collective-permute-start(bf16[512,128]{1,0:T(8,128)(2,1)S(1)} %get-tuple-element.68), channel_id=1, source_target_pairs={{0,2},{1,3},{2,0},{3,1},{4,5},{5,4},{6,7},{7,6},{8,10},{9,11},{10,... | collective-permute-start | bytes 393224 | tf_op jit(solution)/shard_map/ppermute | solution.py:261
  76.9 12.7 %collective-permute-start.25 = (bf16[512,128]{1,0:T(8,128)(2,1)S(1)}, bf16[512,128]{1,0:T(8,128)(2,1)S(1)}, u32[]{:S(2)}, u32[]{:S(2)}) collective-permute-start(bf16[512,128]{1,0:T(8,128)(2,1)S(1)} %get-tuple-element.69), channel_id=1, source_target_pairs={{0,3},{1,2},{2,1},{3,0},{4,7},{5,6},{6,5},{7,4},{8,11},{9,10},{10,... | collective-permute-start | bytes 393224 | tf_op jit(solution)/shard_map/ppermute | solution.py:261
  85.1 5.5 %collective-permute-start.26 = (bf16[256,128]{1,0:T(8,128)(2,1)S(1)}, bf16[256,128]{1,0:T(8,128)(2,1)S(1)}, u32[]{:S(2)}, u32[]{:S(2)}) collective-permute-start(bf16[256,128]{1,0:T(8,128)(2,1)S(1)} %get-tuple-element.71), channel_id=1, source_target_pairs={{0,1},{1,0},{2,3},{3,2},{4,6},{5,7},{6,4},{7,5},{8,9},{9,8},{10,11... | collective-permute-start | bytes 196616 | tf_op jit(solution)/shard_map/ppermute | solution.py:261
  87.1 6.9 %collective-permute-start.27 = (bf16[256,128]{1,0:T(8,128)(2,1)S(1)}, bf16[256,128]{1,0:T(8,128)(2,1)S(1)}, u32[]{:S(2)}, u32[]{:S(2)}) collective-permute-start(bf16[256,128]{1,0:T(8,128)(2,1)S(1)} %get-tuple-element.72), channel_id=1, source_target_pairs={{0,2},{1,3},{2,0},{3,1},{4,5},{5,4},{6,7},{7,6},{8,10},{9,11},{10,... | collective-permute-start | bytes 196616 | tf_op jit(solution)/shard_map/ppermute | solution.py:261
  87.7 6.3 %collective-permute-start.28 = (bf16[256,128]{1,0:T(8,128)(2,1)S(1)}, bf16[256,128]{1,0:T(8,128)(2,1)S(1)}, u32[]{:S(2)}, u32[]{:S(2)}) collective-permute-start(bf16[256,128]{1,0:T(8,128)(2,1)S(1)} %get-tuple-element.73), channel_id=1, source_target_pairs={{0,3},{1,2},{2,1},{3,0},{4,7},{5,6},{6,5},{7,4},{8,11},{9,10},{10,... | collective-permute-start | bytes 196616 | tf_op jit(solution)/shard_map/ppermute | solution.py:261
  89.6 4.5 %collective-permute-start.29 = (bf16[1024,128]{1,0:T(8,128)(2,1)S(1)}, bf16[1024,128]{1,0:T(8,128)(2,1)S(1)}, u32[]{:S(2)}, u32[]{:S(2)}) collective-permute-start(bf16[1024,128]{1,0:T(8,128)(2,1)S(1)} %get-tuple-element.75), channel_id=1, source_target_pairs={{0,4},{1,5},{2,6},{3,7},{4,0},{5,1},{6,2},{7,3},{8,12},{9,13},{10,... | collective-permute-start | bytes 786440 | tf_op jit(solution)/shard_map/ppermute | solution.py:261
  94.0 1.4 %collective-permute-start.30 = (bf16[512,128]{1,0:T(8,128)(2,1)S(1)}, bf16[512,128]{1,0:T(8,128)(2,1)S(1)}, u32[]{:S(2)}, u32[]{:S(2)}) collective-permute-start(bf16[512,128]{1,0:T(8,128)(2,1)S(1)} %get-tuple-element.76), channel_id=1, source_target_pairs={{0,4},{1,5},{2,6},{3,7},{4,0},{5,1},{6,2},{7,3},{8,12},{9,13},{10,... | collective-permute-start | bytes 393224 | tf_op jit(solution)/shard_map/ppermute | solution.py:261
  (4 other events, 4.2 us)

commit v7 on v6

--- a/solution.py
+++ b/solution.py
@@ -220,8 +220,10 @@
             at += rows
 
 
-def join(line, layout, after=()):
+def join(line, layout, after=(), order=()):
     known = Arrays()
+    for array in order:
+        known.piece(array, 0, 0)
     layout = [known.pieces(parts) for parts in layout]
     outs = [sds(sum(rows for _, _, rows in parts), HEAD_DIM) for parts in layout]
     return line.call(
@@ -336,7 +338,7 @@
         for c in range(chunks):
             own += [(a, 2 * c * tokens, tokens) for a in back]
             other += [(a, (2 * c + 1) * tokens, tokens) for a in (kept, first, second, opposite)]
-        own, across = join(line, [own, other])
+        own, across = join(line, [own, other], order=(opposite, first, second, kept) if chunks == 1 else ())
         return own, other_core(across)
 
     def send_back(outs):
@@ -365,8 +367,16 @@
     (own_q,) = pack(line, [[(0, c, KEPT) for c in range(3)]], (q_pair,))
     out0 = attend(line, list(queries_of(0, swap2, 2 * part).values()), blocks_of(0, gathered0), outs)
     gathered2 = end_gather(*gather2, after=swap3)
-    out1 = attend(line, list(queries_of(1, swap3, 0).values()), blocks_of(1, gathered1), outs)
-    back01 = send_back(join(line, [[(x, 0, part), (y, 0, part)] for x, y in zip(out0, out1)]))
+    slots1, blocks1 = queries_of(1, swap3, 0), blocks_of(1, gathered1)
+
+    def both(hops):
+        late = attend(line, [slots1[hop] for hop in hops], blocks1, [part] * 2)
+        return join(line, [[(out0[hop], 0, part), (x, 0, part)] for hop, x in zip(hops, late)])
+
+    opposite, kept = both((OPPOSITE, KEPT))
+    opposite = hop_z(opposite, OPPOSITE)
+    second, first = both((SECOND, FIRST))
+    back01 = [kept, hop_z(second, SECOND), hop_z(first, FIRST), opposite]
     out2 = attend(line, list(queries_of(2, swap3, part).values()), blocks_of(2, gathered2), outs)
     back2 = send_back(out2)
     own01, across01 = core_swap(back01, 2)

time: 96.5 us -> 95.7 us (level)
    pallas_call x25 -> x27, Pallas kernels: 17.1 us -> 17.1 us  [call(): pl.pallas_call(without_last, out_shape=outs, in_specs=[pl.BlockSpec(memor...]
where the time goes in v7:
time: 95.7 us; the launch traced here: 95.5 us
  starting transfers between devices  38.7 us (40%)
  waiting for transfers between devices  35.2 us (37%)
  Pallas kernels  18.8 us (20%)
  local copies, waits for them, and re-layouts  2.39 us (2%)
    ppermute x31, starting transfers between devices, permute(): return lax.ppermute(array, AXES, pairs)  38.7 us
    ppermute x31, waiting for transfers between devices, permute(): return lax.ppermute(array, AXES, pairs)  35.2 us
    pallas_call x27, Pallas kernels, call(): pl.pallas_call(without_last, out_shape=outs, in_specs=[pl.BlockSpec(memor...  17.1 us
    unnamed x10, local copies, waits for them, and re-layouts  2.39 us
  transfers between devices with their start and end apart: 31, of which 13 were waited for; matrix products, arithmetic and copies ran while one was open for 0% of the time, Pallas kernels for 18%

profile of v7, /device:TPU:0, one launch (start us, length us, event | category | flops | bytes accessed | tf_op | source)
XLA Modules:
  0.0 95.5 jit_solution(9855438270400328319)
XLA Ops:
  0.0 1.2 %copy-done.1 = bf16[128,3072]{1,0:T(8,128)(2,1)S(1)} copy-done((bf16[128,3072]{1,0:T(8,128)(2,1)S(1)}, bf16[128,3072]{1,0:T(8,128)(2,1)}, u32[]{:S(2)}) %copy-start.1) | copy-done | bytes 786456
  5.1 3.0 %collective-permute-start.6 = (bf16[1536,128]{1,0:T(8,128)(2,1)S(1)}, bf16[1536,128]{1,0:T(8,128)(2,1)S(1)}, u32[]{:S(2)}, u32[]{:S(2)}) collective-permute-start(bf16[1536,128]{1,0:T(8,128)(2,1)S(1)} %shard_map.59.refs_0_.refs_5_.refs_3_), channel_id=1, source_target_pairs={{0,16},{1,17},{2,18},{3,19},{4,12},{5,13},{6,14},{7,15},{8,24},{9,... | collective-permute-start | bytes 1179656 | tf_op jit(solution)/shard_map/ppermute | solution.py:263
  8.1 1.5 %collective-permute-start.5 = (bf16[1536,128]{1,0:T(8,128)(2,1)S(1)}, bf16[1536,128]{1,0:T(8,128)(2,1)S(1)}, u32[]{:S(2)}, u32[]{:S(2)}) collective-permute-start(bf16[1536,128]{1,0:T(8,128)(2,1)S(1)} %shard_map.59.refs_0_.refs_5_.refs_3_), channel_id=1, source_target_pairs={{0,8},{1,9},{2,10},{3,11},{4,20},{5,21},{6,22},{7,23},{8,0},{9,1},... | collective-permute-start | bytes 1179656 | tf_op jit(solution)/shard_map/ppermute | solution.py:263
  9.5 1.6 %collective-permute-start.2 = (bf16[512,128]{1,0:T(8,128)(2,1)S(1)}, bf16[512,128]{1,0:T(8,128)(2,1)S(1)}, u32[]{:S(2)}, u32[]{:S(2)}) collective-permute-start(bf16[512,128]{1,0:T(8,128)(2,1)S(1)} %get-tuple-element.44.refs_0_), channel_id=1, source_target_pairs={{0,1},{1,0},{2,3},{3,2},{4,6},{5,7},{6,4},{7,5},{8,9},{9,8},{10,11... | collective-permute-start | bytes 393224 | tf_op jit(solution)/shard_map/ppermute | solution.py:263
  11.1 2.6 %collective-permute-start.3 = (bf16[512,128]{1,0:T(8,128)(2,1)S(1)}, bf16[512,128]{1,0:T(8,128)(2,1)S(1)}, u32[]{:S(2)}, u32[]{:S(2)}) collective-permute-start(bf16[512,128]{1,0:T(8,128)(2,1)S(1)} %get-tuple-element.45), channel_id=1, source_target_pairs={{0,2},{1,3},{2,0},{3,1},{4,5},{5,4},{6,7},{7,6},{8,10},{9,11},{10,... | collective-permute-start | bytes 393224 | tf_op jit(solution)/shard_map/ppermute | solution.py:263
  13.9 3.5 %collective-permute-done.2.refs_1_.refs_2_ = bf16[512,128]{1,0:T(8,128)(2,1)S(1)} collective-permute-done((bf16[512,128]{1,0:T(8,128)(2,1)S(1)}, bf16[512,128]{1,0:T(8,128)(2,1)S(1)}, u32[]{:S(2)}, u32[]{:S(2)}) %collective-permute-start.2) | collective-permute-done | bytes 131104 | tf_op jit(solution)/shard_map/ppermute | solution.py:263
  17.4 5.0 %collective-permute-done.3.refs_2_.refs_3_ = bf16[512,128]{1,0:T(8,128)(2,1)S(1)} collective-permute-done((bf16[512,128]{1,0:T(8,128)(2,1)S(1)}, bf16[512,128]{1,0:T(8,128)(2,1)S(1)}, u32[]{:S(2)}, u32[]{:S(2)}) %collective-permute-start.3) | collective-permute-done | bytes 131104 | tf_op jit(solution)/shard_map/ppermute | solution.py:263
  22.6 2.1 %collective-permute-start.7 = (bf16[512,128]{1,0:T(8,128)(2,1)S(1)}, bf16[512,128]{1,0:T(8,128)(2,1)S(1)}, u32[]{:S(2)}, u32[]{:S(2)}) collective-permute-start(bf16[512,128]{1,0:T(8,128)(2,1)S(1)} %get-tuple-element.47.refs_0_), channel_id=1, source_target_pairs={{0,1},{1,0},{2,3},{3,2},{4,6},{5,7},{6,4},{7,5},{8,9},{9,8},{10,11... | collective-permute-start | bytes 393224 | tf_op jit(solution)/shard_map/ppermute | solution.py:263
  25.4 1.9 %collective-permute-start.8 = (bf16[512,128]{1,0:T(8,128)(2,1)S(1)}, bf16[512,128]{1,0:T(8,128)(2,1)S(1)}, u32[]{:S(2)}, u32[]{:S(2)}) collective-permute-start(bf16[512,128]{1,0:T(8,128)(2,1)S(1)} %get-tuple-element.48), channel_id=1, source_target_pairs={{0,2},{1,3},{2,0},{3,1},{4,5},{5,4},{6,7},{7,6},{8,10},{9,11},{10,... | collective-permute-start | bytes 393224 | tf_op jit(solution)/shard_map/ppermute | solution.py:263
  27.3 1.4 %collective-permute-start.9 = (bf16[512,128]{1,0:T(8,128)(2,1)S(1)}, bf16[512,128]{1,0:T(8,128)(2,1)S(1)}, u32[]{:S(2)}, u32[]{:S(2)}) collective-permute-start(bf16[512,128]{1,0:T(8,128)(2,1)S(1)} %get-tuple-element.49), channel_id=1, source_target_pairs={{0,3},{1,2},{2,1},{3,0},{4,7},{5,6},{6,5},{7,4},{8,11},{9,10},{10,... | collective-permute-start | bytes 393224 | tf_op jit(solution)/shard_map/ppermute | solution.py:263
  28.8 7.9 %collective-permute-done.8.refs_2_ = bf16[512,128]{1,0:T(8,128)(2,1)S(1)} collective-permute-done((bf16[512,128]{1,0:T(8,128)(2,1)S(1)}, bf16[512,128]{1,0:T(8,128)(2,1)S(1)}, u32[]{:S(2)}, u32[]{:S(2)}) %collective-permute-start.8) | collective-permute-done | bytes 131104 | tf_op jit(solution)/shard_map/ppermute | solution.py:263
  36.9 1.9 %collective-permute-start.12 = (bf16[768,128]{1,0:T(8,128)(2,1)S(1)}, bf16[768,128]{1,0:T(8,128)(2,1)S(1)}, u32[]{:S(2)}, u32[]{:S(2)}) collective-permute-start(bf16[768,128]{1,0:T(8,128)(2,1)S(1)} %get-tuple-element.51.refs_0_), channel_id=1, source_target_pairs={{0,1},{1,0},{2,3},{3,2},{4,6},{5,7},{6,4},{7,5},{8,9},{9,8},{10,11... | collective-permute-start | bytes 589832 | tf_op jit(solution)/shard_map/ppermute | solution.py:263
  39.7 1.5 %collective-permute-start.16 = (bf16[1536,128]{1,0:T(8,128)(2,1)S(1)}, bf16[1536,128]{1,0:T(8,128)(2,1)S(1)}, u32[]{:S(2)}, u32[]{:S(2)}) collective-permute-start(bf16[1536,128]{1,0:T(8,128)(2,1)S(1)} %shard_map.66.refs_0_.refs_1_.refs_4_), channel_id=1, source_target_pairs={{0,8},{1,9},{2,10},{3,11},{4,20},{5,21},{6,22},{7,23},{8,0},{9,1},... | collective-permute-start | bytes 1179656 | tf_op jit(solution)/shard_map/ppermute | solution.py:263
  42.2 1.4 %collective-permute-start.14 = (bf16[768,128]{1,0:T(8,128)(2,1)S(1)}, bf16[768,128]{1,0:T(8,128)(2,1)S(1)}, u32[]{:S(2)}, u32[]{:S(2)}) collective-permute-start(bf16[768,128]{1,0:T(8,128)(2,1)S(1)} %get-tuple-element.53), channel_id=1, source_target_pairs={{0,3},{1,2},{2,1},{3,0},{4,7},{5,6},{6,5},{7,4},{8,11},{9,10},{10,... | collective-permute-start | bytes 589832 | tf_op jit(solution)/shard_map/ppermute | solution.py:263
  43.6 3.7 %collective-permute-done.12.refs_1_.refs_2_ = bf16[768,128]{1,0:T(8,128)(2,1)S(1)} collective-permute-done((bf16[768,128]{1,0:T(8,128)(2,1)S(1)}, bf16[768,128]{1,0:T(8,128)(2,1)S(1)}, u32[]{:S(2)}, u32[]{:S(2)}) %collective-permute-start.12) | collective-permute-done | bytes 196640 | tf_op jit(solution)/shard_map/ppermute | solution.py:263
  47.4 7.5 %collective-permute-done.13.refs_2_.refs_3_ = bf16[768,128]{1,0:T(8,128)(2,1)S(1)} collective-permute-done((bf16[768,128]{1,0:T(8,128)(2,1)S(1)}, bf16[768,128]{1,0:T(8,128)(2,1)S(1)}, u32[]{:S(2)}, u32[]{:S(2)}) %collective-permute-start.13) | collective-permute-done | bytes 196640 | tf_op jit(solution)/shard_map/ppermute | solution.py:263
  55.4 1.3 %collective-permute-start.21 = (bf16[3072,128]{1,0:T(8,128)(2,1)S(1)}, bf16[3072,128]{1,0:T(8,128)(2,1)S(1)}, u32[]{:S(2)}, u32[]{:S(2)}) collective-permute-start(bf16[3072,128]{1,0:T(8,128)(2,1)S(1)} %shard_map.69.refs_0_), channel_id=1, source_target_pairs={{0,16},{1,17},{2,18},{3,19},{4,12},{5,13},{6,14},{7,15},{8,24},{9,... | collective-permute-start | bytes 2359304 | tf_op jit(solution)/shard_map/ppermute | solution.py:263
  56.7 2.6 %collective-permute-start.17 = (bf16[512,128]{1,0:T(8,128)(2,1)S(1)}, bf16[512,128]{1,0:T(8,128)(2,1)S(1)}, u32[]{:S(2)}, u32[]{:S(2)}) collective-permute-start(bf16[512,128]{1,0:T(8,128)(2,1)S(1)} %get-tuple-element.54.refs_0_), channel_id=1, source_target_pairs={{0,1},{1,0},{2,3},{3,2},{4,6},{5,7},{6,4},{7,5},{8,9},{9,8},{10,11... | collective-permute-start | bytes 393224 | tf_op jit(solution)/shard_map/ppermute | solution.py:263
  59.7 1.9 %collective-permute-start.19 = (bf16[512,128]{1,0:T(8,128)(2,1)S(1)}, bf16[512,128]{1,0:T(8,128)(2,1)S(1)}, u32[]{:S(2)}, u32[]{:S(2)}) collective-permute-start(bf16[512,128]{1,0:T(8,128)(2,1)S(1)} %get-tuple-element.57), channel_id=1, source_target_pairs={{0,3},{1,2},{2,1},{3,0},{4,7},{5,6},{6,5},{7,4},{8,11},{9,10},{10,... | collective-permute-start | bytes 393224 | tf_op jit(solution)/shard_map/ppermute | solution.py:263
  61.7 5.0 %shard_map.72 = (bf16[256,128]{1,0:T(8,128)(2,1)S(1)}, bf16[256,128]{1,0:T(8,128)(2,1)S(1)}, bf16[256,128]{1,0:T(8,128)(2,1)S(1)}, bf16[256,128]{1,0:T(8,128)(2,1)S(1)}) custom-call(bf16[768,128]{1,0:T(8,128)(2,1)S(1)} %shard_map.71.refs_0_.refs_1_.refs_2_, bf16[768,128]{1,0:T(8,128)(2,1)S(1)} %shard_map.71.refs_0_.refs_1_.refs_2_, ...), custom_call_target="tpu_custom_call" | custom-call | flops 2147483648 | bytes 4587520 | tf_op jit(solution)/shard_map/pallas_call | solution.py:40
  66.8 1.2 %collective-permute-done.18.refs_2_.refs_3_ = bf16[512,128]{1,0:T(8,128)(2,1)S(1)} collective-permute-done((bf16[512,128]{1,0:T(8,128)(2,1)S(1)}, bf16[512,128]{1,0:T(8,128)(2,1)S(1)}, u32[]{:S(2)}, u32[]{:S(2)}) %collective-permute-start.18) | collective-permute-done | bytes 131104 | tf_op jit(solution)/shard_map/ppermute | solution.py:263
  68.9 2.5 %shard_map.74 = (bf16[256,128]{1,0:T(8,128)(2,1)S(1)}, bf16[256,128]{1,0:T(8,128)(2,1)S(1)}) custom-call(bf16[3072,128]{1,0:T(8,128)(2,1)S(1)} %shard_map.73.refs_0_, bf16[512,128]{1,0:T(8,128)(2,1)S(1)} %collective-permute-done.19.refs_3_.refs_1_.refs_4_, bf16[768,128]{1,0:T(8,128)(2,1)S(1)} %shard_map.71.refs_0_.refs_1_.refs_2_, ...), custom_call_target="tpu_custom_call" | custom-call | flops 1073741824 | bytes 3997696 | tf_op jit(solution)/shard_map/pallas_call | solution.py:40
  71.4 2.2 %collective-permute-start.25 = (bf16[512,128]{1,0:T(8,128)(2,1)S(1)}, bf16[512,128]{1,0:T(8,128)(2,1)S(1)}, u32[]{:S(2)}, u32[]{:S(2)}) collective-permute-start(bf16[512,128]{1,0:T(8,128)(2,1)S(1)} %get-tuple-element.61.refs_0_), channel_id=1, source_target_pairs={{0,3},{1,2},{2,1},{3,0},{4,7},{5,6},{6,5},{7,4},{8,11},{9,10},{10,... | collective-permute-start | bytes 393224 | tf_op jit(solution)/shard_map/ppermute | solution.py:263
  73.6 2.7 %shard_map.76 = (bf16[256,128]{1,0:T(8,128)(2,1)S(1)}, bf16[256,128]{1,0:T(8,128)(2,1)S(1)}) custom-call(bf16[512,128]{1,0:T(8,128)(2,1)S(1)} %get-tuple-element.61.refs_0_, bf16[512,128]{1,0:T(8,128)(2,1)S(1)} %collective-permute-done.17.refs_1_.refs_2_, bf16[512,128]{1,0:T(8,128)(2,1)S(1)} %collective-permute-done.18.refs_2_.refs_3_, ...), custom_call_target="tpu_custom_call" | custom-call | flops 1073741824 | bytes 3932160 | tf_op jit(solution)/shard_map/pallas_call | solution.py:40
  76.3 1.1 %collective-permute-start.23 = (bf16[512,128]{1,0:T(8,128)(2,1)S(1)}, bf16[512,128]{1,0:T(8,128)(2,1)S(1)}, u32[]{:S(2)}, u32[]{:S(2)}) collective-permute-start(bf16[512,128]{1,0:T(8,128)(2,1)S(1)} %get-tuple-element.66.refs_0_), channel_id=1, source_target_pairs={{0,1},{1,0},{2,3},{3,2},{4,6},{5,7},{6,4},{7,5},{8,9},{9,8},{10,11... | collective-permute-start | bytes 393224 | tf_op jit(solution)/shard_map/ppermute | solution.py:263
  77.4 1.2 %collective-permute-start.24 = (bf16[512,128]{1,0:T(8,128)(2,1)S(1)}, bf16[512,128]{1,0:T(8,128)(2,1)S(1)}, u32[]{:S(2)}, u32[]{:S(2)}) collective-permute-start(bf16[512,128]{1,0:T(8,128)(2,1)S(1)} %get-tuple-element.69), channel_id=1, source_target_pairs={{0,2},{1,3},{2,0},{3,1},{4,5},{5,4},{6,7},{7,6},{8,10},{9,11},{10,... | collective-permute-start | bytes 393224 | tf_op jit(solution)/shard_map/ppermute | solution.py:263
  78.6 1.5 %collective-permute-done.22.refs_10_ = bf16[3072,128]{1,0:T(8,128)(2,1)S(1)} collective-permute-done((bf16[3072,128]{1,0:T(8,128)(2,1)S(1)}, bf16[3072,128]{1,0:T(8,128)(2,1)S(1)}, u32[]{:S(2)}, u32[]{:S(2)}) %collective-permute-start.22) | collective-permute-done | bytes 786464 | tf_op jit(solution)/shard_map/ppermute | solution.py:263
  80.1 5.0 %shard_map.78 = (bf16[256,128]{1,0:T(8,128)(2,1)S(1)}, bf16[256,128]{1,0:T(8,128)(2,1)S(1)}, bf16[256,128]{1,0:T(8,128)(2,1)S(1)}, bf16[256,128]{1,0:T(8,128)(2,1)S(1)}) custom-call(bf16[512,128]{1,0:T(8,128)(2,1)S(1)} %get-tuple-element.66.refs_0_, bf16[768,128]{1,0:T(8,128)(2,1)S(1)} %shard_map.71.refs_0_.refs_1_.refs_2_, ...), custom_call_target="tpu_custom_call" | custom-call | flops 2147483648 | bytes 4390912 | tf_op jit(solution)/shard_map/pallas_call | solution.py:40
  85.1 2.0 %collective-permute-start.26 = (bf16[256,128]{1,0:T(8,128)(2,1)S(1)}, bf16[256,128]{1,0:T(8,128)(2,1)S(1)}, u32[]{:S(2)}, u32[]{:S(2)}) collective-permute-start(bf16[256,128]{1,0:T(8,128)(2,1)S(1)} %get-tuple-element.71), channel_id=1, source_target_pairs={{0,3},{1,2},{2,1},{3,0},{4,7},{5,6},{6,5},{7,4},{8,11},{9,10},{10,... | collective-permute-start | bytes 196616 | tf_op jit(solution)/shard_map/ppermute | solution.py:263
  87.1 1.5 %collective-permute-start.27 = (bf16[256,128]{1,0:T(8,128)(2,1)S(1)}, bf16[256,128]{1,0:T(8,128)(2,1)S(1)}, u32[]{:S(2)}, u32[]{:S(2)}) collective-permute-start(bf16[256,128]{1,0:T(8,128)(2,1)S(1)} %get-tuple-element.72), channel_id=1, source_target_pairs={{0,2},{1,3},{2,0},{3,1},{4,5},{5,4},{6,7},{7,6},{8,10},{9,11},{10,... | collective-permute-start | bytes 196616 | tf_op jit(solution)/shard_map/ppermute | solution.py:263
  89.7 1.6 %collective-permute-done.26.refs_1_ = bf16[256,128]{1,0:T(8,128)(2,1)S(1)} collective-permute-done((bf16[256,128]{1,0:T(8,128)(2,1)S(1)}, bf16[256,128]{1,0:T(8,128)(2,1)S(1)}, u32[]{:S(2)}, u32[]{:S(2)}) %collective-permute-start.26) | collective-permute-done | bytes 65568 | tf_op jit(solution)/shard_map/ppermute | solution.py:263
  91.3 1.9 %collective-permute-done.27.refs_2_ = bf16[256,128]{1,0:T(8,128)(2,1)S(1)} collective-permute-done((bf16[256,128]{1,0:T(8,128)(2,1)S(1)}, bf16[256,128]{1,0:T(8,128)(2,1)S(1)}, u32[]{:S(2)}, u32[]{:S(2)}) %collective-permute-start.27) | collective-permute-done | bytes 65568 | tf_op jit(solution)/shard_map/ppermute | solution.py:263
  (69 shorter events, 11.9 us)
Async XLA Ops:
  0.0 2.4 %copy-start = (bf16[128,3072]{1,0:T(8,128)(2,1)S(1)}, bf16[128,3072]{1,0:T(8,128)(2,1)}, u32[]{:S(2)}) copy-start(bf16[128,3072]{1,0:T(8,128)(2,1)} %refs_7_.1) | copy-start | bytes 2359300
  2.5 1.9 %collective-permute-start.1 = (bf16[128,1536]{1,0:T(8,128)(2,1)S(1)}, bf16[128,1536]{1,0:T(8,128)(2,1)S(1)}, u32[]{:S(2)}, u32[]{:S(2)}) collective-permute-start(bf16[128,1536]{1,0:T(8,128)(2,1)S(1)} %shard_map.56.refs_0_), channel_id=1, source_target_pairs={{0,4},{1,5},{2,6},{3,7},{4,0},{5,1},{6,2},{7,3},{8,12},{9,13},{10,... | collective-permute-start | bytes 1179656 | tf_op jit(solution)/shard_map/ppermute | solution.py:263
  3.0 1.9 %collective-permute-start = (bf16[128,1536]{1,0:T(8,128)(2,1)S(1)}, bf16[128,1536]{1,0:T(8,128)(2,1)S(1)}, u32[]{:S(2)}, u32[]{:S(2)}) collective-permute-start(bf16[128,1536]{1,0:T(8,128)(2,1)S(1)} %get-tuple-element.43), channel_id=1, source_target_pairs={{0,4},{1,5},{2,6},{3,7},{4,0},{5,1},{6,2},{7,3},{8,12},{9,13},{10,... | collective-permute-start | bytes 1179656 | tf_op jit(solution)/shard_map/ppermute | solution.py:263
  5.1 17.4 %collective-permute-start.6 = (bf16[1536,128]{1,0:T(8,128)(2,1)S(1)}, bf16[1536,128]{1,0:T(8,128)(2,1)S(1)}, u32[]{:S(2)}, u32[]{:S(2)}) collective-permute-start(bf16[1536,128]{1,0:T(8,128)(2,1)S(1)} %shard_map.59.refs_0_.refs_5_.refs_3_), channel_id=1, source_target_pairs={{0,16},{1,17},{2,18},{3,19},{4,12},{5,13},{6,14},{7,15},{8,24},{9,... | collective-permute-start | bytes 1179656 | tf_op jit(solution)/shard_map/ppermute | solution.py:263
  8.1 14.4 %collective-permute-start.5 = (bf16[1536,128]{1,0:T(8,128)(2,1)S(1)}, bf16[1536,128]{1,0:T(8,128)(2,1)S(1)}, u32[]{:S(2)}, u32[]{:S(2)}) collective-permute-start(bf16[1536,128]{1,0:T(8,128)(2,1)S(1)} %shard_map.59.refs_0_.refs_5_.refs_3_), channel_id=1, source_target_pairs={{0,8},{1,9},{2,10},{3,11},{4,20},{5,21},{6,22},{7,23},{8,0},{9,1},... | collective-permute-start | bytes 1179656 | tf_op jit(solution)/shard_map/ppermute | solution.py:263
  9.5 7.9 %collective-permute-start.2 = (bf16[512,128]{1,0:T(8,128)(2,1)S(1)}, bf16[512,128]{1,0:T(8,128)(2,1)S(1)}, u32[]{:S(2)}, u32[]{:S(2)}) collective-permute-start(bf16[512,128]{1,0:T(8,128)(2,1)S(1)} %get-tuple-element.44.refs_0_), channel_id=1, source_target_pairs={{0,1},{1,0},{2,3},{3,2},{4,6},{5,7},{6,4},{7,5},{8,9},{9,8},{10,11... | collective-permute-start | bytes 393224 | tf_op jit(solution)/shard_map/ppermute | solution.py:263
  11.1 11.3 %collective-permute-start.3 = (bf16[512,128]{1,0:T(8,128)(2,1)S(1)}, bf16[512,128]{1,0:T(8,128)(2,1)S(1)}, u32[]{:S(2)}, u32[]{:S(2)}) collective-permute-start(bf16[512,128]{1,0:T(8,128)(2,1)S(1)} %get-tuple-element.45), channel_id=1, source_target_pairs={{0,2},{1,3},{2,0},{3,1},{4,5},{5,4},{6,7},{7,6},{8,10},{9,11},{10,... | collective-permute-start | bytes 393224 | tf_op jit(solution)/shard_map/ppermute | solution.py:263
  13.7 8.7 %collective-permute-start.4 = (bf16[512,128]{1,0:T(8,128)(2,1)S(1)}, bf16[512,128]{1,0:T(8,128)(2,1)S(1)}, u32[]{:S(2)}, u32[]{:S(2)}) collective-permute-start(bf16[512,128]{1,0:T(8,128)(2,1)S(1)} %get-tuple-element.46), channel_id=1, source_target_pairs={{0,3},{1,2},{2,1},{3,0},{4,7},{5,6},{6,5},{7,4},{8,11},{9,10},{10,... | collective-permute-start | bytes 393224 | tf_op jit(solution)/shard_map/ppermute | solution.py:263
  17.4 11.3 %collective-permute-start.11 = (bf16[128,1536]{1,0:T(8,128)(2,1)S(1)}, bf16[128,1536]{1,0:T(8,128)(2,1)S(1)}, u32[]{:S(2)}, u32[]{:S(2)}) collective-permute-start(bf16[128,1536]{1,0:T(8,128)(2,1)S(1)} %get-tuple-element.50), channel_id=1, source_target_pairs={{0,4},{1,5},{2,6},{3,7},{4,0},{5,1},{6,2},{7,3},{8,12},{9,13},{10,... | collective-permute-start | bytes 1179656 | tf_op jit(solution)/shard_map/ppermute | solution.py:263
  22.6 6.2 %collective-permute-start.7 = (bf16[512,128]{1,0:T(8,128)(2,1)S(1)}, bf16[512,128]{1,0:T(8,128)(2,1)S(1)}, u32[]{:S(2)}, u32[]{:S(2)}) collective-permute-start(bf16[512,128]{1,0:T(8,128)(2,1)S(1)} %get-tuple-element.47.refs_0_), channel_id=1, source_target_pairs={{0,1},{1,0},{2,3},{3,2},{4,6},{5,7},{6,4},{7,5},{8,9},{9,8},{10,11... | collective-permute-start | bytes 393224 | tf_op jit(solution)/shard_map/ppermute | solution.py:263
  24.7 12.1 %collective-permute-start.10 = (bf16[3072,128]{1,0:T(8,128)(2,1)S(1)}, bf16[3072,128]{1,0:T(8,128)(2,1)S(1)}, u32[]{:S(2)}, u32[]{:S(2)}) collective-permute-start(bf16[3072,128]{1,0:T(8,128)(2,1)S(1)} %shard_map.62.refs_0_.refs_1_.refs_6_), channel_id=1, source_target_pairs={{0,8},{1,9},{2,10},{3,11},{4,20},{5,21},{6,22},{7,23},{8,0},{9,1},... | collective-permute-start | bytes 2359304 | tf_op jit(solution)/shard_map/ppermute | solution.py:263
  25.4 11.3 %collective-permute-start.8 = (bf16[512,128]{1,0:T(8,128)(2,1)S(1)}, bf16[512,128]{1,0:T(8,128)(2,1)S(1)}, u32[]{:S(2)}, u32[]{:S(2)}) collective-permute-start(bf16[512,128]{1,0:T(8,128)(2,1)S(1)} %get-tuple-element.48), channel_id=1, source_target_pairs={{0,2},{1,3},{2,0},{3,1},{4,5},{5,4},{6,7},{7,6},{8,10},{9,11},{10,... | collective-permute-start | bytes 393224 | tf_op jit(solution)/shard_map/ppermute | solution.py:263
  27.3 9.4 %collective-permute-start.9 = (bf16[512,128]{1,0:T(8,128)(2,1)S(1)}, bf16[512,128]{1,0:T(8,128)(2,1)S(1)}, u32[]{:S(2)}, u32[]{:S(2)}) collective-permute-start(bf16[512,128]{1,0:T(8,128)(2,1)S(1)} %get-tuple-element.49), channel_id=1, source_target_pairs={{0,3},{1,2},{2,1},{3,0},{4,7},{5,6},{6,5},{7,4},{8,11},{9,10},{10,... | collective-permute-start | bytes 393224 | tf_op jit(solution)/shard_map/ppermute | solution.py:263
  36.9 10.4 %collective-permute-start.12 = (bf16[768,128]{1,0:T(8,128)(2,1)S(1)}, bf16[768,128]{1,0:T(8,128)(2,1)S(1)}, u32[]{:S(2)}, u32[]{:S(2)}) collective-permute-start(bf16[768,128]{1,0:T(8,128)(2,1)S(1)} %get-tuple-element.51.refs_0_), channel_id=1, source_target_pairs={{0,1},{1,0},{2,3},{3,2},{4,6},{5,7},{6,4},{7,5},{8,9},{9,8},{10,11... | collective-permute-start | bytes 589832 | tf_op jit(solution)/shard_map/ppermute | solution.py:263
  38.9 15.9 %collective-permute-start.15 = (bf16[3072,128]{1,0:T(8,128)(2,1)S(1)}, bf16[3072,128]{1,0:T(8,128)(2,1)S(1)}, u32[]{:S(2)}, u32[]{:S(2)}) collective-permute-start(bf16[3072,128]{1,0:T(8,128)(2,1)S(1)} %shard_map.65.refs_0_), channel_id=1, source_target_pairs={{0,16},{1,17},{2,18},{3,19},{4,12},{5,13},{6,14},{7,15},{8,24},{9,... | collective-permute-start | bytes 2359304 | tf_op jit(solution)/shard_map/ppermute | solution.py:263
  39.7 15.2 %collective-permute-start.16 = (bf16[1536,128]{1,0:T(8,128)(2,1)S(1)}, bf16[1536,128]{1,0:T(8,128)(2,1)S(1)}, u32[]{:S(2)}, u32[]{:S(2)}) collective-permute-start(bf16[1536,128]{1,0:T(8,128)(2,1)S(1)} %shard_map.66.refs_0_.refs_1_.refs_4_), channel_id=1, source_target_pairs={{0,8},{1,9},{2,10},{3,11},{4,20},{5,21},{6,22},{7,23},{8,0},{9,1},... | collective-permute-start | bytes 1179656 | tf_op jit(solution)/shard_map/ppermute | solution.py:263
  41.2 13.7 %collective-permute-start.13 = (bf16[768,128]{1,0:T(8,128)(2,1)S(1)}, bf16[768,128]{1,0:T(8,128)(2,1)S(1)}, u32[]{:S(2)}, u32[]{:S(2)}) collective-permute-start(bf16[768,128]{1,0:T(8,128)(2,1)S(1)} %get-tuple-element.52), channel_id=1, source_target_pairs={{0,2},{1,3},{2,0},{3,1},{4,5},{5,4},{6,7},{7,6},{8,10},{9,11},{10,... | collective-permute-start | bytes 589832 | tf_op jit(solution)/shard_map/ppermute | solution.py:263
  42.2 12.6 %collective-permute-start.14 = (bf16[768,128]{1,0:T(8,128)(2,1)S(1)}, bf16[768,128]{1,0:T(8,128)(2,1)S(1)}, u32[]{:S(2)}, u32[]{:S(2)}) collective-permute-start(bf16[768,128]{1,0:T(8,128)(2,1)S(1)} %get-tuple-element.53), channel_id=1, source_target_pairs={{0,3},{1,2},{2,1},{3,0},{4,7},{5,6},{6,5},{7,4},{8,11},{9,10},{10,... | collective-permute-start | bytes 589832 | tf_op jit(solution)/shard_map/ppermute | solution.py:263
  55.1 12.9 %collective-permute-start.20 = (bf16[1536,128]{1,0:T(8,128)(2,1)S(1)}, bf16[1536,128]{1,0:T(8,128)(2,1)S(1)}, u32[]{:S(2)}, u32[]{:S(2)}) collective-permute-start(bf16[1536,128]{1,0:T(8,128)(2,1)S(1)} %shard_map.70.refs_0_.refs_4_.refs_6_), channel_id=1, source_target_pairs={{0,8},{1,9},{2,10},{3,11},{4,20},{5,21},{6,22},{7,23},{8,0},{9,1},... | collective-permute-start | bytes 1179656 | tf_op jit(solution)/shard_map/ppermute | solution.py:263
  55.4 13.5 %collective-permute-start.21 = (bf16[3072,128]{1,0:T(8,128)(2,1)S(1)}, bf16[3072,128]{1,0:T(8,128)(2,1)S(1)}, u32[]{:S(2)}, u32[]{:S(2)}) collective-permute-start(bf16[3072,128]{1,0:T(8,128)(2,1)S(1)} %shard_map.69.refs_0_), channel_id=1, source_target_pairs={{0,16},{1,17},{2,18},{3,19},{4,12},{5,13},{6,14},{7,15},{8,24},{9,... | collective-permute-start | bytes 2359304 | tf_op jit(solution)/shard_map/ppermute | solution.py:263
  56.7 10.1 %collective-permute-start.17 = (bf16[512,128]{1,0:T(8,128)(2,1)S(1)}, bf16[512,128]{1,0:T(8,128)(2,1)S(1)}, u32[]{:S(2)}, u32[]{:S(2)}) collective-permute-start(bf16[512,128]{1,0:T(8,128)(2,1)S(1)} %get-tuple-element.54.refs_0_), channel_id=1, source_target_pairs={{0,1},{1,0},{2,3},{3,2},{4,6},{5,7},{6,4},{7,5},{8,9},{9,8},{10,11... | collective-permute-start | bytes 393224 | tf_op jit(solution)/shard_map/ppermute | solution.py:263
  59.3 8.7 %collective-permute-start.18 = (bf16[512,128]{1,0:T(8,128)(2,1)S(1)}, bf16[512,128]{1,0:T(8,128)(2,1)S(1)}, u32[]{:S(2)}, u32[]{:S(2)}) collective-permute-start(bf16[512,128]{1,0:T(8,128)(2,1)S(1)} %get-tuple-element.56), channel_id=1, source_target_pairs={{0,2},{1,3},{2,0},{3,1},{4,5},{5,4},{6,7},{7,6},{8,10},{9,11},{10,... | collective-permute-start | bytes 393224 | tf_op jit(solution)/shard_map/ppermute | solution.py:263
  59.7 8.3 %collective-permute-start.19 = (bf16[512,128]{1,0:T(8,128)(2,1)S(1)}, bf16[512,128]{1,0:T(8,128)(2,1)S(1)}, u32[]{:S(2)}, u32[]{:S(2)}) collective-permute-start(bf16[512,128]{1,0:T(8,128)(2,1)S(1)} %get-tuple-element.57), channel_id=1, source_target_pairs={{0,3},{1,2},{2,1},{3,0},{4,7},{5,6},{6,5},{7,4},{8,11},{9,10},{10,... | collective-permute-start | bytes 393224 | tf_op jit(solution)/shard_map/ppermute | solution.py:263
  68.1 12.1 %collective-permute-start.22 = (bf16[3072,128]{1,0:T(8,128)(2,1)S(1)}, bf16[3072,128]{1,0:T(8,128)(2,1)S(1)}, u32[]{:S(2)}, u32[]{:S(2)}) collective-permute-start(bf16[3072,128]{1,0:T(8,128)(2,1)S(1)} %shard_map.73.refs_0_), channel_id=1, source_target_pairs={{0,16},{1,17},{2,18},{3,19},{4,12},{5,13},{6,14},{7,15},{8,24},{9,... | collective-permute-start | bytes 2359304 | tf_op jit(solution)/shard_map/ppermute | solution.py:263
  71.4 18.2 %collective-permute-start.25 = (bf16[512,128]{1,0:T(8,128)(2,1)S(1)}, bf16[512,128]{1,0:T(8,128)(2,1)S(1)}, u32[]{:S(2)}, u32[]{:S(2)}) collective-permute-start(bf16[512,128]{1,0:T(8,128)(2,1)S(1)} %get-tuple-element.61.refs_0_), channel_id=1, source_target_pairs={{0,3},{1,2},{2,1},{3,0},{4,7},{5,6},{6,5},{7,4},{8,11},{9,10},{10,... | collective-permute-start | bytes 393224 | tf_op jit(solution)/shard_map/ppermute | solution.py:263
  76.3 12.3 %collective-permute-start.23 = (bf16[512,128]{1,0:T(8,128)(2,1)S(1)}, bf16[512,128]{1,0:T(8,128)(2,1)S(1)}, u32[]{:S(2)}, u32[]{:S(2)}) collective-permute-start(bf16[512,128]{1,0:T(8,128)(2,1)S(1)} %get-tuple-element.66.refs_0_), channel_id=1, source_target_pairs={{0,1},{1,0},{2,3},{3,2},{4,6},{5,7},{6,4},{7,5},{8,9},{9,8},{10,11... | collective-permute-start | bytes 393224 | tf_op jit(solution)/shard_map/ppermute | solution.py:263
  77.4 12.1 %collective-permute-start.24 = (bf16[512,128]{1,0:T(8,128)(2,1)S(1)}, bf16[512,128]{1,0:T(8,128)(2,1)S(1)}, u32[]{:S(2)}, u32[]{:S(2)}) collective-permute-start(bf16[512,128]{1,0:T(8,128)(2,1)S(1)} %get-tuple-element.69), channel_id=1, source_target_pairs={{0,2},{1,3},{2,0},{3,1},{4,5},{5,4},{6,7},{7,6},{8,10},{9,11},{10,... | collective-permute-start | bytes 393224 | tf_op jit(solution)/shard_map/ppermute | solution.py:263
  85.1 6.2 %collective-permute-start.26 = (bf16[256,128]{1,0:T(8,128)(2,1)S(1)}, bf16[256,128]{1,0:T(8,128)(2,1)S(1)}, u32[]{:S(2)}, u32[]{:S(2)}) collective-permute-start(bf16[256,128]{1,0:T(8,128)(2,1)S(1)} %get-tuple-element.71), channel_id=1, source_target_pairs={{0,3},{1,2},{2,1},{3,0},{4,7},{5,6},{6,5},{7,4},{8,11},{9,10},{10,... | collective-permute-start | bytes 196616 | tf_op jit(solution)/shard_map/ppermute | solution.py:263
  87.1 6.1 %collective-permute-start.27 = (bf16[256,128]{1,0:T(8,128)(2,1)S(1)}, bf16[256,128]{1,0:T(8,128)(2,1)S(1)}, u32[]{:S(2)}, u32[]{:S(2)}) collective-permute-start(bf16[256,128]{1,0:T(8,128)(2,1)S(1)} %get-tuple-element.72), channel_id=1, source_target_pairs={{0,2},{1,3},{2,0},{3,1},{4,5},{5,4},{6,7},{7,6},{8,10},{9,11},{10,... | collective-permute-start | bytes 196616 | tf_op jit(solution)/shard_map/ppermute | solution.py:263
  88.6 4.6 %collective-permute-start.28 = (bf16[256,128]{1,0:T(8,128)(2,1)S(1)}, bf16[256,128]{1,0:T(8,128)(2,1)S(1)}, u32[]{:S(2)}, u32[]{:S(2)}) collective-permute-start(bf16[256,128]{1,0:T(8,128)(2,1)S(1)} %get-tuple-element.73), channel_id=1, source_target_pairs={{0,1},{1,0},{2,3},{3,2},{4,6},{5,7},{6,4},{7,5},{8,9},{9,8},{10,11... | collective-permute-start | bytes 196616 | tf_op jit(solution)/shard_map/ppermute | solution.py:263
  89.6 3.7 %collective-permute-start.29 = (bf16[1024,128]{1,0:T(8,128)(2,1)S(1)}, bf16[1024,128]{1,0:T(8,128)(2,1)S(1)}, u32[]{:S(2)}, u32[]{:S(2)}) collective-permute-start(bf16[1024,128]{1,0:T(8,128)(2,1)S(1)} %get-tuple-element.75), channel_id=1, source_target_pairs={{0,4},{1,5},{2,6},{3,7},{4,0},{5,1},{6,2},{7,3},{8,12},{9,13},{10,... | collective-permute-start | bytes 786440 | tf_op jit(solution)/shard_map/ppermute | solution.py:263
  93.2 1.4 %collective-permute-start.30 = (bf16[512,128]{1,0:T(8,128)(2,1)S(1)}, bf16[512,128]{1,0:T(8,128)(2,1)S(1)}, u32[]{:S(2)}, u32[]{:S(2)}) collective-permute-start(bf16[512,128]{1,0:T(8,128)(2,1)S(1)} %get-tuple-element.76), channel_id=1, source_target_pairs={{0,4},{1,5},{2,6},{3,7},{4,0},{5,1},{6,2},{7,3},{8,12},{9,13},{10,... | collective-permute-start | bytes 393224 | tf_op jit(solution)/shard_map/ppermute | solution.py:263
  (4 other events, 4.2 us)

commit v8 on v7

--- a/solution.py
+++ b/solution.py
@@ -377,8 +377,11 @@
     opposite = hop_z(opposite, OPPOSITE)
     second, first = both((SECOND, FIRST))
     back01 = [kept, hop_z(second, SECOND), hop_z(first, FIRST), opposite]
-    out2 = attend(line, list(queries_of(2, swap3, part).values()), blocks_of(2, gathered2), outs)
-    back2 = send_back(out2)
+    slots2, blocks2 = queries_of(2, swap3, part), blocks_of(2, gathered2)
+    opposite2, kept2 = attend(line, [slots2[OPPOSITE], slots2[KEPT]], blocks2, [part] * 2)
+    opposite2 = hop_z(opposite2, OPPOSITE)
+    second2, first2 = attend(line, [slots2[SECOND], slots2[FIRST]], blocks2, [part] * 2)
+    back2 = [kept2, hop_z(second2, SECOND), hop_z(first2, FIRST), opposite2]
     own01, across01 = core_swap(back01, 2)
     line.mark()
     own2, across2 = core_swap(back2, 1)

time: 95.7 us -> 95.5 us (level)
    pallas_call x27 -> x28, Pallas kernels: 17.1 us -> 17 us  [call(): pl.pallas_call(without_last, out_shape=outs, in_specs=[pl.BlockSpec(memor...]
  transfers between devices with their start and end apart: 31 -> 31, of which waited for: 13 -> 12; matrix products, arithmetic and copies ran while one was open for 0% -> 0% of each run, Pallas kernels for 18% -> 18%
where the time goes in v8:
time: 95.5 us; the launch traced here: 95.3 us
  starting transfers between devices  38.7 us (41%)
  waiting for transfers between devices  35 us (37%)
  Pallas kernels  18.7 us (20%)
  local copies, waits for them, and re-layouts  2.39 us (3%)
    ppermute x31, starting transfers between devices, permute(): return lax.ppermute(array, AXES, pairs)  38.7 us
    ppermute x31, waiting for transfers between devices, permute(): return lax.ppermute(array, AXES, pairs)  35 us
    pallas_call x28, Pallas kernels, call(): pl.pallas_call(without_last, out_shape=outs, in_specs=[pl.BlockSpec(memor...  17 us
    unnamed x10, local copies, waits for them, and re-layouts  2.39 us
  transfers between devices with their start and end apart: 31, of which 12 were waited for; matrix products, arithmetic and copies ran while one was open for 0% of the time, Pallas kernels for 18%

profile of v8, /device:TPU:0, one launch (start us, length us, event | category | flops | bytes accessed | tf_op | source)
XLA Modules:
  0.0 95.3 jit_solution(11143560054352111375)
XLA Ops:
  0.0 1.2 %copy-done.1 = bf16[128,3072]{1,0:T(8,128)(2,1)S(1)} copy-done((bf16[128,3072]{1,0:T(8,128)(2,1)S(1)}, bf16[128,3072]{1,0:T(8,128)(2,1)}, u32[]{:S(2)}) %copy-start.1) | copy-done | bytes 786456
  5.1 3.0 %collective-permute-start.6 = (bf16[1536,128]{1,0:T(8,128)(2,1)S(1)}, bf16[1536,128]{1,0:T(8,128)(2,1)S(1)}, u32[]{:S(2)}, u32[]{:S(2)}) collective-permute-start(bf16[1536,128]{1,0:T(8,128)(2,1)S(1)} %shard_map.59.refs_0_.refs_5_.refs_3_), channel_id=1, source_target_pairs={{0,16},{1,17},{2,18},{3,19},{4,12},{5,13},{6,14},{7,15},{8,24},{9,... | collective-permute-start | bytes 1179656 | tf_op jit(solution)/shard_map/ppermute | solution.py:263
  8.1 1.5 %collective-permute-start.5 = (bf16[1536,128]{1,0:T(8,128)(2,1)S(1)}, bf16[1536,128]{1,0:T(8,128)(2,1)S(1)}, u32[]{:S(2)}, u32[]{:S(2)}) collective-permute-start(bf16[1536,128]{1,0:T(8,128)(2,1)S(1)} %shard_map.59.refs_0_.refs_5_.refs_3_), channel_id=1, source_target_pairs={{0,8},{1,9},{2,10},{3,11},{4,20},{5,21},{6,22},{7,23},{8,0},{9,1},... | collective-permute-start | bytes 1179656 | tf_op jit(solution)/shard_map/ppermute | solution.py:263
  9.5 1.6 %collective-permute-start.2 = (bf16[512,128]{1,0:T(8,128)(2,1)S(1)}, bf16[512,128]{1,0:T(8,128)(2,1)S(1)}, u32[]{:S(2)}, u32[]{:S(2)}) collective-permute-start(bf16[512,128]{1,0:T(8,128)(2,1)S(1)} %get-tuple-element.44.refs_0_), channel_id=1, source_target_pairs={{0,1},{1,0},{2,3},{3,2},{4,6},{5,7},{6,4},{7,5},{8,9},{9,8},{10,11... | collective-permute-start | bytes 393224 | tf_op jit(solution)/shard_map/ppermute | solution.py:263
  11.1 2.6 %collective-permute-start.3 = (bf16[512,128]{1,0:T(8,128)(2,1)S(1)}, bf16[512,128]{1,0:T(8,128)(2,1)S(1)}, u32[]{:S(2)}, u32[]{:S(2)}) collective-permute-start(bf16[512,128]{1,0:T(8,128)(2,1)S(1)} %get-tuple-element.45), channel_id=1, source_target_pairs={{0,2},{1,3},{2,0},{3,1},{4,5},{5,4},{6,7},{7,6},{8,10},{9,11},{10,... | collective-permute-start | bytes 393224 | tf_op jit(solution)/shard_map/ppermute | solution.py:263
  13.9 3.5 %collective-permute-done.2.refs_1_.refs_2_ = bf16[512,128]{1,0:T(8,128)(2,1)S(1)} collective-permute-done((bf16[512,128]{1,0:T(8,128)(2,1)S(1)}, bf16[512,128]{1,0:T(8,128)(2,1)S(1)}, u32[]{:S(2)}, u32[]{:S(2)}) %collective-permute-start.2) | collective-permute-done | bytes 131104 | tf_op jit(solution)/shard_map/ppermute | solution.py:263
  17.4 5.0 %collective-permute-done.3.refs_2_.refs_3_ = bf16[512,128]{1,0:T(8,128)(2,1)S(1)} collective-permute-done((bf16[512,128]{1,0:T(8,128)(2,1)S(1)}, bf16[512,128]{1,0:T(8,128)(2,1)S(1)}, u32[]{:S(2)}, u32[]{:S(2)}) %collective-permute-start.3) | collective-permute-done | bytes 131104 | tf_op jit(solution)/shard_map/ppermute | solution.py:263
  22.6 2.1 %collective-permute-start.7 = (bf16[512,128]{1,0:T(8,128)(2,1)S(1)}, bf16[512,128]{1,0:T(8,128)(2,1)S(1)}, u32[]{:S(2)}, u32[]{:S(2)}) collective-permute-start(bf16[512,128]{1,0:T(8,128)(2,1)S(1)} %get-tuple-element.47.refs_0_), channel_id=1, source_target_pairs={{0,1},{1,0},{2,3},{3,2},{4,6},{5,7},{6,4},{7,5},{8,9},{9,8},{10,11... | collective-permute-start | bytes 393224 | tf_op jit(solution)/shard_map/ppermute | solution.py:263
  25.4 1.9 %collective-permute-start.8 = (bf16[512,128]{1,0:T(8,128)(2,1)S(1)}, bf16[512,128]{1,0:T(8,128)(2,1)S(1)}, u32[]{:S(2)}, u32[]{:S(2)}) collective-permute-start(bf16[512,128]{1,0:T(8,128)(2,1)S(1)} %get-tuple-element.48), channel_id=1, source_target_pairs={{0,2},{1,3},{2,0},{3,1},{4,5},{5,4},{6,7},{7,6},{8,10},{9,11},{10,... | collective-permute-start | bytes 393224 | tf_op jit(solution)/shard_map/ppermute | solution.py:263
  27.3 1.4 %collective-permute-start.9 = (bf16[512,128]{1,0:T(8,128)(2,1)S(1)}, bf16[512,128]{1,0:T(8,128)(2,1)S(1)}, u32[]{:S(2)}, u32[]{:S(2)}) collective-permute-start(bf16[512,128]{1,0:T(8,128)(2,1)S(1)} %get-tuple-element.49), channel_id=1, source_target_pairs={{0,3},{1,2},{2,1},{3,0},{4,7},{5,6},{6,5},{7,4},{8,11},{9,10},{10,... | collective-permute-start | bytes 393224 | tf_op jit(solution)/shard_map/ppermute | solution.py:263
  28.8 7.9 %collective-permute-done.8.refs_2_ = bf16[512,128]{1,0:T(8,128)(2,1)S(1)} collective-permute-done((bf16[512,128]{1,0:T(8,128)(2,1)S(1)}, bf16[512,128]{1,0:T(8,128)(2,1)S(1)}, u32[]{:S(2)}, u32[]{:S(2)}) %collective-permute-start.8) | collective-permute-done | bytes 131104 | tf_op jit(solution)/shard_map/ppermute | solution.py:263
  36.9 1.9 %collective-permute-start.12 = (bf16[768,128]{1,0:T(8,128)(2,1)S(1)}, bf16[768,128]{1,0:T(8,128)(2,1)S(1)}, u32[]{:S(2)}, u32[]{:S(2)}) collective-permute-start(bf16[768,128]{1,0:T(8,128)(2,1)S(1)} %get-tuple-element.51.refs_0_), channel_id=1, source_target_pairs={{0,1},{1,0},{2,3},{3,2},{4,6},{5,7},{6,4},{7,5},{8,9},{9,8},{10,11... | collective-permute-start | bytes 589832 | tf_op jit(solution)/shard_map/ppermute | solution.py:263
  39.7 1.5 %collective-permute-start.16 = (bf16[1536,128]{1,0:T(8,128)(2,1)S(1)}, bf16[1536,128]{1,0:T(8,128)(2,1)S(1)}, u32[]{:S(2)}, u32[]{:S(2)}) collective-permute-start(bf16[1536,128]{1,0:T(8,128)(2,1)S(1)} %shard_map.66.refs_0_.refs_1_.refs_4_), channel_id=1, source_target_pairs={{0,8},{1,9},{2,10},{3,11},{4,20},{5,21},{6,22},{7,23},{8,0},{9,1},... | collective-permute-start | bytes 1179656 | tf_op jit(solution)/shard_map/ppermute | solution.py:263
  42.2 1.4 %collective-permute-start.14 = (bf16[768,128]{1,0:T(8,128)(2,1)S(1)}, bf16[768,128]{1,0:T(8,128)(2,1)S(1)}, u32[]{:S(2)}, u32[]{:S(2)}) collective-permute-start(bf16[768,128]{1,0:T(8,128)(2,1)S(1)} %get-tuple-element.53), channel_id=1, source_target_pairs={{0,3},{1,2},{2,1},{3,0},{4,7},{5,6},{6,5},{7,4},{8,11},{9,10},{10,... | collective-permute-start | bytes 589832 | tf_op jit(solution)/shard_map/ppermute | solution.py:263
  43.6 3.7 %collective-permute-done.12.refs_1_.refs_2_ = bf16[768,128]{1,0:T(8,128)(2,1)S(1)} collective-permute-done((bf16[768,128]{1,0:T(8,128)(2,1)S(1)}, bf16[768,128]{1,0:T(8,128)(2,1)S(1)}, u32[]{:S(2)}, u32[]{:S(2)}) %collective-permute-start.12) | collective-permute-done | bytes 196640 | tf_op jit(solution)/shard_map/ppermute | solution.py:263
  47.4 7.5 %collective-permute-done.13.refs_2_.refs_3_ = bf16[768,128]{1,0:T(8,128)(2,1)S(1)} collective-permute-done((bf16[768,128]{1,0:T(8,128)(2,1)S(1)}, bf16[768,128]{1,0:T(8,128)(2,1)S(1)}, u32[]{:S(2)}, u32[]{:S(2)}) %collective-permute-start.13) | collective-permute-done | bytes 196640 | tf_op jit(solution)/shard_map/ppermute | solution.py:263
  55.4 1.3 %collective-permute-start.21 = (bf16[3072,128]{1,0:T(8,128)(2,1)S(1)}, bf16[3072,128]{1,0:T(8,128)(2,1)S(1)}, u32[]{:S(2)}, u32[]{:S(2)}) collective-permute-start(bf16[3072,128]{1,0:T(8,128)(2,1)S(1)} %shard_map.69.refs_0_), channel_id=1, source_target_pairs={{0,16},{1,17},{2,18},{3,19},{4,12},{5,13},{6,14},{7,15},{8,24},{9,... | collective-permute-start | bytes 2359304 | tf_op jit(solution)/shard_map/ppermute | solution.py:263
  56.7 2.6 %collective-permute-start.17 = (bf16[512,128]{1,0:T(8,128)(2,1)S(1)}, bf16[512,128]{1,0:T(8,128)(2,1)S(1)}, u32[]{:S(2)}, u32[]{:S(2)}) collective-permute-start(bf16[512,128]{1,0:T(8,128)(2,1)S(1)} %get-tuple-element.54.refs_0_), channel_id=1, source_target_pairs={{0,1},{1,0},{2,3},{3,2},{4,6},{5,7},{6,4},{7,5},{8,9},{9,8},{10,11... | collective-permute-start | bytes 393224 | tf_op jit(solution)/shard_map/ppermute | solution.py:263
  59.7 1.9 %collective-permute-start.19 = (bf16[512,128]{1,0:T(8,128)(2,1)S(1)}, bf16[512,128]{1,0:T(8,128)(2,1)S(1)}, u32[]{:S(2)}, u32[]{:S(2)}) collective-permute-start(bf16[512,128]{1,0:T(8,128)(2,1)S(1)} %get-tuple-element.57), channel_id=1, source_target_pairs={{0,3},{1,2},{2,1},{3,0},{4,7},{5,6},{6,5},{7,4},{8,11},{9,10},{10,... | collective-permute-start | bytes 393224 | tf_op jit(solution)/shard_map/ppermute | solution.py:263
  61.7 5.0 %shard_map.72 = (bf16[256,128]{1,0:T(8,128)(2,1)S(1)}, bf16[256,128]{1,0:T(8,128)(2,1)S(1)}, bf16[256,128]{1,0:T(8,128)(2,1)S(1)}, bf16[256,128]{1,0:T(8,128)(2,1)S(1)}) custom-call(bf16[768,128]{1,0:T(8,128)(2,1)S(1)} %shard_map.71.refs_0_.refs_1_.refs_2_, bf16[768,128]{1,0:T(8,128)(2,1)S(1)} %shard_map.71.refs_0_.refs_1_.refs_2_, ...), custom_call_target="tpu_custom_call" | custom-call | flops 2147483648 | bytes 4587520 | tf_op jit(solution)/shard_map/pallas_call | solution.py:40
  66.8 1.2 %collective-permute-done.18.refs_2_ = bf16[512,128]{1,0:T(8,128)(2,1)S(1)} collective-permute-done((bf16[512,128]{1,0:T(8,128)(2,1)S(1)}, bf16[512,128]{1,0:T(8,128)(2,1)S(1)}, u32[]{:S(2)}, u32[]{:S(2)}) %collective-permute-start.18) | collective-permute-done | bytes 131104 | tf_op jit(solution)/shard_map/ppermute | solution.py:263
  68.9 2.5 %shard_map.74 = (bf16[256,128]{1,0:T(8,128)(2,1)S(1)}, bf16[256,128]{1,0:T(8,128)(2,1)S(1)}) custom-call(bf16[3072,128]{1,0:T(8,128)(2,1)S(1)} %shard_map.73.refs_0_, bf16[512,128]{1,0:T(8,128)(2,1)S(1)} %collective-permute-done.19.refs_3_.refs_1_, bf16[768,128]{1,0:T(8,128)(2,1)S(1)} %shard_map.71.refs_0_.refs_1_.refs_2_, ...), custom_call_target="tpu_custom_call" | custom-call | flops 1073741824 | bytes 3997696 | tf_op jit(solution)/shard_map/pallas_call | solution.py:40
  71.4 2.2 %collective-permute-start.25 = (bf16[512,128]{1,0:T(8,128)(2,1)S(1)}, bf16[512,128]{1,0:T(8,128)(2,1)S(1)}, u32[]{:S(2)}, u32[]{:S(2)}) collective-permute-start(bf16[512,128]{1,0:T(8,128)(2,1)S(1)} %get-tuple-element.61.refs_0_), channel_id=1, source_target_pairs={{0,3},{1,2},{2,1},{3,0},{4,7},{5,6},{6,5},{7,4},{8,11},{9,10},{10,... | collective-permute-start | bytes 393224 | tf_op jit(solution)/shard_map/ppermute | solution.py:263
  73.6 2.7 %shard_map.76 = (bf16[256,128]{1,0:T(8,128)(2,1)S(1)}, bf16[256,128]{1,0:T(8,128)(2,1)S(1)}) custom-call(bf16[512,128]{1,0:T(8,128)(2,1)S(1)} %get-tuple-element.61.refs_0_, bf16[512,128]{1,0:T(8,128)(2,1)S(1)} %collective-permute-done.17.refs_1_, bf16[512,128]{1,0:T(8,128)(2,1)S(1)} %collective-permute-done.18.refs_2_, ...), custom_call_target="tpu_custom_call" | custom-call | flops 1073741824 | bytes 3932160 | tf_op jit(solution)/shard_map/pallas_call | solution.py:40
  76.3 1.1 %collective-permute-start.23 = (bf16[512,128]{1,0:T(8,128)(2,1)S(1)}, bf16[512,128]{1,0:T(8,128)(2,1)S(1)}, u32[]{:S(2)}, u32[]{:S(2)}) collective-permute-start(bf16[512,128]{1,0:T(8,128)(2,1)S(1)} %get-tuple-element.66.refs_0_), channel_id=1, source_target_pairs={{0,1},{1,0},{2,3},{3,2},{4,6},{5,7},{6,4},{7,5},{8,9},{9,8},{10,11... | collective-permute-start | bytes 393224 | tf_op jit(solution)/shard_map/ppermute | solution.py:263
  77.4 1.2 %collective-permute-start.24 = (bf16[512,128]{1,0:T(8,128)(2,1)S(1)}, bf16[512,128]{1,0:T(8,128)(2,1)S(1)}, u32[]{:S(2)}, u32[]{:S(2)}) collective-permute-start(bf16[512,128]{1,0:T(8,128)(2,1)S(1)} %get-tuple-element.70), channel_id=1, source_target_pairs={{0,2},{1,3},{2,0},{3,1},{4,5},{5,4},{6,7},{7,6},{8,10},{9,11},{10,... | collective-permute-start | bytes 393224 | tf_op jit(solution)/shard_map/ppermute | solution.py:263
  78.6 1.5 %collective-permute-done.22.refs_8_ = bf16[3072,128]{1,0:T(8,128)(2,1)S(1)} collective-permute-done((bf16[3072,128]{1,0:T(8,128)(2,1)S(1)}, bf16[3072,128]{1,0:T(8,128)(2,1)S(1)}, u32[]{:S(2)}, u32[]{:S(2)}) %collective-permute-start.22) | collective-permute-done | bytes 786464 | tf_op jit(solution)/shard_map/ppermute | solution.py:263
  80.1 2.5 %shard_map.78 = (bf16[256,128]{1,0:T(8,128)(2,1)S(1)}, bf16[256,128]{1,0:T(8,128)(2,1)S(1)}) custom-call(bf16[512,128]{1,0:T(8,128)(2,1)S(1)} %get-tuple-element.66.refs_0_, bf16[512,128]{1,0:T(8,128)(2,1)S(1)} %collective-permute-done.19.refs_3_.refs_1_, bf16[768,128]{1,0:T(8,128)(2,1)S(1)} %shard_map.71.refs_0_.refs_1_.refs_2_, ...), custom_call_target="tpu_custom_call" | custom-call | flops 1073741824 | bytes 3997696 | tf_op jit(solution)/shard_map/pallas_call | solution.py:40
  82.6 2.0 %collective-permute-start.26 = (bf16[256,128]{1,0:T(8,128)(2,1)S(1)}, bf16[256,128]{1,0:T(8,128)(2,1)S(1)}, u32[]{:S(2)}, u32[]{:S(2)}) collective-permute-start(bf16[256,128]{1,0:T(8,128)(2,1)S(1)} %get-tuple-element.67.refs_0_), channel_id=1, source_target_pairs={{0,3},{1,2},{2,1},{3,0},{4,7},{5,6},{6,5},{7,4},{8,11},{9,10},{10,... | collective-permute-start | bytes 196616 | tf_op jit(solution)/shard_map/ppermute | solution.py:263
  84.6 2.5 %shard_map.79 = (bf16[256,128]{1,0:T(8,128)(2,1)S(1)}, bf16[256,128]{1,0:T(8,128)(2,1)S(1)}) custom-call(bf16[256,128]{1,0:T(8,128)(2,1)S(1)} %get-tuple-element.67.refs_0_, bf16[512,128]{1,0:T(8,128)(2,1)S(1)} %collective-permute-done.17.refs_1_, bf16[512,128]{1,0:T(8,128)(2,1)S(1)} %collective-permute-done.18.refs_2_, ...), custom_call_target="tpu_custom_call" | custom-call | flops 1073741824 | bytes 3932160 | tf_op jit(solution)/shard_map/pallas_call | solution.py:40
  87.1 1.5 %collective-permute-start.27 = (bf16[256,128]{1,0:T(8,128)(2,1)S(1)}, bf16[256,128]{1,0:T(8,128)(2,1)S(1)}, u32[]{:S(2)}, u32[]{:S(2)}) collective-permute-start(bf16[256,128]{1,0:T(8,128)(2,1)S(1)} %get-tuple-element.72), channel_id=1, source_target_pairs={{0,2},{1,3},{2,0},{3,1},{4,5},{5,4},{6,7},{7,6},{8,10},{9,11},{10,... | collective-permute-start | bytes 196616 | tf_op jit(solution)/shard_map/ppermute | solution.py:263
  89.7 3.3 %collective-permute-done.27.refs_2_ = bf16[256,128]{1,0:T(8,128)(2,1)S(1)} collective-permute-done((bf16[256,128]{1,0:T(8,128)(2,1)S(1)}, bf16[256,128]{1,0:T(8,128)(2,1)S(1)}, u32[]{:S(2)}, u32[]{:S(2)}) %collective-permute-start.27) | collective-permute-done | bytes 65568 | tf_op jit(solution)/shard_map/ppermute | solution.py:263
  (70 shorter events, 11.9 us)
Async XLA Ops:
  0.0 2.4 %copy-start = (bf16[128,3072]{1,0:T(8,128)(2,1)S(1)}, bf16[128,3072]{1,0:T(8,128)(2,1)}, u32[]{:S(2)}) copy-start(bf16[128,3072]{1,0:T(8,128)(2,1)} %refs_7_.1) | copy-start | bytes 2359300
  2.5 1.9 %collective-permute-start.1 = (bf16[128,1536]{1,0:T(8,128)(2,1)S(1)}, bf16[128,1536]{1,0:T(8,128)(2,1)S(1)}, u32[]{:S(2)}, u32[]{:S(2)}) collective-permute-start(bf16[128,1536]{1,0:T(8,128)(2,1)S(1)} %shard_map.56.refs_0_), channel_id=1, source_target_pairs={{0,4},{1,5},{2,6},{3,7},{4,0},{5,1},{6,2},{7,3},{8,12},{9,13},{10,... | collective-permute-start | bytes 1179656 | tf_op jit(solution)/shard_map/ppermute | solution.py:263
  3.0 1.9 %collective-permute-start = (bf16[128,1536]{1,0:T(8,128)(2,1)S(1)}, bf16[128,1536]{1,0:T(8,128)(2,1)S(1)}, u32[]{:S(2)}, u32[]{:S(2)}) collective-permute-start(bf16[128,1536]{1,0:T(8,128)(2,1)S(1)} %get-tuple-element.43), channel_id=1, source_target_pairs={{0,4},{1,5},{2,6},{3,7},{4,0},{5,1},{6,2},{7,3},{8,12},{9,13},{10,... | collective-permute-start | bytes 1179656 | tf_op jit(solution)/shard_map/ppermute | solution.py:263
  5.1 17.4 %collective-permute-start.6 = (bf16[1536,128]{1,0:T(8,128)(2,1)S(1)}, bf16[1536,128]{1,0:T(8,128)(2,1)S(1)}, u32[]{:S(2)}, u32[]{:S(2)}) collective-permute-start(bf16[1536,128]{1,0:T(8,128)(2,1)S(1)} %shard_map.59.refs_0_.refs_5_.refs_3_), channel_id=1, source_target_pairs={{0,16},{1,17},{2,18},{3,19},{4,12},{5,13},{6,14},{7,15},{8,24},{9,... | collective-permute-start | bytes 1179656 | tf_op jit(solution)/shard_map/ppermute | solution.py:263
  8.1 14.4 %collective-permute-start.5 = (bf16[1536,128]{1,0:T(8,128)(2,1)S(1)}, bf16[1536,128]{1,0:T(8,128)(2,1)S(1)}, u32[]{:S(2)}, u32[]{:S(2)}) collective-permute-start(bf16[1536,128]{1,0:T(8,128)(2,1)S(1)} %shard_map.59.refs_0_.refs_5_.refs_3_), channel_id=1, source_target_pairs={{0,8},{1,9},{2,10},{3,11},{4,20},{5,21},{6,22},{7,23},{8,0},{9,1},... | collective-permute-start | bytes 1179656 | tf_op jit(solution)/shard_map/ppermute | solution.py:263
  9.5 7.9 %collective-permute-start.2 = (bf16[512,128]{1,0:T(8,128)(2,1)S(1)}, bf16[512,128]{1,0:T(8,128)(2,1)S(1)}, u32[]{:S(2)}, u32[]{:S(2)}) collective-permute-start(bf16[512,128]{1,0:T(8,128)(2,1)S(1)} %get-tuple-element.44.refs_0_), channel_id=1, source_target_pairs={{0,1},{1,0},{2,3},{3,2},{4,6},{5,7},{6,4},{7,5},{8,9},{9,8},{10,11... | collective-permute-start | bytes 393224 | tf_op jit(solution)/shard_map/ppermute | solution.py:263
  11.1 11.3 %collective-permute-start.3 = (bf16[512,128]{1,0:T(8,128)(2,1)S(1)}, bf16[512,128]{1,0:T(8,128)(2,1)S(1)}, u32[]{:S(2)}, u32[]{:S(2)}) collective-permute-start(bf16[512,128]{1,0:T(8,128)(2,1)S(1)} %get-tuple-element.45), channel_id=1, source_target_pairs={{0,2},{1,3},{2,0},{3,1},{4,5},{5,4},{6,7},{7,6},{8,10},{9,11},{10,... | collective-permute-start | bytes 393224 | tf_op jit(solution)/shard_map/ppermute | solution.py:263
  13.7 8.7 %collective-permute-start.4 = (bf16[512,128]{1,0:T(8,128)(2,1)S(1)}, bf16[512,128]{1,0:T(8,128)(2,1)S(1)}, u32[]{:S(2)}, u32[]{:S(2)}) collective-permute-start(bf16[512,128]{1,0:T(8,128)(2,1)S(1)} %get-tuple-element.46), channel_id=1, source_target_pairs={{0,3},{1,2},{2,1},{3,0},{4,7},{5,6},{6,5},{7,4},{8,11},{9,10},{10,... | collective-permute-start | bytes 393224 | tf_op jit(solution)/shard_map/ppermute | solution.py:263
  17.4 11.3 %collective-permute-start.11 = (bf16[128,1536]{1,0:T(8,128)(2,1)S(1)}, bf16[128,1536]{1,0:T(8,128)(2,1)S(1)}, u32[]{:S(2)}, u32[]{:S(2)}) collective-permute-start(bf16[128,1536]{1,0:T(8,128)(2,1)S(1)} %get-tuple-element.50), channel_id=1, source_target_pairs={{0,4},{1,5},{2,6},{3,7},{4,0},{5,1},{6,2},{7,3},{8,12},{9,13},{10,... | collective-permute-start | bytes 1179656 | tf_op jit(solution)/shard_map/ppermute | solution.py:263
  22.6 6.2 %collective-permute-start.7 = (bf16[512,128]{1,0:T(8,128)(2,1)S(1)}, bf16[512,128]{1,0:T(8,128)(2,1)S(1)}, u32[]{:S(2)}, u32[]{:S(2)}) collective-permute-start(bf16[512,128]{1,0:T(8,128)(2,1)S(1)} %get-tuple-element.47.refs_0_), channel_id=1, source_target_pairs={{0,1},{1,0},{2,3},{3,2},{4,6},{5,7},{6,4},{7,5},{8,9},{9,8},{10,11... | collective-permute-start | bytes 393224 | tf_op jit(solution)/shard_map/ppermute | solution.py:263
  24.7 12.1 %collective-permute-start.10 = (bf16[3072,128]{1,0:T(8,128)(2,1)S(1)}, bf16[3072,128]{1,0:T(8,128)(2,1)S(1)}, u32[]{:S(2)}, u32[]{:S(2)}) collective-permute-start(bf16[3072,128]{1,0:T(8,128)(2,1)S(1)} %shard_map.62.refs_0_.refs_1_.refs_6_), channel_id=1, source_target_pairs={{0,8},{1,9},{2,10},{3,11},{4,20},{5,21},{6,22},{7,23},{8,0},{9,1},... | collective-permute-start | bytes 2359304 | tf_op jit(solution)/shard_map/ppermute | solution.py:263
  25.4 11.3 %collective-permute-start.8 = (bf16[512,128]{1,0:T(8,128)(2,1)S(1)}, bf16[512,128]{1,0:T(8,128)(2,1)S(1)}, u32[]{:S(2)}, u32[]{:S(2)}) collective-permute-start(bf16[512,128]{1,0:T(8,128)(2,1)S(1)} %get-tuple-element.48), channel_id=1, source_target_pairs={{0,2},{1,3},{2,0},{3,1},{4,5},{5,4},{6,7},{7,6},{8,10},{9,11},{10,... | collective-permute-start | bytes 393224 | tf_op jit(solution)/shard_map/ppermute | solution.py:263
  27.3 9.4 %collective-permute-start.9 = (bf16[512,128]{1,0:T(8,128)(2,1)S(1)}, bf16[512,128]{1,0:T(8,128)(2,1)S(1)}, u32[]{:S(2)}, u32[]{:S(2)}) collective-permute-start(bf16[512,128]{1,0:T(8,128)(2,1)S(1)} %get-tuple-element.49), channel_id=1, source_target_pairs={{0,3},{1,2},{2,1},{3,0},{4,7},{5,6},{6,5},{7,4},{8,11},{9,10},{10,... | collective-permute-start | bytes 393224 | tf_op jit(solution)/shard_map/ppermute | solution.py:263
  36.9 10.4 %collective-permute-start.12 = (bf16[768,128]{1,0:T(8,128)(2,1)S(1)}, bf16[768,128]{1,0:T(8,128)(2,1)S(1)}, u32[]{:S(2)}, u32[]{:S(2)}) collective-permute-start(bf16[768,128]{1,0:T(8,128)(2,1)S(1)} %get-tuple-element.51.refs_0_), channel_id=1, source_target_pairs={{0,1},{1,0},{2,3},{3,2},{4,6},{5,7},{6,4},{7,5},{8,9},{9,8},{10,11... | collective-permute-start | bytes 589832 | tf_op jit(solution)/shard_map/ppermute | solution.py:263
  38.9 15.9 %collective-permute-start.15 = (bf16[3072,128]{1,0:T(8,128)(2,1)S(1)}, bf16[3072,128]{1,0:T(8,128)(2,1)S(1)}, u32[]{:S(2)}, u32[]{:S(2)}) collective-permute-start(bf16[3072,128]{1,0:T(8,128)(2,1)S(1)} %shard_map.65.refs_0_), channel_id=1, source_target_pairs={{0,16},{1,17},{2,18},{3,19},{4,12},{5,13},{6,14},{7,15},{8,24},{9,... | collective-permute-start | bytes 2359304 | tf_op jit(solution)/shard_map/ppermute | solution.py:263
  39.7 15.2 %collective-permute-start.16 = (bf16[1536,128]{1,0:T(8,128)(2,1)S(1)}, bf16[1536,128]{1,0:T(8,128)(2,1)S(1)}, u32[]{:S(2)}, u32[]{:S(2)}) collective-permute-start(bf16[1536,128]{1,0:T(8,128)(2,1)S(1)} %shard_map.66.refs_0_.refs_1_.refs_4_), channel_id=1, source_target_pairs={{0,8},{1,9},{2,10},{3,11},{4,20},{5,21},{6,22},{7,23},{8,0},{9,1},... | collective-permute-start | bytes 1179656 | tf_op jit(solution)/shard_map/ppermute | solution.py:263
  41.2 13.7 %collective-permute-start.13 = (bf16[768,128]{1,0:T(8,128)(2,1)S(1)}, bf16[768,128]{1,0:T(8,128)(2,1)S(1)}, u32[]{:S(2)}, u32[]{:S(2)}) collective-permute-start(bf16[768,128]{1,0:T(8,128)(2,1)S(1)} %get-tuple-element.52), channel_id=1, source_target_pairs={{0,2},{1,3},{2,0},{3,1},{4,5},{5,4},{6,7},{7,6},{8,10},{9,11},{10,... | collective-permute-start | bytes 589832 | tf_op jit(solution)/shard_map/ppermute | solution.py:263
  42.2 12.6 %collective-permute-start.14 = (bf16[768,128]{1,0:T(8,128)(2,1)S(1)}, bf16[768,128]{1,0:T(8,128)(2,1)S(1)}, u32[]{:S(2)}, u32[]{:S(2)}) collective-permute-start(bf16[768,128]{1,0:T(8,128)(2,1)S(1)} %get-tuple-element.53), channel_id=1, source_target_pairs={{0,3},{1,2},{2,1},{3,0},{4,7},{5,6},{6,5},{7,4},{8,11},{9,10},{10,... | collective-permute-start | bytes 589832 | tf_op jit(solution)/shard_map/ppermute | solution.py:263
  55.1 12.9 %collective-permute-start.20 = (bf16[1536,128]{1,0:T(8,128)(2,1)S(1)}, bf16[1536,128]{1,0:T(8,128)(2,1)S(1)}, u32[]{:S(2)}, u32[]{:S(2)}) collective-permute-start(bf16[1536,128]{1,0:T(8,128)(2,1)S(1)} %shard_map.70.refs_0_.refs_4_), channel_id=1, source_target_pairs={{0,8},{1,9},{2,10},{3,11},{4,20},{5,21},{6,22},{7,23},{8,0},{9,1},... | collective-permute-start | bytes 1179656 | tf_op jit(solution)/shard_map/ppermute | solution.py:263
  55.4 13.5 %collective-permute-start.21 = (bf16[3072,128]{1,0:T(8,128)(2,1)S(1)}, bf16[3072,128]{1,0:T(8,128)(2,1)S(1)}, u32[]{:S(2)}, u32[]{:S(2)}) collective-permute-start(bf16[3072,128]{1,0:T(8,128)(2,1)S(1)} %shard_map.69.refs_0_), channel_id=1, source_target_pairs={{0,16},{1,17},{2,18},{3,19},{4,12},{5,13},{6,14},{7,15},{8,24},{9,... | collective-permute-start | bytes 2359304 | tf_op jit(solution)/shard_map/ppermute | solution.py:263
  56.7 10.1 %collective-permute-start.17 = (bf16[512,128]{1,0:T(8,128)(2,1)S(1)}, bf16[512,128]{1,0:T(8,128)(2,1)S(1)}, u32[]{:S(2)}, u32[]{:S(2)}) collective-permute-start(bf16[512,128]{1,0:T(8,128)(2,1)S(1)} %get-tuple-element.54.refs_0_), channel_id=1, source_target_pairs={{0,1},{1,0},{2,3},{3,2},{4,6},{5,7},{6,4},{7,5},{8,9},{9,8},{10,11... | collective-permute-start | bytes 393224 | tf_op jit(solution)/shard_map/ppermute | solution.py:263
  59.3 8.7 %collective-permute-start.18 = (bf16[512,128]{1,0:T(8,128)(2,1)S(1)}, bf16[512,128]{1,0:T(8,128)(2,1)S(1)}, u32[]{:S(2)}, u32[]{:S(2)}) collective-permute-start(bf16[512,128]{1,0:T(8,128)(2,1)S(1)} %get-tuple-element.56), channel_id=1, source_target_pairs={{0,2},{1,3},{2,0},{3,1},{4,5},{5,4},{6,7},{7,6},{8,10},{9,11},{10,... | collective-permute-start | bytes 393224 | tf_op jit(solution)/shard_map/ppermute | solution.py:263
  59.7 8.3 %collective-permute-start.19 = (bf16[512,128]{1,0:T(8,128)(2,1)S(1)}, bf16[512,128]{1,0:T(8,128)(2,1)S(1)}, u32[]{:S(2)}, u32[]{:S(2)}) collective-permute-start(bf16[512,128]{1,0:T(8,128)(2,1)S(1)} %get-tuple-element.57), channel_id=1, source_target_pairs={{0,3},{1,2},{2,1},{3,0},{4,7},{5,6},{6,5},{7,4},{8,11},{9,10},{10,... | collective-permute-start | bytes 393224 | tf_op jit(solution)/shard_map/ppermute | solution.py:263
  68.1 12.1 %collective-permute-start.22 = (bf16[3072,128]{1,0:T(8,128)(2,1)S(1)}, bf16[3072,128]{1,0:T(8,128)(2,1)S(1)}, u32[]{:S(2)}, u32[]{:S(2)}) collective-permute-start(bf16[3072,128]{1,0:T(8,128)(2,1)S(1)} %shard_map.73.refs_0_), channel_id=1, source_target_pairs={{0,16},{1,17},{2,18},{3,19},{4,12},{5,13},{6,14},{7,15},{8,24},{9,... | collective-permute-start | bytes 2359304 | tf_op jit(solution)/shard_map/ppermute | solution.py:263
  71.4 18.2 %collective-permute-start.25 = (bf16[512,128]{1,0:T(8,128)(2,1)S(1)}, bf16[512,128]{1,0:T(8,128)(2,1)S(1)}, u32[]{:S(2)}, u32[]{:S(2)}) collective-permute-start(bf16[512,128]{1,0:T(8,128)(2,1)S(1)} %get-tuple-element.61.refs_0_), channel_id=1, source_target_pairs={{0,3},{1,2},{2,1},{3,0},{4,7},{5,6},{6,5},{7,4},{8,11},{9,10},{10,... | collective-permute-start | bytes 393224 | tf_op jit(solution)/shard_map/ppermute | solution.py:263
  76.3 12.3 %collective-permute-start.23 = (bf16[512,128]{1,0:T(8,128)(2,1)S(1)}, bf16[512,128]{1,0:T(8,128)(2,1)S(1)}, u32[]{:S(2)}, u32[]{:S(2)}) collective-permute-start(bf16[512,128]{1,0:T(8,128)(2,1)S(1)} %get-tuple-element.66.refs_0_), channel_id=1, source_target_pairs={{0,1},{1,0},{2,3},{3,2},{4,6},{5,7},{6,4},{7,5},{8,9},{9,8},{10,11... | collective-permute-start | bytes 393224 | tf_op jit(solution)/shard_map/ppermute | solution.py:263
  77.4 12.2 %collective-permute-start.24 = (bf16[512,128]{1,0:T(8,128)(2,1)S(1)}, bf16[512,128]{1,0:T(8,128)(2,1)S(1)}, u32[]{:S(2)}, u32[]{:S(2)}) collective-permute-start(bf16[512,128]{1,0:T(8,128)(2,1)S(1)} %get-tuple-element.70), channel_id=1, source_target_pairs={{0,2},{1,3},{2,0},{3,1},{4,5},{5,4},{6,7},{7,6},{8,10},{9,11},{10,... | collective-permute-start | bytes 393224 | tf_op jit(solution)/shard_map/ppermute | solution.py:263
  82.6 10.5 %collective-permute-start.26 = (bf16[256,128]{1,0:T(8,128)(2,1)S(1)}, bf16[256,128]{1,0:T(8,128)(2,1)S(1)}, u32[]{:S(2)}, u32[]{:S(2)}) collective-permute-start(bf16[256,128]{1,0:T(8,128)(2,1)S(1)} %get-tuple-element.67.refs_0_), channel_id=1, source_target_pairs={{0,3},{1,2},{2,1},{3,0},{4,7},{5,6},{6,5},{7,4},{8,11},{9,10},{10,... | collective-permute-start | bytes 196616 | tf_op jit(solution)/shard_map/ppermute | solution.py:263
  87.1 5.9 %collective-permute-start.27 = (bf16[256,128]{1,0:T(8,128)(2,1)S(1)}, bf16[256,128]{1,0:T(8,128)(2,1)S(1)}, u32[]{:S(2)}, u32[]{:S(2)}) collective-permute-start(bf16[256,128]{1,0:T(8,128)(2,1)S(1)} %get-tuple-element.72), channel_id=1, source_target_pairs={{0,2},{1,3},{2,0},{3,1},{4,5},{5,4},{6,7},{7,6},{8,10},{9,11},{10,... | collective-permute-start | bytes 196616 | tf_op jit(solution)/shard_map/ppermute | solution.py:263
  88.6 4.4 %collective-permute-start.28 = (bf16[256,128]{1,0:T(8,128)(2,1)S(1)}, bf16[256,128]{1,0:T(8,128)(2,1)S(1)}, u32[]{:S(2)}, u32[]{:S(2)}) collective-permute-start(bf16[256,128]{1,0:T(8,128)(2,1)S(1)} %get-tuple-element.68.refs_0_), channel_id=1, source_target_pairs={{0,1},{1,0},{2,3},{3,2},{4,6},{5,7},{6,4},{7,5},{8,9},{9,8},{10,11... | collective-permute-start | bytes 196616 | tf_op jit(solution)/shard_map/ppermute | solution.py:263
  89.6 3.5 %collective-permute-start.29 = (bf16[1024,128]{1,0:T(8,128)(2,1)S(1)}, bf16[1024,128]{1,0:T(8,128)(2,1)S(1)}, u32[]{:S(2)}, u32[]{:S(2)}) collective-permute-start(bf16[1024,128]{1,0:T(8,128)(2,1)S(1)} %get-tuple-element.75), channel_id=1, source_target_pairs={{0,4},{1,5},{2,6},{3,7},{4,0},{5,1},{6,2},{7,3},{8,12},{9,13},{10,... | collective-permute-start | bytes 786440 | tf_op jit(solution)/shard_map/ppermute | solution.py:263
  93.1 1.4 %collective-permute-start.30 = (bf16[512,128]{1,0:T(8,128)(2,1)S(1)}, bf16[512,128]{1,0:T(8,128)(2,1)S(1)}, u32[]{:S(2)}, u32[]{:S(2)}) collective-permute-start(bf16[512,128]{1,0:T(8,128)(2,1)S(1)} %get-tuple-element.76), channel_id=1, source_target_pairs={{0,4},{1,5},{2,6},{3,7},{4,0},{5,1},{6,2},{7,3},{8,12},{9,13},{10,... | collective-permute-start | bytes 393224 | tf_op jit(solution)/shard_map/ppermute | solution.py:263
  (4 other events, 4.2 us)
